TPU v7x, 32 devices: a whole 2x2x4 slice. The times are simulated.
32 devices in a mesh: row: 8 (over y, x, core), col: 4 (over z).
Axes of the slice: x: 2, y: 2, z: 4, core: 2. Of those that a mesh axis runs over, the one named last changes fastest.
Arguments:
- features: bfloat16 [8192, 1024], P(('row', 'col')), may hold values from -6 to 6
- weight: bfloat16 [1024, 512], replicated, may hold values from -0.1875 to 0.1875
- source_norm: float32 [8192], P(('row', 'col')), may hold values from 0.01 to 0.1
- target_norm: float32 [8192], P(('row', 'col')), may hold values from 0.3 to 3
- tile_weights: bfloat16 [32, 64, 128, 128], P(('row', 'col')), may hold values from 0 to 1
- tile_source: int32 [32, 64], P(('row', 'col')), may hold values from 0 to 7
- tile_target: int32 [32, 64], P(('row', 'col')), may hold values from 0 to 15, as said below
- tile_count: int32 [32], P(('row', 'col')), may hold values from 1 to 64, as said below
- mirror_tile: int32 [32, 16], P(('row', 'col')), may hold values from 0 to 2, as said below
Outputs:
- activated: bfloat16 [8192, 512], P(('row', 'col'))
Inputs may be any that keep to these rules, and one draw needn't show every extreme that they name: `mirror_tile`: the value 2 marks an empty slot; slots k * 2 to k * 2 + 1 hold node tiles of grid row k. In every draw the slots of some grid row are filled on every device. `tile_target`: every slot named holds a node tile of the same device's mirror_tile row, not 2. `tile_count`: some device uses all 64 slots in every draw; counts are uneven.
All inputs are finite; a program needn't handle non-finite values.
Results may differ from a plain program's by a relative error of at most 0.015.
Values may be sent and summed in bfloat16 or wider, within the bound.
No kernel may reach another device: no remote copies, remote signals or barrier semaphores. Data moves between devices by JAX's collectives and lax.ppermute only.
A program may use at most 128 MiB of HBM per device.

v0:
```python
import jax
import jax.numpy as jnp
from jax import lax
from jax.sharding import PartitionSpec as P


def add_tile(totals, tile, block, slot):
    current = lax.dynamic_index_in_dim(totals, slot, 0, keepdims=False)
    updated = current + jnp.dot(tile, block, preferred_element_type=jnp.float32)
    return lax.dynamic_update_index_in_dim(totals, updated, slot, 0)


def per_device(
    features,
    weight,
    source_norm,
    target_norm,
    tile_weights,
    tile_source,
    tile_target,
    tile_count,
    mirror_tile,
):
    tile_rows = tile_weights.shape[-1]
    hidden = weight.shape[1]
    slots = mirror_tile.shape[1]
    tiles = tile_weights[0]
    sources = tile_source[0]
    targets = tile_target[0]
    count = tile_count[0]
    projected = jnp.dot(features, weight, preferred_element_type=jnp.float32)
    empty = jnp.zeros((slots, tile_rows, hidden), jnp.float32)
    rows_in = lax.all_gather(features, "col", axis=0, tiled=True)
    norms = lax.all_gather(source_norm.astype(jnp.bfloat16), "col", axis=0, tiled=True).astype(
        jnp.float32
    )
    block_rows = (
        norms[:, None] * jnp.dot(rows_in, weight, preferred_element_type=jnp.float32)
    ).astype(jnp.bfloat16)
    span = block_rows.shape[0] // tile_rows

    def visit(position, carry):
        offset = sources[position]
        inside = (offset >= 0) & (offset < span)

        def take(inner):
            place = jnp.clip(offset, 0, span - 1) * tile_rows
            block = lax.dynamic_slice_in_dim(block_rows, place, tile_rows, 0)
            return add_tile(inner, tiles[position], block, targets[position])

        return lax.cond(inside, take, lambda inner: inner, carry)

    partial_value = lax.fori_loop(0, count, visit, empty)
    owners = lax.axis_size("row")
    per_owner = slots // owners
    outgoing = partial_value.astype(jnp.bfloat16).reshape(owners, per_owner * tile_rows, hidden)
    labels = mirror_tile[0].reshape(owners, per_owner)
    arrived, arrived_labels = (
        lax.all_to_all(outgoing, "row", split_axis=0, concat_axis=0, tiled=True),
        lax.all_to_all(labels, "row", split_axis=0, concat_axis=0, tiled=True),
    )
    own_tiles = features.shape[0] // tile_rows
    selector = (
        arrived_labels.reshape(slots)[:, None] == jnp.arange(own_tiles, dtype=jnp.int32)[None, :]
    ).astype(jnp.bfloat16)
    summed = jnp.einsum(
        "sv,sik->vik",
        selector,
        arrived.reshape(slots, tile_rows, hidden),
        preferred_element_type=jnp.float32,
    )
    gathered = summed.reshape(own_tiles * tile_rows, hidden) + projected
    return jnp.maximum(target_norm[:, None] * gathered, 0.0).astype(jnp.bfloat16)


def solution(mesh):
    in_specs = (
        P(("row", "col"), None),
        P(),
        P(("row", "col")),
        P(("row", "col")),
        P(("row", "col"), None, None, None),
        P(("row", "col"), None),
        P(("row", "col"), None),
        P(("row", "col")),
        P(("row", "col"), None),
    )
    out_specs = P(("row", "col"), None)
    return jax.shard_map(
        per_device, mesh=mesh, in_specs=in_specs, out_specs=out_specs, check_vma=False
    )
```

profile of v0, /device:TPU:16, one launch (start us, length us, event | category | flops | bytes accessed | tf_op | source)
XLA Modules:
  0.0 635.1 jit_solution(17505561892887142811)
XLA Ops:
  7.8 1.3 reduce.6
  9.8 3.7 all-to-all-start
  14.2 9.4 %all-gather = bf16[4,1,256]{2,1,0:T(2,128)(2,1)S(1)} all-gather(bf16[1,1,256]{2,1,0:T(2,128)(2,1)S(1)} %reshape.19), channel_id=1, replica_groups=mesh['row'=8,'col'=4] {'col'}, dimensions={0}, use_global_device_ids=true | all-gather | bytes 2560 | tf_op jit(solution)/shard_map/all_gather | solution.py:34
  23.6 31.0 %all-gather.3.cloned.1.call-done = bf16[1024,1024]{1,0:T(8,128)(2,1)} async-done(((bf16[256,1024]{1,0:T(8,128)(2,1)}), bf16[1024,1024]{1,0:T(8,128)(2,1)}) %all-gather.3.cloned.1.call-update) | async-done | bytes 2097168 | tf_op jit(solution)/shard_map/all_gather | solution.py:33
  54.6 2.8 multiply_convert_fusion
  57.5 2.5 broadcast_in_dim.10
  60.0 67.3 %while.13 = (s32[]{:T(128)}, f32[16,128,512]{2,1,0:T(8,128)}, s32[]{:T(128)}, s32[64]{0:T(128)S(1)}, s32[64]{0:T(128)S(1)}, /*index=5*/bf16[64,128,128]{2,1,0:T(...) while((s32[]{:T(128)}, f32[16,128,512]{2,1,0:T(8,128)}, ...), condition=%wide.region_3.4_spmd, body=%wide.region_0.3_spmd.sunk | while | flops 16842772 | bytes 1212819 | solution.py:53
  62.4 6.0 conditional.2
  65.1 1.0 constant_dynamic-slice_fusion
  66.7 1.6 fusion.1
  70.7 6.0 conditional.2
  73.5 1.0 constant_dynamic-slice_fusion
  75.0 1.6 fusion.1
  79.0 6.0 conditional.2
  81.8 1.0 constant_dynamic-slice_fusion
  83.3 1.7 fusion.1
  87.4 6.0 conditional.2
  91.7 1.6 fusion.1
  95.7 6.0 conditional.2
  98.5 1.0 constant_dynamic-slice_fusion
  100.0 1.6 fusion.1
  104.0 6.0 conditional.2
  108.3 1.7 fusion.1
  112.4 5.9 conditional.2
  116.7 1.6 fusion.1
  120.7 5.9 conditional.2
  125.0 1.6 fusion.1
  127.3 3.8 convert_element_type.22
  131.1 468.0 %all-to-all-start.1 = ((bf16[8,256,512]{2,1,0:T(8,128)(2,1)}), bf16[8,256,512]{2,1,0:T(8,128)(2,1)S(1)}, u32[]{:S(2)}, u32[]{:S(2)}) async-start(bf16[8,256,512]{2,1,0:T(8,128)(2,1)} %bitcast.12), calls=%async_computation.1 | async-start | bytes 4194304 | tf_op jit(solution)/shard_map/all_to_all | solution.py:59
  599.8 25.9 %all-to-all-done.1 = bf16[8,256,512]{2,1,0:T(8,128)(2,1)S(1)} async-done(((bf16[8,256,512]{2,1,0:T(8,128)(2,1)}), bf16[8,256,512]{2,1,0:T(8,128)(2,1)S(1)}, u32[]{:S(2)}, u32[]{:S(2)}) %all-to-all-start.1) | async-done | bytes 2097184 | tf_op jit(solution)/shard_map/all_to_all | solution.py:59
  625.7 1.3 fusion.6
  627.1 1.2 fusion.10
  (41 shorter events, 17.4 us)
Async XLA Ops:
  6.5 48.1 %copy-start = (bf16[1024,512]{1,0:T(8,128)(2,1)S(1)}, bf16[1024,512]{1,0:T(8,128)(2,1)}, u32[]{:S(2)}) copy-start(bf16[1024,512]{1,0:T(8,128)(2,1)} %param.14) | copy-start | bytes 3145732
  6.5 48.1 %all-gather.3.cloned.1.call-start = ((), (), s32[]{:S(2)}) async-start(), calls=%async_computation.2 | async-start | bytes 2621440 | tf_op jit(solution)/shard_map/all_gather | solution.py:33
  9.8 121.3 %all-to-all-start = ((s32[8,1,2]{2,1,0:T(1,128)}), s32[8,1,2]{2,1,0:T(1,128)S(1)}, u32[]{:S(2)}, u32[]{:S(2)}) async-start(s32[8,1,2]{2,1,0:T(1,128)} %bitcast.5), calls=%async_computation | async-start | bytes 8192 | tf_op jit(solution)/shard_map/all_to_all | solution.py:60
  57.5 2.5 copy-start.3
  57.5 2.5 copy-start.4
  131.1 494.6 %all-to-all-start.1 = ((bf16[8,256,512]{2,1,0:T(8,128)(2,1)}), bf16[8,256,512]{2,1,0:T(8,128)(2,1)S(1)}, u32[]{:S(2)}, u32[]{:S(2)}) async-start(bf16[8,256,512]{2,1,0:T(8,128)(2,1)} %bitcast.12), calls=%async_computation.1 | async-start | bytes 4194304 | tf_op jit(solution)/shard_map/all_to_all | solution.py:59
  599.1 28.0 %copy-start.2 = (f32[256]{0:T(256)S(1)}, f32[256]{0:T(256)}, u32[]{:S(2)}) copy-start(f32[256]{0:T(256)} %param.16) | copy-start | bytes 3076
  625.7 1.4 copy-start.1
Sparse Core Ops, SparseCore 0:
  8.9 45.6 all-gather.2
where the time goes:
time: 647 us; the launch traced here: 635 us
  starting transfers between devices  472 us (73%)
  waiting for transfers between devices  57.6 us (9%)
  loops' own time  36.4 us (6%)
  local copies, waits for them, and re-layouts  21.7 us (3%)
  matrix products  18.4 us (3%)
  between operations  13.5 us (2%)
  blocking collectives  9.41 us (1%)
    all_to_all x1, starting transfers between devices, per_device(): lax.all_to_all(outgoing, 'row', split_axis=0, concat_axis=0, tiled=True)  468 us
    all_gather x1, waiting for transfers between devices, per_device(): rows_in = lax.all_gather(features, 'col', axis=0, tiled=True)  31 us
    all_to_all x1, waiting for transfers between devices, per_device(): lax.all_to_all(outgoing, 'row', split_axis=0, concat_axis=0, tiled=True)  25.9 us
    another operation x8, loops' own time, visit(): return lax.cond(inside, take, lambda inner: inner, carry)  21.4 us
    another operation x1, loops' own time, per_device(): partial_value = lax.fori_loop(0, count, visit, empty)  15 us
    dot_general x8, matrix products, add_tile(): updated = current + jnp.dot(tile, block, preferred_element_type=jnp.float32)  13.1 us
  transfers between devices with their start and end apart: 3, of which 2 were waited for; matrix products, arithmetic and copies ran while one was open for 7% of the time, Pallas kernels for 0%

commit v1 on v0

v1 whole, which is shorter than its diff:
```python
import functools

import jax
import jax.numpy as jnp
from jax import lax
from jax.experimental import pallas as pl
from jax.experimental.pallas import tpu as pltpu
from jax.sharding import PartitionSpec as P

DENSE_ELEMENTS = 4 * 1024 * 1024
CHUNKS = 2
WEIGHTS = ((20, 20), (0, 20))
MIB = 1024 * 1024
SMEM = pl.BlockSpec(memory_space=pltpu.SMEM)
VMEM = pl.BlockSpec(memory_space=pltpu.VMEM)
HBM = pl.BlockSpec(memory_space=pltpu.HBM)


def params(mib):
    return pltpu.CompilerParams(vmem_limit_bytes=int(mib * MIB))


def cost(flops, moved):
    return pl.CostEstimate(flops=flops, bytes_accessed=moved, transcendentals=0)


def in_hbm(*values):
    return [pltpu.with_memory_space_constraint(value, pltpu.HBM) for value in values]


def rows_to_lanes(row, lanes):
    return jnp.broadcast_to(row, (lanes, row.shape[1])).T


def project_kernel(features_hbm, weight_hbm, norm_hbm, projected, *refs):
    *scaled, features, weight, norm, sems = refs
    copies = [
        pltpu.make_async_copy(source, target, sems.at[k])
        for k, (source, target) in enumerate(
            [(weight_hbm, weight), (features_hbm, features), (norm_hbm, norm)]
        )
    ]
    for copy in copies:
        copy.start()
    for copy in copies:
        copy.wait()
    lanes = norm.shape[1]
    value = jnp.dot(features[...], weight[...], preferred_element_type=jnp.float32)
    projected[...] = value
    width = scaled[0].shape[1]
    for part in range(norm.shape[0]):
        factor = rows_to_lanes(norm[part : part + 1, :], lanes)
        for column in range(0, value.shape[1], lanes):
            piece = value[part * lanes : (part + 1) * lanes, column : column + lanes]
            target = scaled[column // width]
            start = column % width
            target[part * lanes : (part + 1) * lanes, start : start + lanes] = (
                factor * piece
            ).astype(target.dtype)


def project(features, weight, source_norm, chunks):
    rows, depth = features.shape
    hidden = weight.shape[1]
    norm = source_norm.reshape(-1, 128)
    return pl.pallas_call(
        project_kernel,
        out_shape=[jax.ShapeDtypeStruct((rows, hidden), jnp.float32)]
        + [jax.ShapeDtypeStruct((rows, hidden // chunks), jnp.bfloat16)] * chunks,
        in_specs=[HBM] * 3,
        out_specs=[VMEM] * (1 + chunks),
        scratch_shapes=[
            pltpu.VMEM(features.shape, features.dtype),
            pltpu.VMEM(weight.shape, weight.dtype),
            pltpu.VMEM(norm.shape, norm.dtype),
            pltpu.SemaphoreType.DMA((3,)),
        ],
        compiler_params=params(12),
        cost_estimate=cost(2 * rows * depth * hidden, 2 * depth * (rows + hidden)),
    )(*in_hbm(features, weight, norm))


def merge_kernel(
    own_tiles, per_owner, row, column, count, sources_hbm, targets_hbm, labels_hbm, tiles_hbm, out,
    total, tiles, sources, targets, labels, sems, tile_sems,
):
    small = [
        pltpu.make_async_copy(source, target, sems.at[k])
        for k, (source, target) in enumerate(
            [(sources_hbm, sources), (targets_hbm, targets), (labels_hbm, labels)]
        )
    ]
    parts = tile_sems.shape[0]
    each = tiles.shape[0] // parts
    large = [
        pltpu.make_async_copy(
            tiles_hbm.at[0, pl.ds(k * each, each)],
            tiles.at[pl.ds(k * each, each)],
            tile_sems.at[k],
        )
        for k in range(parts)
    ]
    for copy in small + large:
        copy.start()
    spare, span = total.shape[0] - 1, total.shape[1]
    owners = spare // own_tiles
    total[...] = jnp.zeros_like(total)
    my_row, my_column, used = row[0], column[0], count[0]
    for copy in small:
        copy.wait()

    def add(slot):
        target, source = targets[0, slot], sources[0, slot]
        label = labels[0, target]
        apart = lax.bitwise_xor(target // per_owner, my_row)
        position = (1 - apart % 2) * (owners // 2) + apart // 2
        place = jnp.where(label < own_tiles, position * own_tiles + label, spare)
        block = lax.bitwise_xor(source // own_tiles, my_column)
        total[place, block * own_tiles + source % own_tiles] += tiles[slot].astype(jnp.float32)

    for k, copy in enumerate(large):
        copy.wait()
        pl.loop(k * each, jnp.minimum(used, (k + 1) * each))(add)

    rows = total.shape[2]
    for source in range(span):
        for place in range(spare):
            out[place * rows : (place + 1) * rows, source * rows : (source + 1) * rows] = total[
                place, source
            ].astype(out.dtype)


def merge_tiles(own_tiles, owners, span, index_args, tile_weights):
    sources, targets, count, labels = index_args
    _, capacity, rows, _ = tile_weights.shape
    places = owners * own_tiles
    row = lax.axis_index("row").astype(jnp.int32).reshape(1)
    column = lax.axis_index("col").astype(jnp.int32).reshape(1)
    return pl.pallas_call(
        functools.partial(merge_kernel, own_tiles, labels.shape[1] // owners),
        out_shape=jax.ShapeDtypeStruct((places * rows, span * rows), jnp.bfloat16),
        in_specs=[SMEM] * 3 + [HBM] * 4,
        out_specs=VMEM,
        scratch_shapes=[
            pltpu.VMEM((places + 1, span, rows, rows), jnp.float32),
            pltpu.VMEM(tile_weights.shape[1:], tile_weights.dtype),
            pltpu.SMEM(sources.shape, jnp.int32),
            pltpu.SMEM(targets.shape, jnp.int32),
            pltpu.SMEM(labels.shape, jnp.int32),
            pltpu.SemaphoreType.DMA((3,)),
            pltpu.SemaphoreType.DMA((4 if capacity % 4 == 0 else 1,)),
        ],
        compiler_params=params(24),
        cost_estimate=cost(8 * MIB, 12 * MIB),
    )(row, column, count, *in_hbm(sources, targets, labels, tile_weights))


def product_kernel(first, matrix, *refs):
    *blocks, out = refs
    rows = blocks[0].shape[0]

    @pl.loop(0, out.shape[0] // rows)
    def _(place):
        from_row = pl.multiple_of((first + place) * rows, rows)
        value = None
        for k, block in enumerate(blocks):
            term = jnp.dot(
                matrix[pl.ds(from_row, rows), k * rows : (k + 1) * rows],
                block[...],
                preferred_element_type=jnp.float32,
            )
            value = term if value is None else value + term
        out[pl.ds(pl.multiple_of(place * rows, rows), rows), :] = value.astype(out.dtype)


def product(matrix, blocks, half, dtype, weight):
    rows, width = blocks[0].shape
    total, depth = matrix.shape
    return pl.pallas_call(
        functools.partial(product_kernel, half * (total // rows // 2)),
        out_shape=jax.ShapeDtypeStruct((total // 2, width), dtype),
        in_specs=[VMEM] * (1 + len(blocks)),
        out_specs=VMEM,
        compiler_params=params(16),
        cost_estimate=cost(weight * total * depth * width, 1),
    )(matrix, *blocks)


def join_kernel(stay, came, kept, *sent):
    rows = kept.shape[0]
    value = stay[...].astype(jnp.float32) + came[...].astype(jnp.float32)
    kept[...] = value[:rows]
    for place, out in enumerate(sent):
        out[...] = value[(place + 1) * rows : (place + 2) * rows].astype(out.dtype)


def join(stay, came, rows):
    total, width = stay.shape
    parts = total // rows
    return pl.pallas_call(
        join_kernel,
        out_shape=[jax.ShapeDtypeStruct((rows, width), jnp.float32)]
        + [jax.ShapeDtypeStruct((rows, width), jnp.bfloat16)] * (parts - 1),
        in_specs=[VMEM] * 2,
        out_specs=[VMEM] * parts,
        compiler_params=params(12),
        cost_estimate=cost(1, 1),
    )(stay, came)


def finish_kernel(chunks, projected, norm, *refs):
    out = refs[-1]
    per_chunk = (len(refs) - 1) // chunks
    lanes = norm.shape[1]
    width = refs[0].shape[1]
    for part in range(norm.shape[0]):
        factor = rows_to_lanes(norm[part : part + 1, :], lanes)
        here = slice(part * lanes, (part + 1) * lanes)
        for column in range(0, out.shape[1], lanes):
            pieces = refs[column // width * per_chunk : (column // width + 1) * per_chunk]
            start = column % width
            value = projected[here, column : column + lanes]
            for piece in pieces:
                value += piece[here, start : start + lanes].astype(jnp.float32)
            out[here, column : column + lanes] = jnp.maximum(factor * value, 0.0).astype(out.dtype)


def finish(projected, target_norm, pieces):
    rows, hidden = projected.shape
    flat = [piece for chunk in pieces for piece in chunk]
    return pl.pallas_call(
        functools.partial(finish_kernel, len(pieces)),
        out_shape=jax.ShapeDtypeStruct((rows, hidden), jnp.bfloat16),
        in_specs=[VMEM] * (2 + len(flat)),
        out_specs=VMEM,
        compiler_params=params(12),
        cost_estimate=cost(6 * rows * hidden, 16 * rows * hidden),
    )(projected, target_norm.reshape(-1, 128), *flat)


def visit_kernel(own_tiles, per_owner, sources, targets, count, labels, tiles, blocks, out, total):
    spare, rows = total.shape[0] - 1, total.shape[1]
    total[...] = jnp.zeros_like(total)

    @pl.loop(0, count[0])
    def _(slot):
        target = targets[0, slot]
        label = labels[0, target]
        place = jnp.where(label < own_tiles, target // per_owner * own_tiles + label, spare)
        start = pl.multiple_of(sources[0, slot] * rows, rows)
        total[place] += jnp.dot(
            tiles[0, slot], blocks[pl.ds(start, rows), :], preferred_element_type=jnp.float32
        )

    @pl.loop(0, spare)
    def _(place):
        out[pl.ds(pl.multiple_of(place * rows, rows), rows), :] = total[place].astype(out.dtype)


def visit_tiles(own_tiles, owners, index_args, tile_weights, blocks):
    slots = index_args[-1].shape[1]
    rows = tile_weights.shape[-1]
    places = owners * own_tiles
    hidden = blocks.shape[1]
    return pl.pallas_call(
        functools.partial(visit_kernel, own_tiles, slots // owners),
        out_shape=jax.ShapeDtypeStruct((places * rows, hidden), jnp.bfloat16),
        in_specs=[SMEM] * 4 + [VMEM] * 2,
        out_specs=VMEM,
        scratch_shapes=[pltpu.VMEM((places + 1, rows, hidden), jnp.float32)],
        compiler_params=params(56),
    )(*index_args, tile_weights, blocks)


def swap(value, axis, apart):
    pairs = [(i, i ^ apart) for i in range(lax.axis_size(axis))]
    return lax.ppermute(value, axis, pairs)


def exchange(sent):
    return [swap(value, "row", 2 * (k + 1)) for k, value in enumerate(sent)]


def per_device(
    features,
    weight,
    source_norm,
    target_norm,
    tile_weights,
    tile_source,
    tile_target,
    tile_count,
    mirror_tile,
):
    tile_rows = tile_weights.shape[-1]
    own_rows = features.shape[0]
    own_tiles = own_rows // tile_rows
    owners, columns = lax.axis_size("row"), lax.axis_size("col")
    span = own_tiles * columns
    index_args = (tile_source, tile_target, tile_count, mirror_tile)

    cells = owners * own_tiles * span * tile_rows * tile_rows
    if columns != 4 or owners & (owners - 1) or cells > DENSE_ELEMENTS:
        projected = jnp.dot(features, weight, preferred_element_type=jnp.float32)
        scaled = (source_norm[:, None] * projected).astype(jnp.bfloat16)
        blocks = lax.all_gather(scaled, "col", axis=0, tiled=True)
        partial_value = visit_tiles(own_tiles, owners, index_args, tile_weights, blocks)
        outgoing = partial_value.reshape(owners, own_rows, -1)
        arrived = lax.all_to_all(outgoing, "row", split_axis=0, concat_axis=0, tiled=True)
        gathered = jnp.sum(arrived.astype(jnp.float32), axis=0) + projected
        return jnp.maximum(target_norm[:, None] * gathered, 0.0).astype(jnp.bfloat16)

    projected, *scaled = project(features, weight, source_norm, CHUNKS)
    matrix = merge_tiles(own_tiles, owners, span, index_args, tile_weights)
    across = [swap(own, "col", 3) for own in scaled]
    beside = [swap(own, "col", 1) for own in scaled]
    across[0], matrix = lax.optimization_barrier((across[0], matrix))
    passed = [swap(value, "col", 1) for value in across]
    pieces, sent = [], None
    for blocks, wait in zip(zip(scaled, beside, passed, across), WEIGHTS):
        late = blocks
        if sent is not None:
            moved = exchange(sent)
            blocks, _ = lax.optimization_barrier((blocks, sent))
            late, moved = lax.optimization_barrier((blocks, moved))
            pieces[-1] += moved
        away = product(matrix, blocks, 0, jnp.bfloat16, wait[0])
        stay = product(matrix, late, 1, jnp.float32, wait[1])
        kept, *sent = join(stay, swap(away, "row", 1), own_rows)
        pieces.append([kept])
    pieces[-1] += exchange(sent)
    return finish(projected, target_norm, pieces)


def solution(mesh):
    in_specs = (
        P(("row", "col"), None),
        P(),
        P(("row", "col")),
        P(("row", "col")),
        P(("row", "col"), None, None, None),
        P(("row", "col"), None),
        P(("row", "col"), None),
        P(("row", "col")),
        P(("row", "col"), None),
    )
    out_specs = P(("row", "col"), None)
    return jax.shard_map(
        per_device, mesh=mesh, in_specs=in_specs, out_specs=out_specs, check_vma=False
    )
```

time: 647 us -> 43.5 us (0.07)
  the two profiles are of different devices: /device:TPU:16 before, /device:TPU:0 now
where the time goes in v1:
time: 43.5 us; the launch traced here: 43.2 us
  starting transfers between devices  18.9 us (43%)
  waiting for transfers between devices  13 us (30%)
  Pallas kernels  10.6 us (24%)
  between operations  0.76 us (2%)
    ppermute x14, starting transfers between devices, swap(): return lax.ppermute(value, axis, pairs)  18.9 us
    ppermute x14, waiting for transfers between devices, swap(): return lax.ppermute(value, axis, pairs)  13 us
    pallas_call x4, Pallas kernels, product(): pl.pallas_call(functools.partial(product_kernel, half * (total // rows //...  4.92 us
    pallas_call x1, Pallas kernels, merge_tiles(): pl.pallas_call(functools.partial(merge_kernel, own_tiles, labels.shape[1]...  2.77 us
    pallas_call x1, Pallas kernels, project(): pl.pallas_call(project_kernel, out_shape=[jax.ShapeDtypeStruct((rows, hid...  1.82 us
    pallas_call x1, Pallas kernels, finish(): pl.pallas_call(functools.partial(finish_kernel, len(pieces)), out_shape=j...  0.88 us
  transfers between devices with their start and end apart: 14, of which 8 were waited for; matrix products, arithmetic and copies ran while one was open for 0% of the time, Pallas kernels for 18%

profile of v1, /device:TPU:0, one launch (start us, length us, event | category | flops | bytes accessed | tf_op | source)
XLA Modules:
  0.0 43.2 jit_solution(9709074395802878158)
XLA Ops:
  0.0 1.8 %shard_map.91 = (f32[256,512]{1,0:T(8,128)S(1)}, bf16[256,256]{1,0:T(8,128)(2,1)S(1)}, bf16[256,256]{1,0:T(8,128)(2,1)S(1)}) custom-call(bf16[256,1024]{1,0:T(8,128)(2,1)} %features_hbm.1, bf16[1024,512]{1,0:T(8,128)(2,1)} %weight_hbm.1, f32[2,128]{1,0:T(2,128)} %bitcast.5), custom_call_target="tpu_custom_call" | custom-call | flops 268435456 | bytes 1572864 | tf_op jit(solution)/shard_map/pallas_call | solution.py:66
  1.8 5.1 %collective-permute-start = (bf16[256,256]{1,0:T(8,128)(2,1)S(1)}, bf16[256,256]{1,0:T(8,128)(2,1)S(1)}, u32[]{:S(2)}, u32[]{:S(2)}) collective-permute-start(bf16[256,256]{1,0:T(8,128)(2,1)S(1)} %get-tuple-element.30.refs_0_), channel_id=1, source_target_pairs={{0,3},{1,2},{2,1},{3,0},{4,7},{5,6},{6,5},{7,4},{8,11},{9,10},{10,... | collective-permute-start | bytes 393224 | tf_op jit(solution)/shard_map/ppermute | solution.py:277
  6.9 0.9 %collective-permute-start.5 = (bf16[256,256]{1,0:T(8,128)(2,1)S(1)}, bf16[256,256]{1,0:T(8,128)(2,1)S(1)}, u32[]{:S(2)}, u32[]{:S(2)}) collective-permute-start(bf16[256,256]{1,0:T(8,128)(2,1)S(1)} %get-tuple-element.45.refs_0_), channel_id=1, source_target_pairs={{0,3},{1,2},{2,1},{3,0},{4,7},{5,6},{6,5},{7,4},{8,11},{9,10},{10,... | collective-permute-start | bytes 393224 | tf_op jit(solution)/shard_map/ppermute | solution.py:277
  8.5 2.8 %shard_map.92.matrix = bf16[2048,1024]{1,0:T(8,128)(2,1)S(1)} custom-call(s32[1]{0:T(128)} %bitcast.2.row, s32[1]{0:T(128)} %bitcast.3.column, s32[1]{0:T(128)S(6)} %copy.10.count, s32[1,64]{1,0:T(1,128)} %sources_hbm.1, s32[1,64]{1,0:T(1,128)} %targets_hbm.1, s32[1,16]{1,0:T(1,128)} %labels_hbm.1, bf16[1,64,128,128]{3,2,1,0:T(8,128)(2,1)} %tiles_hbm.1), custom_call_target="tpu_custom_call" | custom-call | flops 8388608 | bytes 12582912 | tf_op jit(solution)/shard_map/pallas_call | solution.py:139
  11.3 0.0 collective-permute-done.refs_3_
  11.3 3.4 %collective-permute-start.2 = (bf16[256,256]{1,0:T(8,128)(2,1)S(1)}, bf16[256,256]{1,0:T(8,128)(2,1)S(1)}, u32[]{:S(2)}, u32[]{:S(2)}) collective-permute-start(bf16[256,256]{1,0:T(8,128)(2,1)S(1)} %collective-permute-done.refs_3_), channel_id=1, source_target_pairs={{0,1},{1,0},{2,3},{3,2},{4,5},{5,4},{6,7},{7,6},{8,9},{9,8},{10,11... | collective-permute-start | bytes 393224 | tf_op jit(solution)/shard_map/ppermute | solution.py:277
  14.8 0.0 collective-permute-start.4
  14.8 1.7 %collective-permute-done.5.refs_3_ = bf16[256,256]{1,0:T(8,128)(2,1)S(1)} collective-permute-done((bf16[256,256]{1,0:T(8,128)(2,1)S(1)}, bf16[256,256]{1,0:T(8,128)(2,1)S(1)}, u32[]{:S(2)}, u32[]{:S(2)}) %collective-permute-start.5) | collective-permute-done | bytes 131104 | tf_op jit(solution)/shard_map/ppermute | solution.py:277
  16.5 2.1 %collective-permute-start.6 = (bf16[256,256]{1,0:T(8,128)(2,1)S(1)}, bf16[256,256]{1,0:T(8,128)(2,1)S(1)}, u32[]{:S(2)}, u32[]{:S(2)}) collective-permute-start(bf16[256,256]{1,0:T(8,128)(2,1)S(1)} %collective-permute-done.5.refs_3_), channel_id=1, source_target_pairs={{0,1},{1,0},{2,3},{3,2},{4,5},{5,4},{6,7},{7,6},{8,9},{9,8},{10,11... | collective-permute-start | bytes 393224 | tf_op jit(solution)/shard_map/ppermute | solution.py:277
  18.6 0.7 %collective-permute-done.2.refs_2_ = bf16[256,256]{1,0:T(8,128)(2,1)S(1)} collective-permute-done((bf16[256,256]{1,0:T(8,128)(2,1)S(1)}, bf16[256,256]{1,0:T(8,128)(2,1)S(1)}, u32[]{:S(2)}, u32[]{:S(2)}) %collective-permute-start.2) | collective-permute-done | bytes 131104 | tf_op jit(solution)/shard_map/ppermute | solution.py:277
  19.3 1.2 %shard_map.94 = bf16[1024,256]{1,0:T(8,128)(2,1)S(1)} custom-call(bf16[2048,1024]{1,0:T(8,128)(2,1)S(1)} %shard_map.92.matrix, bf16[256,256]{1,0:T(8,128)(2,1)S(1)} %get-tuple-element.30.refs_0_, bf16[256,256]{1,0:T(8,128)(2,1)S(1)} %collective-permute-done.1.refs_1_, bf16[256,256]{1,0:T(8,128)(2,1)S(1)} %collective-permute-done.2.refs_2_, ...), custom_call_target="tpu_custom_call" | custom-call | flops 10737418240 | bytes 1 | tf_op jit(solution)/shard_map/pallas_call | solution.py:179
  20.5 0.1 collective-permute-start.3
  20.6 1.2 %shard_map.93.stay = f32[1024,256]{1,0:T(8,128)S(1)} custom-call(bf16[2048,1024]{1,0:T(8,128)(2,1)S(1)} %shard_map.92.matrix, bf16[256,256]{1,0:T(8,128)(2,1)S(1)} %get-tuple-element.30.refs_0_, bf16[256,256]{1,0:T(8,128)(2,1)S(1)} %collective-permute-done.1.refs_1_, bf16[256,256]{1,0:T(8,128)(2,1)S(1)} %collective-permute-done.2.refs_2_, ...), custom_call_target="tpu_custom_call" | custom-call | flops 10737418240 | bytes 1 | tf_op jit(solution)/shard_map/pallas_call | solution.py:179
  21.8 0.7 %collective-permute-done.3.came = bf16[1024,256]{1,0:T(8,128)(2,1)S(1)} collective-permute-done((bf16[1024,256]{1,0:T(8,128)(2,1)S(1)}, bf16[1024,256]{1,0:T(8,128)(2,1)S(1)}, u32[]{:S(2)}, u32[]{:S(2)}) %collective-permute-start.3) | collective-permute-done | bytes 524320 | tf_op jit(solution)/shard_map/ppermute | solution.py:277
  22.5 0.1 shard_map.95
  22.6 1.8 %collective-permute-start.7 = (bf16[256,256]{1,0:T(8,128)(2,1)S(1)}, bf16[256,256]{1,0:T(8,128)(2,1)S(1)}, u32[]{:S(2)}, u32[]{:S(2)}) collective-permute-start(bf16[256,256]{1,0:T(8,128)(2,1)S(1)} %get-tuple-element.35), channel_id=1, source_target_pairs={{0,8},{4,12},{8,0},{12,4},{16,24},{20,28},{24,16},{28,20},{1,9},{5... | collective-permute-start | bytes 393224 | tf_op jit(solution)/shard_map/ppermute | solution.py:277
  24.4 1.5 %collective-permute-start.8 = (bf16[256,256]{1,0:T(8,128)(2,1)S(1)}, bf16[256,256]{1,0:T(8,128)(2,1)S(1)}, u32[]{:S(2)}, u32[]{:S(2)}) collective-permute-start(bf16[256,256]{1,0:T(8,128)(2,1)S(1)} %get-tuple-element.36), channel_id=1, source_target_pairs={{0,16},{4,20},{8,24},{12,28},{16,0},{20,4},{24,8},{28,12},{1,17},{... | collective-permute-start | bytes 393224 | tf_op jit(solution)/shard_map/ppermute | solution.py:277
  25.9 0.3 collective-permute-start.9
  26.1 1.2 %shard_map.97 = bf16[1024,256]{1,0:T(8,128)(2,1)S(1)} custom-call(bf16[2048,1024]{1,0:T(8,128)(2,1)S(1)} %shard_map.92.matrix, bf16[256,256]{1,0:T(8,128)(2,1)S(1)} %get-tuple-element.45.refs_0_, bf16[256,256]{1,0:T(8,128)(2,1)S(1)} %collective-permute-done.4.refs_1_, bf16[256,256]{1,0:T(8,128)(2,1)S(1)} %collective-permute-done.6.refs_2_, ...), custom_call_target="tpu_custom_call" | custom-call | bytes 1 | tf_op jit(solution)/shard_map/pallas_call | solution.py:179
  27.4 0.0 copy-start
  27.4 0.1 collective-permute-start.10
  27.5 0.8 %collective-permute-done.7.refs_1_ = bf16[256,256]{1,0:T(8,128)(2,1)S(1)} collective-permute-done((bf16[256,256]{1,0:T(8,128)(2,1)S(1)}, bf16[256,256]{1,0:T(8,128)(2,1)S(1)}, u32[]{:S(2)}, u32[]{:S(2)}) %collective-permute-start.7) | collective-permute-done | bytes 131104 | tf_op jit(solution)/shard_map/ppermute | solution.py:277
  28.3 3.2 %collective-permute-done.8.refs_2_ = bf16[256,256]{1,0:T(8,128)(2,1)S(1)} collective-permute-done((bf16[256,256]{1,0:T(8,128)(2,1)S(1)}, bf16[256,256]{1,0:T(8,128)(2,1)S(1)}, u32[]{:S(2)}, u32[]{:S(2)}) %collective-permute-start.8) | collective-permute-done | bytes 131104 | tf_op jit(solution)/shard_map/ppermute | solution.py:277
  31.5 1.0 %collective-permute-done.9.refs_3_ = bf16[256,256]{1,0:T(8,128)(2,1)S(1)} collective-permute-done((bf16[256,256]{1,0:T(8,128)(2,1)S(1)}, bf16[256,256]{1,0:T(8,128)(2,1)S(1)}, u32[]{:S(2)}, u32[]{:S(2)}) %collective-permute-start.9) | collective-permute-done | bytes 131104 | tf_op jit(solution)/shard_map/ppermute | solution.py:277
  32.4 1.2 %shard_map.96.stay = f32[1024,256]{1,0:T(8,128)S(1)} custom-call(bf16[2048,1024]{1,0:T(8,128)(2,1)S(1)} %shard_map.92.matrix, bf16[256,256]{1,0:T(8,128)(2,1)S(1)} %get-tuple-element.45.refs_0_, bf16[256,256]{1,0:T(8,128)(2,1)S(1)} %collective-permute-done.4.refs_1_, bf16[256,256]{1,0:T(8,128)(2,1)S(1)} %collective-permute-done.6.refs_2_, ...), custom_call_target="tpu_custom_call" | custom-call | flops 10737418240 | bytes 1 | tf_op jit(solution)/shard_map/pallas_call | solution.py:179
  33.7 0.1 shard_map.98
  33.8 1.3 %collective-permute-start.11 = (bf16[256,256]{1,0:T(8,128)(2,1)S(1)}, bf16[256,256]{1,0:T(8,128)(2,1)S(1)}, u32[]{:S(2)}, u32[]{:S(2)}) collective-permute-start(bf16[256,256]{1,0:T(8,128)(2,1)S(1)} %get-tuple-element.50), channel_id=1, source_target_pairs={{0,8},{4,12},{8,0},{12,4},{16,24},{20,28},{24,16},{28,20},{1,9},{5... | collective-permute-start | bytes 393224 | tf_op jit(solution)/shard_map/ppermute | solution.py:277
  35.1 1.0 %collective-permute-start.12 = (bf16[256,256]{1,0:T(8,128)(2,1)S(1)}, bf16[256,256]{1,0:T(8,128)(2,1)S(1)}, u32[]{:S(2)}, u32[]{:S(2)}) collective-permute-start(bf16[256,256]{1,0:T(8,128)(2,1)S(1)} %get-tuple-element.51), channel_id=1, source_target_pairs={{0,16},{4,20},{8,24},{12,28},{16,0},{20,4},{24,8},{28,12},{1,17},{... | collective-permute-start | bytes 393224 | tf_op jit(solution)/shard_map/ppermute | solution.py:277
  36.1 1.2 %collective-permute-start.13 = (bf16[256,256]{1,0:T(8,128)(2,1)S(1)}, bf16[256,256]{1,0:T(8,128)(2,1)S(1)}, u32[]{:S(2)}, u32[]{:S(2)}) collective-permute-start(bf16[256,256]{1,0:T(8,128)(2,1)S(1)} %get-tuple-element.52), channel_id=1, source_target_pairs={{0,24},{4,28},{8,16},{12,20},{16,8},{20,12},{24,0},{28,4},{1,25},{... | collective-permute-start | bytes 393224 | tf_op jit(solution)/shard_map/ppermute | solution.py:277
  37.3 2.5 %collective-permute-done.11.refs_5_ = bf16[256,256]{1,0:T(8,128)(2,1)S(1)} collective-permute-done((bf16[256,256]{1,0:T(8,128)(2,1)S(1)}, bf16[256,256]{1,0:T(8,128)(2,1)S(1)}, u32[]{:S(2)}, u32[]{:S(2)}) %collective-permute-start.11) | collective-permute-done | bytes 131104 | tf_op jit(solution)/shard_map/ppermute | solution.py:277
  39.8 2.5 %collective-permute-done.12.refs_6_ = bf16[256,256]{1,0:T(8,128)(2,1)S(1)} collective-permute-done((bf16[256,256]{1,0:T(8,128)(2,1)S(1)}, bf16[256,256]{1,0:T(8,128)(2,1)S(1)}, u32[]{:S(2)}, u32[]{:S(2)}) %collective-permute-start.12) | collective-permute-done | bytes 131104 | tf_op jit(solution)/shard_map/ppermute | solution.py:277
  42.3 0.9 %shard_map.99 = bf16[256,512]{1,0:T(8,128)(2,1)} custom-call(f32[256,512]{1,0:T(8,128)S(1)} %get-tuple-element.29.projected, f32[2,128]{1,0:T(2,128)S(1)} %bitcast.4, f32[256,256]{1,0:T(8,128)S(1)} %get-tuple-element.33.refs_0_, bf16[256,256]{1,0:T(8,128)(2,1)S(1)} %collective-permute-done.7.refs_1_, bf16[256,256]{1,0:T(8,128)(2,1)S(1)} %collective-permute-done.8.refs_2_, ...), custom_call_target="tpu_custom_call" | custom-call | flops 786432 | bytes 2097152 | tf_op jit(solution)/shard_map/pallas_call | solution.py:231
  (7 shorter events, 0.0 us)
Async XLA Ops:
  1.8 9.5 %collective-permute-start = (bf16[256,256]{1,0:T(8,128)(2,1)S(1)}, bf16[256,256]{1,0:T(8,128)(2,1)S(1)}, u32[]{:S(2)}, u32[]{:S(2)}) collective-permute-start(bf16[256,256]{1,0:T(8,128)(2,1)S(1)} %get-tuple-element.30.refs_0_), channel_id=1, source_target_pairs={{0,3},{1,2},{2,1},{3,0},{4,7},{5,6},{6,5},{7,4},{8,11},{9,10},{10,... | collective-permute-start | bytes 393224 | tf_op jit(solution)/shard_map/ppermute | solution.py:277
  6.9 11.6 %collective-permute-start.1 = (bf16[256,256]{1,0:T(8,128)(2,1)S(1)}, bf16[256,256]{1,0:T(8,128)(2,1)S(1)}, u32[]{:S(2)}, u32[]{:S(2)}) collective-permute-start(bf16[256,256]{1,0:T(8,128)(2,1)S(1)} %get-tuple-element.30.refs_0_), channel_id=1, source_target_pairs={{0,1},{1,0},{2,3},{3,2},{4,5},{5,4},{6,7},{7,6},{8,9},{9,8},{10,11... | collective-permute-start | bytes 393224 | tf_op jit(solution)/shard_map/ppermute | solution.py:277
  6.9 9.5 %collective-permute-start.5 = (bf16[256,256]{1,0:T(8,128)(2,1)S(1)}, bf16[256,256]{1,0:T(8,128)(2,1)S(1)}, u32[]{:S(2)}, u32[]{:S(2)}) collective-permute-start(bf16[256,256]{1,0:T(8,128)(2,1)S(1)} %get-tuple-element.45.refs_0_), channel_id=1, source_target_pairs={{0,3},{1,2},{2,1},{3,0},{4,7},{5,6},{6,5},{7,4},{8,11},{9,10},{10,... | collective-permute-start | bytes 393224 | tf_op jit(solution)/shard_map/ppermute | solution.py:277
  11.3 8.0 %collective-permute-start.2 = (bf16[256,256]{1,0:T(8,128)(2,1)S(1)}, bf16[256,256]{1,0:T(8,128)(2,1)S(1)}, u32[]{:S(2)}, u32[]{:S(2)}) collective-permute-start(bf16[256,256]{1,0:T(8,128)(2,1)S(1)} %collective-permute-done.refs_3_), channel_id=1, source_target_pairs={{0,1},{1,0},{2,3},{3,2},{4,5},{5,4},{6,7},{7,6},{8,9},{9,8},{10,11... | collective-permute-start | bytes 393224 | tf_op jit(solution)/shard_map/ppermute | solution.py:277
  14.8 11.4 %collective-permute-start.4 = (bf16[256,256]{1,0:T(8,128)(2,1)S(1)}, bf16[256,256]{1,0:T(8,128)(2,1)S(1)}, u32[]{:S(2)}, u32[]{:S(2)}) collective-permute-start(bf16[256,256]{1,0:T(8,128)(2,1)S(1)} %get-tuple-element.45.refs_0_), channel_id=1, source_target_pairs={{0,1},{1,0},{2,3},{3,2},{4,5},{5,4},{6,7},{7,6},{8,9},{9,8},{10,11... | collective-permute-start | bytes 393224 | tf_op jit(solution)/shard_map/ppermute | solution.py:277
  16.5 9.7 %collective-permute-start.6 = (bf16[256,256]{1,0:T(8,128)(2,1)S(1)}, bf16[256,256]{1,0:T(8,128)(2,1)S(1)}, u32[]{:S(2)}, u32[]{:S(2)}) collective-permute-start(bf16[256,256]{1,0:T(8,128)(2,1)S(1)} %collective-permute-done.5.refs_3_), channel_id=1, source_target_pairs={{0,1},{1,0},{2,3},{3,2},{4,5},{5,4},{6,7},{7,6},{8,9},{9,8},{10,11... | collective-permute-start | bytes 393224 | tf_op jit(solution)/shard_map/ppermute | solution.py:277
  20.5 2.0 %collective-permute-start.3 = (bf16[1024,256]{1,0:T(8,128)(2,1)S(1)}, bf16[1024,256]{1,0:T(8,128)(2,1)S(1)}, u32[]{:S(2)}, u32[]{:S(2)}) collective-permute-start(bf16[1024,256]{1,0:T(8,128)(2,1)S(1)} %shard_map.94), channel_id=1, source_target_pairs={{0,4},{4,0},{8,12},{12,8},{16,20},{20,16},{24,28},{28,24},{1,5},{5... | collective-permute-start | bytes 1572872 | tf_op jit(solution)/shard_map/ppermute | solution.py:277
  22.6 5.7 %collective-permute-start.7 = (bf16[256,256]{1,0:T(8,128)(2,1)S(1)}, bf16[256,256]{1,0:T(8,128)(2,1)S(1)}, u32[]{:S(2)}, u32[]{:S(2)}) collective-permute-start(bf16[256,256]{1,0:T(8,128)(2,1)S(1)} %get-tuple-element.35), channel_id=1, source_target_pairs={{0,8},{4,12},{8,0},{12,4},{16,24},{20,28},{24,16},{28,20},{1,9},{5... | collective-permute-start | bytes 393224 | tf_op jit(solution)/shard_map/ppermute | solution.py:277
  24.4 7.1 %collective-permute-start.8 = (bf16[256,256]{1,0:T(8,128)(2,1)S(1)}, bf16[256,256]{1,0:T(8,128)(2,1)S(1)}, u32[]{:S(2)}, u32[]{:S(2)}) collective-permute-start(bf16[256,256]{1,0:T(8,128)(2,1)S(1)} %get-tuple-element.36), channel_id=1, source_target_pairs={{0,16},{4,20},{8,24},{12,28},{16,0},{20,4},{24,8},{28,12},{1,17},{... | collective-permute-start | bytes 393224 | tf_op jit(solution)/shard_map/ppermute | solution.py:277
  25.9 6.5 %collective-permute-start.9 = (bf16[256,256]{1,0:T(8,128)(2,1)S(1)}, bf16[256,256]{1,0:T(8,128)(2,1)S(1)}, u32[]{:S(2)}, u32[]{:S(2)}) collective-permute-start(bf16[256,256]{1,0:T(8,128)(2,1)S(1)} %get-tuple-element.37), channel_id=1, source_target_pairs={{0,24},{4,28},{8,16},{12,20},{16,8},{20,12},{24,0},{28,4},{1,25},{... | collective-permute-start | bytes 393224 | tf_op jit(solution)/shard_map/ppermute | solution.py:277
  27.4 14.9 %copy-start = (f32[256]{0:T(256)S(1)}, f32[256]{0:T(256)}, u32[]{:S(2)}) copy-start(f32[256]{0:T(256)} %param.12) | copy-start | bytes 3076
  27.4 6.3 %collective-permute-start.10 = (bf16[1024,256]{1,0:T(8,128)(2,1)S(1)}, bf16[1024,256]{1,0:T(8,128)(2,1)S(1)}, u32[]{:S(2)}, u32[]{:S(2)}) collective-permute-start(bf16[1024,256]{1,0:T(8,128)(2,1)S(1)} %shard_map.97), channel_id=1, source_target_pairs={{0,4},{4,0},{8,12},{12,8},{16,20},{20,16},{24,28},{28,24},{1,5},{5... | collective-permute-start | bytes 1572872 | tf_op jit(solution)/shard_map/ppermute | solution.py:277
  33.8 6.0 %collective-permute-start.11 = (bf16[256,256]{1,0:T(8,128)(2,1)S(1)}, bf16[256,256]{1,0:T(8,128)(2,1)S(1)}, u32[]{:S(2)}, u32[]{:S(2)}) collective-permute-start(bf16[256,256]{1,0:T(8,128)(2,1)S(1)} %get-tuple-element.50), channel_id=1, source_target_pairs={{0,8},{4,12},{8,0},{12,4},{16,24},{20,28},{24,16},{28,20},{1,9},{5... | collective-permute-start | bytes 393224 | tf_op jit(solution)/shard_map/ppermute | solution.py:277
  35.1 7.2 %collective-permute-start.12 = (bf16[256,256]{1,0:T(8,128)(2,1)S(1)}, bf16[256,256]{1,0:T(8,128)(2,1)S(1)}, u32[]{:S(2)}, u32[]{:S(2)}) collective-permute-start(bf16[256,256]{1,0:T(8,128)(2,1)S(1)} %get-tuple-element.51), channel_id=1, source_target_pairs={{0,16},{4,20},{8,24},{12,28},{16,0},{20,4},{24,8},{28,12},{1,17},{... | collective-permute-start | bytes 393224 | tf_op jit(solution)/shard_map/ppermute | solution.py:277
  36.1 6.2 %collective-permute-start.13 = (bf16[256,256]{1,0:T(8,128)(2,1)S(1)}, bf16[256,256]{1,0:T(8,128)(2,1)S(1)}, u32[]{:S(2)}, u32[]{:S(2)}) collective-permute-start(bf16[256,256]{1,0:T(8,128)(2,1)S(1)} %get-tuple-element.52), channel_id=1, source_target_pairs={{0,24},{4,28},{8,16},{12,20},{16,8},{20,12},{24,0},{28,4},{1,25},{... | collective-permute-start | bytes 393224 | tf_op jit(solution)/shard_map/ppermute | solution.py:277

commit v2 on v1

--- a/solution.py
+++ b/solution.py
@@ -112,8 +112,8 @@
     def add(slot):
         target, source = targets[0, slot], sources[0, slot]
         label = labels[0, target]
-        apart = lax.bitwise_xor(target // per_owner, my_row)
-        position = (1 - apart % 2) * (owners // 2) + apart // 2
+        owner = target // per_owner
+        position = owner // 2 + jnp.where(owner % 2 == my_row % 2, owners // 2, 0)
         place = jnp.where(label < own_tiles, position * own_tiles + label, spare)
         block = lax.bitwise_xor(source // own_tiles, my_column)
         total[place, block * own_tiles + source % own_tiles] += tiles[slot].astype(jnp.float32)
@@ -186,56 +186,48 @@
     )(matrix, *blocks)
 
 
-def join_kernel(stay, came, kept, *sent):
-    rows = kept.shape[0]
-    value = stay[...].astype(jnp.float32) + came[...].astype(jnp.float32)
-    kept[...] = value[:rows]
-    for place, out in enumerate(sent):
-        out[...] = value[(place + 1) * rows : (place + 2) * rows].astype(out.dtype)
-
-
-def join(stay, came, rows):
-    total, width = stay.shape
-    parts = total // rows
+def join_kernel(stay, came, out):
+    out[...] = (stay[...] + came[...].astype(jnp.float32)).astype(out.dtype)
+
+
+def join(stay, came):
     return pl.pallas_call(
         join_kernel,
-        out_shape=[jax.ShapeDtypeStruct((rows, width), jnp.float32)]
-        + [jax.ShapeDtypeStruct((rows, width), jnp.bfloat16)] * (parts - 1),
+        out_shape=jax.ShapeDtypeStruct(came.shape, came.dtype),
         in_specs=[VMEM] * 2,
-        out_specs=[VMEM] * parts,
+        out_specs=VMEM,
         compiler_params=params(12),
         cost_estimate=cost(1, 1),
     )(stay, came)
 
 
-def finish_kernel(chunks, projected, norm, *refs):
-    out = refs[-1]
-    per_chunk = (len(refs) - 1) // chunks
+def finish_kernel(projected, norm, *refs):
+    *chunks, out = refs
     lanes = norm.shape[1]
-    width = refs[0].shape[1]
+    width = chunks[0].shape[1]
     for part in range(norm.shape[0]):
         factor = rows_to_lanes(norm[part : part + 1, :], lanes)
         here = slice(part * lanes, (part + 1) * lanes)
         for column in range(0, out.shape[1], lanes):
-            pieces = refs[column // width * per_chunk : (column // width + 1) * per_chunk]
+            chunk = chunks[column // width]
             start = column % width
             value = projected[here, column : column + lanes]
-            for piece in pieces:
-                value += piece[here, start : start + lanes].astype(jnp.float32)
+            for block in range(0, chunk.shape[0], out.shape[0]):
+                rows = slice(block + here.start, block + here.stop)
+                value += chunk[rows, start : start + lanes].astype(jnp.float32)
             out[here, column : column + lanes] = jnp.maximum(factor * value, 0.0).astype(out.dtype)
 
 
-def finish(projected, target_norm, pieces):
+def finish(projected, target_norm, chunks):
     rows, hidden = projected.shape
-    flat = [piece for chunk in pieces for piece in chunk]
-    return pl.pallas_call(
-        functools.partial(finish_kernel, len(pieces)),
+    return pl.pallas_call(
+        finish_kernel,
         out_shape=jax.ShapeDtypeStruct((rows, hidden), jnp.bfloat16),
-        in_specs=[VMEM] * (2 + len(flat)),
+        in_specs=[VMEM] * (2 + len(chunks)),
         out_specs=VMEM,
         compiler_params=params(12),
         cost_estimate=cost(6 * rows * hidden, 16 * rows * hidden),
-    )(projected, target_norm.reshape(-1, 128), *flat)
+    )(projected, target_norm.reshape(-1, 128), *chunks)
 
 
 def visit_kernel(own_tiles, per_owner, sources, targets, count, labels, tiles, blocks, out, total):
@@ -277,8 +269,12 @@
     return lax.ppermute(value, axis, pairs)
 
 
-def exchange(sent):
-    return [swap(value, "row", 2 * (k + 1)) for k, value in enumerate(sent)]
+def exchange(value):
+    owners = lax.axis_size("row")
+    groups = [list(range(core, owners, 2)) for core in range(2)]
+    return lax.all_to_all(
+        value, "row", split_axis=0, concat_axis=0, axis_index_groups=groups, tiled=True
+    )
 
 
 def per_device(
@@ -316,20 +312,17 @@
     beside = [swap(own, "col", 1) for own in scaled]
     across[0], matrix = lax.optimization_barrier((across[0], matrix))
     passed = [swap(value, "col", 1) for value in across]
-    pieces, sent = [], None
+    arrived, sent = [], None
     for blocks, wait in zip(zip(scaled, beside, passed, across), WEIGHTS):
         late = blocks
         if sent is not None:
-            moved = exchange(sent)
             blocks, _ = lax.optimization_barrier((blocks, sent))
-            late, moved = lax.optimization_barrier((blocks, moved))
-            pieces[-1] += moved
+            late, arrived[-1] = lax.optimization_barrier((blocks, arrived[-1]))
         away = product(matrix, blocks, 0, jnp.bfloat16, wait[0])
         stay = product(matrix, late, 1, jnp.float32, wait[1])
-        kept, *sent = join(stay, swap(away, "row", 1), own_rows)
-        pieces.append([kept])
-    pieces[-1] += exchange(sent)
-    return finish(projected, target_norm, pieces)
+        sent = join(stay, swap(away, "row", 1))
+        arrived.append(exchange(sent))
+    return finish(projected, target_norm, arrived)
 
 
 def solution(mesh):

time: 43.5 us -> 58.9 us (1.35)
  blocking collectives: 0 us -> 13.2 us
  local copies, waits for them, and re-layouts: 0.01 us -> 4.38 us
  starting transfers between devices: 18.9 us -> 15.9 us
  Pallas kernels: 10.6 us -> 11.4 us
    all_to_all x0 -> x1, blocking collectives: none -> 13.2 us  [exchange(): lax.all_to_all(value, 'row', split_axis=0, concat_axis=0, axis_index_grou...]
    ppermute x14 -> x8, starting transfers between devices: 18.9 us -> 11.9 us  [swap(): return lax.ppermute(value, axis, pairs)]
    unnamed x2 -> x8, local copies, waits for them, and re-layouts: 0.01 us -> 4.38 us
    all_to_all x0 -> x1, starting transfers between devices: none -> 3.92 us  [exchange(): lax.all_to_all(value, 'row', split_axis=0, concat_axis=0, axis_index_grou...]
    pallas_call x3, Pallas kernels: 1.06 us -> 1.9 us  [the longest x2 0.98 us: join(): pl.pallas_call(join_kernel, out_shape=jax.ShapeDtypeStruct(came.shape, ca...]
    ppermute x14 -> x8, waiting for transfers between devices: 13 us -> 13 us  [swap(): return lax.ppermute(value, axis, pairs)]
  transfers between devices with their start and end apart: 14 -> 9, of which waited for: 8 -> 7; matrix products, arithmetic and copies ran while one was open for 0% -> 0% of each run, Pallas kernels for 18% -> 11%
where the time goes in v2:
time: 58.9 us; the launch traced here: 58.6 us
  starting transfers between devices  15.9 us (27%)
  blocking collectives  13.2 us (22%)
  waiting for transfers between devices  13 us (22%)
  Pallas kernels  11.4 us (19%)
  local copies, waits for them, and re-layouts  4.38 us (7%)
  between operations  0.77 us (1%)
    all_to_all x1, blocking collectives, exchange(): lax.all_to_all(value, 'row', split_axis=0, concat_axis=0, axis_index_grou...  13.2 us
    ppermute x8, waiting for transfers between devices, swap(): return lax.ppermute(value, axis, pairs)  13 us
    ppermute x8, starting transfers between devices, swap(): return lax.ppermute(value, axis, pairs)  11.9 us
    pallas_call x4, Pallas kernels, product(): pl.pallas_call(functools.partial(product_kernel, half * (total // rows //...  4.89 us
    unnamed x8, local copies, waits for them, and re-layouts  4.38 us
    all_to_all x1, starting transfers between devices, exchange(): lax.all_to_all(value, 'row', split_axis=0, concat_axis=0, axis_index_grou...  3.92 us
    pallas_call x1, Pallas kernels, merge_tiles(): pl.pallas_call(functools.partial(merge_kernel, own_tiles, labels.shape[1]...  2.77 us
    pallas_call x1, Pallas kernels, project(): pl.pallas_call(project_kernel, out_shape=[jax.ShapeDtypeStruct((rows, hid...  1.82 us
  transfers between devices with their start and end apart: 9, of which 7 were waited for; matrix products, arithmetic and copies ran while one was open for 0% of the time, Pallas kernels for 11%

profile of v2, /device:TPU:0, one launch (start us, length us, event | category | flops | bytes accessed | tf_op | source)
XLA Modules:
  0.0 58.6 jit_solution(10751905718404263805)
XLA Ops:
  0.0 1.8 %shard_map.91 = (f32[256,512]{1,0:T(8,128)S(1)}, bf16[256,256]{1,0:T(8,128)(2,1)S(1)}, bf16[256,256]{1,0:T(8,128)(2,1)S(1)}) custom-call(bf16[256,1024]{1,0:T(8,128)(2,1)} %features_hbm.1, bf16[1024,512]{1,0:T(8,128)(2,1)} %weight_hbm.1, f32[2,128]{1,0:T(2,128)} %bitcast.12), custom_call_target="tpu_custom_call" | custom-call | flops 268435456 | bytes 1572864 | tf_op jit(solution)/shard_map/pallas_call | solution.py:66
  1.8 5.1 %collective-permute-start.3 = (bf16[256,256]{1,0:T(8,128)(2,1)S(1)}, bf16[256,256]{1,0:T(8,128)(2,1)S(1)}, u32[]{:S(2)}, u32[]{:S(2)}) collective-permute-start(bf16[256,256]{1,0:T(8,128)(2,1)S(1)} %get-tuple-element.21.refs_0_), channel_id=1, source_target_pairs={{0,3},{1,2},{2,1},{3,0},{4,7},{5,6},{6,5},{7,4},{8,11},{9,10},{10,... | collective-permute-start | bytes 393224 | tf_op jit(solution)/shard_map/ppermute | solution.py:269
  6.9 0.0 collective-permute-start.4
  7.6 2.8 %shard_map.92.matrix = bf16[2048,1024]{1,0:T(8,128)(2,1)S(1)} custom-call(s32[1]{0:T(128)} %bitcast.2.row, s32[1]{0:T(128)} %bitcast.3.column, s32[1]{0:T(128)S(6)} %copy.10.count, s32[1,64]{1,0:T(1,128)} %sources_hbm.1, s32[1,64]{1,0:T(1,128)} %targets_hbm.1, s32[1,16]{1,0:T(1,128)} %labels_hbm.1, bf16[1,64,128,128]{3,2,1,0:T(8,128)(2,1)} %tiles_hbm.1), custom_call_target="tpu_custom_call" | custom-call | flops 8388608 | bytes 12582912 | tf_op jit(solution)/shard_map/pallas_call | solution.py:139
  10.4 0.0 copy-start
  10.4 0.9 %collective-permute-done.3.refs_3_ = bf16[256,256]{1,0:T(8,128)(2,1)S(1)} collective-permute-done((bf16[256,256]{1,0:T(8,128)(2,1)S(1)}, bf16[256,256]{1,0:T(8,128)(2,1)S(1)}, u32[]{:S(2)}, u32[]{:S(2)}) %collective-permute-start.3) | collective-permute-done | bytes 131104 | tf_op jit(solution)/shard_map/ppermute | solution.py:269
  11.3 1.6 %collective-permute-start.5 = (bf16[256,256]{1,0:T(8,128)(2,1)S(1)}, bf16[256,256]{1,0:T(8,128)(2,1)S(1)}, u32[]{:S(2)}, u32[]{:S(2)}) collective-permute-start(bf16[256,256]{1,0:T(8,128)(2,1)S(1)} %collective-permute-done.3.refs_3_), channel_id=1, source_target_pairs={{0,1},{1,0},{2,3},{3,2},{4,5},{5,4},{6,7},{7,6},{8,9},{9,8},{10,11... | collective-permute-start | bytes 393224 | tf_op jit(solution)/shard_map/ppermute | solution.py:269
  13.0 0.7 %collective-permute-done.4.refs_1_ = bf16[256,256]{1,0:T(8,128)(2,1)S(1)} collective-permute-done((bf16[256,256]{1,0:T(8,128)(2,1)S(1)}, bf16[256,256]{1,0:T(8,128)(2,1)S(1)}, u32[]{:S(2)}, u32[]{:S(2)}) %collective-permute-start.4) | collective-permute-done | bytes 131104 | tf_op jit(solution)/shard_map/ppermute | solution.py:269
  13.7 2.6 %collective-permute-done.5.refs_2_ = bf16[256,256]{1,0:T(8,128)(2,1)S(1)} collective-permute-done((bf16[256,256]{1,0:T(8,128)(2,1)S(1)}, bf16[256,256]{1,0:T(8,128)(2,1)S(1)}, u32[]{:S(2)}, u32[]{:S(2)}) %collective-permute-start.5) | collective-permute-done | bytes 131104 | tf_op jit(solution)/shard_map/ppermute | solution.py:269
  16.3 1.2 %shard_map.94 = bf16[1024,256]{1,0:T(8,128)(2,1)S(1)} custom-call(bf16[2048,1024]{1,0:T(8,128)(2,1)S(1)} %shard_map.92.matrix, bf16[256,256]{1,0:T(8,128)(2,1)S(1)} %get-tuple-element.21.refs_0_, bf16[256,256]{1,0:T(8,128)(2,1)S(1)} %collective-permute-done.4.refs_1_, bf16[256,256]{1,0:T(8,128)(2,1)S(1)} %collective-permute-done.5.refs_2_, ...), custom_call_target="tpu_custom_call" | custom-call | flops 10737418240 | bytes 1 | tf_op jit(solution)/shard_map/pallas_call | solution.py:179
  17.5 0.1 collective-permute-start.6
  17.6 0.0 copy-done
  17.6 1.2 %shard_map.93.stay = f32[1024,256]{1,0:T(8,128)S(1)} custom-call(bf16[2048,1024]{1,0:T(8,128)(2,1)S(1)} %shard_map.92.matrix, bf16[256,256]{1,0:T(8,128)(2,1)S(1)} %get-tuple-element.21.refs_0_, bf16[256,256]{1,0:T(8,128)(2,1)S(1)} %collective-permute-done.4.refs_1_, bf16[256,256]{1,0:T(8,128)(2,1)S(1)} %collective-permute-done.5.refs_2_, ...), custom_call_target="tpu_custom_call" | custom-call | flops 10737418240 | bytes 1 | tf_op jit(solution)/shard_map/pallas_call | solution.py:179
  18.9 0.6 %collective-permute-done.6.came = bf16[1024,256]{1,0:T(8,128)(2,1)S(1)} collective-permute-done((bf16[1024,256]{1,0:T(8,128)(2,1)S(1)}, bf16[1024,256]{1,0:T(8,128)(2,1)S(1)}, u32[]{:S(2)}, u32[]{:S(2)}) %collective-permute-start.6) | collective-permute-done | bytes 524320 | tf_op jit(solution)/shard_map/ppermute | solution.py:269
  19.5 0.9 %shard_map.95 = bf16[1024,256]{1,0:T(8,128)(2,1)} custom-call(f32[1024,256]{1,0:T(8,128)S(1)} %shard_map.93.stay, bf16[1024,256]{1,0:T(8,128)(2,1)S(1)} %collective-permute-done.6.came), custom_call_target="tpu_custom_call" | custom-call | flops 1 | bytes 1 | tf_op jit(solution)/shard_map/pallas_call | solution.py:194
  20.4 3.9 %all-to-all-start = ((bf16[4,256,256]{2,1,0:T(8,128)(2,1)}), bf16[4,256,256]{2,1,0:T(8,128)(2,1)S(1)}, u32[]{:S(2)}, u32[]{:S(2)}) async-start(bf16[4,256,256]{2,1,0:T(8,128)(2,1)} %bitcast.4), calls=%async_computation | async-start | bytes 1048576 | tf_op jit(solution)/shard_map/all_to_all | solution.py:275
  24.3 3.6 %collective-permute-start.1 = (bf16[256,256]{1,0:T(8,128)(2,1)S(1)}, bf16[256,256]{1,0:T(8,128)(2,1)S(1)}, u32[]{:S(2)}, u32[]{:S(2)}) collective-permute-start(bf16[256,256]{1,0:T(8,128)(2,1)S(1)} %get-tuple-element.29.refs_0_), channel_id=1, source_target_pairs={{0,3},{1,2},{2,1},{3,0},{4,7},{5,6},{6,5},{7,4},{8,11},{9,10},{10,... | collective-permute-start | bytes 393224 | tf_op jit(solution)/shard_map/ppermute | solution.py:269
  27.9 0.0 collective-permute-start
  27.9 4.6 %collective-permute-done.1.refs_3_ = bf16[256,256]{1,0:T(8,128)(2,1)S(1)} collective-permute-done((bf16[256,256]{1,0:T(8,128)(2,1)S(1)}, bf16[256,256]{1,0:T(8,128)(2,1)S(1)}, u32[]{:S(2)}, u32[]{:S(2)}) %collective-permute-start.1) | collective-permute-done | bytes 131104 | tf_op jit(solution)/shard_map/ppermute | solution.py:269
  32.5 1.4 %collective-permute-start.2 = (bf16[256,256]{1,0:T(8,128)(2,1)S(1)}, bf16[256,256]{1,0:T(8,128)(2,1)S(1)}, u32[]{:S(2)}, u32[]{:S(2)}) collective-permute-start(bf16[256,256]{1,0:T(8,128)(2,1)S(1)} %collective-permute-done.1.refs_3_), channel_id=1, source_target_pairs={{0,1},{1,0},{2,3},{3,2},{4,5},{5,4},{6,7},{7,6},{8,9},{9,8},{10,11... | collective-permute-start | bytes 393224 | tf_op jit(solution)/shard_map/ppermute | solution.py:269
  33.9 0.9 %collective-permute-done.refs_1_ = bf16[256,256]{1,0:T(8,128)(2,1)S(1)} collective-permute-done((bf16[256,256]{1,0:T(8,128)(2,1)S(1)}, bf16[256,256]{1,0:T(8,128)(2,1)S(1)}, u32[]{:S(2)}, u32[]{:S(2)}) %collective-permute-start) | collective-permute-done | bytes 131104 | tf_op jit(solution)/shard_map/ppermute | solution.py:269
  34.8 2.6 %collective-permute-done.2.refs_2_ = bf16[256,256]{1,0:T(8,128)(2,1)S(1)} collective-permute-done((bf16[256,256]{1,0:T(8,128)(2,1)S(1)}, bf16[256,256]{1,0:T(8,128)(2,1)S(1)}, u32[]{:S(2)}, u32[]{:S(2)}) %collective-permute-start.2) | collective-permute-done | bytes 131104 | tf_op jit(solution)/shard_map/ppermute | solution.py:269
  37.5 2.2 %copy-done.1 = bf16[2048,1024]{1,0:T(8,128)(2,1)S(1)} copy-done((bf16[2048,1024]{1,0:T(8,128)(2,1)S(1)}, bf16[2048,1024]{1,0:T(8,128)(2,1)}, u32[]{:S(2)}) %copy-start.1) | copy-done | bytes 4194328
  39.7 1.2 %shard_map.97 = bf16[1024,256]{1,0:T(8,128)(2,1)S(1)} custom-call(bf16[2048,1024]{1,0:T(8,128)(2,1)S(1)} %copy-done.1, bf16[256,256]{1,0:T(8,128)(2,1)S(1)} %get-tuple-element.29.refs_0_, bf16[256,256]{1,0:T(8,128)(2,1)S(1)} %collective-permute-done.refs_1_, bf16[256,256]{1,0:T(8,128)(2,1)S(1)} %collective-permute-done.2.refs_2_, ...), custom_call_target="tpu_custom_call" | custom-call | bytes 1 | tf_op jit(solution)/shard_map/pallas_call | solution.py:179
  40.9 0.1 collective-permute-start.7
  41.0 0.0 all-to-all-done
  41.0 2.2 %copy-done.2 = bf16[2048,1024]{1,0:T(8,128)(2,1)S(1)} copy-done((bf16[2048,1024]{1,0:T(8,128)(2,1)S(1)}, bf16[2048,1024]{1,0:T(8,128)(2,1)}, u32[]{:S(2)}) %copy-start.2) | copy-done | bytes 4194328
  43.2 1.2 %shard_map.96.stay = f32[1024,256]{1,0:T(8,128)S(1)} custom-call(bf16[2048,1024]{1,0:T(8,128)(2,1)S(1)} %copy-done.2, bf16[256,256]{1,0:T(8,128)(2,1)S(1)} %get-tuple-element.29.refs_0_, bf16[256,256]{1,0:T(8,128)(2,1)S(1)} %collective-permute-done.refs_1_, bf16[256,256]{1,0:T(8,128)(2,1)S(1)} %collective-permute-done.2.refs_2_, ...), custom_call_target="tpu_custom_call" | custom-call | flops 10737418240 | bytes 1 | tf_op jit(solution)/shard_map/pallas_call | solution.py:179
  44.4 0.0 collective-permute-done.7.came
  44.4 0.1 shard_map.98
  44.5 13.2 %all_to_all.23 = bf16[4,256,256]{2,1,0:T(8,128)(2,1)S(1)} all-to-all(bf16[4,256,256]{2,1,0:T(8,128)(2,1)S(1)} %bitcast.10), channel_id=1, replica_groups={{0,8,16,24},{4,12,20,28},{1,9,17,25},{5,13,21,29},{2,10,18,26},{6,14,22..., dimensions={0} | all-to-all | bytes 1048576 | tf_op jit(solution)/shard_map/all_to_all | solution.py:275
  57.7 0.9 %shard_map.99 = bf16[256,512]{1,0:T(8,128)(2,1)} custom-call(f32[256,512]{1,0:T(8,128)S(1)} %get-tuple-element.19.projected, f32[2,128]{1,0:T(2,128)S(1)} %bitcast.11, bf16[1024,256]{1,0:T(8,128)(2,1)S(1)} %bitcast.8, bf16[1024,256]{1,0:T(8,128)(2,1)S(1)} %bitcast.9), custom_call_target="tpu_custom_call" | custom-call | flops 786432 | bytes 2097152 | tf_op jit(solution)/shard_map/pallas_call | solution.py:223
  (4 shorter events, 0.0 us)
Async XLA Ops:
  1.8 9.5 %collective-permute-start.3 = (bf16[256,256]{1,0:T(8,128)(2,1)S(1)}, bf16[256,256]{1,0:T(8,128)(2,1)S(1)}, u32[]{:S(2)}, u32[]{:S(2)}) collective-permute-start(bf16[256,256]{1,0:T(8,128)(2,1)S(1)} %get-tuple-element.21.refs_0_), channel_id=1, source_target_pairs={{0,3},{1,2},{2,1},{3,0},{4,7},{5,6},{6,5},{7,4},{8,11},{9,10},{10,... | collective-permute-start | bytes 393224 | tf_op jit(solution)/shard_map/ppermute | solution.py:269
  6.9 6.7 %collective-permute-start.4 = (bf16[256,256]{1,0:T(8,128)(2,1)S(1)}, bf16[256,256]{1,0:T(8,128)(2,1)S(1)}, u32[]{:S(2)}, u32[]{:S(2)}) collective-permute-start(bf16[256,256]{1,0:T(8,128)(2,1)S(1)} %get-tuple-element.21.refs_0_), channel_id=1, source_target_pairs={{0,1},{1,0},{2,3},{3,2},{4,5},{5,4},{6,7},{7,6},{8,9},{9,8},{10,11... | collective-permute-start | bytes 393224 | tf_op jit(solution)/shard_map/ppermute | solution.py:269
  10.4 7.2 %copy-start = (bf16[2048,1024]{1,0:T(8,128)(2,1)}, bf16[2048,1024]{1,0:T(8,128)(2,1)S(1)}, u32[]{:S(2)}) copy-start(bf16[2048,1024]{1,0:T(8,128)(2,1)S(1)} %shard_map.92.matrix) | copy-start | bytes 12582916
  11.3 5.0 %collective-permute-start.5 = (bf16[256,256]{1,0:T(8,128)(2,1)S(1)}, bf16[256,256]{1,0:T(8,128)(2,1)S(1)}, u32[]{:S(2)}, u32[]{:S(2)}) collective-permute-start(bf16[256,256]{1,0:T(8,128)(2,1)S(1)} %collective-permute-done.3.refs_3_), channel_id=1, source_target_pairs={{0,1},{1,0},{2,3},{3,2},{4,5},{5,4},{6,7},{7,6},{8,9},{9,8},{10,11... | collective-permute-start | bytes 393224 | tf_op jit(solution)/shard_map/ppermute | solution.py:269
  17.5 2.0 %collective-permute-start.6 = (bf16[1024,256]{1,0:T(8,128)(2,1)S(1)}, bf16[1024,256]{1,0:T(8,128)(2,1)S(1)}, u32[]{:S(2)}, u32[]{:S(2)}) collective-permute-start(bf16[1024,256]{1,0:T(8,128)(2,1)S(1)} %shard_map.94), channel_id=1, source_target_pairs={{0,4},{4,0},{8,12},{12,8},{16,20},{20,16},{24,28},{28,24},{1,5},{5... | collective-permute-start | bytes 1572872 | tf_op jit(solution)/shard_map/ppermute | solution.py:269
  20.4 20.6 %all-to-all-start = ((bf16[4,256,256]{2,1,0:T(8,128)(2,1)}), bf16[4,256,256]{2,1,0:T(8,128)(2,1)S(1)}, u32[]{:S(2)}, u32[]{:S(2)}) async-start(bf16[4,256,256]{2,1,0:T(8,128)(2,1)} %bitcast.4), calls=%async_computation | async-start | bytes 1048576 | tf_op jit(solution)/shard_map/all_to_all | solution.py:275
  24.3 8.2 %collective-permute-start.1 = (bf16[256,256]{1,0:T(8,128)(2,1)S(1)}, bf16[256,256]{1,0:T(8,128)(2,1)S(1)}, u32[]{:S(2)}, u32[]{:S(2)}) collective-permute-start(bf16[256,256]{1,0:T(8,128)(2,1)S(1)} %get-tuple-element.29.refs_0_), channel_id=1, source_target_pairs={{0,3},{1,2},{2,1},{3,0},{4,7},{5,6},{6,5},{7,4},{8,11},{9,10},{10,... | collective-permute-start | bytes 393224 | tf_op jit(solution)/shard_map/ppermute | solution.py:269
  27.9 6.9 %collective-permute-start = (bf16[256,256]{1,0:T(8,128)(2,1)S(1)}, bf16[256,256]{1,0:T(8,128)(2,1)S(1)}, u32[]{:S(2)}, u32[]{:S(2)}) collective-permute-start(bf16[256,256]{1,0:T(8,128)(2,1)S(1)} %get-tuple-element.29.refs_0_), channel_id=1, source_target_pairs={{0,1},{1,0},{2,3},{3,2},{4,5},{5,4},{6,7},{7,6},{8,9},{9,8},{10,11... | collective-permute-start | bytes 393224 | tf_op jit(solution)/shard_map/ppermute | solution.py:269
  32.5 5.0 %collective-permute-start.2 = (bf16[256,256]{1,0:T(8,128)(2,1)S(1)}, bf16[256,256]{1,0:T(8,128)(2,1)S(1)}, u32[]{:S(2)}, u32[]{:S(2)}) collective-permute-start(bf16[256,256]{1,0:T(8,128)(2,1)S(1)} %collective-permute-done.1.refs_3_), channel_id=1, source_target_pairs={{0,1},{1,0},{2,3},{3,2},{4,5},{5,4},{6,7},{7,6},{8,9},{9,8},{10,11... | collective-permute-start | bytes 393224 | tf_op jit(solution)/shard_map/ppermute | solution.py:269
  37.5 2.2 %copy-start.1 = (bf16[2048,1024]{1,0:T(8,128)(2,1)S(1)}, bf16[2048,1024]{1,0:T(8,128)(2,1)}, u32[]{:S(2)}) copy-start(bf16[2048,1024]{1,0:T(8,128)(2,1)} %copy-done) | copy-start | bytes 12582916
  40.9 3.5 %collective-permute-start.7 = (bf16[1024,256]{1,0:T(8,128)(2,1)S(1)}, bf16[1024,256]{1,0:T(8,128)(2,1)S(1)}, u32[]{:S(2)}, u32[]{:S(2)}) collective-permute-start(bf16[1024,256]{1,0:T(8,128)(2,1)S(1)} %shard_map.97), channel_id=1, source_target_pairs={{0,4},{4,0},{8,12},{12,8},{16,20},{20,16},{24,28},{28,24},{1,5},{5... | collective-permute-start | bytes 1572872 | tf_op jit(solution)/shard_map/ppermute | solution.py:269
  41.0 2.2 %copy-start.2 = (bf16[2048,1024]{1,0:T(8,128)(2,1)S(1)}, bf16[2048,1024]{1,0:T(8,128)(2,1)}, u32[]{:S(2)}) copy-start(bf16[2048,1024]{1,0:T(8,128)(2,1)} %copy-done) | copy-start | bytes 12582916
  43.2 14.5 %copy-start.3 = (f32[256]{0:T(256)S(1)}, f32[256]{0:T(256)}, u32[]{:S(2)}) copy-start(f32[256]{0:T(256)} %param.12) | copy-start | bytes 3076

commit v3 on v1

--- a/solution.py
+++ b/solution.py
@@ -156,31 +156,27 @@
 
 
 def product_kernel(first, matrix, *refs):
-    *blocks, out = refs
+    *blocks, out, gathered = refs
     rows = blocks[0].shape[0]
-
-    @pl.loop(0, out.shape[0] // rows)
-    def _(place):
-        from_row = pl.multiple_of((first + place) * rows, rows)
-        value = None
-        for k, block in enumerate(blocks):
-            term = jnp.dot(
-                matrix[pl.ds(from_row, rows), k * rows : (k + 1) * rows],
-                block[...],
-                preferred_element_type=jnp.float32,
-            )
-            value = term if value is None else value + term
-        out[pl.ds(pl.multiple_of(place * rows, rows), rows), :] = value.astype(out.dtype)
+    for k, block in enumerate(blocks):
+        gathered[k * rows : (k + 1) * rows, :] = block[...]
+    value = jnp.dot(
+        matrix[first : first + out.shape[0], :],
+        gathered[...],
+        preferred_element_type=jnp.float32,
+    )
+    out[...] = value.astype(out.dtype)
 
 
 def product(matrix, blocks, half, dtype, weight):
     rows, width = blocks[0].shape
     total, depth = matrix.shape
     return pl.pallas_call(
-        functools.partial(product_kernel, half * (total // rows // 2)),
+        functools.partial(product_kernel, half * (total // 2)),
         out_shape=jax.ShapeDtypeStruct((total // 2, width), dtype),
         in_specs=[VMEM] * (1 + len(blocks)),
         out_specs=VMEM,
+        scratch_shapes=[pltpu.VMEM((depth, width), blocks[0].dtype)],
         compiler_params=params(16),
         cost_estimate=cost(weight * total * depth * width, 1),
     )(matrix, *blocks)
@@ -278,7 +274,7 @@
 
 
 def exchange(sent):
-    return [swap(value, "row", 2 * (k + 1)) for k, value in enumerate(sent)]
+    return [swap(sent[k], "row", 2 * (k + 1)) for k in reversed(range(len(sent)))]
 
 
 def per_device(
@@ -318,14 +314,11 @@
     passed = [swap(value, "col", 1) for value in across]
     pieces, sent = [], None
     for blocks, wait in zip(zip(scaled, beside, passed, across), WEIGHTS):
-        late = blocks
         if sent is not None:
-            moved = exchange(sent)
+            pieces[-1] += exchange(sent)
             blocks, _ = lax.optimization_barrier((blocks, sent))
-            late, moved = lax.optimization_barrier((blocks, moved))
-            pieces[-1] += moved
         away = product(matrix, blocks, 0, jnp.bfloat16, wait[0])
-        stay = product(matrix, late, 1, jnp.float32, wait[1])
+        stay = product(matrix, blocks, 1, jnp.float32, wait[1])
         kept, *sent = join(stay, swap(away, "row", 1), own_rows)
         pieces.append([kept])
     pieces[-1] += exchange(sent)

time: 43.5 us -> 39 us (0.90)
  waiting for transfers between devices: 13 us -> 10.8 us
  Pallas kernels: 10.6 us -> 8.79 us
  starting transfers between devices: 18.9 us -> 18.4 us
    ppermute x14, waiting for transfers between devices: 13 us -> 10.8 us  [swap(): return lax.ppermute(value, axis, pairs)]
    pallas_call x4, Pallas kernels: 4.92 us -> 2.85 us  [product(): pl.pallas_call(functools.partial(product_kernel, half * (total // 2)), ou...]
    ppermute x14, starting transfers between devices: 18.9 us -> 18.4 us  [swap(): return lax.ppermute(value, axis, pairs)]
  transfers between devices with their start and end apart: 14 -> 14, of which waited for: 8 -> 6; matrix products, arithmetic and copies ran while one was open for 0% -> 0% of each run, Pallas kernels for 18% -> 16%
where the time goes in v3:
time: 39 us; the launch traced here: 38.7 us
  starting transfers between devices  18.4 us (47%)
  waiting for transfers between devices  10.8 us (28%)
  Pallas kernels  8.79 us (23%)
  between operations  0.75 us (2%)
    ppermute x14, starting transfers between devices, swap(): return lax.ppermute(value, axis, pairs)  18.4 us
    ppermute x14, waiting for transfers between devices, swap(): return lax.ppermute(value, axis, pairs)  10.8 us
    pallas_call x1, Pallas kernels, merge_tiles(): pl.pallas_call(functools.partial(merge_kernel, own_tiles, labels.shape[1]...  3.06 us
    pallas_call x4, Pallas kernels, product(): pl.pallas_call(functools.partial(product_kernel, half * (total // 2)), ou...  2.85 us
    pallas_call x1, Pallas kernels, project(): pl.pallas_call(project_kernel, out_shape=[jax.ShapeDtypeStruct((rows, hid...  1.82 us
    pallas_call x1, Pallas kernels, finish(): pl.pallas_call(functools.partial(finish_kernel, len(pieces)), out_shape=j...  0.88 us
  transfers between devices with their start and end apart: 14, of which 6 were waited for; matrix products, arithmetic and copies ran while one was open for 0% of the time, Pallas kernels for 16%

profile of v3, /device:TPU:0, one launch (start us, length us, event | category | flops | bytes accessed | tf_op | source)
XLA Modules:
  0.0 38.7 jit_solution(2870959559375795404)
XLA Ops:
  0.0 1.8 %shard_map.91 = (f32[256,512]{1,0:T(8,128)S(1)}, bf16[256,256]{1,0:T(8,128)(2,1)S(1)}, bf16[256,256]{1,0:T(8,128)(2,1)S(1)}) custom-call(bf16[256,1024]{1,0:T(8,128)(2,1)} %features_hbm.1, bf16[1024,512]{1,0:T(8,128)(2,1)} %weight_hbm.1, f32[2,128]{1,0:T(2,128)} %bitcast.5), custom_call_target="tpu_custom_call" | custom-call | flops 268435456 | bytes 1572864 | tf_op jit(solution)/shard_map/pallas_call | solution.py:66
  1.8 5.1 %collective-permute-start = (bf16[256,256]{1,0:T(8,128)(2,1)S(1)}, bf16[256,256]{1,0:T(8,128)(2,1)S(1)}, u32[]{:S(2)}, u32[]{:S(2)}) collective-permute-start(bf16[256,256]{1,0:T(8,128)(2,1)S(1)} %get-tuple-element.23.refs_0_), channel_id=1, source_target_pairs={{0,3},{1,2},{2,1},{3,0},{4,7},{5,6},{6,5},{7,4},{8,11},{9,10},{10,... | collective-permute-start | bytes 393224 | tf_op jit(solution)/shard_map/ppermute | solution.py:273
  6.9 0.0 collective-permute-start.1
  6.9 0.9 %collective-permute-start.8 = (bf16[256,256]{1,0:T(8,128)(2,1)S(1)}, bf16[256,256]{1,0:T(8,128)(2,1)S(1)}, u32[]{:S(2)}, u32[]{:S(2)}) collective-permute-start(bf16[256,256]{1,0:T(8,128)(2,1)S(1)} %get-tuple-element.31.refs_0_), channel_id=1, source_target_pairs={{0,3},{1,2},{2,1},{3,0},{4,7},{5,6},{6,5},{7,4},{8,11},{9,10},{10,... | collective-permute-start | bytes 393224 | tf_op jit(solution)/shard_map/ppermute | solution.py:273
  8.5 3.1 %shard_map.92.matrix = bf16[2048,1024]{1,0:T(8,128)(2,1)S(1)} custom-call(s32[1]{0:T(128)} %bitcast.2.row, s32[1]{0:T(128)} %bitcast.3.column, s32[1]{0:T(128)S(6)} %copy.10.count, s32[1,64]{1,0:T(1,128)} %sources_hbm.1, s32[1,64]{1,0:T(1,128)} %targets_hbm.1, s32[1,16]{1,0:T(1,128)} %labels_hbm.1, bf16[1,64,128,128]{3,2,1,0:T(8,128)(2,1)} %tiles_hbm.1), custom_call_target="tpu_custom_call" | custom-call | flops 8388608 | bytes 12582912 | tf_op jit(solution)/shard_map/pallas_call | solution.py:139
  11.6 3.2 %collective-permute-start.2 = (bf16[256,256]{1,0:T(8,128)(2,1)S(1)}, bf16[256,256]{1,0:T(8,128)(2,1)S(1)}, u32[]{:S(2)}, u32[]{:S(2)}) collective-permute-start(bf16[256,256]{1,0:T(8,128)(2,1)S(1)} %collective-permute-done.refs_3_), channel_id=1, source_target_pairs={{0,1},{1,0},{2,3},{3,2},{4,5},{5,4},{6,7},{7,6},{8,9},{9,8},{10,11... | collective-permute-start | bytes 393224 | tf_op jit(solution)/shard_map/ppermute | solution.py:273
  14.8 0.0 collective-permute-start.7
  14.8 1.9 %collective-permute-done.8.refs_3_ = bf16[256,256]{1,0:T(8,128)(2,1)S(1)} collective-permute-done((bf16[256,256]{1,0:T(8,128)(2,1)S(1)}, bf16[256,256]{1,0:T(8,128)(2,1)S(1)}, u32[]{:S(2)}, u32[]{:S(2)}) %collective-permute-start.8) | collective-permute-done | bytes 131104 | tf_op jit(solution)/shard_map/ppermute | solution.py:273
  16.7 1.9 %collective-permute-start.9 = (bf16[256,256]{1,0:T(8,128)(2,1)S(1)}, bf16[256,256]{1,0:T(8,128)(2,1)S(1)}, u32[]{:S(2)}, u32[]{:S(2)}) collective-permute-start(bf16[256,256]{1,0:T(8,128)(2,1)S(1)} %collective-permute-done.8.refs_3_), channel_id=1, source_target_pairs={{0,1},{1,0},{2,3},{3,2},{4,5},{5,4},{6,7},{7,6},{8,9},{9,8},{10,11... | collective-permute-start | bytes 393224 | tf_op jit(solution)/shard_map/ppermute | solution.py:273
  18.6 0.0 collective-permute-done.1.refs_1_
  18.6 0.8 %collective-permute-done.2.refs_2_ = bf16[256,256]{1,0:T(8,128)(2,1)S(1)} collective-permute-done((bf16[256,256]{1,0:T(8,128)(2,1)S(1)}, bf16[256,256]{1,0:T(8,128)(2,1)S(1)}, u32[]{:S(2)}, u32[]{:S(2)}) %collective-permute-start.2) | collective-permute-done | bytes 131104 | tf_op jit(solution)/shard_map/ppermute | solution.py:273
  19.4 0.7 %shard_map.94 = bf16[1024,256]{1,0:T(8,128)(2,1)S(1)} custom-call(bf16[2048,1024]{1,0:T(8,128)(2,1)S(1)} %shard_map.92.matrix, bf16[256,256]{1,0:T(8,128)(2,1)S(1)} %get-tuple-element.23.refs_0_, bf16[256,256]{1,0:T(8,128)(2,1)S(1)} %collective-permute-done.1.refs_1_, bf16[256,256]{1,0:T(8,128)(2,1)S(1)} %collective-permute-done.2.refs_2_, ...), custom_call_target="tpu_custom_call" | custom-call | flops 10737418240 | bytes 1 | tf_op jit(solution)/shard_map/pallas_call | solution.py:174
  20.1 0.1 collective-permute-start.3
  20.2 0.7 %shard_map.93.stay = f32[1024,256]{1,0:T(8,128)S(1)} custom-call(bf16[2048,1024]{1,0:T(8,128)(2,1)S(1)} %shard_map.92.matrix, bf16[256,256]{1,0:T(8,128)(2,1)S(1)} %get-tuple-element.23.refs_0_, bf16[256,256]{1,0:T(8,128)(2,1)S(1)} %collective-permute-done.1.refs_1_, bf16[256,256]{1,0:T(8,128)(2,1)S(1)} %collective-permute-done.2.refs_2_, ...), custom_call_target="tpu_custom_call" | custom-call | flops 10737418240 | bytes 1 | tf_op jit(solution)/shard_map/pallas_call | solution.py:174
  20.9 1.2 %collective-permute-done.3.came = bf16[1024,256]{1,0:T(8,128)(2,1)S(1)} collective-permute-done((bf16[1024,256]{1,0:T(8,128)(2,1)S(1)}, bf16[1024,256]{1,0:T(8,128)(2,1)S(1)}, u32[]{:S(2)}, u32[]{:S(2)}) %collective-permute-start.3) | collective-permute-done | bytes 524320 | tf_op jit(solution)/shard_map/ppermute | solution.py:273
  22.1 0.1 shard_map.95
  22.2 2.6 %collective-permute-start.4 = (bf16[256,256]{1,0:T(8,128)(2,1)S(1)}, bf16[256,256]{1,0:T(8,128)(2,1)S(1)}, u32[]{:S(2)}, u32[]{:S(2)}) collective-permute-start(bf16[256,256]{1,0:T(8,128)(2,1)S(1)} %get-tuple-element.27), channel_id=1, source_target_pairs={{0,24},{4,28},{8,16},{12,20},{16,8},{20,12},{24,0},{28,4},{1,25},{... | collective-permute-start | bytes 393224 | tf_op jit(solution)/shard_map/ppermute | solution.py:273
  24.8 0.7 %collective-permute-start.5 = (bf16[256,256]{1,0:T(8,128)(2,1)S(1)}, bf16[256,256]{1,0:T(8,128)(2,1)S(1)}, u32[]{:S(2)}, u32[]{:S(2)}) collective-permute-start(bf16[256,256]{1,0:T(8,128)(2,1)S(1)} %get-tuple-element.28), channel_id=1, source_target_pairs={{0,16},{4,20},{8,24},{12,28},{16,0},{20,4},{24,8},{28,12},{1,17},{... | collective-permute-start | bytes 393224 | tf_op jit(solution)/shard_map/ppermute | solution.py:273
  25.5 0.2 collective-permute-start.6
  25.7 0.7 %shard_map.97 = bf16[1024,256]{1,0:T(8,128)(2,1)S(1)} custom-call(bf16[2048,1024]{1,0:T(8,128)(2,1)S(1)} %shard_map.92.matrix, bf16[256,256]{1,0:T(8,128)(2,1)S(1)} %get-tuple-element.31.refs_0_, bf16[256,256]{1,0:T(8,128)(2,1)S(1)} %collective-permute-done.7.refs_1_, bf16[256,256]{1,0:T(8,128)(2,1)S(1)} %collective-permute-done.9.refs_2_, ...), custom_call_target="tpu_custom_call" | custom-call | bytes 1 | tf_op jit(solution)/shard_map/pallas_call | solution.py:174
  26.4 0.0 copy-start
  26.5 0.1 collective-permute-start.10
  26.5 0.7 %shard_map.96.stay = f32[1024,256]{1,0:T(8,128)S(1)} custom-call(bf16[2048,1024]{1,0:T(8,128)(2,1)S(1)} %shard_map.92.matrix, bf16[256,256]{1,0:T(8,128)(2,1)S(1)} %get-tuple-element.31.refs_0_, bf16[256,256]{1,0:T(8,128)(2,1)S(1)} %collective-permute-done.7.refs_1_, bf16[256,256]{1,0:T(8,128)(2,1)S(1)} %collective-permute-done.9.refs_2_, ...), custom_call_target="tpu_custom_call" | custom-call | flops 10737418240 | bytes 1 | tf_op jit(solution)/shard_map/pallas_call | solution.py:174
  27.3 1.2 %collective-permute-done.10.came = bf16[1024,256]{1,0:T(8,128)(2,1)S(1)} collective-permute-done((bf16[1024,256]{1,0:T(8,128)(2,1)S(1)}, bf16[1024,256]{1,0:T(8,128)(2,1)S(1)}, u32[]{:S(2)}, u32[]{:S(2)}) %collective-permute-start.10) | collective-permute-done | bytes 524320 | tf_op jit(solution)/shard_map/ppermute | solution.py:273
  28.4 0.1 shard_map.98
  28.5 2.6 %collective-permute-start.11 = (bf16[256,256]{1,0:T(8,128)(2,1)S(1)}, bf16[256,256]{1,0:T(8,128)(2,1)S(1)}, u32[]{:S(2)}, u32[]{:S(2)}) collective-permute-start(bf16[256,256]{1,0:T(8,128)(2,1)S(1)} %get-tuple-element.36), channel_id=1, source_target_pairs={{0,24},{4,28},{8,16},{12,20},{16,8},{20,12},{24,0},{28,4},{1,25},{... | collective-permute-start | bytes 393224 | tf_op jit(solution)/shard_map/ppermute | solution.py:273
  31.2 0.7 %collective-permute-start.12 = (bf16[256,256]{1,0:T(8,128)(2,1)S(1)}, bf16[256,256]{1,0:T(8,128)(2,1)S(1)}, u32[]{:S(2)}, u32[]{:S(2)}) collective-permute-start(bf16[256,256]{1,0:T(8,128)(2,1)S(1)} %get-tuple-element.37), channel_id=1, source_target_pairs={{0,16},{4,20},{8,24},{12,28},{16,0},{20,4},{24,8},{28,12},{1,17},{... | collective-permute-start | bytes 393224 | tf_op jit(solution)/shard_map/ppermute | solution.py:273
  31.9 0.2 collective-permute-start.13
  32.1 3.1 %collective-permute-done.11.refs_5_ = bf16[256,256]{1,0:T(8,128)(2,1)S(1)} collective-permute-done((bf16[256,256]{1,0:T(8,128)(2,1)S(1)}, bf16[256,256]{1,0:T(8,128)(2,1)S(1)}, u32[]{:S(2)}, u32[]{:S(2)}) %collective-permute-start.11) | collective-permute-done | bytes 131104 | tf_op jit(solution)/shard_map/ppermute | solution.py:273
  35.2 2.6 %collective-permute-done.12.refs_6_ = bf16[256,256]{1,0:T(8,128)(2,1)S(1)} collective-permute-done((bf16[256,256]{1,0:T(8,128)(2,1)S(1)}, bf16[256,256]{1,0:T(8,128)(2,1)S(1)}, u32[]{:S(2)}, u32[]{:S(2)}) %collective-permute-start.12) | collective-permute-done | bytes 131104 | tf_op jit(solution)/shard_map/ppermute | solution.py:273
  37.8 0.0 collective-permute-done.13.refs_7_
  37.9 0.9 %shard_map.99 = bf16[256,512]{1,0:T(8,128)(2,1)} custom-call(f32[256,512]{1,0:T(8,128)S(1)} %get-tuple-element.22.projected, f32[2,128]{1,0:T(2,128)S(1)} %bitcast.4, f32[256,256]{1,0:T(8,128)S(1)} %get-tuple-element.26.refs_0_, bf16[256,256]{1,0:T(8,128)(2,1)S(1)} %collective-permute-done.4.refs_1_, bf16[256,256]{1,0:T(8,128)(2,1)S(1)} %collective-permute-done.5.refs_2_, ...), custom_call_target="tpu_custom_call" | custom-call | flops 786432 | bytes 2097152 | tf_op jit(solution)/shard_map/pallas_call | solution.py:227
  (7 shorter events, 0.0 us)
Async XLA Ops:
  1.8 9.7 %collective-permute-start = (bf16[256,256]{1,0:T(8,128)(2,1)S(1)}, bf16[256,256]{1,0:T(8,128)(2,1)S(1)}, u32[]{:S(2)}, u32[]{:S(2)}) collective-permute-start(bf16[256,256]{1,0:T(8,128)(2,1)S(1)} %get-tuple-element.23.refs_0_), channel_id=1, source_target_pairs={{0,3},{1,2},{2,1},{3,0},{4,7},{5,6},{6,5},{7,4},{8,11},{9,10},{10,... | collective-permute-start | bytes 393224 | tf_op jit(solution)/shard_map/ppermute | solution.py:273
  6.9 11.6 %collective-permute-start.1 = (bf16[256,256]{1,0:T(8,128)(2,1)S(1)}, bf16[256,256]{1,0:T(8,128)(2,1)S(1)}, u32[]{:S(2)}, u32[]{:S(2)}) collective-permute-start(bf16[256,256]{1,0:T(8,128)(2,1)S(1)} %get-tuple-element.23.refs_0_), channel_id=1, source_target_pairs={{0,1},{1,0},{2,3},{3,2},{4,5},{5,4},{6,7},{7,6},{8,9},{9,8},{10,11... | collective-permute-start | bytes 393224 | tf_op jit(solution)/shard_map/ppermute | solution.py:273
  6.9 9.8 %collective-permute-start.8 = (bf16[256,256]{1,0:T(8,128)(2,1)S(1)}, bf16[256,256]{1,0:T(8,128)(2,1)S(1)}, u32[]{:S(2)}, u32[]{:S(2)}) collective-permute-start(bf16[256,256]{1,0:T(8,128)(2,1)S(1)} %get-tuple-element.31.refs_0_), channel_id=1, source_target_pairs={{0,3},{1,2},{2,1},{3,0},{4,7},{5,6},{6,5},{7,4},{8,11},{9,10},{10,... | collective-permute-start | bytes 393224 | tf_op jit(solution)/shard_map/ppermute | solution.py:273
  11.6 7.8 %collective-permute-start.2 = (bf16[256,256]{1,0:T(8,128)(2,1)S(1)}, bf16[256,256]{1,0:T(8,128)(2,1)S(1)}, u32[]{:S(2)}, u32[]{:S(2)}) collective-permute-start(bf16[256,256]{1,0:T(8,128)(2,1)S(1)} %collective-permute-done.refs_3_), channel_id=1, source_target_pairs={{0,1},{1,0},{2,3},{3,2},{4,5},{5,4},{6,7},{7,6},{8,9},{9,8},{10,11... | collective-permute-start | bytes 393224 | tf_op jit(solution)/shard_map/ppermute | solution.py:273
  14.8 11.0 %collective-permute-start.7 = (bf16[256,256]{1,0:T(8,128)(2,1)S(1)}, bf16[256,256]{1,0:T(8,128)(2,1)S(1)}, u32[]{:S(2)}, u32[]{:S(2)}) collective-permute-start(bf16[256,256]{1,0:T(8,128)(2,1)S(1)} %get-tuple-element.31.refs_0_), channel_id=1, source_target_pairs={{0,1},{1,0},{2,3},{3,2},{4,5},{5,4},{6,7},{7,6},{8,9},{9,8},{10,11... | collective-permute-start | bytes 393224 | tf_op jit(solution)/shard_map/ppermute | solution.py:273
  16.7 9.0 %collective-permute-start.9 = (bf16[256,256]{1,0:T(8,128)(2,1)S(1)}, bf16[256,256]{1,0:T(8,128)(2,1)S(1)}, u32[]{:S(2)}, u32[]{:S(2)}) collective-permute-start(bf16[256,256]{1,0:T(8,128)(2,1)S(1)} %collective-permute-done.8.refs_3_), channel_id=1, source_target_pairs={{0,1},{1,0},{2,3},{3,2},{4,5},{5,4},{6,7},{7,6},{8,9},{9,8},{10,11... | collective-permute-start | bytes 393224 | tf_op jit(solution)/shard_map/ppermute | solution.py:273
  20.1 2.0 %collective-permute-start.3 = (bf16[1024,256]{1,0:T(8,128)(2,1)S(1)}, bf16[1024,256]{1,0:T(8,128)(2,1)S(1)}, u32[]{:S(2)}, u32[]{:S(2)}) collective-permute-start(bf16[1024,256]{1,0:T(8,128)(2,1)S(1)} %shard_map.94), channel_id=1, source_target_pairs={{0,4},{4,0},{8,12},{12,8},{16,20},{20,16},{24,28},{28,24},{1,5},{5... | collective-permute-start | bytes 1572872 | tf_op jit(solution)/shard_map/ppermute | solution.py:273
  22.2 9.7 %collective-permute-start.4 = (bf16[256,256]{1,0:T(8,128)(2,1)S(1)}, bf16[256,256]{1,0:T(8,128)(2,1)S(1)}, u32[]{:S(2)}, u32[]{:S(2)}) collective-permute-start(bf16[256,256]{1,0:T(8,128)(2,1)S(1)} %get-tuple-element.27), channel_id=1, source_target_pairs={{0,24},{4,28},{8,16},{12,20},{16,8},{20,12},{24,0},{28,4},{1,25},{... | collective-permute-start | bytes 393224 | tf_op jit(solution)/shard_map/ppermute | solution.py:273
  24.8 7.3 %collective-permute-start.5 = (bf16[256,256]{1,0:T(8,128)(2,1)S(1)}, bf16[256,256]{1,0:T(8,128)(2,1)S(1)}, u32[]{:S(2)}, u32[]{:S(2)}) collective-permute-start(bf16[256,256]{1,0:T(8,128)(2,1)S(1)} %get-tuple-element.28), channel_id=1, source_target_pairs={{0,16},{4,20},{8,24},{12,28},{16,0},{20,4},{24,8},{28,12},{1,17},{... | collective-permute-start | bytes 393224 | tf_op jit(solution)/shard_map/ppermute | solution.py:273
  25.5 6.6 %collective-permute-start.6 = (bf16[256,256]{1,0:T(8,128)(2,1)S(1)}, bf16[256,256]{1,0:T(8,128)(2,1)S(1)}, u32[]{:S(2)}, u32[]{:S(2)}) collective-permute-start(bf16[256,256]{1,0:T(8,128)(2,1)S(1)} %get-tuple-element.29), channel_id=1, source_target_pairs={{0,8},{4,12},{8,0},{12,4},{16,24},{20,28},{24,16},{28,20},{1,9},{5... | collective-permute-start | bytes 393224 | tf_op jit(solution)/shard_map/ppermute | solution.py:273
  26.4 11.4 %copy-start = (f32[256]{0:T(256)S(1)}, f32[256]{0:T(256)}, u32[]{:S(2)}) copy-start(f32[256]{0:T(256)} %param.12) | copy-start | bytes 3076
  26.5 2.0 %collective-permute-start.10 = (bf16[1024,256]{1,0:T(8,128)(2,1)S(1)}, bf16[1024,256]{1,0:T(8,128)(2,1)S(1)}, u32[]{:S(2)}, u32[]{:S(2)}) collective-permute-start(bf16[1024,256]{1,0:T(8,128)(2,1)S(1)} %shard_map.97), channel_id=1, source_target_pairs={{0,4},{4,0},{8,12},{12,8},{16,20},{20,16},{24,28},{28,24},{1,5},{5... | collective-permute-start | bytes 1572872 | tf_op jit(solution)/shard_map/ppermute | solution.py:273
  28.5 6.7 %collective-permute-start.11 = (bf16[256,256]{1,0:T(8,128)(2,1)S(1)}, bf16[256,256]{1,0:T(8,128)(2,1)S(1)}, u32[]{:S(2)}, u32[]{:S(2)}) collective-permute-start(bf16[256,256]{1,0:T(8,128)(2,1)S(1)} %get-tuple-element.36), channel_id=1, source_target_pairs={{0,24},{4,28},{8,16},{12,20},{16,8},{20,12},{24,0},{28,4},{1,25},{... | collective-permute-start | bytes 393224 | tf_op jit(solution)/shard_map/ppermute | solution.py:273
  31.2 6.7 %collective-permute-start.12 = (bf16[256,256]{1,0:T(8,128)(2,1)S(1)}, bf16[256,256]{1,0:T(8,128)(2,1)S(1)}, u32[]{:S(2)}, u32[]{:S(2)}) collective-permute-start(bf16[256,256]{1,0:T(8,128)(2,1)S(1)} %get-tuple-element.37), channel_id=1, source_target_pairs={{0,16},{4,20},{8,24},{12,28},{16,0},{20,4},{24,8},{28,12},{1,17},{... | collective-permute-start | bytes 393224 | tf_op jit(solution)/shard_map/ppermute | solution.py:273
  31.9 6.0 %collective-permute-start.13 = (bf16[256,256]{1,0:T(8,128)(2,1)S(1)}, bf16[256,256]{1,0:T(8,128)(2,1)S(1)}, u32[]{:S(2)}, u32[]{:S(2)}) collective-permute-start(bf16[256,256]{1,0:T(8,128)(2,1)S(1)} %get-tuple-element.38), channel_id=1, source_target_pairs={{0,8},{4,12},{8,0},{12,4},{16,24},{20,28},{24,16},{28,20},{1,9},{5... | collective-permute-start | bytes 393224 | tf_op jit(solution)/shard_map/ppermute | solution.py:273

commit v4 on v3

--- a/solution.py
+++ b/solution.py
@@ -274,7 +274,7 @@
 
 
 def exchange(sent):
-    return [swap(sent[k], "row", 2 * (k + 1)) for k in reversed(range(len(sent)))]
+    return [swap(value, "row", 2 * (k + 1)) for k, value in enumerate(sent)]
 
 
 def per_device(
@@ -308,13 +308,21 @@
 
     projected, *scaled = project(features, weight, source_norm, CHUNKS)
     matrix = merge_tiles(own_tiles, owners, span, index_args, tile_weights)
-    across = [swap(own, "col", 3) for own in scaled]
-    beside = [swap(own, "col", 1) for own in scaled]
-    across[0], matrix = lax.optimization_barrier((across[0], matrix))
-    passed = [swap(value, "col", 1) for value in across]
     pieces, sent = [], None
-    for blocks, wait in zip(zip(scaled, beside, passed, across), WEIGHTS):
-        if sent is not None:
+    for chunk, (own, wait) in enumerate(zip(scaled, WEIGHTS)):
+        lead = trail = own
+        if chunk:
+            lead, _ = lax.optimization_barrier((own, across))
+            trail, _ = lax.optimization_barrier((own, away))
+        across = swap(lead, "col", 3)
+        beside = swap(trail, "col", 1)
+        if chunk:
+            onward, _ = lax.optimization_barrier((across, sent))
+        else:
+            onward, beside, matrix = lax.optimization_barrier((across, beside, matrix))
+        passed = swap(onward, "col", 1)
+        blocks = own, beside, passed, across
+        if chunk:
             pieces[-1] += exchange(sent)
             blocks, _ = lax.optimization_barrier((blocks, sent))
         away = product(matrix, blocks, 0, jnp.bfloat16, wait[0])

time: 39 us -> 42.9 us (1.100)
  waiting for transfers between devices: 10.8 us -> 16.1 us
  starting transfers between devices: 18.4 us -> 17.3 us
    ppermute x14, waiting for transfers between devices: 10.8 us -> 16.1 us  [swap(): return lax.ppermute(value, axis, pairs)]
    ppermute x14, starting transfers between devices: 18.4 us -> 17.3 us  [swap(): return lax.ppermute(value, axis, pairs)]
  transfers between devices with their start and end apart: 14 -> 14, of which waited for: 6 -> 7; matrix products, arithmetic and copies ran while one was open for 0% -> 0% of each run, Pallas kernels for 16% -> 14%
where the time goes in v4:
time: 42.9 us; the launch traced here: 42.7 us
  starting transfers between devices  17.3 us (40%)
  waiting for transfers between devices  16.1 us (38%)
  Pallas kernels  8.49 us (20%)
  between operations  0.76 us (2%)
    ppermute x14, starting transfers between devices, swap(): return lax.ppermute(value, axis, pairs)  17.3 us
    ppermute x14, waiting for transfers between devices, swap(): return lax.ppermute(value, axis, pairs)  16.1 us
    pallas_call x4, Pallas kernels, product(): pl.pallas_call(functools.partial(product_kernel, half * (total // 2)), ou...  2.84 us
    pallas_call x1, Pallas kernels, merge_tiles(): pl.pallas_call(functools.partial(merge_kernel, own_tiles, labels.shape[1]...  2.77 us
    pallas_call x1, Pallas kernels, project(): pl.pallas_call(project_kernel, out_shape=[jax.ShapeDtypeStruct((rows, hid...  1.82 us
    pallas_call x1, Pallas kernels, finish(): pl.pallas_call(functools.partial(finish_kernel, len(pieces)), out_shape=j...  0.88 us
  transfers between devices with their start and end apart: 14, of which 7 were waited for; matrix products, arithmetic and copies ran while one was open for 0% of the time, Pallas kernels for 14%

profile of v4, /device:TPU:0, one launch (start us, length us, event | category | flops | bytes accessed | tf_op | source)
XLA Modules:
  0.0 42.7 jit_solution(18445212121530049132)
XLA Ops:
  0.0 1.8 %shard_map.91 = (f32[256,512]{1,0:T(8,128)S(1)}, bf16[256,256]{1,0:T(8,128)(2,1)S(1)}, bf16[256,256]{1,0:T(8,128)(2,1)S(1)}) custom-call(bf16[256,1024]{1,0:T(8,128)(2,1)} %features_hbm.1, bf16[1024,512]{1,0:T(8,128)(2,1)} %weight_hbm.1, f32[2,128]{1,0:T(2,128)} %bitcast.5), custom_call_target="tpu_custom_call" | custom-call | flops 268435456 | bytes 1572864 | tf_op jit(solution)/shard_map/pallas_call | solution.py:66
  1.8 3.1 %collective-permute-start.1 = (bf16[256,256]{1,0:T(8,128)(2,1)S(1)}, bf16[256,256]{1,0:T(8,128)(2,1)S(1)}, u32[]{:S(2)}, u32[]{:S(2)}) collective-permute-start(bf16[256,256]{1,0:T(8,128)(2,1)S(1)} %get-tuple-element.27.refs_0_), channel_id=1, source_target_pairs={{0,1},{1,0},{2,3},{3,2},{4,5},{5,4},{6,7},{7,6},{8,9},{9,8},{10,11... | collective-permute-start | bytes 393224 | tf_op jit(solution)/shard_map/ppermute | solution.py:273
  4.9 2.5 %collective-permute-start = (bf16[256,256]{1,0:T(8,128)(2,1)S(1)}, bf16[256,256]{1,0:T(8,128)(2,1)S(1)}, u32[]{:S(2)}, u32[]{:S(2)}) collective-permute-start(bf16[256,256]{1,0:T(8,128)(2,1)S(1)} %get-tuple-element.27.refs_0_), channel_id=1, source_target_pairs={{0,3},{1,2},{2,1},{3,0},{4,7},{5,6},{6,5},{7,4},{8,11},{9,10},{10,... | collective-permute-start | bytes 393224 | tf_op jit(solution)/shard_map/ppermute | solution.py:273
  8.0 2.8 %shard_map.92.matrix = bf16[2048,1024]{1,0:T(8,128)(2,1)S(1)} custom-call(s32[1]{0:T(128)} %bitcast.2.row, s32[1]{0:T(128)} %bitcast.3.column, s32[1]{0:T(128)S(6)} %copy.10.count, s32[1,64]{1,0:T(1,128)} %sources_hbm.1, s32[1,64]{1,0:T(1,128)} %targets_hbm.1, s32[1,16]{1,0:T(1,128)} %labels_hbm.1, bf16[1,64,128,128]{3,2,1,0:T(8,128)(2,1)} %tiles_hbm.1), custom_call_target="tpu_custom_call" | custom-call | flops 8388608 | bytes 12582912 | tf_op jit(solution)/shard_map/pallas_call | solution.py:139
  10.8 0.0 collective-permute-done.1.refs_1_
  10.8 2.7 %collective-permute-done.refs_3_ = bf16[256,256]{1,0:T(8,128)(2,1)S(1)} collective-permute-done((bf16[256,256]{1,0:T(8,128)(2,1)S(1)}, bf16[256,256]{1,0:T(8,128)(2,1)S(1)}, u32[]{:S(2)}, u32[]{:S(2)}) %collective-permute-start) | collective-permute-done | bytes 131104 | tf_op jit(solution)/shard_map/ppermute | solution.py:273
  13.5 0.6 %collective-permute-start.2 = (bf16[256,256]{1,0:T(8,128)(2,1)S(1)}, bf16[256,256]{1,0:T(8,128)(2,1)S(1)}, u32[]{:S(2)}, u32[]{:S(2)}) collective-permute-start(bf16[256,256]{1,0:T(8,128)(2,1)S(1)} %collective-permute-done.refs_3_), channel_id=1, source_target_pairs={{0,1},{1,0},{2,3},{3,2},{4,5},{5,4},{6,7},{7,6},{8,9},{9,8},{10,11... | collective-permute-start | bytes 393224 | tf_op jit(solution)/shard_map/ppermute | solution.py:273
  14.1 2.6 %collective-permute-start.8 = (bf16[256,256]{1,0:T(8,128)(2,1)S(1)}, bf16[256,256]{1,0:T(8,128)(2,1)S(1)}, u32[]{:S(2)}, u32[]{:S(2)}) collective-permute-start(bf16[256,256]{1,0:T(8,128)(2,1)S(1)} %get-tuple-element.39.refs_0_), channel_id=1, source_target_pairs={{0,3},{1,2},{2,1},{3,0},{4,7},{5,6},{6,5},{7,4},{8,11},{9,10},{10,... | collective-permute-start | bytes 393224 | tf_op jit(solution)/shard_map/ppermute | solution.py:273
  16.7 3.2 %collective-permute-done.2.refs_2_ = bf16[256,256]{1,0:T(8,128)(2,1)S(1)} collective-permute-done((bf16[256,256]{1,0:T(8,128)(2,1)S(1)}, bf16[256,256]{1,0:T(8,128)(2,1)S(1)}, u32[]{:S(2)}, u32[]{:S(2)}) %collective-permute-start.2) | collective-permute-done | bytes 131104 | tf_op jit(solution)/shard_map/ppermute | solution.py:273
  19.9 0.7 %shard_map.94 = bf16[1024,256]{1,0:T(8,128)(2,1)S(1)} custom-call(bf16[2048,1024]{1,0:T(8,128)(2,1)S(1)} %shard_map.92.matrix, bf16[256,256]{1,0:T(8,128)(2,1)S(1)} %get-tuple-element.27.refs_0_, bf16[256,256]{1,0:T(8,128)(2,1)S(1)} %collective-permute-done.1.refs_1_, bf16[256,256]{1,0:T(8,128)(2,1)S(1)} %collective-permute-done.2.refs_2_, ...), custom_call_target="tpu_custom_call" | custom-call | flops 10737418240 | bytes 1 | tf_op jit(solution)/shard_map/pallas_call | solution.py:174
  20.6 0.1 collective-permute-start.3
  20.7 0.4 collective-permute-start.7
  21.1 0.7 %shard_map.93.stay = f32[1024,256]{1,0:T(8,128)S(1)} custom-call(bf16[2048,1024]{1,0:T(8,128)(2,1)S(1)} %shard_map.92.matrix, bf16[256,256]{1,0:T(8,128)(2,1)S(1)} %get-tuple-element.27.refs_0_, bf16[256,256]{1,0:T(8,128)(2,1)S(1)} %collective-permute-done.1.refs_1_, bf16[256,256]{1,0:T(8,128)(2,1)S(1)} %collective-permute-done.2.refs_2_, ...), custom_call_target="tpu_custom_call" | custom-call | flops 10737418240 | bytes 1 | tf_op jit(solution)/shard_map/pallas_call | solution.py:174
  21.8 0.8 %collective-permute-done.3.came = bf16[1024,256]{1,0:T(8,128)(2,1)S(1)} collective-permute-done((bf16[1024,256]{1,0:T(8,128)(2,1)S(1)}, bf16[1024,256]{1,0:T(8,128)(2,1)S(1)}, u32[]{:S(2)}, u32[]{:S(2)}) %collective-permute-start.3) | collective-permute-done | bytes 524320 | tf_op jit(solution)/shard_map/ppermute | solution.py:273
  22.6 0.1 shard_map.95
  22.7 1.0 %collective-permute-start.9 = (bf16[256,256]{1,0:T(8,128)(2,1)S(1)}, bf16[256,256]{1,0:T(8,128)(2,1)S(1)}, u32[]{:S(2)}, u32[]{:S(2)}) collective-permute-start(bf16[256,256]{1,0:T(8,128)(2,1)S(1)} %collective-permute-done.8.refs_3_), channel_id=1, source_target_pairs={{0,1},{1,0},{2,3},{3,2},{4,5},{5,4},{6,7},{7,6},{8,9},{9,8},{10,11... | collective-permute-start | bytes 393224 | tf_op jit(solution)/shard_map/ppermute | solution.py:273
  23.7 1.5 %collective-permute-start.4 = (bf16[256,256]{1,0:T(8,128)(2,1)S(1)}, bf16[256,256]{1,0:T(8,128)(2,1)S(1)}, u32[]{:S(2)}, u32[]{:S(2)}) collective-permute-start(bf16[256,256]{1,0:T(8,128)(2,1)S(1)} %get-tuple-element.32), channel_id=1, source_target_pairs={{0,8},{4,12},{8,0},{12,4},{16,24},{20,28},{24,16},{28,20},{1,9},{5... | collective-permute-start | bytes 393224 | tf_op jit(solution)/shard_map/ppermute | solution.py:273
  25.2 1.5 %collective-permute-start.5 = (bf16[256,256]{1,0:T(8,128)(2,1)S(1)}, bf16[256,256]{1,0:T(8,128)(2,1)S(1)}, u32[]{:S(2)}, u32[]{:S(2)}) collective-permute-start(bf16[256,256]{1,0:T(8,128)(2,1)S(1)} %get-tuple-element.33), channel_id=1, source_target_pairs={{0,16},{4,20},{8,24},{12,28},{16,0},{20,4},{24,8},{28,12},{1,17},{... | collective-permute-start | bytes 393224 | tf_op jit(solution)/shard_map/ppermute | solution.py:273
  26.7 0.5 %collective-permute-start.6 = (bf16[256,256]{1,0:T(8,128)(2,1)S(1)}, bf16[256,256]{1,0:T(8,128)(2,1)S(1)}, u32[]{:S(2)}, u32[]{:S(2)}) collective-permute-start(bf16[256,256]{1,0:T(8,128)(2,1)S(1)} %get-tuple-element.34), channel_id=1, source_target_pairs={{0,24},{4,28},{8,16},{12,20},{16,8},{20,12},{24,0},{28,4},{1,25},{... | collective-permute-start | bytes 393224 | tf_op jit(solution)/shard_map/ppermute | solution.py:273
  27.2 2.2 %collective-permute-done.9.refs_2_ = bf16[256,256]{1,0:T(8,128)(2,1)S(1)} collective-permute-done((bf16[256,256]{1,0:T(8,128)(2,1)S(1)}, bf16[256,256]{1,0:T(8,128)(2,1)S(1)}, u32[]{:S(2)}, u32[]{:S(2)}) %collective-permute-start.9) | collective-permute-done | bytes 131104 | tf_op jit(solution)/shard_map/ppermute | solution.py:273
  29.4 0.7 %shard_map.97 = bf16[1024,256]{1,0:T(8,128)(2,1)S(1)} custom-call(bf16[2048,1024]{1,0:T(8,128)(2,1)S(1)} %shard_map.92.matrix, bf16[256,256]{1,0:T(8,128)(2,1)S(1)} %get-tuple-element.39.refs_0_, bf16[256,256]{1,0:T(8,128)(2,1)S(1)} %collective-permute-done.7.refs_1_, bf16[256,256]{1,0:T(8,128)(2,1)S(1)} %collective-permute-done.9.refs_2_, ...), custom_call_target="tpu_custom_call" | custom-call | bytes 1 | tf_op jit(solution)/shard_map/pallas_call | solution.py:174
  30.1 0.0 copy-start
  30.1 0.1 collective-permute-start.10
  30.2 0.7 %shard_map.96.stay = f32[1024,256]{1,0:T(8,128)S(1)} custom-call(bf16[2048,1024]{1,0:T(8,128)(2,1)S(1)} %shard_map.92.matrix, bf16[256,256]{1,0:T(8,128)(2,1)S(1)} %get-tuple-element.39.refs_0_, bf16[256,256]{1,0:T(8,128)(2,1)S(1)} %collective-permute-done.7.refs_1_, bf16[256,256]{1,0:T(8,128)(2,1)S(1)} %collective-permute-done.9.refs_2_, ...), custom_call_target="tpu_custom_call" | custom-call | flops 10737418240 | bytes 1 | tf_op jit(solution)/shard_map/pallas_call | solution.py:174
  30.9 1.2 %collective-permute-done.10.came = bf16[1024,256]{1,0:T(8,128)(2,1)S(1)} collective-permute-done((bf16[1024,256]{1,0:T(8,128)(2,1)S(1)}, bf16[1024,256]{1,0:T(8,128)(2,1)S(1)}, u32[]{:S(2)}, u32[]{:S(2)}) %collective-permute-start.10) | collective-permute-done | bytes 524320 | tf_op jit(solution)/shard_map/ppermute | solution.py:273
  32.1 0.1 shard_map.98
  32.2 1.6 %collective-permute-start.11 = (bf16[256,256]{1,0:T(8,128)(2,1)S(1)}, bf16[256,256]{1,0:T(8,128)(2,1)S(1)}, u32[]{:S(2)}, u32[]{:S(2)}) collective-permute-start(bf16[256,256]{1,0:T(8,128)(2,1)S(1)} %get-tuple-element.44), channel_id=1, source_target_pairs={{0,8},{4,12},{8,0},{12,4},{16,24},{20,28},{24,16},{28,20},{1,9},{5... | collective-permute-start | bytes 393224 | tf_op jit(solution)/shard_map/ppermute | solution.py:273
  33.8 1.5 %collective-permute-start.12 = (bf16[256,256]{1,0:T(8,128)(2,1)S(1)}, bf16[256,256]{1,0:T(8,128)(2,1)S(1)}, u32[]{:S(2)}, u32[]{:S(2)}) collective-permute-start(bf16[256,256]{1,0:T(8,128)(2,1)S(1)} %get-tuple-element.45), channel_id=1, source_target_pairs={{0,16},{4,20},{8,24},{12,28},{16,0},{20,4},{24,8},{28,12},{1,17},{... | collective-permute-start | bytes 393224 | tf_op jit(solution)/shard_map/ppermute | solution.py:273
  35.3 0.5 %collective-permute-start.13 = (bf16[256,256]{1,0:T(8,128)(2,1)S(1)}, bf16[256,256]{1,0:T(8,128)(2,1)S(1)}, u32[]{:S(2)}, u32[]{:S(2)}) collective-permute-start(bf16[256,256]{1,0:T(8,128)(2,1)S(1)} %get-tuple-element.46), channel_id=1, source_target_pairs={{0,24},{4,28},{8,16},{12,20},{16,8},{20,12},{24,0},{28,4},{1,25},{... | collective-permute-start | bytes 393224 | tf_op jit(solution)/shard_map/ppermute | solution.py:273
  35.8 2.4 %collective-permute-done.11.refs_5_ = bf16[256,256]{1,0:T(8,128)(2,1)S(1)} collective-permute-done((bf16[256,256]{1,0:T(8,128)(2,1)S(1)}, bf16[256,256]{1,0:T(8,128)(2,1)S(1)}, u32[]{:S(2)}, u32[]{:S(2)}) %collective-permute-start.11) | collective-permute-done | bytes 131104 | tf_op jit(solution)/shard_map/ppermute | solution.py:273
  38.2 3.7 %collective-permute-done.12.refs_6_ = bf16[256,256]{1,0:T(8,128)(2,1)S(1)} collective-permute-done((bf16[256,256]{1,0:T(8,128)(2,1)S(1)}, bf16[256,256]{1,0:T(8,128)(2,1)S(1)}, u32[]{:S(2)}, u32[]{:S(2)}) %collective-permute-start.12) | collective-permute-done | bytes 131104 | tf_op jit(solution)/shard_map/ppermute | solution.py:273
  41.8 0.9 %shard_map.99 = bf16[256,512]{1,0:T(8,128)(2,1)} custom-call(f32[256,512]{1,0:T(8,128)S(1)} %get-tuple-element.26.projected, f32[2,128]{1,0:T(2,128)S(1)} %bitcast.4, f32[256,256]{1,0:T(8,128)S(1)} %get-tuple-element.31.refs_0_, bf16[256,256]{1,0:T(8,128)(2,1)S(1)} %collective-permute-done.4.refs_1_, bf16[256,256]{1,0:T(8,128)(2,1)S(1)} %collective-permute-done.5.refs_2_, ...), custom_call_target="tpu_custom_call" | custom-call | flops 786432 | bytes 2097152 | tf_op jit(solution)/shard_map/pallas_call | solution.py:227
  (7 shorter events, 0.0 us)
Async XLA Ops:
  1.8 9.0 %collective-permute-start.1 = (bf16[256,256]{1,0:T(8,128)(2,1)S(1)}, bf16[256,256]{1,0:T(8,128)(2,1)S(1)}, u32[]{:S(2)}, u32[]{:S(2)}) collective-permute-start(bf16[256,256]{1,0:T(8,128)(2,1)S(1)} %get-tuple-element.27.refs_0_), channel_id=1, source_target_pairs={{0,1},{1,0},{2,3},{3,2},{4,5},{5,4},{6,7},{7,6},{8,9},{9,8},{10,11... | collective-permute-start | bytes 393224 | tf_op jit(solution)/shard_map/ppermute | solution.py:273
  4.9 8.6 %collective-permute-start = (bf16[256,256]{1,0:T(8,128)(2,1)S(1)}, bf16[256,256]{1,0:T(8,128)(2,1)S(1)}, u32[]{:S(2)}, u32[]{:S(2)}) collective-permute-start(bf16[256,256]{1,0:T(8,128)(2,1)S(1)} %get-tuple-element.27.refs_0_), channel_id=1, source_target_pairs={{0,3},{1,2},{2,1},{3,0},{4,7},{5,6},{6,5},{7,4},{8,11},{9,10},{10,... | collective-permute-start | bytes 393224 | tf_op jit(solution)/shard_map/ppermute | solution.py:273
  13.5 6.4 %collective-permute-start.2 = (bf16[256,256]{1,0:T(8,128)(2,1)S(1)}, bf16[256,256]{1,0:T(8,128)(2,1)S(1)}, u32[]{:S(2)}, u32[]{:S(2)}) collective-permute-start(bf16[256,256]{1,0:T(8,128)(2,1)S(1)} %collective-permute-done.refs_3_), channel_id=1, source_target_pairs={{0,1},{1,0},{2,3},{3,2},{4,5},{5,4},{6,7},{7,6},{8,9},{9,8},{10,11... | collective-permute-start | bytes 393224 | tf_op jit(solution)/shard_map/ppermute | solution.py:273
  14.1 8.6 %collective-permute-start.8 = (bf16[256,256]{1,0:T(8,128)(2,1)S(1)}, bf16[256,256]{1,0:T(8,128)(2,1)S(1)}, u32[]{:S(2)}, u32[]{:S(2)}) collective-permute-start(bf16[256,256]{1,0:T(8,128)(2,1)S(1)} %get-tuple-element.39.refs_0_), channel_id=1, source_target_pairs={{0,3},{1,2},{2,1},{3,0},{4,7},{5,6},{6,5},{7,4},{8,11},{9,10},{10,... | collective-permute-start | bytes 393224 | tf_op jit(solution)/shard_map/ppermute | solution.py:273
  20.6 2.0 %collective-permute-start.3 = (bf16[1024,256]{1,0:T(8,128)(2,1)S(1)}, bf16[1024,256]{1,0:T(8,128)(2,1)S(1)}, u32[]{:S(2)}, u32[]{:S(2)}) collective-permute-start(bf16[1024,256]{1,0:T(8,128)(2,1)S(1)} %shard_map.94), channel_id=1, source_target_pairs={{0,4},{4,0},{8,12},{12,8},{16,20},{20,16},{24,28},{28,24},{1,5},{5... | collective-permute-start | bytes 1572872 | tf_op jit(solution)/shard_map/ppermute | solution.py:273
  20.7 6.5 %collective-permute-start.7 = (bf16[256,256]{1,0:T(8,128)(2,1)S(1)}, bf16[256,256]{1,0:T(8,128)(2,1)S(1)}, u32[]{:S(2)}, u32[]{:S(2)}) collective-permute-start(bf16[256,256]{1,0:T(8,128)(2,1)S(1)} %get-tuple-element.39.refs_0_), channel_id=1, source_target_pairs={{0,1},{1,0},{2,3},{3,2},{4,5},{5,4},{6,7},{7,6},{8,9},{9,8},{10,11... | collective-permute-start | bytes 393224 | tf_op jit(solution)/shard_map/ppermute | solution.py:273
  22.7 6.7 %collective-permute-start.9 = (bf16[256,256]{1,0:T(8,128)(2,1)S(1)}, bf16[256,256]{1,0:T(8,128)(2,1)S(1)}, u32[]{:S(2)}, u32[]{:S(2)}) collective-permute-start(bf16[256,256]{1,0:T(8,128)(2,1)S(1)} %collective-permute-done.8.refs_3_), channel_id=1, source_target_pairs={{0,1},{1,0},{2,3},{3,2},{4,5},{5,4},{6,7},{7,6},{8,9},{9,8},{10,11... | collective-permute-start | bytes 393224 | tf_op jit(solution)/shard_map/ppermute | solution.py:273
  23.7 11.6 %collective-permute-start.4 = (bf16[256,256]{1,0:T(8,128)(2,1)S(1)}, bf16[256,256]{1,0:T(8,128)(2,1)S(1)}, u32[]{:S(2)}, u32[]{:S(2)}) collective-permute-start(bf16[256,256]{1,0:T(8,128)(2,1)S(1)} %get-tuple-element.32), channel_id=1, source_target_pairs={{0,8},{4,12},{8,0},{12,4},{16,24},{20,28},{24,16},{28,20},{1,9},{5... | collective-permute-start | bytes 393224 | tf_op jit(solution)/shard_map/ppermute | solution.py:273
  25.2 10.6 %collective-permute-start.5 = (bf16[256,256]{1,0:T(8,128)(2,1)S(1)}, bf16[256,256]{1,0:T(8,128)(2,1)S(1)}, u32[]{:S(2)}, u32[]{:S(2)}) collective-permute-start(bf16[256,256]{1,0:T(8,128)(2,1)S(1)} %get-tuple-element.33), channel_id=1, source_target_pairs={{0,16},{4,20},{8,24},{12,28},{16,0},{20,4},{24,8},{28,12},{1,17},{... | collective-permute-start | bytes 393224 | tf_op jit(solution)/shard_map/ppermute | solution.py:273
  26.7 9.1 %collective-permute-start.6 = (bf16[256,256]{1,0:T(8,128)(2,1)S(1)}, bf16[256,256]{1,0:T(8,128)(2,1)S(1)}, u32[]{:S(2)}, u32[]{:S(2)}) collective-permute-start(bf16[256,256]{1,0:T(8,128)(2,1)S(1)} %get-tuple-element.34), channel_id=1, source_target_pairs={{0,24},{4,28},{8,16},{12,20},{16,8},{20,12},{24,0},{28,4},{1,25},{... | collective-permute-start | bytes 393224 | tf_op jit(solution)/shard_map/ppermute | solution.py:273
  30.1 11.7 %copy-start = (f32[256]{0:T(256)S(1)}, f32[256]{0:T(256)}, u32[]{:S(2)}) copy-start(f32[256]{0:T(256)} %param.12) | copy-start | bytes 3076
  30.1 2.0 %collective-permute-start.10 = (bf16[1024,256]{1,0:T(8,128)(2,1)S(1)}, bf16[1024,256]{1,0:T(8,128)(2,1)S(1)}, u32[]{:S(2)}, u32[]{:S(2)}) collective-permute-start(bf16[1024,256]{1,0:T(8,128)(2,1)S(1)} %shard_map.97), channel_id=1, source_target_pairs={{0,4},{4,0},{8,12},{12,8},{16,20},{20,16},{24,28},{28,24},{1,5},{5... | collective-permute-start | bytes 1572872 | tf_op jit(solution)/shard_map/ppermute | solution.py:273
  32.2 5.9 %collective-permute-start.11 = (bf16[256,256]{1,0:T(8,128)(2,1)S(1)}, bf16[256,256]{1,0:T(8,128)(2,1)S(1)}, u32[]{:S(2)}, u32[]{:S(2)}) collective-permute-start(bf16[256,256]{1,0:T(8,128)(2,1)S(1)} %get-tuple-element.44), channel_id=1, source_target_pairs={{0,8},{4,12},{8,0},{12,4},{16,24},{20,28},{24,16},{28,20},{1,9},{5... | collective-permute-start | bytes 393224 | tf_op jit(solution)/shard_map/ppermute | solution.py:273
  33.8 8.1 %collective-permute-start.12 = (bf16[256,256]{1,0:T(8,128)(2,1)S(1)}, bf16[256,256]{1,0:T(8,128)(2,1)S(1)}, u32[]{:S(2)}, u32[]{:S(2)}) collective-permute-start(bf16[256,256]{1,0:T(8,128)(2,1)S(1)} %get-tuple-element.45), channel_id=1, source_target_pairs={{0,16},{4,20},{8,24},{12,28},{16,0},{20,4},{24,8},{28,12},{1,17},{... | collective-permute-start | bytes 393224 | tf_op jit(solution)/shard_map/ppermute | solution.py:273
  35.3 6.5 %collective-permute-start.13 = (bf16[256,256]{1,0:T(8,128)(2,1)S(1)}, bf16[256,256]{1,0:T(8,128)(2,1)S(1)}, u32[]{:S(2)}, u32[]{:S(2)}) collective-permute-start(bf16[256,256]{1,0:T(8,128)(2,1)S(1)} %get-tuple-element.46), channel_id=1, source_target_pairs={{0,24},{4,28},{8,16},{12,20},{16,8},{20,12},{24,0},{28,4},{1,25},{... | collective-permute-start | bytes 393224 | tf_op jit(solution)/shard_map/ppermute | solution.py:273

commit v5 on v3

--- a/solution.py
+++ b/solution.py
@@ -274,7 +274,7 @@
 
 
 def exchange(sent):
-    return [swap(sent[k], "row", 2 * (k + 1)) for k in reversed(range(len(sent)))]
+    return [swap(value, "row", 2 * (k + 1)) for k, value in enumerate(sent)]
 
 
 def per_device(
@@ -309,11 +309,14 @@
     projected, *scaled = project(features, weight, source_norm, CHUNKS)
     matrix = merge_tiles(own_tiles, owners, span, index_args, tile_weights)
     across = [swap(own, "col", 3) for own in scaled]
-    beside = [swap(own, "col", 1) for own in scaled]
     across[0], matrix = lax.optimization_barrier((across[0], matrix))
     passed = [swap(value, "col", 1) for value in across]
     pieces, sent = [], None
-    for blocks, wait in zip(zip(scaled, beside, passed, across), WEIGHTS):
+    for own, far, near, wait in zip(scaled, across, passed, WEIGHTS):
+        ready = own
+        if sent is not None:
+            ready, _ = lax.optimization_barrier((own, away))
+        blocks = own, swap(ready, "col", 1), near, far
         if sent is not None:
             pieces[-1] += exchange(sent)
             blocks, _ = lax.optimization_barrier((blocks, sent))

time: 39 us -> 39.7 us (1.018)
  starting transfers between devices: 18.4 us -> 20 us
  waiting for transfers between devices: 10.8 us -> 10.2 us
    ppermute x14, starting transfers between devices: 18.4 us -> 20 us  [swap(): return lax.ppermute(value, axis, pairs)]
    ppermute x14, waiting for transfers between devices: 10.8 us -> 10.2 us  [swap(): return lax.ppermute(value, axis, pairs)]
  transfers between devices with their start and end apart: 14 -> 14, of which waited for: 6 -> 5; matrix products, arithmetic and copies ran while one was open for 0% -> 0% of each run, Pallas kernels for 16% -> 15%
where the time goes in v5:
time: 39.7 us; the launch traced here: 39.5 us
  starting transfers between devices  20 us (50%)
  waiting for transfers between devices  10.2 us (26%)
  Pallas kernels  8.5 us (21%)
  between operations  0.75 us (2%)
    ppermute x14, starting transfers between devices, swap(): return lax.ppermute(value, axis, pairs)  20 us
    ppermute x14, waiting for transfers between devices, swap(): return lax.ppermute(value, axis, pairs)  10.2 us
    pallas_call x4, Pallas kernels, product(): pl.pallas_call(functools.partial(product_kernel, half * (total // 2)), ou...  2.85 us
    pallas_call x1, Pallas kernels, merge_tiles(): pl.pallas_call(functools.partial(merge_kernel, own_tiles, labels.shape[1]...  2.77 us
    pallas_call x1, Pallas kernels, project(): pl.pallas_call(project_kernel, out_shape=[jax.ShapeDtypeStruct((rows, hid...  1.82 us
    pallas_call x1, Pallas kernels, finish(): pl.pallas_call(functools.partial(finish_kernel, len(pieces)), out_shape=j...  0.88 us
  transfers between devices with their start and end apart: 14, of which 5 were waited for; matrix products, arithmetic and copies ran while one was open for 0% of the time, Pallas kernels for 15%

profile of v5, /device:TPU:0, one launch (start us, length us, event | category | flops | bytes accessed | tf_op | source)
XLA Modules:
  0.0 39.5 jit_solution(8803605164383483446)
XLA Ops:
  0.0 1.8 %shard_map.91 = (f32[256,512]{1,0:T(8,128)S(1)}, bf16[256,256]{1,0:T(8,128)(2,1)S(1)}, bf16[256,256]{1,0:T(8,128)(2,1)S(1)}) custom-call(bf16[256,1024]{1,0:T(8,128)(2,1)} %features_hbm.1, bf16[1024,512]{1,0:T(8,128)(2,1)} %weight_hbm.1, f32[2,128]{1,0:T(2,128)} %bitcast.5), custom_call_target="tpu_custom_call" | custom-call | flops 268435456 | bytes 1572864 | tf_op jit(solution)/shard_map/pallas_call | solution.py:66
  1.8 5.1 %collective-permute-start = (bf16[256,256]{1,0:T(8,128)(2,1)S(1)}, bf16[256,256]{1,0:T(8,128)(2,1)S(1)}, u32[]{:S(2)}, u32[]{:S(2)}) collective-permute-start(bf16[256,256]{1,0:T(8,128)(2,1)S(1)} %get-tuple-element.24.refs_0_), channel_id=1, source_target_pairs={{0,3},{1,2},{2,1},{3,0},{4,7},{5,6},{6,5},{7,4},{8,11},{9,10},{10,... | collective-permute-start | bytes 393224 | tf_op jit(solution)/shard_map/ppermute | solution.py:273
  6.9 0.9 %collective-permute-start.8 = (bf16[256,256]{1,0:T(8,128)(2,1)S(1)}, bf16[256,256]{1,0:T(8,128)(2,1)S(1)}, u32[]{:S(2)}, u32[]{:S(2)}) collective-permute-start(bf16[256,256]{1,0:T(8,128)(2,1)S(1)} %get-tuple-element.33.refs_0_), channel_id=1, source_target_pairs={{0,3},{1,2},{2,1},{3,0},{4,7},{5,6},{6,5},{7,4},{8,11},{9,10},{10,... | collective-permute-start | bytes 393224 | tf_op jit(solution)/shard_map/ppermute | solution.py:273
  8.5 2.8 %shard_map.92.matrix = bf16[2048,1024]{1,0:T(8,128)(2,1)S(1)} custom-call(s32[1]{0:T(128)} %bitcast.2.row, s32[1]{0:T(128)} %bitcast.3.column, s32[1]{0:T(128)S(6)} %copy.10.count, s32[1,64]{1,0:T(1,128)} %sources_hbm.1, s32[1,64]{1,0:T(1,128)} %targets_hbm.1, s32[1,16]{1,0:T(1,128)} %labels_hbm.1, bf16[1,64,128,128]{3,2,1,0:T(8,128)(2,1)} %tiles_hbm.1), custom_call_target="tpu_custom_call" | custom-call | flops 8388608 | bytes 12582912 | tf_op jit(solution)/shard_map/pallas_call | solution.py:139
  11.3 0.0 collective-permute-done.refs_3_
  11.3 3.4 %collective-permute-start.2 = (bf16[256,256]{1,0:T(8,128)(2,1)S(1)}, bf16[256,256]{1,0:T(8,128)(2,1)S(1)}, u32[]{:S(2)}, u32[]{:S(2)}) collective-permute-start(bf16[256,256]{1,0:T(8,128)(2,1)S(1)} %collective-permute-done.refs_3_), channel_id=1, source_target_pairs={{0,1},{1,0},{2,3},{3,2},{4,5},{5,4},{6,7},{7,6},{8,9},{9,8},{10,11... | collective-permute-start | bytes 393224 | tf_op jit(solution)/shard_map/ppermute | solution.py:273
  14.8 2.2 %collective-permute-done.8.refs_3_ = bf16[256,256]{1,0:T(8,128)(2,1)S(1)} collective-permute-done((bf16[256,256]{1,0:T(8,128)(2,1)S(1)}, bf16[256,256]{1,0:T(8,128)(2,1)S(1)}, u32[]{:S(2)}, u32[]{:S(2)}) %collective-permute-start.8) | collective-permute-done | bytes 131104 | tf_op jit(solution)/shard_map/ppermute | solution.py:273
  17.0 1.6 %collective-permute-start.9 = (bf16[256,256]{1,0:T(8,128)(2,1)S(1)}, bf16[256,256]{1,0:T(8,128)(2,1)S(1)}, u32[]{:S(2)}, u32[]{:S(2)}) collective-permute-start(bf16[256,256]{1,0:T(8,128)(2,1)S(1)} %collective-permute-done.8.refs_3_), channel_id=1, source_target_pairs={{0,1},{1,0},{2,3},{3,2},{4,5},{5,4},{6,7},{7,6},{8,9},{9,8},{10,11... | collective-permute-start | bytes 393224 | tf_op jit(solution)/shard_map/ppermute | solution.py:273
  18.6 0.0 collective-permute-done.1.refs_1_
  18.6 0.7 %collective-permute-done.2.refs_2_ = bf16[256,256]{1,0:T(8,128)(2,1)S(1)} collective-permute-done((bf16[256,256]{1,0:T(8,128)(2,1)S(1)}, bf16[256,256]{1,0:T(8,128)(2,1)S(1)}, u32[]{:S(2)}, u32[]{:S(2)}) %collective-permute-start.2) | collective-permute-done | bytes 131104 | tf_op jit(solution)/shard_map/ppermute | solution.py:273
  19.3 0.7 %shard_map.94 = bf16[1024,256]{1,0:T(8,128)(2,1)S(1)} custom-call(bf16[2048,1024]{1,0:T(8,128)(2,1)S(1)} %shard_map.92.matrix, bf16[256,256]{1,0:T(8,128)(2,1)S(1)} %get-tuple-element.24.refs_0_, bf16[256,256]{1,0:T(8,128)(2,1)S(1)} %collective-permute-done.1.refs_1_, bf16[256,256]{1,0:T(8,128)(2,1)S(1)} %collective-permute-done.2.refs_2_, ...), custom_call_target="tpu_custom_call" | custom-call | flops 10737418240 | bytes 1 | tf_op jit(solution)/shard_map/pallas_call | solution.py:174
  20.0 0.1 collective-permute-start.3
  20.1 1.7 %collective-permute-start.7 = (bf16[256,256]{1,0:T(8,128)(2,1)S(1)}, bf16[256,256]{1,0:T(8,128)(2,1)S(1)}, u32[]{:S(2)}, u32[]{:S(2)}) collective-permute-start(bf16[256,256]{1,0:T(8,128)(2,1)S(1)} %get-tuple-element.33.refs_0_), channel_id=1, source_target_pairs={{0,1},{1,0},{2,3},{3,2},{4,5},{5,4},{6,7},{7,6},{8,9},{9,8},{10,11... | collective-permute-start | bytes 393224 | tf_op jit(solution)/shard_map/ppermute | solution.py:273
  21.8 0.7 %shard_map.93.stay = f32[1024,256]{1,0:T(8,128)S(1)} custom-call(bf16[2048,1024]{1,0:T(8,128)(2,1)S(1)} %shard_map.92.matrix, bf16[256,256]{1,0:T(8,128)(2,1)S(1)} %get-tuple-element.24.refs_0_, bf16[256,256]{1,0:T(8,128)(2,1)S(1)} %collective-permute-done.1.refs_1_, bf16[256,256]{1,0:T(8,128)(2,1)S(1)} %collective-permute-done.2.refs_2_, ...), custom_call_target="tpu_custom_call" | custom-call | flops 10737418240 | bytes 1 | tf_op jit(solution)/shard_map/pallas_call | solution.py:174
  22.5 0.1 shard_map.95
  22.6 1.6 %collective-permute-start.4 = (bf16[256,256]{1,0:T(8,128)(2,1)S(1)}, bf16[256,256]{1,0:T(8,128)(2,1)S(1)}, u32[]{:S(2)}, u32[]{:S(2)}) collective-permute-start(bf16[256,256]{1,0:T(8,128)(2,1)S(1)} %get-tuple-element.28), channel_id=1, source_target_pairs={{0,8},{4,12},{8,0},{12,4},{16,24},{20,28},{24,16},{28,20},{1,9},{5... | collective-permute-start | bytes 393224 | tf_op jit(solution)/shard_map/ppermute | solution.py:273
  24.2 1.6 %collective-permute-start.5 = (bf16[256,256]{1,0:T(8,128)(2,1)S(1)}, bf16[256,256]{1,0:T(8,128)(2,1)S(1)}, u32[]{:S(2)}, u32[]{:S(2)}) collective-permute-start(bf16[256,256]{1,0:T(8,128)(2,1)S(1)} %get-tuple-element.29), channel_id=1, source_target_pairs={{0,16},{4,20},{8,24},{12,28},{16,0},{20,4},{24,8},{28,12},{1,17},{... | collective-permute-start | bytes 393224 | tf_op jit(solution)/shard_map/ppermute | solution.py:273
  25.8 0.4 collective-permute-start.6
  26.2 0.0 collective-permute-done.9.refs_2_
  26.2 0.7 %shard_map.97 = bf16[1024,256]{1,0:T(8,128)(2,1)S(1)} custom-call(bf16[2048,1024]{1,0:T(8,128)(2,1)S(1)} %shard_map.92.matrix, bf16[256,256]{1,0:T(8,128)(2,1)S(1)} %get-tuple-element.33.refs_0_, bf16[256,256]{1,0:T(8,128)(2,1)S(1)} %collective-permute-done.7.refs_1_, bf16[256,256]{1,0:T(8,128)(2,1)S(1)} %collective-permute-done.9.refs_2_, ...), custom_call_target="tpu_custom_call" | custom-call | bytes 1 | tf_op jit(solution)/shard_map/pallas_call | solution.py:174
  26.9 0.0 copy-start
  26.9 0.1 collective-permute-start.10
  27.0 0.7 %shard_map.96.stay = f32[1024,256]{1,0:T(8,128)S(1)} custom-call(bf16[2048,1024]{1,0:T(8,128)(2,1)S(1)} %shard_map.92.matrix, bf16[256,256]{1,0:T(8,128)(2,1)S(1)} %get-tuple-element.33.refs_0_, bf16[256,256]{1,0:T(8,128)(2,1)S(1)} %collective-permute-done.7.refs_1_, bf16[256,256]{1,0:T(8,128)(2,1)S(1)} %collective-permute-done.9.refs_2_, ...), custom_call_target="tpu_custom_call" | custom-call | flops 10737418240 | bytes 1 | tf_op jit(solution)/shard_map/pallas_call | solution.py:174
  27.7 1.2 %collective-permute-done.10.came = bf16[1024,256]{1,0:T(8,128)(2,1)S(1)} collective-permute-done((bf16[1024,256]{1,0:T(8,128)(2,1)S(1)}, bf16[1024,256]{1,0:T(8,128)(2,1)S(1)}, u32[]{:S(2)}, u32[]{:S(2)}) %collective-permute-start.10) | collective-permute-done | bytes 524320 | tf_op jit(solution)/shard_map/ppermute | solution.py:273
  28.9 0.1 shard_map.98
  29.0 1.6 %collective-permute-start.11 = (bf16[256,256]{1,0:T(8,128)(2,1)S(1)}, bf16[256,256]{1,0:T(8,128)(2,1)S(1)}, u32[]{:S(2)}, u32[]{:S(2)}) collective-permute-start(bf16[256,256]{1,0:T(8,128)(2,1)S(1)} %get-tuple-element.38), channel_id=1, source_target_pairs={{0,8},{4,12},{8,0},{12,4},{16,24},{20,28},{24,16},{28,20},{1,9},{5... | collective-permute-start | bytes 393224 | tf_op jit(solution)/shard_map/ppermute | solution.py:273
  30.5 1.6 %collective-permute-start.12 = (bf16[256,256]{1,0:T(8,128)(2,1)S(1)}, bf16[256,256]{1,0:T(8,128)(2,1)S(1)}, u32[]{:S(2)}, u32[]{:S(2)}) collective-permute-start(bf16[256,256]{1,0:T(8,128)(2,1)S(1)} %get-tuple-element.39), channel_id=1, source_target_pairs={{0,16},{4,20},{8,24},{12,28},{16,0},{20,4},{24,8},{28,12},{1,17},{... | collective-permute-start | bytes 393224 | tf_op jit(solution)/shard_map/ppermute | solution.py:273
  32.1 0.0 collective-permute-done.4.refs_1_
  32.1 0.4 collective-permute-start.13
  32.5 2.4 %collective-permute-done.11.refs_5_ = bf16[256,256]{1,0:T(8,128)(2,1)S(1)} collective-permute-done((bf16[256,256]{1,0:T(8,128)(2,1)S(1)}, bf16[256,256]{1,0:T(8,128)(2,1)S(1)}, u32[]{:S(2)}, u32[]{:S(2)}) %collective-permute-start.11) | collective-permute-done | bytes 131104 | tf_op jit(solution)/shard_map/ppermute | solution.py:273
  34.9 3.7 %collective-permute-done.12.refs_6_ = bf16[256,256]{1,0:T(8,128)(2,1)S(1)} collective-permute-done((bf16[256,256]{1,0:T(8,128)(2,1)S(1)}, bf16[256,256]{1,0:T(8,128)(2,1)S(1)}, u32[]{:S(2)}, u32[]{:S(2)}) %collective-permute-start.12) | collective-permute-done | bytes 131104 | tf_op jit(solution)/shard_map/ppermute | solution.py:273
  38.6 0.9 %shard_map.99 = bf16[256,512]{1,0:T(8,128)(2,1)} custom-call(f32[256,512]{1,0:T(8,128)S(1)} %get-tuple-element.23.projected, f32[2,128]{1,0:T(2,128)S(1)} %bitcast.4, f32[256,256]{1,0:T(8,128)S(1)} %get-tuple-element.27.refs_0_, bf16[256,256]{1,0:T(8,128)(2,1)S(1)} %collective-permute-done.4.refs_1_, bf16[256,256]{1,0:T(8,128)(2,1)S(1)} %collective-permute-done.5.refs_2_, ...), custom_call_target="tpu_custom_call" | custom-call | flops 786432 | bytes 2097152 | tf_op jit(solution)/shard_map/pallas_call | solution.py:227
  (7 shorter events, 0.0 us)
Async XLA Ops:
  1.8 9.5 %collective-permute-start = (bf16[256,256]{1,0:T(8,128)(2,1)S(1)}, bf16[256,256]{1,0:T(8,128)(2,1)S(1)}, u32[]{:S(2)}, u32[]{:S(2)}) collective-permute-start(bf16[256,256]{1,0:T(8,128)(2,1)S(1)} %get-tuple-element.24.refs_0_), channel_id=1, source_target_pairs={{0,3},{1,2},{2,1},{3,0},{4,7},{5,6},{6,5},{7,4},{8,11},{9,10},{10,... | collective-permute-start | bytes 393224 | tf_op jit(solution)/shard_map/ppermute | solution.py:273
  6.9 11.6 %collective-permute-start.1 = (bf16[256,256]{1,0:T(8,128)(2,1)S(1)}, bf16[256,256]{1,0:T(8,128)(2,1)S(1)}, u32[]{:S(2)}, u32[]{:S(2)}) collective-permute-start(bf16[256,256]{1,0:T(8,128)(2,1)S(1)} %get-tuple-element.24.refs_0_), channel_id=1, source_target_pairs={{0,1},{1,0},{2,3},{3,2},{4,5},{5,4},{6,7},{7,6},{8,9},{9,8},{10,11... | collective-permute-start | bytes 393224 | tf_op jit(solution)/shard_map/ppermute | solution.py:273
  6.9 10.0 %collective-permute-start.8 = (bf16[256,256]{1,0:T(8,128)(2,1)S(1)}, bf16[256,256]{1,0:T(8,128)(2,1)S(1)}, u32[]{:S(2)}, u32[]{:S(2)}) collective-permute-start(bf16[256,256]{1,0:T(8,128)(2,1)S(1)} %get-tuple-element.33.refs_0_), channel_id=1, source_target_pairs={{0,3},{1,2},{2,1},{3,0},{4,7},{5,6},{6,5},{7,4},{8,11},{9,10},{10,... | collective-permute-start | bytes 393224 | tf_op jit(solution)/shard_map/ppermute | solution.py:273
  11.3 8.0 %collective-permute-start.2 = (bf16[256,256]{1,0:T(8,128)(2,1)S(1)}, bf16[256,256]{1,0:T(8,128)(2,1)S(1)}, u32[]{:S(2)}, u32[]{:S(2)}) collective-permute-start(bf16[256,256]{1,0:T(8,128)(2,1)S(1)} %collective-permute-done.refs_3_), channel_id=1, source_target_pairs={{0,1},{1,0},{2,3},{3,2},{4,5},{5,4},{6,7},{7,6},{8,9},{9,8},{10,11... | collective-permute-start | bytes 393224 | tf_op jit(solution)/shard_map/ppermute | solution.py:273
  17.0 9.2 %collective-permute-start.9 = (bf16[256,256]{1,0:T(8,128)(2,1)S(1)}, bf16[256,256]{1,0:T(8,128)(2,1)S(1)}, u32[]{:S(2)}, u32[]{:S(2)}) collective-permute-start(bf16[256,256]{1,0:T(8,128)(2,1)S(1)} %collective-permute-done.8.refs_3_), channel_id=1, source_target_pairs={{0,1},{1,0},{2,3},{3,2},{4,5},{5,4},{6,7},{7,6},{8,9},{9,8},{10,11... | collective-permute-start | bytes 393224 | tf_op jit(solution)/shard_map/ppermute | solution.py:273
  20.0 2.5 %collective-permute-start.3 = (bf16[1024,256]{1,0:T(8,128)(2,1)S(1)}, bf16[1024,256]{1,0:T(8,128)(2,1)S(1)}, u32[]{:S(2)}, u32[]{:S(2)}) collective-permute-start(bf16[1024,256]{1,0:T(8,128)(2,1)S(1)} %shard_map.94), channel_id=1, source_target_pairs={{0,4},{4,0},{8,12},{12,8},{16,20},{20,16},{24,28},{28,24},{1,5},{5... | collective-permute-start | bytes 1572872 | tf_op jit(solution)/shard_map/ppermute | solution.py:273
  20.1 6.1 %collective-permute-start.7 = (bf16[256,256]{1,0:T(8,128)(2,1)S(1)}, bf16[256,256]{1,0:T(8,128)(2,1)S(1)}, u32[]{:S(2)}, u32[]{:S(2)}) collective-permute-start(bf16[256,256]{1,0:T(8,128)(2,1)S(1)} %get-tuple-element.33.refs_0_), channel_id=1, source_target_pairs={{0,1},{1,0},{2,3},{3,2},{4,5},{5,4},{6,7},{7,6},{8,9},{9,8},{10,11... | collective-permute-start | bytes 393224 | tf_op jit(solution)/shard_map/ppermute | solution.py:273
  22.6 9.5 %collective-permute-start.4 = (bf16[256,256]{1,0:T(8,128)(2,1)S(1)}, bf16[256,256]{1,0:T(8,128)(2,1)S(1)}, u32[]{:S(2)}, u32[]{:S(2)}) collective-permute-start(bf16[256,256]{1,0:T(8,128)(2,1)S(1)} %get-tuple-element.28), channel_id=1, source_target_pairs={{0,8},{4,12},{8,0},{12,4},{16,24},{20,28},{24,16},{28,20},{1,9},{5... | collective-permute-start | bytes 393224 | tf_op jit(solution)/shard_map/ppermute | solution.py:273
  24.2 8.4 %collective-permute-start.5 = (bf16[256,256]{1,0:T(8,128)(2,1)S(1)}, bf16[256,256]{1,0:T(8,128)(2,1)S(1)}, u32[]{:S(2)}, u32[]{:S(2)}) collective-permute-start(bf16[256,256]{1,0:T(8,128)(2,1)S(1)} %get-tuple-element.29), channel_id=1, source_target_pairs={{0,16},{4,20},{8,24},{12,28},{16,0},{20,4},{24,8},{28,12},{1,17},{... | collective-permute-start | bytes 393224 | tf_op jit(solution)/shard_map/ppermute | solution.py:273
  25.8 6.8 %collective-permute-start.6 = (bf16[256,256]{1,0:T(8,128)(2,1)S(1)}, bf16[256,256]{1,0:T(8,128)(2,1)S(1)}, u32[]{:S(2)}, u32[]{:S(2)}) collective-permute-start(bf16[256,256]{1,0:T(8,128)(2,1)S(1)} %get-tuple-element.30), channel_id=1, source_target_pairs={{0,24},{4,28},{8,16},{12,20},{16,8},{20,12},{24,0},{28,4},{1,25},{... | collective-permute-start | bytes 393224 | tf_op jit(solution)/shard_map/ppermute | solution.py:273
  26.9 11.7 %copy-start = (f32[256]{0:T(256)S(1)}, f32[256]{0:T(256)}, u32[]{:S(2)}) copy-start(f32[256]{0:T(256)} %param.12) | copy-start | bytes 3076
  26.9 2.0 %collective-permute-start.10 = (bf16[1024,256]{1,0:T(8,128)(2,1)S(1)}, bf16[1024,256]{1,0:T(8,128)(2,1)S(1)}, u32[]{:S(2)}, u32[]{:S(2)}) collective-permute-start(bf16[1024,256]{1,0:T(8,128)(2,1)S(1)} %shard_map.97), channel_id=1, source_target_pairs={{0,4},{4,0},{8,12},{12,8},{16,20},{20,16},{24,28},{28,24},{1,5},{5... | collective-permute-start | bytes 1572872 | tf_op jit(solution)/shard_map/ppermute | solution.py:273
  29.0 5.9 %collective-permute-start.11 = (bf16[256,256]{1,0:T(8,128)(2,1)S(1)}, bf16[256,256]{1,0:T(8,128)(2,1)S(1)}, u32[]{:S(2)}, u32[]{:S(2)}) collective-permute-start(bf16[256,256]{1,0:T(8,128)(2,1)S(1)} %get-tuple-element.38), channel_id=1, source_target_pairs={{0,8},{4,12},{8,0},{12,4},{16,24},{20,28},{24,16},{28,20},{1,9},{5... | collective-permute-start | bytes 393224 | tf_op jit(solution)/shard_map/ppermute | solution.py:273
  30.5 8.1 %collective-permute-start.12 = (bf16[256,256]{1,0:T(8,128)(2,1)S(1)}, bf16[256,256]{1,0:T(8,128)(2,1)S(1)}, u32[]{:S(2)}, u32[]{:S(2)}) collective-permute-start(bf16[256,256]{1,0:T(8,128)(2,1)S(1)} %get-tuple-element.39), channel_id=1, source_target_pairs={{0,16},{4,20},{8,24},{12,28},{16,0},{20,4},{24,8},{28,12},{1,17},{... | collective-permute-start | bytes 393224 | tf_op jit(solution)/shard_map/ppermute | solution.py:273
  32.1 6.5 %collective-permute-start.13 = (bf16[256,256]{1,0:T(8,128)(2,1)S(1)}, bf16[256,256]{1,0:T(8,128)(2,1)S(1)}, u32[]{:S(2)}, u32[]{:S(2)}) collective-permute-start(bf16[256,256]{1,0:T(8,128)(2,1)S(1)} %get-tuple-element.40), channel_id=1, source_target_pairs={{0,24},{4,28},{8,16},{12,20},{16,8},{20,12},{24,0},{28,4},{1,25},{... | collective-permute-start | bytes 393224 | tf_op jit(solution)/shard_map/ppermute | solution.py:273

commit v6 on v5

--- a/solution.py
+++ b/solution.py
@@ -103,7 +103,6 @@
     for copy in small + large:
         copy.start()
     spare, span = total.shape[0] - 1, total.shape[1]
-    owners = spare // own_tiles
     total[...] = jnp.zeros_like(total)
     my_row, my_column, used = row[0], column[0], count[0]
     for copy in small:
@@ -112,9 +111,15 @@
     def add(slot):
         target, source = targets[0, slot], sources[0, slot]
         label = labels[0, target]
-        apart = lax.bitwise_xor(target // per_owner, my_row)
-        position = (1 - apart % 2) * (owners // 2) + apart // 2
-        place = jnp.where(label < own_tiles, position * own_tiles + label, spare)
+        owner = target // per_owner
+        apart = lax.bitwise_xor(owner, my_row)
+        core = label // (own_tiles // 2)
+        x, y = apart // 2 % 2, apart // 4
+        first, second = jnp.where(core == 0, x, y), jnp.where(core == 0, y, x)
+        place = jnp.where(core == my_row % 2, 8, 0) + (1 - first) * 4 + (1 - second) * 2
+        place += jnp.where(owner % 2 == core, 1, 0)
+        place = place * (own_tiles // 2) + label % (own_tiles // 2)
+        place = jnp.where(label < own_tiles, place, spare)
         block = lax.bitwise_xor(source // own_tiles, my_column)
         total[place, block * own_tiles + source % own_tiles] += tiles[slot].astype(jnp.float32)
 
@@ -182,56 +187,59 @@
     )(matrix, *blocks)
 
 
-def join_kernel(stay, came, kept, *sent):
-    rows = kept.shape[0]
-    value = stay[...].astype(jnp.float32) + came[...].astype(jnp.float32)
-    kept[...] = value[:rows]
-    for place, out in enumerate(sent):
-        out[...] = value[(place + 1) * rows : (place + 2) * rows].astype(out.dtype)
-
-
-def join(stay, came, rows):
-    total, width = stay.shape
-    parts = total // rows
+def join_kernel(stay, came, sent, kept):
+    value = stay[...] + came[...].astype(jnp.float32)
+    away = sent.shape[0]
+    sent[...] = value[:away].astype(sent.dtype)
+    kept[...] = value[away:]
+
+
+def join(stay, came):
+    rows, width = stay.shape
     return pl.pallas_call(
         join_kernel,
-        out_shape=[jax.ShapeDtypeStruct((rows, width), jnp.float32)]
-        + [jax.ShapeDtypeStruct((rows, width), jnp.bfloat16)] * (parts - 1),
+        out_shape=[
+            jax.ShapeDtypeStruct((rows // 2, width), jnp.bfloat16),
+            jax.ShapeDtypeStruct((rows // 2, width), jnp.float32),
+        ],
         in_specs=[VMEM] * 2,
-        out_specs=[VMEM] * parts,
+        out_specs=[VMEM] * 2,
         compiler_params=params(12),
         cost_estimate=cost(1, 1),
     )(stay, came)
 
 
-def finish_kernel(chunks, projected, norm, *refs):
-    out = refs[-1]
-    per_chunk = (len(refs) - 1) // chunks
+def finish_kernel(row, projected, norm, *refs):
+    *pieces, out = refs
     lanes = norm.shape[1]
-    width = refs[0].shape[1]
-    for part in range(norm.shape[0]):
-        factor = rows_to_lanes(norm[part : part + 1, :], lanes)
-        here = slice(part * lanes, (part + 1) * lanes)
-        for column in range(0, out.shape[1], lanes):
-            pieces = refs[column // width * per_chunk : (column // width + 1) * per_chunk]
-            start = column % width
-            value = projected[here, column : column + lanes]
-            for piece in pieces:
-                value += piece[here, start : start + lanes].astype(jnp.float32)
-            out[here, column : column + lanes] = jnp.maximum(factor * value, 0.0).astype(out.dtype)
-
-
-def finish(projected, target_norm, pieces):
+    half, width = pieces[0].shape
+    core = row[0] % 2
+    for part in range(2):
+        base = (core if part == 0 else 1 - core) * half
+        for step in range(0, half, lanes):
+            here = pl.ds(pl.multiple_of(base + step, lanes), lanes)
+            factor = rows_to_lanes(norm[pl.ds(base // lanes + step // lanes, 1), :], lanes)
+            for column in range(0, out.shape[1], lanes):
+                piece = pieces[column // width * 2 + part]
+                start = column % width
+                value = projected[here, column : column + lanes] + piece[
+                    step : step + lanes, start : start + lanes
+                ].astype(jnp.float32)
+                out[here, column : column + lanes] = jnp.maximum(factor * value, 0.0).astype(
+                    out.dtype
+                )
+
+
+def finish(row, projected, target_norm, pieces):
     rows, hidden = projected.shape
-    flat = [piece for chunk in pieces for piece in chunk]
-    return pl.pallas_call(
-        functools.partial(finish_kernel, len(pieces)),
+    return pl.pallas_call(
+        finish_kernel,
         out_shape=jax.ShapeDtypeStruct((rows, hidden), jnp.bfloat16),
-        in_specs=[VMEM] * (2 + len(flat)),
+        in_specs=[SMEM] + [VMEM] * (2 + len(pieces)),
         out_specs=VMEM,
         compiler_params=params(12),
         cost_estimate=cost(6 * rows * hidden, 16 * rows * hidden),
-    )(projected, target_norm.reshape(-1, 128), *flat)
+    )(row, projected, target_norm.reshape(-1, 128), *pieces)
 
 
 def visit_kernel(own_tiles, per_owner, sources, targets, count, labels, tiles, blocks, out, total):
@@ -273,8 +281,10 @@
     return lax.ppermute(value, axis, pairs)
 
 
-def exchange(sent):
-    return [swap(value, "row", 2 * (k + 1)) for k, value in enumerate(sent)]
+def swap_round(value, round_):
+    owners = lax.axis_size("row")
+    pairs = [(i, i ^ (2 if (i + round_) % 2 == 0 else 4)) for i in range(owners)]
+    return lax.ppermute(value, "row", pairs)
 
 
 def per_device(
@@ -296,7 +306,7 @@
     index_args = (tile_source, tile_target, tile_count, mirror_tile)
 
     cells = owners * own_tiles * span * tile_rows * tile_rows
-    if columns != 4 or owners & (owners - 1) or cells > DENSE_ELEMENTS:
+    if columns != 4 or owners != 8 or own_tiles % 2 or cells > DENSE_ELEMENTS:
         projected = jnp.dot(features, weight, preferred_element_type=jnp.float32)
         scaled = (source_norm[:, None] * projected).astype(jnp.bfloat16)
         blocks = lax.all_gather(scaled, "col", axis=0, tiled=True)
@@ -318,14 +328,15 @@
             ready, _ = lax.optimization_barrier((own, away))
         blocks = own, swap(ready, "col", 1), near, far
         if sent is not None:
-            pieces[-1] += exchange(sent)
             blocks, _ = lax.optimization_barrier((blocks, sent))
         away = product(matrix, blocks, 0, jnp.bfloat16, wait[0])
         stay = product(matrix, blocks, 1, jnp.float32, wait[1])
-        kept, *sent = join(stay, swap(away, "row", 1), own_rows)
-        pieces.append([kept])
-    pieces[-1] += exchange(sent)
-    return finish(projected, target_norm, pieces)
+        sent, kept = join(stay, swap(away, "row", 1))
+        last, kept = join(kept, swap_round(sent, 0))
+        last, kept = join(kept, swap_round(last, 1))
+        pieces += [kept, swap(last, "row", 1)]
+    row = lax.axis_index("row").astype(jnp.int32).reshape(1)
+    return finish(row, projected, target_norm, pieces)
 
 
 def solution(mesh):

time: 39.7 us -> 44.1 us (1.11)
  waiting for transfers between devices: 10.2 us -> 15.8 us
  starting transfers between devices: 20 us -> 18.2 us
  Pallas kernels: 8.5 us -> 9.18 us
    ppermute x0 -> x4, waiting for transfers between devices: none -> 8.57 us  [swap_round(): return lax.ppermute(value, 'row', pairs)]
    ppermute x14 -> x10, starting transfers between devices: 20 us -> 12.4 us  [swap(): return lax.ppermute(value, axis, pairs)]
    ppermute x0 -> x4, starting transfers between devices: none -> 5.79 us  [swap_round(): return lax.ppermute(value, 'row', pairs)]
    ppermute x14 -> x10, waiting for transfers between devices: 10.2 us -> 7.26 us  [swap(): return lax.ppermute(value, axis, pairs)]
    pallas_call x1, Pallas kernels: 2.77 us -> 3.38 us  [merge_tiles(): pl.pallas_call(functools.partial(merge_kernel, own_tiles, labels.shape[1]...]
    pallas_call x3 -> x7, Pallas kernels: 1.06 us -> 1.13 us  [the longest x1 0.83 us: finish(): pl.pallas_call(finish_kernel, out_shape=jax.ShapeDtypeStruct((rows, hidde...]
  transfers between devices with their start and end apart: 14 -> 14, of which waited for: 5 -> 7; matrix products, arithmetic and copies ran while one was open for 0% -> 0% of each run, Pallas kernels for 15% -> 15%
where the time goes in v6:
time: 44.1 us; the launch traced here: 44 us
  starting transfers between devices  18.2 us (41%)
  waiting for transfers between devices  15.8 us (36%)
  Pallas kernels  9.18 us (21%)
  between operations  0.8 us (2%)
    ppermute x10, starting transfers between devices, swap(): return lax.ppermute(value, axis, pairs)  12.4 us
    ppermute x4, waiting for transfers between devices, swap_round(): return lax.ppermute(value, 'row', pairs)  8.57 us
    ppermute x10, waiting for transfers between devices, swap(): return lax.ppermute(value, axis, pairs)  7.26 us
    ppermute x4, starting transfers between devices, swap_round(): return lax.ppermute(value, 'row', pairs)  5.79 us
    pallas_call x1, Pallas kernels, merge_tiles(): pl.pallas_call(functools.partial(merge_kernel, own_tiles, labels.shape[1]...  3.38 us
    pallas_call x4, Pallas kernels, product(): pl.pallas_call(functools.partial(product_kernel, half * (total // 2)), ou...  2.84 us
    pallas_call x1, Pallas kernels, project(): pl.pallas_call(project_kernel, out_shape=[jax.ShapeDtypeStruct((rows, hid...  1.82 us
  transfers between devices with their start and end apart: 14, of which 7 were waited for; matrix products, arithmetic and copies ran while one was open for 0% of the time, Pallas kernels for 15%

profile of v6, /device:TPU:0, one launch (start us, length us, event | category | flops | bytes accessed | tf_op | source)
XLA Modules:
  0.0 44.0 jit_solution(10474491015099942375)
XLA Ops:
  0.0 1.8 %shard_map.91 = (f32[256,512]{1,0:T(8,128)S(1)}, bf16[256,256]{1,0:T(8,128)(2,1)S(1)}, bf16[256,256]{1,0:T(8,128)(2,1)S(1)}) custom-call(bf16[256,1024]{1,0:T(8,128)(2,1)} %features_hbm.1, bf16[1024,512]{1,0:T(8,128)(2,1)} %weight_hbm.1, f32[2,128]{1,0:T(2,128)} %bitcast.5), custom_call_target="tpu_custom_call" | custom-call | flops 268435456 | bytes 1572864 | tf_op jit(solution)/shard_map/pallas_call | solution.py:66
  1.8 5.1 %collective-permute-start = (bf16[256,256]{1,0:T(8,128)(2,1)S(1)}, bf16[256,256]{1,0:T(8,128)(2,1)S(1)}, u32[]{:S(2)}, u32[]{:S(2)}) collective-permute-start(bf16[256,256]{1,0:T(8,128)(2,1)S(1)} %get-tuple-element.28.refs_0_), channel_id=1, source_target_pairs={{0,3},{1,2},{2,1},{3,0},{4,7},{5,6},{6,5},{7,4},{8,11},{9,10},{10,... | collective-permute-start | bytes 393224 | tf_op jit(solution)/shard_map/ppermute | solution.py:281
  6.9 0.9 %collective-permute-start.8 = (bf16[256,256]{1,0:T(8,128)(2,1)S(1)}, bf16[256,256]{1,0:T(8,128)(2,1)S(1)}, u32[]{:S(2)}, u32[]{:S(2)}) collective-permute-start(bf16[256,256]{1,0:T(8,128)(2,1)S(1)} %get-tuple-element.39.refs_0_), channel_id=1, source_target_pairs={{0,3},{1,2},{2,1},{3,0},{4,7},{5,6},{6,5},{7,4},{8,11},{9,10},{10,... | collective-permute-start | bytes 393224 | tf_op jit(solution)/shard_map/ppermute | solution.py:281
  8.5 3.4 %shard_map.92.matrix = bf16[2048,1024]{1,0:T(8,128)(2,1)S(1)} custom-call(s32[1]{0:T(128)} %bitcast.row, s32[1]{0:T(128)} %bitcast.3.column, s32[1]{0:T(128)S(6)} %copy.10.count, s32[1,64]{1,0:T(1,128)} %sources_hbm.1, s32[1,64]{1,0:T(1,128)} %targets_hbm.1, s32[1,16]{1,0:T(1,128)} %labels_hbm.1, bf16[1,64,128,128]{3,2,1,0:T(8,128)(2,1)} %tiles_hbm.1), custom_call_target="tpu_custom_call" | custom-call | flops 8388608 | bytes 12582912 | tf_op jit(solution)/shard_map/pallas_call | solution.py:144
  11.9 0.0 collective-permute-done.refs_3_
  11.9 2.9 %collective-permute-start.2 = (bf16[256,256]{1,0:T(8,128)(2,1)S(1)}, bf16[256,256]{1,0:T(8,128)(2,1)S(1)}, u32[]{:S(2)}, u32[]{:S(2)}) collective-permute-start(bf16[256,256]{1,0:T(8,128)(2,1)S(1)} %collective-permute-done.refs_3_), channel_id=1, source_target_pairs={{0,1},{1,0},{2,3},{3,2},{4,5},{5,4},{6,7},{7,6},{8,9},{9,8},{10,11... | collective-permute-start | bytes 393224 | tf_op jit(solution)/shard_map/ppermute | solution.py:281
  14.8 2.2 %collective-permute-done.8.refs_3_ = bf16[256,256]{1,0:T(8,128)(2,1)S(1)} collective-permute-done((bf16[256,256]{1,0:T(8,128)(2,1)S(1)}, bf16[256,256]{1,0:T(8,128)(2,1)S(1)}, u32[]{:S(2)}, u32[]{:S(2)}) %collective-permute-start.8) | collective-permute-done | bytes 131104 | tf_op jit(solution)/shard_map/ppermute | solution.py:281
  17.0 1.6 %collective-permute-start.9 = (bf16[256,256]{1,0:T(8,128)(2,1)S(1)}, bf16[256,256]{1,0:T(8,128)(2,1)S(1)}, u32[]{:S(2)}, u32[]{:S(2)}) collective-permute-start(bf16[256,256]{1,0:T(8,128)(2,1)S(1)} %collective-permute-done.8.refs_3_), channel_id=1, source_target_pairs={{0,1},{1,0},{2,3},{3,2},{4,5},{5,4},{6,7},{7,6},{8,9},{9,8},{10,11... | collective-permute-start | bytes 393224 | tf_op jit(solution)/shard_map/ppermute | solution.py:281
  18.6 0.0 collective-permute-done.1.refs_1_
  18.6 0.8 %collective-permute-done.2.refs_2_ = bf16[256,256]{1,0:T(8,128)(2,1)S(1)} collective-permute-done((bf16[256,256]{1,0:T(8,128)(2,1)S(1)}, bf16[256,256]{1,0:T(8,128)(2,1)S(1)}, u32[]{:S(2)}, u32[]{:S(2)}) %collective-permute-start.2) | collective-permute-done | bytes 131104 | tf_op jit(solution)/shard_map/ppermute | solution.py:281
  19.4 0.7 %shard_map.94 = bf16[1024,256]{1,0:T(8,128)(2,1)S(1)} custom-call(bf16[2048,1024]{1,0:T(8,128)(2,1)S(1)} %shard_map.92.matrix, bf16[256,256]{1,0:T(8,128)(2,1)S(1)} %get-tuple-element.28.refs_0_, bf16[256,256]{1,0:T(8,128)(2,1)S(1)} %collective-permute-done.1.refs_1_, bf16[256,256]{1,0:T(8,128)(2,1)S(1)} %collective-permute-done.2.refs_2_, ...), custom_call_target="tpu_custom_call" | custom-call | flops 10737418240 | bytes 1 | tf_op jit(solution)/shard_map/pallas_call | solution.py:179
  20.1 0.1 collective-permute-start.3
  20.2 1.6 %collective-permute-start.7 = (bf16[256,256]{1,0:T(8,128)(2,1)S(1)}, bf16[256,256]{1,0:T(8,128)(2,1)S(1)}, u32[]{:S(2)}, u32[]{:S(2)}) collective-permute-start(bf16[256,256]{1,0:T(8,128)(2,1)S(1)} %get-tuple-element.39.refs_0_), channel_id=1, source_target_pairs={{0,1},{1,0},{2,3},{3,2},{4,5},{5,4},{6,7},{7,6},{8,9},{9,8},{10,11... | collective-permute-start | bytes 393224 | tf_op jit(solution)/shard_map/ppermute | solution.py:281
  21.8 0.7 %shard_map.93.stay = f32[1024,256]{1,0:T(8,128)S(1)} custom-call(bf16[2048,1024]{1,0:T(8,128)(2,1)S(1)} %shard_map.92.matrix, bf16[256,256]{1,0:T(8,128)(2,1)S(1)} %get-tuple-element.28.refs_0_, bf16[256,256]{1,0:T(8,128)(2,1)S(1)} %collective-permute-done.1.refs_1_, bf16[256,256]{1,0:T(8,128)(2,1)S(1)} %collective-permute-done.2.refs_2_, ...), custom_call_target="tpu_custom_call" | custom-call | flops 10737418240 | bytes 1 | tf_op jit(solution)/shard_map/pallas_call | solution.py:179
  22.5 0.1 shard_map.95
  22.6 1.6 %collective-permute-start.4 = (bf16[512,256]{1,0:T(8,128)(2,1)S(1)}, bf16[512,256]{1,0:T(8,128)(2,1)S(1)}, u32[]{:S(2)}, u32[]{:S(2)}) collective-permute-start(bf16[512,256]{1,0:T(8,128)(2,1)S(1)} %get-tuple-element.32), channel_id=1, source_target_pairs={{0,8},{4,20},{8,0},{12,28},{16,24},{20,4},{24,16},{28,12},{1,9},{5... | collective-permute-start | bytes 786440 | tf_op jit(solution)/shard_map/ppermute | solution.py:287
  24.2 1.8 %collective-permute-done.7.refs_1_ = bf16[256,256]{1,0:T(8,128)(2,1)S(1)} collective-permute-done((bf16[256,256]{1,0:T(8,128)(2,1)S(1)}, bf16[256,256]{1,0:T(8,128)(2,1)S(1)}, u32[]{:S(2)}, u32[]{:S(2)}) %collective-permute-start.7) | collective-permute-done | bytes 131104 | tf_op jit(solution)/shard_map/ppermute | solution.py:281
  26.1 0.7 %shard_map.99 = bf16[1024,256]{1,0:T(8,128)(2,1)S(1)} custom-call(bf16[2048,1024]{1,0:T(8,128)(2,1)S(1)} %shard_map.92.matrix, bf16[256,256]{1,0:T(8,128)(2,1)S(1)} %get-tuple-element.39.refs_0_, bf16[256,256]{1,0:T(8,128)(2,1)S(1)} %collective-permute-done.7.refs_1_, bf16[256,256]{1,0:T(8,128)(2,1)S(1)} %collective-permute-done.9.refs_2_, ...), custom_call_target="tpu_custom_call" | custom-call | bytes 1 | tf_op jit(solution)/shard_map/pallas_call | solution.py:179
  26.8 0.0 copy-start
  26.8 0.1 collective-permute-start.10
  26.9 0.7 %shard_map.98.stay = f32[1024,256]{1,0:T(8,128)S(1)} custom-call(bf16[2048,1024]{1,0:T(8,128)(2,1)S(1)} %shard_map.92.matrix, bf16[256,256]{1,0:T(8,128)(2,1)S(1)} %get-tuple-element.39.refs_0_, bf16[256,256]{1,0:T(8,128)(2,1)S(1)} %collective-permute-done.7.refs_1_, bf16[256,256]{1,0:T(8,128)(2,1)S(1)} %collective-permute-done.9.refs_2_, ...), custom_call_target="tpu_custom_call" | custom-call | flops 10737418240 | bytes 1 | tf_op jit(solution)/shard_map/pallas_call | solution.py:179
  27.6 1.2 %collective-permute-done.10.came = bf16[1024,256]{1,0:T(8,128)(2,1)S(1)} collective-permute-done((bf16[1024,256]{1,0:T(8,128)(2,1)S(1)}, bf16[1024,256]{1,0:T(8,128)(2,1)S(1)}, u32[]{:S(2)}, u32[]{:S(2)}) %collective-permute-start.10) | collective-permute-done | bytes 524320 | tf_op jit(solution)/shard_map/ppermute | solution.py:281
  28.8 0.1 shard_map.100
  28.9 1.6 %collective-permute-start.11 = (bf16[512,256]{1,0:T(8,128)(2,1)S(1)}, bf16[512,256]{1,0:T(8,128)(2,1)S(1)}, u32[]{:S(2)}, u32[]{:S(2)}) collective-permute-start(bf16[512,256]{1,0:T(8,128)(2,1)S(1)} %get-tuple-element.44), channel_id=1, source_target_pairs={{0,8},{4,20},{8,0},{12,28},{16,24},{20,4},{24,16},{28,12},{1,9},{5... | collective-permute-start | bytes 786440 | tf_op jit(solution)/shard_map/ppermute | solution.py:287
  30.5 1.5 %collective-permute-start.5 = (bf16[256,256]{1,0:T(8,128)(2,1)S(1)}, bf16[256,256]{1,0:T(8,128)(2,1)S(1)}, u32[]{:S(2)}, u32[]{:S(2)}) collective-permute-start(bf16[256,256]{1,0:T(8,128)(2,1)S(1)} %get-tuple-element.34), channel_id=1, source_target_pairs={{0,16},{4,12},{8,24},{12,4},{16,0},{20,28},{24,8},{28,20},{1,17},{... | collective-permute-start | bytes 393224 | tf_op jit(solution)/shard_map/ppermute | solution.py:287
  32.0 4.7 %collective-permute-done.11.came = bf16[512,256]{1,0:T(8,128)(2,1)S(1)} collective-permute-done((bf16[512,256]{1,0:T(8,128)(2,1)S(1)}, bf16[512,256]{1,0:T(8,128)(2,1)S(1)}, u32[]{:S(2)}, u32[]{:S(2)}) %collective-permute-start.11) | collective-permute-done | bytes 262176 | tf_op jit(solution)/shard_map/ppermute | solution.py:287
  36.8 1.1 %collective-permute-start.12 = (bf16[256,256]{1,0:T(8,128)(2,1)S(1)}, bf16[256,256]{1,0:T(8,128)(2,1)S(1)}, u32[]{:S(2)}, u32[]{:S(2)}) collective-permute-start(bf16[256,256]{1,0:T(8,128)(2,1)S(1)} %get-tuple-element.46), channel_id=1, source_target_pairs={{0,16},{4,12},{8,24},{12,4},{16,0},{20,28},{24,8},{28,20},{1,17},{... | collective-permute-start | bytes 393224 | tf_op jit(solution)/shard_map/ppermute | solution.py:287
  37.9 0.1 collective-permute-start.6
  38.0 3.8 %collective-permute-done.12.came = bf16[256,256]{1,0:T(8,128)(2,1)S(1)} collective-permute-done((bf16[256,256]{1,0:T(8,128)(2,1)S(1)}, bf16[256,256]{1,0:T(8,128)(2,1)S(1)}, u32[]{:S(2)}, u32[]{:S(2)}) %collective-permute-start.12) | collective-permute-done | bytes 131104 | tf_op jit(solution)/shard_map/ppermute | solution.py:287
  41.8 0.1 collective-permute-start.13
  41.9 1.2 %collective-permute-done.13.refs_3_ = bf16[128,256]{1,0:T(8,128)(2,1)S(1)} collective-permute-done((bf16[128,256]{1,0:T(8,128)(2,1)S(1)}, bf16[128,256]{1,0:T(8,128)(2,1)S(1)}, u32[]{:S(2)}, u32[]{:S(2)}) %collective-permute-start.13) | collective-permute-done | bytes 65568 | tf_op jit(solution)/shard_map/ppermute | solution.py:281
  43.1 0.8 %shard_map.103 = bf16[256,512]{1,0:T(8,128)(2,1)} custom-call(s32[1]{0:T(128)} %bitcast.row, f32[256,512]{1,0:T(8,128)S(1)} %get-tuple-element.27.projected, f32[2,128]{1,0:T(2,128)S(1)} %bitcast.4, f32[128,256]{1,0:T(8,128)S(1)} %get-tuple-element.35.refs_0_, bf16[128,256]{1,0:T(8,128)(2,1)S(1)} %collective-permute-done.6.refs_1_, ...), custom_call_target="tpu_custom_call" | custom-call | flops 786432 | bytes 2097152 | tf_op jit(solution)/shard_map/pallas_call | solution.py:235
  (11 shorter events, 0.1 us)
Async XLA Ops:
  1.8 10.1 %collective-permute-start = (bf16[256,256]{1,0:T(8,128)(2,1)S(1)}, bf16[256,256]{1,0:T(8,128)(2,1)S(1)}, u32[]{:S(2)}, u32[]{:S(2)}) collective-permute-start(bf16[256,256]{1,0:T(8,128)(2,1)S(1)} %get-tuple-element.28.refs_0_), channel_id=1, source_target_pairs={{0,3},{1,2},{2,1},{3,0},{4,7},{5,6},{6,5},{7,4},{8,11},{9,10},{10,... | collective-permute-start | bytes 393224 | tf_op jit(solution)/shard_map/ppermute | solution.py:281
  6.9 11.6 %collective-permute-start.1 = (bf16[256,256]{1,0:T(8,128)(2,1)S(1)}, bf16[256,256]{1,0:T(8,128)(2,1)S(1)}, u32[]{:S(2)}, u32[]{:S(2)}) collective-permute-start(bf16[256,256]{1,0:T(8,128)(2,1)S(1)} %get-tuple-element.28.refs_0_), channel_id=1, source_target_pairs={{0,1},{1,0},{2,3},{3,2},{4,5},{5,4},{6,7},{7,6},{8,9},{9,8},{10,11... | collective-permute-start | bytes 393224 | tf_op jit(solution)/shard_map/ppermute | solution.py:281
  6.9 10.0 %collective-permute-start.8 = (bf16[256,256]{1,0:T(8,128)(2,1)S(1)}, bf16[256,256]{1,0:T(8,128)(2,1)S(1)}, u32[]{:S(2)}, u32[]{:S(2)}) collective-permute-start(bf16[256,256]{1,0:T(8,128)(2,1)S(1)} %get-tuple-element.39.refs_0_), channel_id=1, source_target_pairs={{0,3},{1,2},{2,1},{3,0},{4,7},{5,6},{6,5},{7,4},{8,11},{9,10},{10,... | collective-permute-start | bytes 393224 | tf_op jit(solution)/shard_map/ppermute | solution.py:281
  11.9 7.5 %collective-permute-start.2 = (bf16[256,256]{1,0:T(8,128)(2,1)S(1)}, bf16[256,256]{1,0:T(8,128)(2,1)S(1)}, u32[]{:S(2)}, u32[]{:S(2)}) collective-permute-start(bf16[256,256]{1,0:T(8,128)(2,1)S(1)} %collective-permute-done.refs_3_), channel_id=1, source_target_pairs={{0,1},{1,0},{2,3},{3,2},{4,5},{5,4},{6,7},{7,6},{8,9},{9,8},{10,11... | collective-permute-start | bytes 393224 | tf_op jit(solution)/shard_map/ppermute | solution.py:281
  17.0 7.3 %collective-permute-start.9 = (bf16[256,256]{1,0:T(8,128)(2,1)S(1)}, bf16[256,256]{1,0:T(8,128)(2,1)S(1)}, u32[]{:S(2)}, u32[]{:S(2)}) collective-permute-start(bf16[256,256]{1,0:T(8,128)(2,1)S(1)} %collective-permute-done.8.refs_3_), channel_id=1, source_target_pairs={{0,1},{1,0},{2,3},{3,2},{4,5},{5,4},{6,7},{7,6},{8,9},{9,8},{10,11... | collective-permute-start | bytes 393224 | tf_op jit(solution)/shard_map/ppermute | solution.py:281
  20.1 2.4 %collective-permute-start.3 = (bf16[1024,256]{1,0:T(8,128)(2,1)S(1)}, bf16[1024,256]{1,0:T(8,128)(2,1)S(1)}, u32[]{:S(2)}, u32[]{:S(2)}) collective-permute-start(bf16[1024,256]{1,0:T(8,128)(2,1)S(1)} %shard_map.94), channel_id=1, source_target_pairs={{0,4},{4,0},{8,12},{12,8},{16,20},{20,16},{24,28},{28,24},{1,5},{5... | collective-permute-start | bytes 1572872 | tf_op jit(solution)/shard_map/ppermute | solution.py:281
  20.2 5.9 %collective-permute-start.7 = (bf16[256,256]{1,0:T(8,128)(2,1)S(1)}, bf16[256,256]{1,0:T(8,128)(2,1)S(1)}, u32[]{:S(2)}, u32[]{:S(2)}) collective-permute-start(bf16[256,256]{1,0:T(8,128)(2,1)S(1)} %get-tuple-element.39.refs_0_), channel_id=1, source_target_pairs={{0,1},{1,0},{2,3},{3,2},{4,5},{5,4},{6,7},{7,6},{8,9},{9,8},{10,11... | collective-permute-start | bytes 393224 | tf_op jit(solution)/shard_map/ppermute | solution.py:281
  22.6 7.8 %collective-permute-start.4 = (bf16[512,256]{1,0:T(8,128)(2,1)S(1)}, bf16[512,256]{1,0:T(8,128)(2,1)S(1)}, u32[]{:S(2)}, u32[]{:S(2)}) collective-permute-start(bf16[512,256]{1,0:T(8,128)(2,1)S(1)} %get-tuple-element.32), channel_id=1, source_target_pairs={{0,8},{4,20},{8,0},{12,28},{16,24},{20,4},{24,16},{28,12},{1,9},{5... | collective-permute-start | bytes 786440 | tf_op jit(solution)/shard_map/ppermute | solution.py:287
  26.8 16.3 %copy-start = (f32[256]{0:T(256)S(1)}, f32[256]{0:T(256)}, u32[]{:S(2)}) copy-start(f32[256]{0:T(256)} %param.12) | copy-start | bytes 3076
  26.8 2.0 %collective-permute-start.10 = (bf16[1024,256]{1,0:T(8,128)(2,1)S(1)}, bf16[1024,256]{1,0:T(8,128)(2,1)S(1)}, u32[]{:S(2)}, u32[]{:S(2)}) collective-permute-start(bf16[1024,256]{1,0:T(8,128)(2,1)S(1)} %shard_map.99), channel_id=1, source_target_pairs={{0,4},{4,0},{8,12},{12,8},{16,20},{20,16},{24,28},{28,24},{1,5},{5... | collective-permute-start | bytes 1572872 | tf_op jit(solution)/shard_map/ppermute | solution.py:281
  28.9 7.8 %collective-permute-start.11 = (bf16[512,256]{1,0:T(8,128)(2,1)S(1)}, bf16[512,256]{1,0:T(8,128)(2,1)S(1)}, u32[]{:S(2)}, u32[]{:S(2)}) collective-permute-start(bf16[512,256]{1,0:T(8,128)(2,1)S(1)} %get-tuple-element.44), channel_id=1, source_target_pairs={{0,8},{4,20},{8,0},{12,28},{16,24},{20,4},{24,16},{28,12},{1,9},{5... | collective-permute-start | bytes 786440 | tf_op jit(solution)/shard_map/ppermute | solution.py:287
  30.5 7.4 %collective-permute-start.5 = (bf16[256,256]{1,0:T(8,128)(2,1)S(1)}, bf16[256,256]{1,0:T(8,128)(2,1)S(1)}, u32[]{:S(2)}, u32[]{:S(2)}) collective-permute-start(bf16[256,256]{1,0:T(8,128)(2,1)S(1)} %get-tuple-element.34), channel_id=1, source_target_pairs={{0,16},{4,12},{8,24},{12,4},{16,0},{20,28},{24,8},{28,20},{1,17},{... | collective-permute-start | bytes 393224 | tf_op jit(solution)/shard_map/ppermute | solution.py:287
  36.8 5.0 %collective-permute-start.12 = (bf16[256,256]{1,0:T(8,128)(2,1)S(1)}, bf16[256,256]{1,0:T(8,128)(2,1)S(1)}, u32[]{:S(2)}, u32[]{:S(2)}) collective-permute-start(bf16[256,256]{1,0:T(8,128)(2,1)S(1)} %get-tuple-element.46), channel_id=1, source_target_pairs={{0,16},{4,12},{8,24},{12,4},{16,0},{20,28},{24,8},{28,20},{1,17},{... | collective-permute-start | bytes 393224 | tf_op jit(solution)/shard_map/ppermute | solution.py:287
  37.9 4.0 %collective-permute-start.6 = (bf16[128,256]{1,0:T(8,128)(2,1)S(1)}, bf16[128,256]{1,0:T(8,128)(2,1)S(1)}, u32[]{:S(2)}, u32[]{:S(2)}) collective-permute-start(bf16[128,256]{1,0:T(8,128)(2,1)S(1)} %get-tuple-element.36), channel_id=1, source_target_pairs={{0,4},{4,0},{8,12},{12,8},{16,20},{20,16},{24,28},{28,24},{1,5},{5... | collective-permute-start | bytes 196616 | tf_op jit(solution)/shard_map/ppermute | solution.py:281
  41.8 1.3 %collective-permute-start.13 = (bf16[128,256]{1,0:T(8,128)(2,1)S(1)}, bf16[128,256]{1,0:T(8,128)(2,1)S(1)}, u32[]{:S(2)}, u32[]{:S(2)}) collective-permute-start(bf16[128,256]{1,0:T(8,128)(2,1)S(1)} %get-tuple-element.48), channel_id=1, source_target_pairs={{0,4},{4,0},{8,12},{12,8},{16,20},{20,16},{24,28},{28,24},{1,5},{5... | collective-permute-start | bytes 196616 | tf_op jit(solution)/shard_map/ppermute | solution.py:281

commit v7 on v3

--- a/solution.py
+++ b/solution.py
@@ -103,7 +103,6 @@
     for copy in small + large:
         copy.start()
     spare, span = total.shape[0] - 1, total.shape[1]
-    owners = spare // own_tiles
     total[...] = jnp.zeros_like(total)
     my_row, my_column, used = row[0], column[0], count[0]
     for copy in small:
@@ -112,8 +111,11 @@
     def add(slot):
         target, source = targets[0, slot], sources[0, slot]
         label = labels[0, target]
-        apart = lax.bitwise_xor(target // per_owner, my_row)
-        position = (1 - apart % 2) * (owners // 2) + apart // 2
+        owner = target // per_owner
+        core, apart = owner % 2, lax.bitwise_xor(owner, my_row)
+        x, y = apart // 2 % 2, apart // 4
+        first, second = jnp.where(core == 0, x, y), jnp.where(core == 0, y, x)
+        position = jnp.where(core == my_row % 2, 4, 0) + second * 2 + first
         place = jnp.where(label < own_tiles, position * own_tiles + label, spare)
         block = lax.bitwise_xor(source // own_tiles, my_column)
         total[place, block * own_tiles + source % own_tiles] += tiles[slot].astype(jnp.float32)
@@ -274,7 +276,12 @@
 
 
 def exchange(sent):
-    return [swap(sent[k], "row", 2 * (k + 1)) for k in reversed(range(len(sent)))]
+    owners = lax.axis_size("row")
+    steps = [(2, 4), (4, 2), (6, 6)]
+    return [
+        lax.ppermute(value, "row", [(i, i ^ step[i % 2]) for i in range(owners)])
+        for value, step in zip(sent, steps)
+    ]
 
 
 def per_device(
@@ -296,7 +303,7 @@
     index_args = (tile_source, tile_target, tile_count, mirror_tile)
 
     cells = owners * own_tiles * span * tile_rows * tile_rows
-    if columns != 4 or owners & (owners - 1) or cells > DENSE_ELEMENTS:
+    if columns != 4 or owners != 8 or cells > DENSE_ELEMENTS:
         projected = jnp.dot(features, weight, preferred_element_type=jnp.float32)
         scaled = (source_norm[:, None] * projected).astype(jnp.bfloat16)
         blocks = lax.all_gather(scaled, "col", axis=0, tiled=True)

time: 39 us -> 39.6 us (1.015)
  Pallas kernels: 8.79 us -> 10.4 us
  starting transfers between devices: 18.4 us -> 17 us
  waiting for transfers between devices: 10.8 us -> 11.3 us
    ppermute x14 -> x8, starting transfers between devices: 18.4 us -> 9.85 us  [swap(): return lax.ppermute(value, axis, pairs)]
    ppermute x0 -> x6, starting transfers between devices: none -> 7.11 us  [exchange(): lax.ppermute(value, 'row', [(i, i ^ step[i % 2]) for i in range(owners)])]
    ppermute x0 -> x6, waiting for transfers between devices: none -> 6.04 us  [exchange(): lax.ppermute(value, 'row', [(i, i ^ step[i % 2]) for i in range(owners)])]
    ppermute x14 -> x8, waiting for transfers between devices: 10.8 us -> 5.26 us  [swap(): return lax.ppermute(value, axis, pairs)]
    pallas_call x1, Pallas kernels: 3.06 us -> 4.64 us  [merge_tiles(): pl.pallas_call(functools.partial(merge_kernel, own_tiles, labels.shape[1]...]
  transfers between devices with their start and end apart: 14 -> 14, of which waited for: 6 -> 6; matrix products, arithmetic and copies ran while one was open for 0% -> 0% of each run, Pallas kernels for 16% -> 19%
where the time goes in v7:
time: 39.6 us; the launch traced here: 39.4 us
  starting transfers between devices  17 us (43%)
  waiting for transfers between devices  11.3 us (29%)
  Pallas kernels  10.4 us (26%)
  between operations  0.75 us (2%)
    ppermute x8, starting transfers between devices, swap(): return lax.ppermute(value, axis, pairs)  9.85 us
    ppermute x6, starting transfers between devices, exchange(): lax.ppermute(value, 'row', [(i, i ^ step[i % 2]) for i in range(owners)])  7.11 us
    ppermute x6, waiting for transfers between devices, exchange(): lax.ppermute(value, 'row', [(i, i ^ step[i % 2]) for i in range(owners)])  6.04 us
    ppermute x8, waiting for transfers between devices, swap(): return lax.ppermute(value, axis, pairs)  5.26 us
    pallas_call x1, Pallas kernels, merge_tiles(): pl.pallas_call(functools.partial(merge_kernel, own_tiles, labels.shape[1]...  4.64 us
    pallas_call x4, Pallas kernels, product(): pl.pallas_call(functools.partial(product_kernel, half * (total // 2)), ou...  2.85 us
    pallas_call x1, Pallas kernels, project(): pl.pallas_call(project_kernel, out_shape=[jax.ShapeDtypeStruct((rows, hid...  1.82 us
    pallas_call x1, Pallas kernels, finish(): pl.pallas_call(functools.partial(finish_kernel, len(pieces)), out_shape=j...  0.88 us
  transfers between devices with their start and end apart: 14, of which 6 were waited for; matrix products, arithmetic and copies ran while one was open for 0% of the time, Pallas kernels for 19%

profile of v7, /device:TPU:0, one launch (start us, length us, event | category | flops | bytes accessed | tf_op | source)
XLA Modules:
  0.0 39.4 jit_solution(12396392910886221980)
XLA Ops:
  0.0 1.8 %shard_map.91 = (f32[256,512]{1,0:T(8,128)S(1)}, bf16[256,256]{1,0:T(8,128)(2,1)S(1)}, bf16[256,256]{1,0:T(8,128)(2,1)S(1)}) custom-call(bf16[256,1024]{1,0:T(8,128)(2,1)} %features_hbm.1, bf16[1024,512]{1,0:T(8,128)(2,1)} %weight_hbm.1, f32[2,128]{1,0:T(2,128)} %bitcast.5), custom_call_target="tpu_custom_call" | custom-call | flops 268435456 | bytes 1572864 | tf_op jit(solution)/shard_map/pallas_call | solution.py:66
  1.8 5.1 %collective-permute-start = (bf16[256,256]{1,0:T(8,128)(2,1)S(1)}, bf16[256,256]{1,0:T(8,128)(2,1)S(1)}, u32[]{:S(2)}, u32[]{:S(2)}) collective-permute-start(bf16[256,256]{1,0:T(8,128)(2,1)S(1)} %get-tuple-element.23.refs_0_), channel_id=1, source_target_pairs={{0,3},{1,2},{2,1},{3,0},{4,7},{5,6},{6,5},{7,4},{8,11},{9,10},{10,... | collective-permute-start | bytes 393224 | tf_op jit(solution)/shard_map/ppermute | solution.py:275
  6.9 0.9 %collective-permute-start.8 = (bf16[256,256]{1,0:T(8,128)(2,1)S(1)}, bf16[256,256]{1,0:T(8,128)(2,1)S(1)}, u32[]{:S(2)}, u32[]{:S(2)}) collective-permute-start(bf16[256,256]{1,0:T(8,128)(2,1)S(1)} %get-tuple-element.31.refs_0_), channel_id=1, source_target_pairs={{0,3},{1,2},{2,1},{3,0},{4,7},{5,6},{6,5},{7,4},{8,11},{9,10},{10,... | collective-permute-start | bytes 393224 | tf_op jit(solution)/shard_map/ppermute | solution.py:275
  8.5 4.6 %shard_map.92.matrix = bf16[2048,1024]{1,0:T(8,128)(2,1)S(1)} custom-call(s32[1]{0:T(128)} %bitcast.2.row, s32[1]{0:T(128)} %bitcast.3.column, s32[1]{0:T(128)S(6)} %copy.10.count, s32[1,64]{1,0:T(1,128)} %sources_hbm.1, s32[1,64]{1,0:T(1,128)} %targets_hbm.1, s32[1,16]{1,0:T(1,128)} %labels_hbm.1, bf16[1,64,128,128]{3,2,1,0:T(8,128)(2,1)} %tiles_hbm.1), custom_call_target="tpu_custom_call" | custom-call | flops 8388608 | bytes 12582912 | tf_op jit(solution)/shard_map/pallas_call | solution.py:141
  13.2 1.6 %collective-permute-start.2 = (bf16[256,256]{1,0:T(8,128)(2,1)S(1)}, bf16[256,256]{1,0:T(8,128)(2,1)S(1)}, u32[]{:S(2)}, u32[]{:S(2)}) collective-permute-start(bf16[256,256]{1,0:T(8,128)(2,1)S(1)} %collective-permute-done.refs_3_), channel_id=1, source_target_pairs={{0,1},{1,0},{2,3},{3,2},{4,5},{5,4},{6,7},{7,6},{8,9},{9,8},{10,11... | collective-permute-start | bytes 393224 | tf_op jit(solution)/shard_map/ppermute | solution.py:275
  14.8 0.5 %collective-permute-start.7 = (bf16[256,256]{1,0:T(8,128)(2,1)S(1)}, bf16[256,256]{1,0:T(8,128)(2,1)S(1)}, u32[]{:S(2)}, u32[]{:S(2)}) collective-permute-start(bf16[256,256]{1,0:T(8,128)(2,1)S(1)} %get-tuple-element.31.refs_0_), channel_id=1, source_target_pairs={{0,1},{1,0},{2,3},{3,2},{4,5},{5,4},{6,7},{7,6},{8,9},{9,8},{10,11... | collective-permute-start | bytes 393224 | tf_op jit(solution)/shard_map/ppermute | solution.py:275
  15.2 1.7 %collective-permute-done.8.refs_3_ = bf16[256,256]{1,0:T(8,128)(2,1)S(1)} collective-permute-done((bf16[256,256]{1,0:T(8,128)(2,1)S(1)}, bf16[256,256]{1,0:T(8,128)(2,1)S(1)}, u32[]{:S(2)}, u32[]{:S(2)}) %collective-permute-start.8) | collective-permute-done | bytes 131104 | tf_op jit(solution)/shard_map/ppermute | solution.py:275
  17.0 1.6 %collective-permute-start.9 = (bf16[256,256]{1,0:T(8,128)(2,1)S(1)}, bf16[256,256]{1,0:T(8,128)(2,1)S(1)}, u32[]{:S(2)}, u32[]{:S(2)}) collective-permute-start(bf16[256,256]{1,0:T(8,128)(2,1)S(1)} %collective-permute-done.8.refs_3_), channel_id=1, source_target_pairs={{0,1},{1,0},{2,3},{3,2},{4,5},{5,4},{6,7},{7,6},{8,9},{9,8},{10,11... | collective-permute-start | bytes 393224 | tf_op jit(solution)/shard_map/ppermute | solution.py:275
  18.6 0.0 collective-permute-done.1.refs_1_
  18.6 1.2 %collective-permute-done.2.refs_2_ = bf16[256,256]{1,0:T(8,128)(2,1)S(1)} collective-permute-done((bf16[256,256]{1,0:T(8,128)(2,1)S(1)}, bf16[256,256]{1,0:T(8,128)(2,1)S(1)}, u32[]{:S(2)}, u32[]{:S(2)}) %collective-permute-start.2) | collective-permute-done | bytes 131104 | tf_op jit(solution)/shard_map/ppermute | solution.py:275
  19.8 0.7 %shard_map.94 = bf16[1024,256]{1,0:T(8,128)(2,1)S(1)} custom-call(bf16[2048,1024]{1,0:T(8,128)(2,1)S(1)} %shard_map.92.matrix, bf16[256,256]{1,0:T(8,128)(2,1)S(1)} %get-tuple-element.23.refs_0_, bf16[256,256]{1,0:T(8,128)(2,1)S(1)} %collective-permute-done.1.refs_1_, bf16[256,256]{1,0:T(8,128)(2,1)S(1)} %collective-permute-done.2.refs_2_, ...), custom_call_target="tpu_custom_call" | custom-call | flops 10737418240 | bytes 1 | tf_op jit(solution)/shard_map/pallas_call | solution.py:176
  20.5 0.1 collective-permute-start.3
  20.5 0.7 %shard_map.93.stay = f32[1024,256]{1,0:T(8,128)S(1)} custom-call(bf16[2048,1024]{1,0:T(8,128)(2,1)S(1)} %shard_map.92.matrix, bf16[256,256]{1,0:T(8,128)(2,1)S(1)} %get-tuple-element.23.refs_0_, bf16[256,256]{1,0:T(8,128)(2,1)S(1)} %collective-permute-done.1.refs_1_, bf16[256,256]{1,0:T(8,128)(2,1)S(1)} %collective-permute-done.2.refs_2_, ...), custom_call_target="tpu_custom_call" | custom-call | flops 10737418240 | bytes 1 | tf_op jit(solution)/shard_map/pallas_call | solution.py:176
  21.3 1.2 %collective-permute-done.3.came = bf16[1024,256]{1,0:T(8,128)(2,1)S(1)} collective-permute-done((bf16[1024,256]{1,0:T(8,128)(2,1)S(1)}, bf16[1024,256]{1,0:T(8,128)(2,1)S(1)}, u32[]{:S(2)}, u32[]{:S(2)}) %collective-permute-start.3) | collective-permute-done | bytes 524320 | tf_op jit(solution)/shard_map/ppermute | solution.py:275
  22.4 0.1 shard_map.95
  22.5 1.3 %collective-permute-start.4 = (bf16[256,256]{1,0:T(8,128)(2,1)S(1)}, bf16[256,256]{1,0:T(8,128)(2,1)S(1)}, u32[]{:S(2)}, u32[]{:S(2)}) collective-permute-start(bf16[256,256]{1,0:T(8,128)(2,1)S(1)} %get-tuple-element.27), channel_id=1, source_target_pairs={{0,8},{4,20},{8,0},{12,28},{16,24},{20,4},{24,16},{28,12},{1,9},{5... | collective-permute-start | bytes 393224 | tf_op jit(solution)/shard_map/ppermute | solution.py:282
  23.8 1.9 %collective-permute-start.5 = (bf16[256,256]{1,0:T(8,128)(2,1)S(1)}, bf16[256,256]{1,0:T(8,128)(2,1)S(1)}, u32[]{:S(2)}, u32[]{:S(2)}) collective-permute-start(bf16[256,256]{1,0:T(8,128)(2,1)S(1)} %get-tuple-element.28), channel_id=1, source_target_pairs={{0,16},{4,12},{8,24},{12,4},{16,0},{20,28},{24,8},{28,20},{1,17},{... | collective-permute-start | bytes 393224 | tf_op jit(solution)/shard_map/ppermute | solution.py:282
  25.7 0.4 %collective-permute-start.6 = (bf16[256,256]{1,0:T(8,128)(2,1)S(1)}, bf16[256,256]{1,0:T(8,128)(2,1)S(1)}, u32[]{:S(2)}, u32[]{:S(2)}) collective-permute-start(bf16[256,256]{1,0:T(8,128)(2,1)S(1)} %get-tuple-element.29), channel_id=1, source_target_pairs={{0,24},{4,28},{8,16},{12,20},{16,8},{20,12},{24,0},{28,4},{1,25},{... | collective-permute-start | bytes 393224 | tf_op jit(solution)/shard_map/ppermute | solution.py:282
  26.1 0.0 collective-permute-done.7.refs_1_
  26.1 0.7 %shard_map.97 = bf16[1024,256]{1,0:T(8,128)(2,1)S(1)} custom-call(bf16[2048,1024]{1,0:T(8,128)(2,1)S(1)} %shard_map.92.matrix, bf16[256,256]{1,0:T(8,128)(2,1)S(1)} %get-tuple-element.31.refs_0_, bf16[256,256]{1,0:T(8,128)(2,1)S(1)} %collective-permute-done.7.refs_1_, bf16[256,256]{1,0:T(8,128)(2,1)S(1)} %collective-permute-done.9.refs_2_, ...), custom_call_target="tpu_custom_call" | custom-call | bytes 1 | tf_op jit(solution)/shard_map/pallas_call | solution.py:176
  26.8 0.0 copy-start
  26.8 0.1 collective-permute-start.10
  26.9 0.7 %shard_map.96.stay = f32[1024,256]{1,0:T(8,128)S(1)} custom-call(bf16[2048,1024]{1,0:T(8,128)(2,1)S(1)} %shard_map.92.matrix, bf16[256,256]{1,0:T(8,128)(2,1)S(1)} %get-tuple-element.31.refs_0_, bf16[256,256]{1,0:T(8,128)(2,1)S(1)} %collective-permute-done.7.refs_1_, bf16[256,256]{1,0:T(8,128)(2,1)S(1)} %collective-permute-done.9.refs_2_, ...), custom_call_target="tpu_custom_call" | custom-call | flops 10737418240 | bytes 1 | tf_op jit(solution)/shard_map/pallas_call | solution.py:176
  27.6 1.2 %collective-permute-done.10.came = bf16[1024,256]{1,0:T(8,128)(2,1)S(1)} collective-permute-done((bf16[1024,256]{1,0:T(8,128)(2,1)S(1)}, bf16[1024,256]{1,0:T(8,128)(2,1)S(1)}, u32[]{:S(2)}, u32[]{:S(2)}) %collective-permute-start.10) | collective-permute-done | bytes 524320 | tf_op jit(solution)/shard_map/ppermute | solution.py:275
  28.8 0.1 shard_map.98
  28.9 1.3 %collective-permute-start.11 = (bf16[256,256]{1,0:T(8,128)(2,1)S(1)}, bf16[256,256]{1,0:T(8,128)(2,1)S(1)}, u32[]{:S(2)}, u32[]{:S(2)}) collective-permute-start(bf16[256,256]{1,0:T(8,128)(2,1)S(1)} %get-tuple-element.36), channel_id=1, source_target_pairs={{0,8},{4,20},{8,0},{12,28},{16,24},{20,4},{24,16},{28,12},{1,9},{5... | collective-permute-start | bytes 393224 | tf_op jit(solution)/shard_map/ppermute | solution.py:282
  30.2 1.9 %collective-permute-start.12 = (bf16[256,256]{1,0:T(8,128)(2,1)S(1)}, bf16[256,256]{1,0:T(8,128)(2,1)S(1)}, u32[]{:S(2)}, u32[]{:S(2)}) collective-permute-start(bf16[256,256]{1,0:T(8,128)(2,1)S(1)} %get-tuple-element.37), channel_id=1, source_target_pairs={{0,16},{4,12},{8,24},{12,4},{16,0},{20,28},{24,8},{28,20},{1,17},{... | collective-permute-start | bytes 393224 | tf_op jit(solution)/shard_map/ppermute | solution.py:282
  32.0 0.4 %collective-permute-start.13 = (bf16[256,256]{1,0:T(8,128)(2,1)S(1)}, bf16[256,256]{1,0:T(8,128)(2,1)S(1)}, u32[]{:S(2)}, u32[]{:S(2)}) collective-permute-start(bf16[256,256]{1,0:T(8,128)(2,1)S(1)} %get-tuple-element.38), channel_id=1, source_target_pairs={{0,24},{4,28},{8,16},{12,20},{16,8},{20,12},{24,0},{28,4},{1,25},{... | collective-permute-start | bytes 393224 | tf_op jit(solution)/shard_map/ppermute | solution.py:282
  32.5 2.7 %collective-permute-done.11.refs_5_ = bf16[256,256]{1,0:T(8,128)(2,1)S(1)} collective-permute-done((bf16[256,256]{1,0:T(8,128)(2,1)S(1)}, bf16[256,256]{1,0:T(8,128)(2,1)S(1)}, u32[]{:S(2)}, u32[]{:S(2)}) %collective-permute-start.11) | collective-permute-done | bytes 131104 | tf_op jit(solution)/shard_map/ppermute | solution.py:282
  35.1 0.0 collective-permute-done.12.refs_6_
  35.1 3.4 %collective-permute-done.13.refs_7_ = bf16[256,256]{1,0:T(8,128)(2,1)S(1)} collective-permute-done((bf16[256,256]{1,0:T(8,128)(2,1)S(1)}, bf16[256,256]{1,0:T(8,128)(2,1)S(1)}, u32[]{:S(2)}, u32[]{:S(2)}) %collective-permute-start.13) | collective-permute-done | bytes 131104 | tf_op jit(solution)/shard_map/ppermute | solution.py:282
  38.5 0.9 %shard_map.99 = bf16[256,512]{1,0:T(8,128)(2,1)} custom-call(f32[256,512]{1,0:T(8,128)S(1)} %get-tuple-element.22.projected, f32[2,128]{1,0:T(2,128)S(1)} %bitcast.4, f32[256,256]{1,0:T(8,128)S(1)} %get-tuple-element.26.refs_0_, bf16[256,256]{1,0:T(8,128)(2,1)S(1)} %collective-permute-done.4.refs_1_, bf16[256,256]{1,0:T(8,128)(2,1)S(1)} %collective-permute-done.5.refs_2_, ...), custom_call_target="tpu_custom_call" | custom-call | flops 786432 | bytes 2097152 | tf_op jit(solution)/shard_map/pallas_call | solution.py:229
  (7 shorter events, 0.0 us)
Async XLA Ops:
  1.8 11.3 %collective-permute-start = (bf16[256,256]{1,0:T(8,128)(2,1)S(1)}, bf16[256,256]{1,0:T(8,128)(2,1)S(1)}, u32[]{:S(2)}, u32[]{:S(2)}) collective-permute-start(bf16[256,256]{1,0:T(8,128)(2,1)S(1)} %get-tuple-element.23.refs_0_), channel_id=1, source_target_pairs={{0,3},{1,2},{2,1},{3,0},{4,7},{5,6},{6,5},{7,4},{8,11},{9,10},{10,... | collective-permute-start | bytes 393224 | tf_op jit(solution)/shard_map/ppermute | solution.py:275
  6.9 11.6 %collective-permute-start.1 = (bf16[256,256]{1,0:T(8,128)(2,1)S(1)}, bf16[256,256]{1,0:T(8,128)(2,1)S(1)}, u32[]{:S(2)}, u32[]{:S(2)}) collective-permute-start(bf16[256,256]{1,0:T(8,128)(2,1)S(1)} %get-tuple-element.23.refs_0_), channel_id=1, source_target_pairs={{0,1},{1,0},{2,3},{3,2},{4,5},{5,4},{6,7},{7,6},{8,9},{9,8},{10,11... | collective-permute-start | bytes 393224 | tf_op jit(solution)/shard_map/ppermute | solution.py:275
  6.9 10.0 %collective-permute-start.8 = (bf16[256,256]{1,0:T(8,128)(2,1)S(1)}, bf16[256,256]{1,0:T(8,128)(2,1)S(1)}, u32[]{:S(2)}, u32[]{:S(2)}) collective-permute-start(bf16[256,256]{1,0:T(8,128)(2,1)S(1)} %get-tuple-element.31.refs_0_), channel_id=1, source_target_pairs={{0,3},{1,2},{2,1},{3,0},{4,7},{5,6},{6,5},{7,4},{8,11},{9,10},{10,... | collective-permute-start | bytes 393224 | tf_op jit(solution)/shard_map/ppermute | solution.py:275
  13.2 6.6 %collective-permute-start.2 = (bf16[256,256]{1,0:T(8,128)(2,1)S(1)}, bf16[256,256]{1,0:T(8,128)(2,1)S(1)}, u32[]{:S(2)}, u32[]{:S(2)}) collective-permute-start(bf16[256,256]{1,0:T(8,128)(2,1)S(1)} %collective-permute-done.refs_3_), channel_id=1, source_target_pairs={{0,1},{1,0},{2,3},{3,2},{4,5},{5,4},{6,7},{7,6},{8,9},{9,8},{10,11... | collective-permute-start | bytes 393224 | tf_op jit(solution)/shard_map/ppermute | solution.py:275
  14.8 11.3 %collective-permute-start.7 = (bf16[256,256]{1,0:T(8,128)(2,1)S(1)}, bf16[256,256]{1,0:T(8,128)(2,1)S(1)}, u32[]{:S(2)}, u32[]{:S(2)}) collective-permute-start(bf16[256,256]{1,0:T(8,128)(2,1)S(1)} %get-tuple-element.31.refs_0_), channel_id=1, source_target_pairs={{0,1},{1,0},{2,3},{3,2},{4,5},{5,4},{6,7},{7,6},{8,9},{9,8},{10,11... | collective-permute-start | bytes 393224 | tf_op jit(solution)/shard_map/ppermute | solution.py:275
  17.0 9.1 %collective-permute-start.9 = (bf16[256,256]{1,0:T(8,128)(2,1)S(1)}, bf16[256,256]{1,0:T(8,128)(2,1)S(1)}, u32[]{:S(2)}, u32[]{:S(2)}) collective-permute-start(bf16[256,256]{1,0:T(8,128)(2,1)S(1)} %collective-permute-done.8.refs_3_), channel_id=1, source_target_pairs={{0,1},{1,0},{2,3},{3,2},{4,5},{5,4},{6,7},{7,6},{8,9},{9,8},{10,11... | collective-permute-start | bytes 393224 | tf_op jit(solution)/shard_map/ppermute | solution.py:275
  20.5 2.0 %collective-permute-start.3 = (bf16[1024,256]{1,0:T(8,128)(2,1)S(1)}, bf16[1024,256]{1,0:T(8,128)(2,1)S(1)}, u32[]{:S(2)}, u32[]{:S(2)}) collective-permute-start(bf16[1024,256]{1,0:T(8,128)(2,1)S(1)} %shard_map.94), channel_id=1, source_target_pairs={{0,4},{4,0},{8,12},{12,8},{16,20},{20,16},{24,28},{28,24},{1,5},{5... | collective-permute-start | bytes 1572872 | tf_op jit(solution)/shard_map/ppermute | solution.py:275
  22.5 9.5 %collective-permute-start.4 = (bf16[256,256]{1,0:T(8,128)(2,1)S(1)}, bf16[256,256]{1,0:T(8,128)(2,1)S(1)}, u32[]{:S(2)}, u32[]{:S(2)}) collective-permute-start(bf16[256,256]{1,0:T(8,128)(2,1)S(1)} %get-tuple-element.27), channel_id=1, source_target_pairs={{0,8},{4,20},{8,0},{12,28},{16,24},{20,4},{24,16},{28,12},{1,9},{5... | collective-permute-start | bytes 393224 | tf_op jit(solution)/shard_map/ppermute | solution.py:282
  23.8 8.7 %collective-permute-start.5 = (bf16[256,256]{1,0:T(8,128)(2,1)S(1)}, bf16[256,256]{1,0:T(8,128)(2,1)S(1)}, u32[]{:S(2)}, u32[]{:S(2)}) collective-permute-start(bf16[256,256]{1,0:T(8,128)(2,1)S(1)} %get-tuple-element.28), channel_id=1, source_target_pairs={{0,16},{4,12},{8,24},{12,4},{16,0},{20,28},{24,8},{28,20},{1,17},{... | collective-permute-start | bytes 393224 | tf_op jit(solution)/shard_map/ppermute | solution.py:282
  25.7 6.8 %collective-permute-start.6 = (bf16[256,256]{1,0:T(8,128)(2,1)S(1)}, bf16[256,256]{1,0:T(8,128)(2,1)S(1)}, u32[]{:S(2)}, u32[]{:S(2)}) collective-permute-start(bf16[256,256]{1,0:T(8,128)(2,1)S(1)} %get-tuple-element.29), channel_id=1, source_target_pairs={{0,24},{4,28},{8,16},{12,20},{16,8},{20,12},{24,0},{28,4},{1,25},{... | collective-permute-start | bytes 393224 | tf_op jit(solution)/shard_map/ppermute | solution.py:282
  26.8 11.7 %copy-start = (f32[256]{0:T(256)S(1)}, f32[256]{0:T(256)}, u32[]{:S(2)}) copy-start(f32[256]{0:T(256)} %param.12) | copy-start | bytes 3076
  26.8 2.0 %collective-permute-start.10 = (bf16[1024,256]{1,0:T(8,128)(2,1)S(1)}, bf16[1024,256]{1,0:T(8,128)(2,1)S(1)}, u32[]{:S(2)}, u32[]{:S(2)}) collective-permute-start(bf16[1024,256]{1,0:T(8,128)(2,1)S(1)} %shard_map.97), channel_id=1, source_target_pairs={{0,4},{4,0},{8,12},{12,8},{16,20},{20,16},{24,28},{28,24},{1,5},{5... | collective-permute-start | bytes 1572872 | tf_op jit(solution)/shard_map/ppermute | solution.py:275
  28.9 6.2 %collective-permute-start.11 = (bf16[256,256]{1,0:T(8,128)(2,1)S(1)}, bf16[256,256]{1,0:T(8,128)(2,1)S(1)}, u32[]{:S(2)}, u32[]{:S(2)}) collective-permute-start(bf16[256,256]{1,0:T(8,128)(2,1)S(1)} %get-tuple-element.36), channel_id=1, source_target_pairs={{0,8},{4,20},{8,0},{12,28},{16,24},{20,4},{24,16},{28,12},{1,9},{5... | collective-permute-start | bytes 393224 | tf_op jit(solution)/shard_map/ppermute | solution.py:282
  30.2 5.0 %collective-permute-start.12 = (bf16[256,256]{1,0:T(8,128)(2,1)S(1)}, bf16[256,256]{1,0:T(8,128)(2,1)S(1)}, u32[]{:S(2)}, u32[]{:S(2)}) collective-permute-start(bf16[256,256]{1,0:T(8,128)(2,1)S(1)} %get-tuple-element.37), channel_id=1, source_target_pairs={{0,16},{4,12},{8,24},{12,4},{16,0},{20,28},{24,8},{28,20},{1,17},{... | collective-permute-start | bytes 393224 | tf_op jit(solution)/shard_map/ppermute | solution.py:282
  32.0 6.5 %collective-permute-start.13 = (bf16[256,256]{1,0:T(8,128)(2,1)S(1)}, bf16[256,256]{1,0:T(8,128)(2,1)S(1)}, u32[]{:S(2)}, u32[]{:S(2)}) collective-permute-start(bf16[256,256]{1,0:T(8,128)(2,1)S(1)} %get-tuple-element.38), channel_id=1, source_target_pairs={{0,24},{4,28},{8,16},{12,20},{16,8},{20,12},{24,0},{28,4},{1,25},{... | collective-permute-start | bytes 393224 | tf_op jit(solution)/shard_map/ppermute | solution.py:282

commit v8 on v7

--- a/solution.py
+++ b/solution.py
@@ -157,39 +157,59 @@
     )(row, column, count, *in_hbm(sources, targets, labels, tile_weights))
 
 
-def product_kernel(first, matrix, *refs):
-    *blocks, out, gathered = refs
-    rows = blocks[0].shape[0]
-    for k, block in enumerate(blocks):
-        gathered[k * rows : (k + 1) * rows, :] = block[...]
-    value = jnp.dot(
-        matrix[first : first + out.shape[0], :],
-        gathered[...],
-        preferred_element_type=jnp.float32,
+def early_kernel(matrix, own, beside, across, out):
+    rows = own.shape[0]
+    value = jnp.dot(matrix[:, :rows], own[...], preferred_element_type=jnp.float32)
+    value += jnp.dot(
+        matrix[:, rows : 2 * rows], beside[...], preferred_element_type=jnp.float32
+    )
+    value += jnp.dot(matrix[:, 3 * rows :], across[...], preferred_element_type=jnp.float32)
+    out[...] = value
+
+
+def early_product(matrix, own, beside, across):
+    total, depth = matrix.shape
+    width = own.shape[1]
+    return pl.pallas_call(
+        early_kernel,
+        out_shape=jax.ShapeDtypeStruct((total, width), jnp.float32),
+        in_specs=[VMEM] * 4,
+        out_specs=VMEM,
+        compiler_params=params(16),
+        cost_estimate=cost(20 * total * depth * width, 1),
+    )(matrix, own, beside, across)
+
+
+def late_kernel(first, matrix, early, passed, out):
+    rows = passed.shape[0]
+    here = slice(first, first + out.shape[0])
+    value = early[here, :] + jnp.dot(
+        matrix[here, 2 * rows : 3 * rows], passed[...], preferred_element_type=jnp.float32
     )
     out[...] = value.astype(out.dtype)
 
 
-def product(matrix, blocks, half, dtype, weight):
-    rows, width = blocks[0].shape
+def late_product(matrix, early, passed, first, count, dtype, weight):
     total, depth = matrix.shape
-    return pl.pallas_call(
-        functools.partial(product_kernel, half * (total // 2)),
-        out_shape=jax.ShapeDtypeStruct((total // 2, width), dtype),
-        in_specs=[VMEM] * (1 + len(blocks)),
-        out_specs=VMEM,
-        scratch_shapes=[pltpu.VMEM((depth, width), blocks[0].dtype)],
+    width = passed.shape[1]
+    return pl.pallas_call(
+        functools.partial(late_kernel, first),
+        out_shape=jax.ShapeDtypeStruct((count, width), dtype),
+        in_specs=[VMEM] * 3,
+        out_specs=VMEM,
         compiler_params=params(16),
         cost_estimate=cost(weight * total * depth * width, 1),
-    )(matrix, *blocks)
-
-
-def join_kernel(stay, came, kept, *sent):
-    rows = kept.shape[0]
-    value = stay[...].astype(jnp.float32) + came[...].astype(jnp.float32)
-    kept[...] = value[:rows]
-    for place, out in enumerate(sent):
-        out[...] = value[(place + 1) * rows : (place + 2) * rows].astype(out.dtype)
+    )(matrix, early, passed)
+
+
+def join_kernel(stay, *refs):
+    came, (kept, *sent) = refs[:2], refs[2:]
+    rows, half = kept.shape[0], came[0].shape[0]
+    for place, out in enumerate([kept] + sent):
+        start = place * rows
+        other = came[start // half][start % half : start % half + rows, :]
+        value = stay[start : start + rows, :] + other.astype(jnp.float32)
+        out[...] = value.astype(out.dtype)
 
 
 def join(stay, came, rows):
@@ -199,11 +219,11 @@
         join_kernel,
         out_shape=[jax.ShapeDtypeStruct((rows, width), jnp.float32)]
         + [jax.ShapeDtypeStruct((rows, width), jnp.bfloat16)] * (parts - 1),
-        in_specs=[VMEM] * 2,
+        in_specs=[VMEM] * 3,
         out_specs=[VMEM] * parts,
         compiler_params=params(12),
         cost_estimate=cost(1, 1),
-    )(stay, came)
+    )(stay, *came)
 
 
 def finish_kernel(chunks, projected, norm, *refs):
@@ -314,19 +334,30 @@
         return jnp.maximum(target_norm[:, None] * gathered, 0.0).astype(jnp.bfloat16)
 
     projected, *scaled = project(features, weight, source_norm, CHUNKS)
-    matrix = merge_tiles(own_tiles, owners, span, index_args, tile_weights)
+    built = merge_tiles(own_tiles, owners, span, index_args, tile_weights)
+    half = built.shape[0] // 2
     across = [swap(own, "col", 3) for own in scaled]
-    beside = [swap(own, "col", 1) for own in scaled]
-    across[0], matrix = lax.optimization_barrier((across[0], matrix))
-    passed = [swap(value, "col", 1) for value in across]
-    pieces, sent = [], None
-    for blocks, wait in zip(zip(scaled, beside, passed, across), WEIGHTS):
-        if sent is not None:
+    pieces, sent, away, early = [], None, None, None
+    for chunk, (own, far, wait) in enumerate(zip(scaled, across, WEIGHTS)):
+        ready, onward = own, far
+        if chunk:
+            ready, _ = lax.optimization_barrier((own, built))
+            onward, _ = lax.optimization_barrier((far, early))
+        else:
+            onward, matrix = lax.optimization_barrier((far, built))
+        last, near = swap(onward, "col", 1), swap(ready, "col", 1)
+        if chunk:
+            near, _ = lax.optimization_barrier((near, away))
+        early = early_product(matrix, own, near, far)
+        if chunk:
             pieces[-1] += exchange(sent)
-            blocks, _ = lax.optimization_barrier((blocks, sent))
-        away = product(matrix, blocks, 0, jnp.bfloat16, wait[0])
-        stay = product(matrix, blocks, 1, jnp.float32, wait[1])
-        kept, *sent = join(stay, swap(away, "row", 1), own_rows)
+            last, _ = lax.optimization_barrier((last, sent))
+        away = [
+            late_product(matrix, early, last, k * half // 2, half // 2, jnp.bfloat16, wait[0])
+            for k in range(2)
+        ]
+        stay = late_product(matrix, early, last, half, half, jnp.float32, wait[1])
+        kept, *sent = join(stay, [swap(value, "row", 1) for value in away], own_rows)
         pieces.append([kept])
     pieces[-1] += exchange(sent)
     return finish(projected, target_norm, pieces)

time: 39.6 us -> 41.7 us (1.053)
  starting transfers between devices: 17 us -> 19.7 us
  Pallas kernels: 10.4 us -> 9.34 us
    ppermute x8 -> x10, starting transfers between devices: 9.85 us -> 12.6 us  [swap(): return lax.ppermute(value, axis, pairs)]
    pallas_call x1, Pallas kernels: 4.64 us -> 2.94 us  [merge_tiles(): pl.pallas_call(functools.partial(merge_kernel, own_tiles, labels.shape[1]...]
    pallas_call x4 -> x8, Pallas kernels: 2.85 us -> 3.5 us  [the longest x2 1.97 us: early_product(): pl.pallas_call(early_kernel, out_shape=jax.ShapeDtypeStruct((total, width...]
    ppermute x8 -> x10, waiting for transfers between devices: 5.26 us -> 5.3 us  [swap(): return lax.ppermute(value, axis, pairs)]
  transfers between devices with their start and end apart: 14 -> 16, of which waited for: 6 -> 8; matrix products, arithmetic and copies ran while one was open for 0% -> 0% of each run, Pallas kernels for 19% -> 16%
where the time goes in v8:
time: 41.7 us; the launch traced here: 41.4 us
  starting transfers between devices  19.7 us (47%)
  waiting for transfers between devices  11.5 us (28%)
  Pallas kernels  9.34 us (22%)
  between operations  0.78 us (2%)
    ppermute x10, starting transfers between devices, swap(): return lax.ppermute(value, axis, pairs)  12.6 us
    ppermute x6, starting transfers between devices, exchange(): lax.ppermute(value, 'row', [(i, i ^ step[i % 2]) for i in range(owners)])  7.11 us
    ppermute x6, waiting for transfers between devices, exchange(): lax.ppermute(value, 'row', [(i, i ^ step[i % 2]) for i in range(owners)])  6.23 us
    ppermute x10, waiting for transfers between devices, swap(): return lax.ppermute(value, axis, pairs)  5.3 us
    pallas_call x1, Pallas kernels, merge_tiles(): pl.pallas_call(functools.partial(merge_kernel, own_tiles, labels.shape[1]...  2.94 us
    pallas_call x2, Pallas kernels, early_product(): pl.pallas_call(early_kernel, out_shape=jax.ShapeDtypeStruct((total, width...  1.97 us
    pallas_call x1, Pallas kernels, project(): pl.pallas_call(project_kernel, out_shape=[jax.ShapeDtypeStruct((rows, hid...  1.82 us
    pallas_call x6, Pallas kernels, late_product(): pl.pallas_call(functools.partial(late_kernel, first), out_shape=jax.Shape...  1.53 us
  transfers between devices with their start and end apart: 16, of which 8 were waited for; matrix products, arithmetic and copies ran while one was open for 0% of the time, Pallas kernels for 16%

profile of v8, /device:TPU:0, one launch (start us, length us, event | category | flops | bytes accessed | tf_op | source)
XLA Modules:
  0.0 41.4 jit_solution(16630899419354800262)
XLA Ops:
  0.0 1.8 %shard_map.91 = (f32[256,512]{1,0:T(8,128)S(1)}, bf16[256,256]{1,0:T(8,128)(2,1)S(1)}, bf16[256,256]{1,0:T(8,128)(2,1)S(1)}) custom-call(bf16[256,1024]{1,0:T(8,128)(2,1)} %features_hbm.1, bf16[1024,512]{1,0:T(8,128)(2,1)} %weight_hbm.1, f32[2,128]{1,0:T(2,128)} %bitcast.5), custom_call_target="tpu_custom_call" | custom-call | flops 268435456 | bytes 1572864 | tf_op jit(solution)/shard_map/pallas_call | solution.py:66
  1.8 5.1 %collective-permute-start = (bf16[256,256]{1,0:T(8,128)(2,1)S(1)}, bf16[256,256]{1,0:T(8,128)(2,1)S(1)}, u32[]{:S(2)}, u32[]{:S(2)}) collective-permute-start(bf16[256,256]{1,0:T(8,128)(2,1)S(1)} %get-tuple-element.23.own), channel_id=1, source_target_pairs={{0,3},{1,2},{2,1},{3,0},{4,7},{5,6},{6,5},{7,4},{8,11},{9,10},{10,... | collective-permute-start | bytes 393224 | tf_op jit(solution)/shard_map/ppermute | solution.py:295
  6.9 0.9 %collective-permute-start.9 = (bf16[256,256]{1,0:T(8,128)(2,1)S(1)}, bf16[256,256]{1,0:T(8,128)(2,1)S(1)}, u32[]{:S(2)}, u32[]{:S(2)}) collective-permute-start(bf16[256,256]{1,0:T(8,128)(2,1)S(1)} %get-tuple-element.31.own), channel_id=1, source_target_pairs={{0,3},{1,2},{2,1},{3,0},{4,7},{5,6},{6,5},{7,4},{8,11},{9,10},{10,... | collective-permute-start | bytes 393224 | tf_op jit(solution)/shard_map/ppermute | solution.py:295
  8.5 2.9 %shard_map.92.matrix = bf16[2048,1024]{1,0:T(8,128)(2,1)S(1)} custom-call(s32[1]{0:T(128)} %bitcast.2.row, s32[1]{0:T(128)} %bitcast.3.column, s32[1]{0:T(128)S(6)} %copy.10.count, s32[1,64]{1,0:T(1,128)} %sources_hbm.1, s32[1,64]{1,0:T(1,128)} %targets_hbm.1, s32[1,16]{1,0:T(1,128)} %labels_hbm.1, bf16[1,64,128,128]{3,2,1,0:T(8,128)(2,1)} %tiles_hbm.1), custom_call_target="tpu_custom_call" | custom-call | flops 8388608 | bytes 12582912 | tf_op jit(solution)/shard_map/pallas_call | solution.py:141
  11.4 1.1 %collective-permute-start.8 = (bf16[256,256]{1,0:T(8,128)(2,1)S(1)}, bf16[256,256]{1,0:T(8,128)(2,1)S(1)}, u32[]{:S(2)}, u32[]{:S(2)}) collective-permute-start(bf16[256,256]{1,0:T(8,128)(2,1)S(1)} %get-tuple-element.31.own), channel_id=1, source_target_pairs={{0,1},{1,0},{2,3},{3,2},{4,5},{5,4},{6,7},{7,6},{8,9},{9,8},{10,11... | collective-permute-start | bytes 393224 | tf_op jit(solution)/shard_map/ppermute | solution.py:295
  12.6 2.2 %collective-permute-start.2 = (bf16[256,256]{1,0:T(8,128)(2,1)S(1)}, bf16[256,256]{1,0:T(8,128)(2,1)S(1)}, u32[]{:S(2)}, u32[]{:S(2)}) collective-permute-start(bf16[256,256]{1,0:T(8,128)(2,1)S(1)} %collective-permute-done.across), channel_id=1, source_target_pairs={{0,1},{1,0},{2,3},{3,2},{4,5},{5,4},{6,7},{7,6},{8,9},{9,8},{10,11... | collective-permute-start | bytes 393224 | tf_op jit(solution)/shard_map/ppermute | solution.py:295
  14.8 1.0 %shard_map.93.early = f32[2048,256]{1,0:T(8,128)S(1)} custom-call(bf16[2048,1024]{1,0:T(8,128)(2,1)S(1)} %shard_map.92.matrix, bf16[256,256]{1,0:T(8,128)(2,1)S(1)} %get-tuple-element.23.own, bf16[256,256]{1,0:T(8,128)(2,1)S(1)} %collective-permute-done.1.beside, bf16[256,256]{1,0:T(8,128)(2,1)S(1)} %collective-permute-done.across), custom_call_target="tpu_custom_call" | custom-call | flops 10737418240 | bytes 1 | tf_op jit(solution)/shard_map/pallas_call | solution.py:173
  15.8 0.7 %collective-permute-done.9.across = bf16[256,256]{1,0:T(8,128)(2,1)S(1)} collective-permute-done((bf16[256,256]{1,0:T(8,128)(2,1)S(1)}, bf16[256,256]{1,0:T(8,128)(2,1)S(1)}, u32[]{:S(2)}, u32[]{:S(2)}) %collective-permute-start.9) | collective-permute-done | bytes 131104 | tf_op jit(solution)/shard_map/ppermute | solution.py:295
  16.5 2.1 %collective-permute-start.10 = (bf16[256,256]{1,0:T(8,128)(2,1)S(1)}, bf16[256,256]{1,0:T(8,128)(2,1)S(1)}, u32[]{:S(2)}, u32[]{:S(2)}) collective-permute-start(bf16[256,256]{1,0:T(8,128)(2,1)S(1)} %collective-permute-done.9.across), channel_id=1, source_target_pairs={{0,1},{1,0},{2,3},{3,2},{4,5},{5,4},{6,7},{7,6},{8,9},{9,8},{10,11... | collective-permute-start | bytes 393224 | tf_op jit(solution)/shard_map/ppermute | solution.py:295
  18.6 3.5 %collective-permute-done.2.passed = bf16[256,256]{1,0:T(8,128)(2,1)S(1)} collective-permute-done((bf16[256,256]{1,0:T(8,128)(2,1)S(1)}, bf16[256,256]{1,0:T(8,128)(2,1)S(1)}, u32[]{:S(2)}, u32[]{:S(2)}) %collective-permute-start.2) | collective-permute-done | bytes 131104 | tf_op jit(solution)/shard_map/ppermute | solution.py:295
  22.1 0.2 shard_map.95
  22.4 0.2 shard_map.96
  22.6 0.6 %collective-permute-start.4 = (bf16[512,256]{1,0:T(8,128)(2,1)S(1)}, bf16[512,256]{1,0:T(8,128)(2,1)S(1)}, u32[]{:S(2)}, u32[]{:S(2)}) collective-permute-start(bf16[512,256]{1,0:T(8,128)(2,1)S(1)} %shard_map.96), channel_id=1, source_target_pairs={{0,4},{4,0},{8,12},{12,8},{16,20},{20,16},{24,28},{28,24},{1,5},{5... | collective-permute-start | bytes 786440 | tf_op jit(solution)/shard_map/ppermute | solution.py:295
  23.2 0.3 shard_map.94.stay
  23.5 1.0 %shard_map.98.early = f32[2048,256]{1,0:T(8,128)S(1)} custom-call(bf16[2048,1024]{1,0:T(8,128)(2,1)S(1)} %shard_map.92.matrix, bf16[256,256]{1,0:T(8,128)(2,1)S(1)} %get-tuple-element.31.own, bf16[256,256]{1,0:T(8,128)(2,1)S(1)} %collective-permute-done.8.beside, bf16[256,256]{1,0:T(8,128)(2,1)S(1)} %collective-permute-done.9.across), custom_call_target="tpu_custom_call" | custom-call | flops 10737418240 | bytes 1 | tf_op jit(solution)/shard_map/pallas_call | solution.py:173
  24.6 2.0 %collective-permute-start.5 = (bf16[256,256]{1,0:T(8,128)(2,1)S(1)}, bf16[256,256]{1,0:T(8,128)(2,1)S(1)}, u32[]{:S(2)}, u32[]{:S(2)}) collective-permute-start(bf16[256,256]{1,0:T(8,128)(2,1)S(1)} %get-tuple-element.27), channel_id=1, source_target_pairs={{0,8},{4,20},{8,0},{12,28},{16,24},{20,4},{24,16},{28,12},{1,9},{5... | collective-permute-start | bytes 393224 | tf_op jit(solution)/shard_map/ppermute | solution.py:302
  26.6 1.1 %collective-permute-start.6 = (bf16[256,256]{1,0:T(8,128)(2,1)S(1)}, bf16[256,256]{1,0:T(8,128)(2,1)S(1)}, u32[]{:S(2)}, u32[]{:S(2)}) collective-permute-start(bf16[256,256]{1,0:T(8,128)(2,1)S(1)} %get-tuple-element.28), channel_id=1, source_target_pairs={{0,16},{4,12},{8,24},{12,4},{16,0},{20,28},{24,8},{28,20},{1,17},{... | collective-permute-start | bytes 393224 | tf_op jit(solution)/shard_map/ppermute | solution.py:302
  27.7 0.5 %collective-permute-start.7 = (bf16[256,256]{1,0:T(8,128)(2,1)S(1)}, bf16[256,256]{1,0:T(8,128)(2,1)S(1)}, u32[]{:S(2)}, u32[]{:S(2)}) collective-permute-start(bf16[256,256]{1,0:T(8,128)(2,1)S(1)} %get-tuple-element.29), channel_id=1, source_target_pairs={{0,24},{4,28},{8,16},{12,20},{16,8},{20,12},{24,0},{28,4},{1,25},{... | collective-permute-start | bytes 393224 | tf_op jit(solution)/shard_map/ppermute | solution.py:302
  28.2 0.2 shard_map.101
  28.4 0.2 shard_map.100
  28.7 0.5 %collective-permute-start.12 = (bf16[512,256]{1,0:T(8,128)(2,1)S(1)}, bf16[512,256]{1,0:T(8,128)(2,1)S(1)}, u32[]{:S(2)}, u32[]{:S(2)}) collective-permute-start(bf16[512,256]{1,0:T(8,128)(2,1)S(1)} %shard_map.101), channel_id=1, source_target_pairs={{0,4},{4,0},{8,12},{12,8},{16,20},{20,16},{24,28},{28,24},{1,5},{5... | collective-permute-start | bytes 786440 | tf_op jit(solution)/shard_map/ppermute | solution.py:295
  29.2 0.3 shard_map.99.stay
  29.5 0.7 %collective-permute-done.11.refs_0_ = bf16[512,256]{1,0:T(8,128)(2,1)S(1)} collective-permute-done((bf16[512,256]{1,0:T(8,128)(2,1)S(1)}, bf16[512,256]{1,0:T(8,128)(2,1)S(1)}, u32[]{:S(2)}, u32[]{:S(2)}) %collective-permute-start.11) | collective-permute-done | bytes 262176 | tf_op jit(solution)/shard_map/ppermute | solution.py:295
  30.2 0.4 collective-permute-done.12.refs_1_
  30.7 2.0 %collective-permute-start.13 = (bf16[256,256]{1,0:T(8,128)(2,1)S(1)}, bf16[256,256]{1,0:T(8,128)(2,1)S(1)}, u32[]{:S(2)}, u32[]{:S(2)}) collective-permute-start(bf16[256,256]{1,0:T(8,128)(2,1)S(1)} %get-tuple-element.36), channel_id=1, source_target_pairs={{0,8},{4,20},{8,0},{12,28},{16,24},{20,4},{24,16},{28,12},{1,9},{5... | collective-permute-start | bytes 393224 | tf_op jit(solution)/shard_map/ppermute | solution.py:302
  32.7 1.1 %collective-permute-start.14 = (bf16[256,256]{1,0:T(8,128)(2,1)S(1)}, bf16[256,256]{1,0:T(8,128)(2,1)S(1)}, u32[]{:S(2)}, u32[]{:S(2)}) collective-permute-start(bf16[256,256]{1,0:T(8,128)(2,1)S(1)} %get-tuple-element.37), channel_id=1, source_target_pairs={{0,16},{4,12},{8,24},{12,4},{16,0},{20,28},{24,8},{28,20},{1,17},{... | collective-permute-start | bytes 393224 | tf_op jit(solution)/shard_map/ppermute | solution.py:302
  33.8 0.5 %collective-permute-start.15 = (bf16[256,256]{1,0:T(8,128)(2,1)S(1)}, bf16[256,256]{1,0:T(8,128)(2,1)S(1)}, u32[]{:S(2)}, u32[]{:S(2)}) collective-permute-start(bf16[256,256]{1,0:T(8,128)(2,1)S(1)} %get-tuple-element.38), channel_id=1, source_target_pairs={{0,24},{4,28},{8,16},{12,20},{16,8},{20,12},{24,0},{28,4},{1,25},{... | collective-permute-start | bytes 393224 | tf_op jit(solution)/shard_map/ppermute | solution.py:302
  34.3 0.3 collective-permute-done.7.refs_3_
  34.6 2.3 %collective-permute-done.13.refs_5_ = bf16[256,256]{1,0:T(8,128)(2,1)S(1)} collective-permute-done((bf16[256,256]{1,0:T(8,128)(2,1)S(1)}, bf16[256,256]{1,0:T(8,128)(2,1)S(1)}, u32[]{:S(2)}, u32[]{:S(2)}) %collective-permute-start.13) | collective-permute-done | bytes 131104 | tf_op jit(solution)/shard_map/ppermute | solution.py:302
  36.8 1.2 %collective-permute-done.14.refs_6_ = bf16[256,256]{1,0:T(8,128)(2,1)S(1)} collective-permute-done((bf16[256,256]{1,0:T(8,128)(2,1)S(1)}, bf16[256,256]{1,0:T(8,128)(2,1)S(1)}, u32[]{:S(2)}, u32[]{:S(2)}) %collective-permute-start.14) | collective-permute-done | bytes 131104 | tf_op jit(solution)/shard_map/ppermute | solution.py:302
  38.0 2.5 %collective-permute-done.15.refs_7_ = bf16[256,256]{1,0:T(8,128)(2,1)S(1)} collective-permute-done((bf16[256,256]{1,0:T(8,128)(2,1)S(1)}, bf16[256,256]{1,0:T(8,128)(2,1)S(1)}, u32[]{:S(2)}, u32[]{:S(2)}) %collective-permute-start.15) | collective-permute-done | bytes 131104 | tf_op jit(solution)/shard_map/ppermute | solution.py:302
  40.5 0.9 %shard_map.103 = bf16[256,512]{1,0:T(8,128)(2,1)} custom-call(f32[256,512]{1,0:T(8,128)S(1)} %get-tuple-element.22.projected, f32[2,128]{1,0:T(2,128)S(1)} %bitcast.4, f32[256,256]{1,0:T(8,128)S(1)} %get-tuple-element.26.refs_0_, bf16[256,256]{1,0:T(8,128)(2,1)S(1)} %collective-permute-done.5.refs_1_, bf16[256,256]{1,0:T(8,128)(2,1)S(1)} %collective-permute-done.6.refs_2_, ...), custom_call_target="tpu_custom_call" | custom-call | flops 786432 | bytes 2097152 | tf_op jit(solution)/shard_map/pallas_call | solution.py:249
  (15 shorter events, 0.4 us)
Async XLA Ops:
  1.8 10.7 %collective-permute-start = (bf16[256,256]{1,0:T(8,128)(2,1)S(1)}, bf16[256,256]{1,0:T(8,128)(2,1)S(1)}, u32[]{:S(2)}, u32[]{:S(2)}) collective-permute-start(bf16[256,256]{1,0:T(8,128)(2,1)S(1)} %get-tuple-element.23.own), channel_id=1, source_target_pairs={{0,3},{1,2},{2,1},{3,0},{4,7},{5,6},{6,5},{7,4},{8,11},{9,10},{10,... | collective-permute-start | bytes 393224 | tf_op jit(solution)/shard_map/ppermute | solution.py:295
  6.9 7.8 %collective-permute-start.1 = (bf16[256,256]{1,0:T(8,128)(2,1)S(1)}, bf16[256,256]{1,0:T(8,128)(2,1)S(1)}, u32[]{:S(2)}, u32[]{:S(2)}) collective-permute-start(bf16[256,256]{1,0:T(8,128)(2,1)S(1)} %get-tuple-element.23.own), channel_id=1, source_target_pairs={{0,1},{1,0},{2,3},{3,2},{4,5},{5,4},{6,7},{7,6},{8,9},{9,8},{10,11... | collective-permute-start | bytes 393224 | tf_op jit(solution)/shard_map/ppermute | solution.py:295
  6.9 9.5 %collective-permute-start.9 = (bf16[256,256]{1,0:T(8,128)(2,1)S(1)}, bf16[256,256]{1,0:T(8,128)(2,1)S(1)}, u32[]{:S(2)}, u32[]{:S(2)}) collective-permute-start(bf16[256,256]{1,0:T(8,128)(2,1)S(1)} %get-tuple-element.31.own), channel_id=1, source_target_pairs={{0,3},{1,2},{2,1},{3,0},{4,7},{5,6},{6,5},{7,4},{8,11},{9,10},{10,... | collective-permute-start | bytes 393224 | tf_op jit(solution)/shard_map/ppermute | solution.py:295
  11.4 11.7 %collective-permute-start.8 = (bf16[256,256]{1,0:T(8,128)(2,1)S(1)}, bf16[256,256]{1,0:T(8,128)(2,1)S(1)}, u32[]{:S(2)}, u32[]{:S(2)}) collective-permute-start(bf16[256,256]{1,0:T(8,128)(2,1)S(1)} %get-tuple-element.31.own), channel_id=1, source_target_pairs={{0,1},{1,0},{2,3},{3,2},{4,5},{5,4},{6,7},{7,6},{8,9},{9,8},{10,11... | collective-permute-start | bytes 393224 | tf_op jit(solution)/shard_map/ppermute | solution.py:295
  12.6 9.5 %collective-permute-start.2 = (bf16[256,256]{1,0:T(8,128)(2,1)S(1)}, bf16[256,256]{1,0:T(8,128)(2,1)S(1)}, u32[]{:S(2)}, u32[]{:S(2)}) collective-permute-start(bf16[256,256]{1,0:T(8,128)(2,1)S(1)} %collective-permute-done.across), channel_id=1, source_target_pairs={{0,1},{1,0},{2,3},{3,2},{4,5},{5,4},{6,7},{7,6},{8,9},{9,8},{10,11... | collective-permute-start | bytes 393224 | tf_op jit(solution)/shard_map/ppermute | solution.py:295
  16.5 11.7 %collective-permute-start.10 = (bf16[256,256]{1,0:T(8,128)(2,1)S(1)}, bf16[256,256]{1,0:T(8,128)(2,1)S(1)}, u32[]{:S(2)}, u32[]{:S(2)}) collective-permute-start(bf16[256,256]{1,0:T(8,128)(2,1)S(1)} %collective-permute-done.9.across), channel_id=1, source_target_pairs={{0,1},{1,0},{2,3},{3,2},{4,5},{5,4},{6,7},{7,6},{8,9},{9,8},{10,11... | collective-permute-start | bytes 393224 | tf_op jit(solution)/shard_map/ppermute | solution.py:295
  22.3 2.2 %collective-permute-start.3 = (bf16[512,256]{1,0:T(8,128)(2,1)S(1)}, bf16[512,256]{1,0:T(8,128)(2,1)S(1)}, u32[]{:S(2)}, u32[]{:S(2)}) collective-permute-start(bf16[512,256]{1,0:T(8,128)(2,1)S(1)} %shard_map.95), channel_id=1, source_target_pairs={{0,4},{4,0},{8,12},{12,8},{16,20},{20,16},{24,28},{28,24},{1,5},{5... | collective-permute-start | bytes 786440 | tf_op jit(solution)/shard_map/ppermute | solution.py:295
  22.6 1.9 %collective-permute-start.4 = (bf16[512,256]{1,0:T(8,128)(2,1)S(1)}, bf16[512,256]{1,0:T(8,128)(2,1)S(1)}, u32[]{:S(2)}, u32[]{:S(2)}) collective-permute-start(bf16[512,256]{1,0:T(8,128)(2,1)S(1)} %shard_map.96), channel_id=1, source_target_pairs={{0,4},{4,0},{8,12},{12,8},{16,20},{20,16},{24,28},{28,24},{1,5},{5... | collective-permute-start | bytes 786440 | tf_op jit(solution)/shard_map/ppermute | solution.py:295
  24.6 9.2 %collective-permute-start.5 = (bf16[256,256]{1,0:T(8,128)(2,1)S(1)}, bf16[256,256]{1,0:T(8,128)(2,1)S(1)}, u32[]{:S(2)}, u32[]{:S(2)}) collective-permute-start(bf16[256,256]{1,0:T(8,128)(2,1)S(1)} %get-tuple-element.27), channel_id=1, source_target_pairs={{0,8},{4,20},{8,0},{12,28},{16,24},{20,4},{24,16},{28,12},{1,9},{5... | collective-permute-start | bytes 393224 | tf_op jit(solution)/shard_map/ppermute | solution.py:302
  26.6 7.7 %collective-permute-start.6 = (bf16[256,256]{1,0:T(8,128)(2,1)S(1)}, bf16[256,256]{1,0:T(8,128)(2,1)S(1)}, u32[]{:S(2)}, u32[]{:S(2)}) collective-permute-start(bf16[256,256]{1,0:T(8,128)(2,1)S(1)} %get-tuple-element.28), channel_id=1, source_target_pairs={{0,16},{4,12},{8,24},{12,4},{16,0},{20,28},{24,8},{28,20},{1,17},{... | collective-permute-start | bytes 393224 | tf_op jit(solution)/shard_map/ppermute | solution.py:302
  27.7 6.9 %collective-permute-start.7 = (bf16[256,256]{1,0:T(8,128)(2,1)S(1)}, bf16[256,256]{1,0:T(8,128)(2,1)S(1)}, u32[]{:S(2)}, u32[]{:S(2)}) collective-permute-start(bf16[256,256]{1,0:T(8,128)(2,1)S(1)} %get-tuple-element.29), channel_id=1, source_target_pairs={{0,24},{4,28},{8,16},{12,20},{16,8},{20,12},{24,0},{28,4},{1,25},{... | collective-permute-start | bytes 393224 | tf_op jit(solution)/shard_map/ppermute | solution.py:302
  28.6 11.9 %copy-start = (f32[256]{0:T(256)S(1)}, f32[256]{0:T(256)}, u32[]{:S(2)}) copy-start(f32[256]{0:T(256)} %param.12) | copy-start | bytes 3076
  28.6 1.6 %collective-permute-start.11 = (bf16[512,256]{1,0:T(8,128)(2,1)S(1)}, bf16[512,256]{1,0:T(8,128)(2,1)S(1)}, u32[]{:S(2)}, u32[]{:S(2)}) collective-permute-start(bf16[512,256]{1,0:T(8,128)(2,1)S(1)} %shard_map.100), channel_id=1, source_target_pairs={{0,4},{4,0},{8,12},{12,8},{16,20},{20,16},{24,28},{28,24},{1,5},{5... | collective-permute-start | bytes 786440 | tf_op jit(solution)/shard_map/ppermute | solution.py:295
  28.7 1.9 %collective-permute-start.12 = (bf16[512,256]{1,0:T(8,128)(2,1)S(1)}, bf16[512,256]{1,0:T(8,128)(2,1)S(1)}, u32[]{:S(2)}, u32[]{:S(2)}) collective-permute-start(bf16[512,256]{1,0:T(8,128)(2,1)S(1)} %shard_map.101), channel_id=1, source_target_pairs={{0,4},{4,0},{8,12},{12,8},{16,20},{20,16},{24,28},{28,24},{1,5},{5... | collective-permute-start | bytes 786440 | tf_op jit(solution)/shard_map/ppermute | solution.py:295
  30.7 6.1 %collective-permute-start.13 = (bf16[256,256]{1,0:T(8,128)(2,1)S(1)}, bf16[256,256]{1,0:T(8,128)(2,1)S(1)}, u32[]{:S(2)}, u32[]{:S(2)}) collective-permute-start(bf16[256,256]{1,0:T(8,128)(2,1)S(1)} %get-tuple-element.36), channel_id=1, source_target_pairs={{0,8},{4,20},{8,0},{12,28},{16,24},{20,4},{24,16},{28,12},{1,9},{5... | collective-permute-start | bytes 393224 | tf_op jit(solution)/shard_map/ppermute | solution.py:302
  32.7 5.3 %collective-permute-start.14 = (bf16[256,256]{1,0:T(8,128)(2,1)S(1)}, bf16[256,256]{1,0:T(8,128)(2,1)S(1)}, u32[]{:S(2)}, u32[]{:S(2)}) collective-permute-start(bf16[256,256]{1,0:T(8,128)(2,1)S(1)} %get-tuple-element.37), channel_id=1, source_target_pairs={{0,16},{4,12},{8,24},{12,4},{16,0},{20,28},{24,8},{28,20},{1,17},{... | collective-permute-start | bytes 393224 | tf_op jit(solution)/shard_map/ppermute | solution.py:302
  33.8 6.7 %collective-permute-start.15 = (bf16[256,256]{1,0:T(8,128)(2,1)S(1)}, bf16[256,256]{1,0:T(8,128)(2,1)S(1)}, u32[]{:S(2)}, u32[]{:S(2)}) collective-permute-start(bf16[256,256]{1,0:T(8,128)(2,1)S(1)} %get-tuple-element.38), channel_id=1, source_target_pairs={{0,24},{4,28},{8,16},{12,20},{16,8},{20,12},{24,0},{28,4},{1,25},{... | collective-permute-start | bytes 393224 | tf_op jit(solution)/shard_map/ppermute | solution.py:302

commit v9 on v7

--- a/solution.py
+++ b/solution.py
@@ -82,7 +82,7 @@
 
 def merge_kernel(
     own_tiles, per_owner, row, column, count, sources_hbm, targets_hbm, labels_hbm, tiles_hbm, out,
-    total, tiles, sources, targets, labels, sems, tile_sems,
+    total, tiles, sources, targets, labels, bases, seen, sems, tile_sems,
 ):
     small = [
         pltpu.make_async_copy(source, target, sems.at[k])
@@ -102,34 +102,44 @@
     ]
     for copy in small + large:
         copy.start()
-    spare, span = total.shape[0] - 1, total.shape[1]
-    total[...] = jnp.zeros_like(total)
-    my_row, my_column, used = row[0], column[0], count[0]
+    rows = total.shape[1]
+    places, span = out.shape[0] // rows, out.shape[1] // rows
+    spare = places * span
+    for cell in range(spare + 1):
+        seen[cell] = 0
+    my_core, used = row[0] % 2, count[0]
+    toggle = column[0] * own_tiles
     for copy in small:
         copy.wait()
 
+    for slot in range(bases.shape[0]):
+        owner, label = slot // per_owner, labels[0, slot]
+        core, apart = owner % 2, lax.bitwise_xor(row[0], owner)
+        x, y = lax.bitwise_and(apart, 2), lax.bitwise_and(lax.shift_right_logical(apart, 1), 2)
+        first, second = (x, y) if core == 0 else (y, x)
+        position = jnp.where(my_core == core, 4, 0) + second + lax.shift_right_logical(first, 1)
+        base = (position * own_tiles + label) * span
+        bases[slot] = jnp.where(label < own_tiles, base, spare)
+
     def add(slot):
-        target, source = targets[0, slot], sources[0, slot]
-        label = labels[0, target]
-        owner = target // per_owner
-        core, apart = owner % 2, lax.bitwise_xor(owner, my_row)
-        x, y = apart // 2 % 2, apart // 4
-        first, second = jnp.where(core == 0, x, y), jnp.where(core == 0, y, x)
-        position = jnp.where(core == my_row % 2, 4, 0) + second * 2 + first
-        place = jnp.where(label < own_tiles, position * own_tiles + label, spare)
-        block = lax.bitwise_xor(source // own_tiles, my_column)
-        total[place, block * own_tiles + source % own_tiles] += tiles[slot].astype(jnp.float32)
+        base = bases[targets[0, slot]]
+        here = base + lax.bitwise_xor(sources[0, slot], toggle)
+        cell = jnp.where((base < spare) & (slot < used), here, spare)
+        before = jnp.where(seen[cell] > 0, total[cell], 0.0)
+        seen[cell] = 1
+        total[cell] = before + tiles[slot].astype(jnp.float32)
 
     for k, copy in enumerate(large):
         copy.wait()
-        pl.loop(k * each, jnp.minimum(used, (k + 1) * each))(add)
-
-    rows = total.shape[2]
-    for source in range(span):
-        for place in range(spare):
-            out[place * rows : (place + 1) * rows, source * rows : (source + 1) * rows] = total[
-                place, source
-            ].astype(out.dtype)
+        pl.loop(k * each, (k + 1) * each, unroll=4)(add)
+
+    for place in range(places):
+        for source in range(span):
+            cell = place * span + source
+            value = jnp.where(seen[cell] > 0, total[cell], 0.0)
+            out[place * rows : (place + 1) * rows, source * rows : (source + 1) * rows] = (
+                value.astype(out.dtype)
+            )
 
 
 def merge_tiles(own_tiles, owners, span, index_args, tile_weights):
@@ -144,11 +154,13 @@
         in_specs=[SMEM] * 3 + [HBM] * 4,
         out_specs=VMEM,
         scratch_shapes=[
-            pltpu.VMEM((places + 1, span, rows, rows), jnp.float32),
+            pltpu.VMEM((places * span + 1, rows, rows), jnp.float32),
             pltpu.VMEM(tile_weights.shape[1:], tile_weights.dtype),
             pltpu.SMEM(sources.shape, jnp.int32),
             pltpu.SMEM(targets.shape, jnp.int32),
             pltpu.SMEM(labels.shape, jnp.int32),
+            pltpu.SMEM((labels.shape[1],), jnp.int32),
+            pltpu.SMEM((places * span + 1,), jnp.int32),
             pltpu.SemaphoreType.DMA((3,)),
             pltpu.SemaphoreType.DMA((4 if capacity % 4 == 0 else 1,)),
         ],
@@ -303,7 +315,7 @@
     index_args = (tile_source, tile_target, tile_count, mirror_tile)
 
     cells = owners * own_tiles * span * tile_rows * tile_rows
-    if columns != 4 or owners != 8 or cells > DENSE_ELEMENTS:
+    if columns != 4 or owners != 8 or own_tiles & (own_tiles - 1) or cells > DENSE_ELEMENTS:
         projected = jnp.dot(features, weight, preferred_element_type=jnp.float32)
         scaled = (source_norm[:, None] * projected).astype(jnp.bfloat16)
         blocks = lax.all_gather(scaled, "col", axis=0, tiled=True)

time: 39.6 us -> 39.3 us (level)
  Pallas kernels: 10.4 us -> 8.49 us
  starting transfers between devices: 17 us -> 18.4 us
    pallas_call x1, Pallas kernels: 4.64 us -> 2.76 us  [merge_tiles(): pl.pallas_call(functools.partial(merge_kernel, own_tiles, labels.shape[1]...]
    ppermute x8, starting transfers between devices: 9.85 us -> 11.2 us  [swap(): return lax.ppermute(value, axis, pairs)]
  transfers between devices with their start and end apart: 14 -> 14, of which waited for: 6 -> 7; matrix products, arithmetic and copies ran while one was open for 0% -> 0% of each run, Pallas kernels for 19% -> 15%
where the time goes in v9:
time: 39.3 us; the launch traced here: 39.2 us
  starting transfers between devices  18.4 us (47%)
  waiting for transfers between devices  11.6 us (30%)
  Pallas kernels  8.49 us (22%)
  between operations  0.74 us (2%)
    ppermute x8, starting transfers between devices, swap(): return lax.ppermute(value, axis, pairs)  11.2 us
    ppermute x6, starting transfers between devices, exchange(): lax.ppermute(value, 'row', [(i, i ^ step[i % 2]) for i in range(owners)])  7.11 us
    ppermute x6, waiting for transfers between devices, exchange(): lax.ppermute(value, 'row', [(i, i ^ step[i % 2]) for i in range(owners)])  6.07 us
    ppermute x8, waiting for transfers between devices, swap(): return lax.ppermute(value, axis, pairs)  5.51 us
    pallas_call x4, Pallas kernels, product(): pl.pallas_call(functools.partial(product_kernel, half * (total // 2)), ou...  2.84 us
    pallas_call x1, Pallas kernels, merge_tiles(): pl.pallas_call(functools.partial(merge_kernel, own_tiles, labels.shape[1]...  2.76 us
    pallas_call x1, Pallas kernels, project(): pl.pallas_call(project_kernel, out_shape=[jax.ShapeDtypeStruct((rows, hid...  1.82 us
    pallas_call x1, Pallas kernels, finish(): pl.pallas_call(functools.partial(finish_kernel, len(pieces)), out_shape=j...  0.88 us
  transfers between devices with their start and end apart: 14, of which 7 were waited for; matrix products, arithmetic and copies ran while one was open for 0% of the time, Pallas kernels for 15%

profile of v9, /device:TPU:0, one launch (start us, length us, event | category | flops | bytes accessed | tf_op | source)
XLA Modules:
  0.0 39.2 jit_solution(12096225838328442164)
XLA Ops:
  0.0 1.8 %shard_map.91 = (f32[256,512]{1,0:T(8,128)S(1)}, bf16[256,256]{1,0:T(8,128)(2,1)S(1)}, bf16[256,256]{1,0:T(8,128)(2,1)S(1)}) custom-call(bf16[256,1024]{1,0:T(8,128)(2,1)} %features_hbm.1, bf16[1024,512]{1,0:T(8,128)(2,1)} %weight_hbm.1, f32[2,128]{1,0:T(2,128)} %bitcast.5), custom_call_target="tpu_custom_call" | custom-call | flops 268435456 | bytes 1572864 | tf_op jit(solution)/shard_map/pallas_call | solution.py:66
  1.8 5.1 %collective-permute-start = (bf16[256,256]{1,0:T(8,128)(2,1)S(1)}, bf16[256,256]{1,0:T(8,128)(2,1)S(1)}, u32[]{:S(2)}, u32[]{:S(2)}) collective-permute-start(bf16[256,256]{1,0:T(8,128)(2,1)S(1)} %get-tuple-element.23.refs_0_), channel_id=1, source_target_pairs={{0,3},{1,2},{2,1},{3,0},{4,7},{5,6},{6,5},{7,4},{8,11},{9,10},{10,... | collective-permute-start | bytes 393224 | tf_op jit(solution)/shard_map/ppermute | solution.py:287
  6.9 0.0 collective-permute-start.1
  6.9 0.9 %collective-permute-start.8 = (bf16[256,256]{1,0:T(8,128)(2,1)S(1)}, bf16[256,256]{1,0:T(8,128)(2,1)S(1)}, u32[]{:S(2)}, u32[]{:S(2)}) collective-permute-start(bf16[256,256]{1,0:T(8,128)(2,1)S(1)} %get-tuple-element.31.refs_0_), channel_id=1, source_target_pairs={{0,3},{1,2},{2,1},{3,0},{4,7},{5,6},{6,5},{7,4},{8,11},{9,10},{10,... | collective-permute-start | bytes 393224 | tf_op jit(solution)/shard_map/ppermute | solution.py:287
  8.5 2.8 %shard_map.92.matrix = bf16[2048,1024]{1,0:T(8,128)(2,1)S(1)} custom-call(s32[1]{0:T(128)} %bitcast.2.row, s32[1]{0:T(128)} %bitcast.3.column, s32[1]{0:T(128)S(6)} %copy.10.count, s32[1,64]{1,0:T(1,128)} %sources_hbm.1, s32[1,64]{1,0:T(1,128)} %targets_hbm.1, s32[1,16]{1,0:T(1,128)} %labels_hbm.1, bf16[1,64,128,128]{3,2,1,0:T(8,128)(2,1)} %tiles_hbm.1), custom_call_target="tpu_custom_call" | custom-call | flops 8388608 | bytes 12582912 | tf_op jit(solution)/shard_map/pallas_call | solution.py:151
  11.3 0.0 collective-permute-done.refs_3_
  11.3 3.4 %collective-permute-start.2 = (bf16[256,256]{1,0:T(8,128)(2,1)S(1)}, bf16[256,256]{1,0:T(8,128)(2,1)S(1)}, u32[]{:S(2)}, u32[]{:S(2)}) collective-permute-start(bf16[256,256]{1,0:T(8,128)(2,1)S(1)} %collective-permute-done.refs_3_), channel_id=1, source_target_pairs={{0,1},{1,0},{2,3},{3,2},{4,5},{5,4},{6,7},{7,6},{8,9},{9,8},{10,11... | collective-permute-start | bytes 393224 | tf_op jit(solution)/shard_map/ppermute | solution.py:287
  14.8 0.0 collective-permute-start.7
  14.8 2.2 %collective-permute-done.8.refs_3_ = bf16[256,256]{1,0:T(8,128)(2,1)S(1)} collective-permute-done((bf16[256,256]{1,0:T(8,128)(2,1)S(1)}, bf16[256,256]{1,0:T(8,128)(2,1)S(1)}, u32[]{:S(2)}, u32[]{:S(2)}) %collective-permute-start.8) | collective-permute-done | bytes 131104 | tf_op jit(solution)/shard_map/ppermute | solution.py:287
  17.0 1.6 %collective-permute-start.9 = (bf16[256,256]{1,0:T(8,128)(2,1)S(1)}, bf16[256,256]{1,0:T(8,128)(2,1)S(1)}, u32[]{:S(2)}, u32[]{:S(2)}) collective-permute-start(bf16[256,256]{1,0:T(8,128)(2,1)S(1)} %collective-permute-done.8.refs_3_), channel_id=1, source_target_pairs={{0,1},{1,0},{2,3},{3,2},{4,5},{5,4},{6,7},{7,6},{8,9},{9,8},{10,11... | collective-permute-start | bytes 393224 | tf_op jit(solution)/shard_map/ppermute | solution.py:287
  18.6 0.9 %collective-permute-done.2.refs_2_ = bf16[256,256]{1,0:T(8,128)(2,1)S(1)} collective-permute-done((bf16[256,256]{1,0:T(8,128)(2,1)S(1)}, bf16[256,256]{1,0:T(8,128)(2,1)S(1)}, u32[]{:S(2)}, u32[]{:S(2)}) %collective-permute-start.2) | collective-permute-done | bytes 131104 | tf_op jit(solution)/shard_map/ppermute | solution.py:287
  19.5 0.7 %shard_map.94 = bf16[1024,256]{1,0:T(8,128)(2,1)S(1)} custom-call(bf16[2048,1024]{1,0:T(8,128)(2,1)S(1)} %shard_map.92.matrix, bf16[256,256]{1,0:T(8,128)(2,1)S(1)} %get-tuple-element.23.refs_0_, bf16[256,256]{1,0:T(8,128)(2,1)S(1)} %collective-permute-done.1.refs_1_, bf16[256,256]{1,0:T(8,128)(2,1)S(1)} %collective-permute-done.2.refs_2_, ...), custom_call_target="tpu_custom_call" | custom-call | flops 10737418240 | bytes 1 | tf_op jit(solution)/shard_map/pallas_call | solution.py:188
  20.2 0.1 collective-permute-start.3
  20.3 0.7 %shard_map.93.stay = f32[1024,256]{1,0:T(8,128)S(1)} custom-call(bf16[2048,1024]{1,0:T(8,128)(2,1)S(1)} %shard_map.92.matrix, bf16[256,256]{1,0:T(8,128)(2,1)S(1)} %get-tuple-element.23.refs_0_, bf16[256,256]{1,0:T(8,128)(2,1)S(1)} %collective-permute-done.1.refs_1_, bf16[256,256]{1,0:T(8,128)(2,1)S(1)} %collective-permute-done.2.refs_2_, ...), custom_call_target="tpu_custom_call" | custom-call | flops 10737418240 | bytes 1 | tf_op jit(solution)/shard_map/pallas_call | solution.py:188
  21.0 1.2 %collective-permute-done.3.came = bf16[1024,256]{1,0:T(8,128)(2,1)S(1)} collective-permute-done((bf16[1024,256]{1,0:T(8,128)(2,1)S(1)}, bf16[1024,256]{1,0:T(8,128)(2,1)S(1)}, u32[]{:S(2)}, u32[]{:S(2)}) %collective-permute-start.3) | collective-permute-done | bytes 524320 | tf_op jit(solution)/shard_map/ppermute | solution.py:287
  22.2 0.1 shard_map.95
  22.3 1.7 %collective-permute-start.4 = (bf16[256,256]{1,0:T(8,128)(2,1)S(1)}, bf16[256,256]{1,0:T(8,128)(2,1)S(1)}, u32[]{:S(2)}, u32[]{:S(2)}) collective-permute-start(bf16[256,256]{1,0:T(8,128)(2,1)S(1)} %get-tuple-element.27), channel_id=1, source_target_pairs={{0,8},{4,20},{8,0},{12,28},{16,24},{20,4},{24,16},{28,12},{1,9},{5... | collective-permute-start | bytes 393224 | tf_op jit(solution)/shard_map/ppermute | solution.py:294
  24.0 1.5 %collective-permute-start.5 = (bf16[256,256]{1,0:T(8,128)(2,1)S(1)}, bf16[256,256]{1,0:T(8,128)(2,1)S(1)}, u32[]{:S(2)}, u32[]{:S(2)}) collective-permute-start(bf16[256,256]{1,0:T(8,128)(2,1)S(1)} %get-tuple-element.28), channel_id=1, source_target_pairs={{0,16},{4,12},{8,24},{12,4},{16,0},{20,28},{24,8},{28,20},{1,17},{... | collective-permute-start | bytes 393224 | tf_op jit(solution)/shard_map/ppermute | solution.py:294
  25.6 0.3 collective-permute-start.6
  25.9 0.7 %shard_map.97 = bf16[1024,256]{1,0:T(8,128)(2,1)S(1)} custom-call(bf16[2048,1024]{1,0:T(8,128)(2,1)S(1)} %shard_map.92.matrix, bf16[256,256]{1,0:T(8,128)(2,1)S(1)} %get-tuple-element.31.refs_0_, bf16[256,256]{1,0:T(8,128)(2,1)S(1)} %collective-permute-done.7.refs_1_, bf16[256,256]{1,0:T(8,128)(2,1)S(1)} %collective-permute-done.9.refs_2_, ...), custom_call_target="tpu_custom_call" | custom-call | bytes 1 | tf_op jit(solution)/shard_map/pallas_call | solution.py:188
  26.6 0.0 copy-start
  26.6 0.1 collective-permute-start.10
  26.7 0.7 %shard_map.96.stay = f32[1024,256]{1,0:T(8,128)S(1)} custom-call(bf16[2048,1024]{1,0:T(8,128)(2,1)S(1)} %shard_map.92.matrix, bf16[256,256]{1,0:T(8,128)(2,1)S(1)} %get-tuple-element.31.refs_0_, bf16[256,256]{1,0:T(8,128)(2,1)S(1)} %collective-permute-done.7.refs_1_, bf16[256,256]{1,0:T(8,128)(2,1)S(1)} %collective-permute-done.9.refs_2_, ...), custom_call_target="tpu_custom_call" | custom-call | flops 10737418240 | bytes 1 | tf_op jit(solution)/shard_map/pallas_call | solution.py:188
  27.4 1.2 %collective-permute-done.10.came = bf16[1024,256]{1,0:T(8,128)(2,1)S(1)} collective-permute-done((bf16[1024,256]{1,0:T(8,128)(2,1)S(1)}, bf16[1024,256]{1,0:T(8,128)(2,1)S(1)}, u32[]{:S(2)}, u32[]{:S(2)}) %collective-permute-start.10) | collective-permute-done | bytes 524320 | tf_op jit(solution)/shard_map/ppermute | solution.py:287
  28.6 0.1 shard_map.98
  28.7 1.7 %collective-permute-start.11 = (bf16[256,256]{1,0:T(8,128)(2,1)S(1)}, bf16[256,256]{1,0:T(8,128)(2,1)S(1)}, u32[]{:S(2)}, u32[]{:S(2)}) collective-permute-start(bf16[256,256]{1,0:T(8,128)(2,1)S(1)} %get-tuple-element.36), channel_id=1, source_target_pairs={{0,8},{4,20},{8,0},{12,28},{16,24},{20,4},{24,16},{28,12},{1,9},{5... | collective-permute-start | bytes 393224 | tf_op jit(solution)/shard_map/ppermute | solution.py:294
  30.4 1.5 %collective-permute-start.12 = (bf16[256,256]{1,0:T(8,128)(2,1)S(1)}, bf16[256,256]{1,0:T(8,128)(2,1)S(1)}, u32[]{:S(2)}, u32[]{:S(2)}) collective-permute-start(bf16[256,256]{1,0:T(8,128)(2,1)S(1)} %get-tuple-element.37), channel_id=1, source_target_pairs={{0,16},{4,12},{8,24},{12,4},{16,0},{20,28},{24,8},{28,20},{1,17},{... | collective-permute-start | bytes 393224 | tf_op jit(solution)/shard_map/ppermute | solution.py:294
  31.9 0.3 collective-permute-start.13
  32.2 2.3 %collective-permute-done.11.refs_5_ = bf16[256,256]{1,0:T(8,128)(2,1)S(1)} collective-permute-done((bf16[256,256]{1,0:T(8,128)(2,1)S(1)}, bf16[256,256]{1,0:T(8,128)(2,1)S(1)}, u32[]{:S(2)}, u32[]{:S(2)}) %collective-permute-start.11) | collective-permute-done | bytes 131104 | tf_op jit(solution)/shard_map/ppermute | solution.py:294
  34.6 2.7 %collective-permute-done.12.refs_6_ = bf16[256,256]{1,0:T(8,128)(2,1)S(1)} collective-permute-done((bf16[256,256]{1,0:T(8,128)(2,1)S(1)}, bf16[256,256]{1,0:T(8,128)(2,1)S(1)}, u32[]{:S(2)}, u32[]{:S(2)}) %collective-permute-start.12) | collective-permute-done | bytes 131104 | tf_op jit(solution)/shard_map/ppermute | solution.py:294
  37.3 1.0 %collective-permute-done.13.refs_7_ = bf16[256,256]{1,0:T(8,128)(2,1)S(1)} collective-permute-done((bf16[256,256]{1,0:T(8,128)(2,1)S(1)}, bf16[256,256]{1,0:T(8,128)(2,1)S(1)}, u32[]{:S(2)}, u32[]{:S(2)}) %collective-permute-start.13) | collective-permute-done | bytes 131104 | tf_op jit(solution)/shard_map/ppermute | solution.py:294
  38.3 0.9 %shard_map.99 = bf16[256,512]{1,0:T(8,128)(2,1)} custom-call(f32[256,512]{1,0:T(8,128)S(1)} %get-tuple-element.22.projected, f32[2,128]{1,0:T(2,128)S(1)} %bitcast.4, f32[256,256]{1,0:T(8,128)S(1)} %get-tuple-element.26.refs_0_, bf16[256,256]{1,0:T(8,128)(2,1)S(1)} %collective-permute-done.4.refs_1_, bf16[256,256]{1,0:T(8,128)(2,1)S(1)} %collective-permute-done.5.refs_2_, ...), custom_call_target="tpu_custom_call" | custom-call | flops 786432 | bytes 2097152 | tf_op jit(solution)/shard_map/pallas_call | solution.py:241
  (7 shorter events, 0.0 us)
Async XLA Ops:
  1.8 9.5 %collective-permute-start = (bf16[256,256]{1,0:T(8,128)(2,1)S(1)}, bf16[256,256]{1,0:T(8,128)(2,1)S(1)}, u32[]{:S(2)}, u32[]{:S(2)}) collective-permute-start(bf16[256,256]{1,0:T(8,128)(2,1)S(1)} %get-tuple-element.23.refs_0_), channel_id=1, source_target_pairs={{0,3},{1,2},{2,1},{3,0},{4,7},{5,6},{6,5},{7,4},{8,11},{9,10},{10,... | collective-permute-start | bytes 393224 | tf_op jit(solution)/shard_map/ppermute | solution.py:287
  6.9 11.6 %collective-permute-start.1 = (bf16[256,256]{1,0:T(8,128)(2,1)S(1)}, bf16[256,256]{1,0:T(8,128)(2,1)S(1)}, u32[]{:S(2)}, u32[]{:S(2)}) collective-permute-start(bf16[256,256]{1,0:T(8,128)(2,1)S(1)} %get-tuple-element.23.refs_0_), channel_id=1, source_target_pairs={{0,1},{1,0},{2,3},{3,2},{4,5},{5,4},{6,7},{7,6},{8,9},{9,8},{10,11... | collective-permute-start | bytes 393224 | tf_op jit(solution)/shard_map/ppermute | solution.py:287
  6.9 10.0 %collective-permute-start.8 = (bf16[256,256]{1,0:T(8,128)(2,1)S(1)}, bf16[256,256]{1,0:T(8,128)(2,1)S(1)}, u32[]{:S(2)}, u32[]{:S(2)}) collective-permute-start(bf16[256,256]{1,0:T(8,128)(2,1)S(1)} %get-tuple-element.31.refs_0_), channel_id=1, source_target_pairs={{0,3},{1,2},{2,1},{3,0},{4,7},{5,6},{6,5},{7,4},{8,11},{9,10},{10,... | collective-permute-start | bytes 393224 | tf_op jit(solution)/shard_map/ppermute | solution.py:287
  11.3 8.2 %collective-permute-start.2 = (bf16[256,256]{1,0:T(8,128)(2,1)S(1)}, bf16[256,256]{1,0:T(8,128)(2,1)S(1)}, u32[]{:S(2)}, u32[]{:S(2)}) collective-permute-start(bf16[256,256]{1,0:T(8,128)(2,1)S(1)} %collective-permute-done.refs_3_), channel_id=1, source_target_pairs={{0,1},{1,0},{2,3},{3,2},{4,5},{5,4},{6,7},{7,6},{8,9},{9,8},{10,11... | collective-permute-start | bytes 393224 | tf_op jit(solution)/shard_map/ppermute | solution.py:287
  14.8 11.1 %collective-permute-start.7 = (bf16[256,256]{1,0:T(8,128)(2,1)S(1)}, bf16[256,256]{1,0:T(8,128)(2,1)S(1)}, u32[]{:S(2)}, u32[]{:S(2)}) collective-permute-start(bf16[256,256]{1,0:T(8,128)(2,1)S(1)} %get-tuple-element.31.refs_0_), channel_id=1, source_target_pairs={{0,1},{1,0},{2,3},{3,2},{4,5},{5,4},{6,7},{7,6},{8,9},{9,8},{10,11... | collective-permute-start | bytes 393224 | tf_op jit(solution)/shard_map/ppermute | solution.py:287
  17.0 8.9 %collective-permute-start.9 = (bf16[256,256]{1,0:T(8,128)(2,1)S(1)}, bf16[256,256]{1,0:T(8,128)(2,1)S(1)}, u32[]{:S(2)}, u32[]{:S(2)}) collective-permute-start(bf16[256,256]{1,0:T(8,128)(2,1)S(1)} %collective-permute-done.8.refs_3_), channel_id=1, source_target_pairs={{0,1},{1,0},{2,3},{3,2},{4,5},{5,4},{6,7},{7,6},{8,9},{9,8},{10,11... | collective-permute-start | bytes 393224 | tf_op jit(solution)/shard_map/ppermute | solution.py:287
  20.2 2.0 %collective-permute-start.3 = (bf16[1024,256]{1,0:T(8,128)(2,1)S(1)}, bf16[1024,256]{1,0:T(8,128)(2,1)S(1)}, u32[]{:S(2)}, u32[]{:S(2)}) collective-permute-start(bf16[1024,256]{1,0:T(8,128)(2,1)S(1)} %shard_map.94), channel_id=1, source_target_pairs={{0,4},{4,0},{8,12},{12,8},{16,20},{20,16},{24,28},{28,24},{1,5},{5... | collective-permute-start | bytes 1572872 | tf_op jit(solution)/shard_map/ppermute | solution.py:287
  22.3 9.6 %collective-permute-start.4 = (bf16[256,256]{1,0:T(8,128)(2,1)S(1)}, bf16[256,256]{1,0:T(8,128)(2,1)S(1)}, u32[]{:S(2)}, u32[]{:S(2)}) collective-permute-start(bf16[256,256]{1,0:T(8,128)(2,1)S(1)} %get-tuple-element.27), channel_id=1, source_target_pairs={{0,8},{4,20},{8,0},{12,28},{16,24},{20,4},{24,16},{28,12},{1,9},{5... | collective-permute-start | bytes 393224 | tf_op jit(solution)/shard_map/ppermute | solution.py:294
  24.0 8.2 %collective-permute-start.5 = (bf16[256,256]{1,0:T(8,128)(2,1)S(1)}, bf16[256,256]{1,0:T(8,128)(2,1)S(1)}, u32[]{:S(2)}, u32[]{:S(2)}) collective-permute-start(bf16[256,256]{1,0:T(8,128)(2,1)S(1)} %get-tuple-element.28), channel_id=1, source_target_pairs={{0,16},{4,12},{8,24},{12,4},{16,0},{20,28},{24,8},{28,20},{1,17},{... | collective-permute-start | bytes 393224 | tf_op jit(solution)/shard_map/ppermute | solution.py:294
  25.6 6.7 %collective-permute-start.6 = (bf16[256,256]{1,0:T(8,128)(2,1)S(1)}, bf16[256,256]{1,0:T(8,128)(2,1)S(1)}, u32[]{:S(2)}, u32[]{:S(2)}) collective-permute-start(bf16[256,256]{1,0:T(8,128)(2,1)S(1)} %get-tuple-element.29), channel_id=1, source_target_pairs={{0,24},{4,28},{8,16},{12,20},{16,8},{20,12},{24,0},{28,4},{1,25},{... | collective-permute-start | bytes 393224 | tf_op jit(solution)/shard_map/ppermute | solution.py:294
  26.6 11.7 %copy-start = (f32[256]{0:T(256)S(1)}, f32[256]{0:T(256)}, u32[]{:S(2)}) copy-start(f32[256]{0:T(256)} %param.12) | copy-start | bytes 3076
  26.6 2.0 %collective-permute-start.10 = (bf16[1024,256]{1,0:T(8,128)(2,1)S(1)}, bf16[1024,256]{1,0:T(8,128)(2,1)S(1)}, u32[]{:S(2)}, u32[]{:S(2)}) collective-permute-start(bf16[1024,256]{1,0:T(8,128)(2,1)S(1)} %shard_map.97), channel_id=1, source_target_pairs={{0,4},{4,0},{8,12},{12,8},{16,20},{20,16},{24,28},{28,24},{1,5},{5... | collective-permute-start | bytes 1572872 | tf_op jit(solution)/shard_map/ppermute | solution.py:287
  28.7 5.9 %collective-permute-start.11 = (bf16[256,256]{1,0:T(8,128)(2,1)S(1)}, bf16[256,256]{1,0:T(8,128)(2,1)S(1)}, u32[]{:S(2)}, u32[]{:S(2)}) collective-permute-start(bf16[256,256]{1,0:T(8,128)(2,1)S(1)} %get-tuple-element.36), channel_id=1, source_target_pairs={{0,8},{4,20},{8,0},{12,28},{16,24},{20,4},{24,16},{28,12},{1,9},{5... | collective-permute-start | bytes 393224 | tf_op jit(solution)/shard_map/ppermute | solution.py:294
  30.4 6.9 %collective-permute-start.12 = (bf16[256,256]{1,0:T(8,128)(2,1)S(1)}, bf16[256,256]{1,0:T(8,128)(2,1)S(1)}, u32[]{:S(2)}, u32[]{:S(2)}) collective-permute-start(bf16[256,256]{1,0:T(8,128)(2,1)S(1)} %get-tuple-element.37), channel_id=1, source_target_pairs={{0,16},{4,12},{8,24},{12,4},{16,0},{20,28},{24,8},{28,20},{1,17},{... | collective-permute-start | bytes 393224 | tf_op jit(solution)/shard_map/ppermute | solution.py:294
  31.9 6.4 %collective-permute-start.13 = (bf16[256,256]{1,0:T(8,128)(2,1)S(1)}, bf16[256,256]{1,0:T(8,128)(2,1)S(1)}, u32[]{:S(2)}, u32[]{:S(2)}) collective-permute-start(bf16[256,256]{1,0:T(8,128)(2,1)S(1)} %get-tuple-element.38), channel_id=1, source_target_pairs={{0,24},{4,28},{8,16},{12,20},{16,8},{20,12},{24,0},{28,4},{1,25},{... | collective-permute-start | bytes 393224 | tf_op jit(solution)/shard_map/ppermute | solution.py:294

commit v10 on v9

--- a/solution.py
+++ b/solution.py
@@ -9,7 +9,7 @@
 
 DENSE_ELEMENTS = 4 * 1024 * 1024
 CHUNKS = 2
-WEIGHTS = ((20, 20), (0, 20))
+WEIGHTS = (20, 20, 0, 20)
 MIB = 1024 * 1024
 SMEM = pl.BlockSpec(memory_space=pltpu.SMEM)
 VMEM = pl.BlockSpec(memory_space=pltpu.VMEM)
@@ -51,12 +51,11 @@
     for part in range(norm.shape[0]):
         factor = rows_to_lanes(norm[part : part + 1, :], lanes)
         for column in range(0, value.shape[1], lanes):
-            piece = value[part * lanes : (part + 1) * lanes, column : column + lanes]
+            here = slice(part * lanes, (part + 1) * lanes)
+            piece = factor * value[here, column : column + lanes]
             target = scaled[column // width]
             start = column % width
-            target[part * lanes : (part + 1) * lanes, start : start + lanes] = (
-                factor * piece
-            ).astype(target.dtype)
+            target[here, start : start + lanes] = piece.astype(target.dtype)
 
 
 def project(features, weight, source_norm, chunks):
@@ -169,6 +168,51 @@
     )(row, column, count, *in_hbm(sources, targets, labels, tile_weights))
 
 
+def early_kernel(matrix, own, beside, across, out):
+    rows = own.shape[0]
+    value = jnp.dot(matrix[:, :rows], own[...], preferred_element_type=jnp.float32)
+    value += jnp.dot(
+        matrix[:, rows : 2 * rows], beside[...], preferred_element_type=jnp.float32
+    )
+    value += jnp.dot(matrix[:, 3 * rows :], across[...], preferred_element_type=jnp.float32)
+    out[...] = value
+
+
+def early_product(matrix, own, beside, across):
+    total, depth = matrix.shape
+    width = own.shape[1]
+    return pl.pallas_call(
+        early_kernel,
+        out_shape=jax.ShapeDtypeStruct((total, width), jnp.float32),
+        in_specs=[VMEM] * 4,
+        out_specs=VMEM,
+        compiler_params=params(16),
+        cost_estimate=cost(20 * total * depth * width, 1),
+    )(matrix, own, beside, across)
+
+
+def late_kernel(first, matrix, early, passed, out):
+    rows = passed.shape[0]
+    here = slice(first, first + out.shape[0])
+    value = early[here, :] + jnp.dot(
+        matrix[here, 2 * rows : 3 * rows], passed[...], preferred_element_type=jnp.float32
+    )
+    out[...] = value.astype(out.dtype)
+
+
+def late_product(matrix, early, passed, first, count, dtype, weight):
+    total, depth = matrix.shape
+    width = passed.shape[1]
+    return pl.pallas_call(
+        functools.partial(late_kernel, first),
+        out_shape=jax.ShapeDtypeStruct((count, width), dtype),
+        in_specs=[VMEM] * 3,
+        out_specs=VMEM,
+        compiler_params=params(16),
+        cost_estimate=cost(weight * total * depth * width, 1),
+    )(matrix, early, passed)
+
+
 def product_kernel(first, matrix, *refs):
     *blocks, out, gathered = refs
     rows = blocks[0].shape[0]
@@ -182,12 +226,12 @@
     out[...] = value.astype(out.dtype)
 
 
-def product(matrix, blocks, half, dtype, weight):
+def product(matrix, blocks, first, count, dtype, weight):
     rows, width = blocks[0].shape
     total, depth = matrix.shape
     return pl.pallas_call(
-        functools.partial(product_kernel, half * (total // 2)),
-        out_shape=jax.ShapeDtypeStruct((total // 2, width), dtype),
+        functools.partial(product_kernel, first),
+        out_shape=jax.ShapeDtypeStruct((count, width), dtype),
         in_specs=[VMEM] * (1 + len(blocks)),
         out_specs=VMEM,
         scratch_shapes=[pltpu.VMEM((depth, width), blocks[0].dtype)],
@@ -196,26 +240,28 @@
     )(matrix, *blocks)
 
 
-def join_kernel(stay, came, kept, *sent):
-    rows = kept.shape[0]
-    value = stay[...].astype(jnp.float32) + came[...].astype(jnp.float32)
-    kept[...] = value[:rows]
-    for place, out in enumerate(sent):
-        out[...] = value[(place + 1) * rows : (place + 2) * rows].astype(out.dtype)
+def join_kernel(count, stay, *refs):
+    came, (kept, *sent) = refs[:count], refs[count:]
+    rows, part = kept.shape[0], came[0].shape[0]
+    for place, out in enumerate([kept] + sent):
+        start = place * rows
+        other = came[start // part][start % part : start % part + rows, :]
+        value = stay[start : start + rows, :] + other.astype(jnp.float32)
+        out[...] = value.astype(out.dtype)
 
 
 def join(stay, came, rows):
     total, width = stay.shape
     parts = total // rows
     return pl.pallas_call(
-        join_kernel,
+        functools.partial(join_kernel, len(came)),
         out_shape=[jax.ShapeDtypeStruct((rows, width), jnp.float32)]
         + [jax.ShapeDtypeStruct((rows, width), jnp.bfloat16)] * (parts - 1),
-        in_specs=[VMEM] * 2,
+        in_specs=[VMEM] * (1 + len(came)),
         out_specs=[VMEM] * parts,
         compiler_params=params(12),
         cost_estimate=cost(1, 1),
-    )(stay, came)
+    )(stay, *came)
 
 
 def finish_kernel(chunks, projected, norm, *refs):
@@ -326,21 +372,31 @@
         return jnp.maximum(target_norm[:, None] * gathered, 0.0).astype(jnp.bfloat16)
 
     projected, *scaled = project(features, weight, source_norm, CHUNKS)
-    matrix = merge_tiles(own_tiles, owners, span, index_args, tile_weights)
+    built = merge_tiles(own_tiles, owners, span, index_args, tile_weights)
+    half = built.shape[0] // 2
     across = [swap(own, "col", 3) for own in scaled]
     beside = [swap(own, "col", 1) for own in scaled]
-    across[0], matrix = lax.optimization_barrier((across[0], matrix))
-    passed = [swap(value, "col", 1) for value in across]
-    pieces, sent = [], None
-    for blocks, wait in zip(zip(scaled, beside, passed, across), WEIGHTS):
-        if sent is not None:
-            pieces[-1] += exchange(sent)
-            blocks, _ = lax.optimization_barrier((blocks, sent))
-        away = product(matrix, blocks, 0, jnp.bfloat16, wait[0])
-        stay = product(matrix, blocks, 1, jnp.float32, wait[1])
-        kept, *sent = join(stay, swap(away, "row", 1), own_rows)
-        pieces.append([kept])
-    pieces[-1] += exchange(sent)
+    onward, matrix = lax.optimization_barrier((across[0], built))
+    passed = swap(onward, "col", 1)
+    early = early_product(matrix, scaled[0], beside[0], across[0])
+    away = [
+        late_product(matrix, early, passed, k * half // 2, half // 2, jnp.bfloat16, WEIGHTS[0])
+        for k in range(2)
+    ]
+    stay = late_product(matrix, early, passed, half, half, jnp.float32, WEIGHTS[1])
+    kept, *sent = join(stay, [swap(value, "row", 1) for value in away], own_rows)
+    pieces = [[kept] + exchange(sent)]
+
+    onward, _ = lax.optimization_barrier((across[1], early))
+    blocks = scaled[1], beside[1], swap(onward, "col", 1), across[1]
+    blocks, _ = lax.optimization_barrier((blocks, sent))
+    away = [
+        product(matrix, blocks, k * half // 2, half // 2, jnp.bfloat16, WEIGHTS[2])
+        for k in range(2)
+    ]
+    stay = product(matrix, blocks, half, half, jnp.float32, WEIGHTS[3])
+    kept, *sent = join(stay, [swap(value, "row", 1) for value in away], own_rows)
+    pieces.append([kept] + exchange(sent))
     return finish(projected, target_norm, pieces)
 
 

time: 39.3 us -> 41.8 us (1.064)
  waiting for transfers between devices: 11.6 us -> 12.6 us
  starting transfers between devices: 18.4 us -> 19.2 us
  Pallas kernels: 8.49 us -> 8.98 us
    ppermute x8 -> x10, waiting for transfers between devices: 5.51 us -> 6.59 us  [swap(): return lax.ppermute(value, axis, pairs)]
    ppermute x8 -> x10, starting transfers between devices: 11.2 us -> 12.1 us  [swap(): return lax.ppermute(value, axis, pairs)]
    pallas_call x6 -> x9, Pallas kernels: 3.02 us -> 3.51 us  [the longest x3 1.6 us: product(): pl.pallas_call(functools.partial(product_kernel, first), out_shape=jax.Sh...]
  transfers between devices with their start and end apart: 14 -> 16, of which waited for: 7 -> 9; matrix products, arithmetic and copies ran while one was open for 0% -> 0% of each run, Pallas kernels for 15% -> 15%
where the time goes in v10:
time: 41.8 us; the launch traced here: 41.6 us
  starting transfers between devices  19.2 us (46%)
  waiting for transfers between devices  12.6 us (30%)
  Pallas kernels  8.98 us (21%)
  between operations  0.77 us (2%)
    ppermute x10, starting transfers between devices, swap(): return lax.ppermute(value, axis, pairs)  12.1 us
    ppermute x6, starting transfers between devices, exchange(): lax.ppermute(value, 'row', [(i, i ^ step[i % 2]) for i in range(owners)])  7.11 us
    ppermute x10, waiting for transfers between devices, swap(): return lax.ppermute(value, axis, pairs)  6.59 us
    ppermute x6, waiting for transfers between devices, exchange(): lax.ppermute(value, 'row', [(i, i ^ step[i % 2]) for i in range(owners)])  6.04 us
    pallas_call x1, Pallas kernels, merge_tiles(): pl.pallas_call(functools.partial(merge_kernel, own_tiles, labels.shape[1]...  2.75 us
    pallas_call x1, Pallas kernels, project(): pl.pallas_call(project_kernel, out_shape=[jax.ShapeDtypeStruct((rows, hid...  1.82 us
    pallas_call x3, Pallas kernels, product(): pl.pallas_call(functools.partial(product_kernel, first), out_shape=jax.Sh...  1.6 us
    pallas_call x1, Pallas kernels, early_product(): pl.pallas_call(early_kernel, out_shape=jax.ShapeDtypeStruct((total, width...  0.99 us
  transfers between devices with their start and end apart: 16, of which 9 were waited for; matrix products, arithmetic and copies ran while one was open for 0% of the time, Pallas kernels for 15%

profile of v10, /device:TPU:0, one launch (start us, length us, event | category | flops | bytes accessed | tf_op | source)
XLA Modules:
  0.0 41.6 jit_solution(12369432712101042984)
XLA Ops:
  0.0 1.8 %shard_map.91 = (f32[256,512]{1,0:T(8,128)S(1)}, bf16[256,256]{1,0:T(8,128)(2,1)S(1)}, bf16[256,256]{1,0:T(8,128)(2,1)S(1)}) custom-call(bf16[256,1024]{1,0:T(8,128)(2,1)} %features_hbm.1, bf16[1024,512]{1,0:T(8,128)(2,1)} %weight_hbm.1, f32[2,128]{1,0:T(2,128)} %bitcast.5), custom_call_target="tpu_custom_call" | custom-call | flops 268435456 | bytes 1572864 | tf_op jit(solution)/shard_map/pallas_call | solution.py:65
  1.8 5.1 %collective-permute-start = (bf16[256,256]{1,0:T(8,128)(2,1)S(1)}, bf16[256,256]{1,0:T(8,128)(2,1)S(1)}, u32[]{:S(2)}, u32[]{:S(2)}) collective-permute-start(bf16[256,256]{1,0:T(8,128)(2,1)S(1)} %get-tuple-element.24.own), channel_id=1, source_target_pairs={{0,3},{1,2},{2,1},{3,0},{4,7},{5,6},{6,5},{7,4},{8,11},{9,10},{10,... | collective-permute-start | bytes 393224 | tf_op jit(solution)/shard_map/ppermute | solution.py:333
  6.9 0.9 %collective-permute-start.9 = (bf16[256,256]{1,0:T(8,128)(2,1)S(1)}, bf16[256,256]{1,0:T(8,128)(2,1)S(1)}, u32[]{:S(2)}, u32[]{:S(2)}) collective-permute-start(bf16[256,256]{1,0:T(8,128)(2,1)S(1)} %get-tuple-element.33.refs_0_), channel_id=1, source_target_pairs={{0,3},{1,2},{2,1},{3,0},{4,7},{5,6},{6,5},{7,4},{8,11},{9,10},{10,... | collective-permute-start | bytes 393224 | tf_op jit(solution)/shard_map/ppermute | solution.py:333
  7.8 1.1 %collective-permute-start.8 = (bf16[256,256]{1,0:T(8,128)(2,1)S(1)}, bf16[256,256]{1,0:T(8,128)(2,1)S(1)}, u32[]{:S(2)}, u32[]{:S(2)}) collective-permute-start(bf16[256,256]{1,0:T(8,128)(2,1)S(1)} %get-tuple-element.33.refs_0_), channel_id=1, source_target_pairs={{0,1},{1,0},{2,3},{3,2},{4,5},{5,4},{6,7},{7,6},{8,9},{9,8},{10,11... | collective-permute-start | bytes 393224 | tf_op jit(solution)/shard_map/ppermute | solution.py:333
  9.6 2.8 %shard_map.92.matrix = bf16[2048,1024]{1,0:T(8,128)(2,1)S(1)} custom-call(s32[1]{0:T(128)} %bitcast.2.row, s32[1]{0:T(128)} %bitcast.3.column, s32[1]{0:T(128)S(6)} %copy.10.count, s32[1,64]{1,0:T(1,128)} %sources_hbm.1, s32[1,64]{1,0:T(1,128)} %targets_hbm.1, s32[1,16]{1,0:T(1,128)} %labels_hbm.1, bf16[1,64,128,128]{3,2,1,0:T(8,128)(2,1)} %tiles_hbm.1), custom_call_target="tpu_custom_call" | custom-call | flops 8388608 | bytes 12582912 | tf_op jit(solution)/shard_map/pallas_call | solution.py:150
  12.4 2.4 %collective-permute-start.2 = (bf16[256,256]{1,0:T(8,128)(2,1)S(1)}, bf16[256,256]{1,0:T(8,128)(2,1)S(1)}, u32[]{:S(2)}, u32[]{:S(2)}) collective-permute-start(bf16[256,256]{1,0:T(8,128)(2,1)S(1)} %collective-permute-done.across), channel_id=1, source_target_pairs={{0,1},{1,0},{2,3},{3,2},{4,5},{5,4},{6,7},{7,6},{8,9},{9,8},{10,11... | collective-permute-start | bytes 393224 | tf_op jit(solution)/shard_map/ppermute | solution.py:333
  14.8 1.4 %collective-permute-done.1.beside = bf16[256,256]{1,0:T(8,128)(2,1)S(1)} collective-permute-done((bf16[256,256]{1,0:T(8,128)(2,1)S(1)}, bf16[256,256]{1,0:T(8,128)(2,1)S(1)}, u32[]{:S(2)}, u32[]{:S(2)}) %collective-permute-start.1) | collective-permute-done | bytes 131104 | tf_op jit(solution)/shard_map/ppermute | solution.py:333
  16.2 1.0 %shard_map.93.early = f32[2048,256]{1,0:T(8,128)S(1)} custom-call(bf16[2048,1024]{1,0:T(8,128)(2,1)S(1)} %shard_map.92.matrix, bf16[256,256]{1,0:T(8,128)(2,1)S(1)} %get-tuple-element.24.own, bf16[256,256]{1,0:T(8,128)(2,1)S(1)} %collective-permute-done.1.beside, bf16[256,256]{1,0:T(8,128)(2,1)S(1)} %collective-permute-done.across), custom_call_target="tpu_custom_call" | custom-call | flops 10737418240 | bytes 1 | tf_op jit(solution)/shard_map/pallas_call | solution.py:184
  17.2 1.4 %collective-permute-start.10 = (bf16[256,256]{1,0:T(8,128)(2,1)S(1)}, bf16[256,256]{1,0:T(8,128)(2,1)S(1)}, u32[]{:S(2)}, u32[]{:S(2)}) collective-permute-start(bf16[256,256]{1,0:T(8,128)(2,1)S(1)} %collective-permute-done.9.refs_3_), channel_id=1, source_target_pairs={{0,1},{1,0},{2,3},{3,2},{4,5},{5,4},{6,7},{7,6},{8,9},{9,8},{10,11... | collective-permute-start | bytes 393224 | tf_op jit(solution)/shard_map/ppermute | solution.py:333
  18.6 3.6 %collective-permute-done.2.passed = bf16[256,256]{1,0:T(8,128)(2,1)S(1)} collective-permute-done((bf16[256,256]{1,0:T(8,128)(2,1)S(1)}, bf16[256,256]{1,0:T(8,128)(2,1)S(1)}, u32[]{:S(2)}, u32[]{:S(2)}) %collective-permute-start.2) | collective-permute-done | bytes 131104 | tf_op jit(solution)/shard_map/ppermute | solution.py:333
  22.2 0.2 shard_map.95
  22.5 0.2 shard_map.96
  22.7 0.6 %collective-permute-start.4 = (bf16[512,256]{1,0:T(8,128)(2,1)S(1)}, bf16[512,256]{1,0:T(8,128)(2,1)S(1)}, u32[]{:S(2)}, u32[]{:S(2)}) collective-permute-start(bf16[512,256]{1,0:T(8,128)(2,1)S(1)} %shard_map.96), channel_id=1, source_target_pairs={{0,4},{4,0},{8,12},{12,8},{16,20},{20,16},{24,28},{28,24},{1,5},{5... | collective-permute-start | bytes 786440 | tf_op jit(solution)/shard_map/ppermute | solution.py:333
  23.3 0.3 shard_map.94.stay
  23.6 0.4 %collective-permute-done.3.refs_0_ = bf16[512,256]{1,0:T(8,128)(2,1)S(1)} collective-permute-done((bf16[512,256]{1,0:T(8,128)(2,1)S(1)}, bf16[512,256]{1,0:T(8,128)(2,1)S(1)}, u32[]{:S(2)}, u32[]{:S(2)}) %collective-permute-start.3) | collective-permute-done | bytes 262176 | tf_op jit(solution)/shard_map/ppermute | solution.py:333
  24.0 0.4 %collective-permute-done.4.refs_1_ = bf16[512,256]{1,0:T(8,128)(2,1)S(1)} collective-permute-done((bf16[512,256]{1,0:T(8,128)(2,1)S(1)}, bf16[512,256]{1,0:T(8,128)(2,1)S(1)}, u32[]{:S(2)}, u32[]{:S(2)}) %collective-permute-start.4) | collective-permute-done | bytes 262176 | tf_op jit(solution)/shard_map/ppermute | solution.py:333
  24.6 1.7 %collective-permute-start.5 = (bf16[256,256]{1,0:T(8,128)(2,1)S(1)}, bf16[256,256]{1,0:T(8,128)(2,1)S(1)}, u32[]{:S(2)}, u32[]{:S(2)}) collective-permute-start(bf16[256,256]{1,0:T(8,128)(2,1)S(1)} %get-tuple-element.28), channel_id=1, source_target_pairs={{0,8},{4,20},{8,0},{12,28},{16,24},{20,4},{24,16},{28,12},{1,9},{5... | collective-permute-start | bytes 393224 | tf_op jit(solution)/shard_map/ppermute | solution.py:340
  26.2 1.5 %collective-permute-start.6 = (bf16[256,256]{1,0:T(8,128)(2,1)S(1)}, bf16[256,256]{1,0:T(8,128)(2,1)S(1)}, u32[]{:S(2)}, u32[]{:S(2)}) collective-permute-start(bf16[256,256]{1,0:T(8,128)(2,1)S(1)} %get-tuple-element.29), channel_id=1, source_target_pairs={{0,16},{4,12},{8,24},{12,4},{16,0},{20,28},{24,8},{28,20},{1,17},{... | collective-permute-start | bytes 393224 | tf_op jit(solution)/shard_map/ppermute | solution.py:340
  27.7 0.4 collective-permute-start.7
  28.1 0.4 %shard_map.100 = bf16[512,256]{1,0:T(8,128)(2,1)S(1)} custom-call(bf16[2048,1024]{1,0:T(8,128)(2,1)S(1)} %shard_map.92.matrix, bf16[256,256]{1,0:T(8,128)(2,1)S(1)} %get-tuple-element.33.refs_0_, bf16[256,256]{1,0:T(8,128)(2,1)S(1)} %collective-permute-done.8.refs_1_, bf16[256,256]{1,0:T(8,128)(2,1)S(1)} %collective-permute-done.10.refs_2_, ...), custom_call_target="tpu_custom_call" | custom-call | bytes 1 | tf_op jit(solution)/shard_map/pallas_call | solution.py:232
  28.6 0.4 %shard_map.99 = bf16[512,256]{1,0:T(8,128)(2,1)S(1)} custom-call(bf16[2048,1024]{1,0:T(8,128)(2,1)S(1)} %shard_map.92.matrix, bf16[256,256]{1,0:T(8,128)(2,1)S(1)} %get-tuple-element.33.refs_0_, bf16[256,256]{1,0:T(8,128)(2,1)S(1)} %collective-permute-done.8.refs_1_, bf16[256,256]{1,0:T(8,128)(2,1)S(1)} %collective-permute-done.10.refs_2_, ...), custom_call_target="tpu_custom_call" | custom-call | bytes 1 | tf_op jit(solution)/shard_map/pallas_call | solution.py:232
  29.1 0.5 %collective-permute-start.12 = (bf16[512,256]{1,0:T(8,128)(2,1)S(1)}, bf16[512,256]{1,0:T(8,128)(2,1)S(1)}, u32[]{:S(2)}, u32[]{:S(2)}) collective-permute-start(bf16[512,256]{1,0:T(8,128)(2,1)S(1)} %shard_map.100), channel_id=1, source_target_pairs={{0,4},{4,0},{8,12},{12,8},{16,20},{20,16},{24,28},{28,24},{1,5},{5... | collective-permute-start | bytes 786440 | tf_op jit(solution)/shard_map/ppermute | solution.py:333
  29.6 0.7 %shard_map.98.stay = f32[1024,256]{1,0:T(8,128)S(1)} custom-call(bf16[2048,1024]{1,0:T(8,128)(2,1)S(1)} %shard_map.92.matrix, bf16[256,256]{1,0:T(8,128)(2,1)S(1)} %get-tuple-element.33.refs_0_, bf16[256,256]{1,0:T(8,128)(2,1)S(1)} %collective-permute-done.8.refs_1_, bf16[256,256]{1,0:T(8,128)(2,1)S(1)} %collective-permute-done.10.refs_2_, ...), custom_call_target="tpu_custom_call" | custom-call | flops 10737418240 | bytes 1 | tf_op jit(solution)/shard_map/pallas_call | solution.py:232
  30.3 0.3 collective-permute-done.11.refs_0_
  30.6 0.4 collective-permute-done.12.refs_1_
  31.1 1.7 %collective-permute-start.13 = (bf16[256,256]{1,0:T(8,128)(2,1)S(1)}, bf16[256,256]{1,0:T(8,128)(2,1)S(1)}, u32[]{:S(2)}, u32[]{:S(2)}) collective-permute-start(bf16[256,256]{1,0:T(8,128)(2,1)S(1)} %get-tuple-element.38), channel_id=1, source_target_pairs={{0,8},{4,20},{8,0},{12,28},{16,24},{20,4},{24,16},{28,12},{1,9},{5... | collective-permute-start | bytes 393224 | tf_op jit(solution)/shard_map/ppermute | solution.py:340
  32.8 1.5 %collective-permute-start.14 = (bf16[256,256]{1,0:T(8,128)(2,1)S(1)}, bf16[256,256]{1,0:T(8,128)(2,1)S(1)}, u32[]{:S(2)}, u32[]{:S(2)}) collective-permute-start(bf16[256,256]{1,0:T(8,128)(2,1)S(1)} %get-tuple-element.39), channel_id=1, source_target_pairs={{0,16},{4,12},{8,24},{12,4},{16,0},{20,28},{24,8},{28,20},{1,17},{... | collective-permute-start | bytes 393224 | tf_op jit(solution)/shard_map/ppermute | solution.py:340
  34.3 0.4 collective-permute-start.15
  34.7 2.4 %collective-permute-done.13.refs_5_ = bf16[256,256]{1,0:T(8,128)(2,1)S(1)} collective-permute-done((bf16[256,256]{1,0:T(8,128)(2,1)S(1)}, bf16[256,256]{1,0:T(8,128)(2,1)S(1)}, u32[]{:S(2)}, u32[]{:S(2)}) %collective-permute-start.13) | collective-permute-done | bytes 131104 | tf_op jit(solution)/shard_map/ppermute | solution.py:340
  37.1 0.9 %collective-permute-done.14.refs_6_ = bf16[256,256]{1,0:T(8,128)(2,1)S(1)} collective-permute-done((bf16[256,256]{1,0:T(8,128)(2,1)S(1)}, bf16[256,256]{1,0:T(8,128)(2,1)S(1)}, u32[]{:S(2)}, u32[]{:S(2)}) %collective-permute-start.14) | collective-permute-done | bytes 131104 | tf_op jit(solution)/shard_map/ppermute | solution.py:340
  38.0 2.7 %collective-permute-done.15.refs_7_ = bf16[256,256]{1,0:T(8,128)(2,1)S(1)} collective-permute-done((bf16[256,256]{1,0:T(8,128)(2,1)S(1)}, bf16[256,256]{1,0:T(8,128)(2,1)S(1)}, u32[]{:S(2)}, u32[]{:S(2)}) %collective-permute-start.15) | collective-permute-done | bytes 131104 | tf_op jit(solution)/shard_map/ppermute | solution.py:340
  40.7 0.9 %shard_map.102 = bf16[256,512]{1,0:T(8,128)(2,1)} custom-call(f32[256,512]{1,0:T(8,128)S(1)} %get-tuple-element.23.projected, f32[2,128]{1,0:T(2,128)S(1)} %bitcast.4, f32[256,256]{1,0:T(8,128)S(1)} %get-tuple-element.27.refs_0_, bf16[256,256]{1,0:T(8,128)(2,1)S(1)} %collective-permute-done.5.refs_1_, bf16[256,256]{1,0:T(8,128)(2,1)S(1)} %collective-permute-done.6.refs_2_, ...), custom_call_target="tpu_custom_call" | custom-call | flops 786432 | bytes 2097152 | tf_op jit(solution)/shard_map/pallas_call | solution.py:287
  (14 shorter events, 0.3 us)
Async XLA Ops:
  1.8 10.6 %collective-permute-start = (bf16[256,256]{1,0:T(8,128)(2,1)S(1)}, bf16[256,256]{1,0:T(8,128)(2,1)S(1)}, u32[]{:S(2)}, u32[]{:S(2)}) collective-permute-start(bf16[256,256]{1,0:T(8,128)(2,1)S(1)} %get-tuple-element.24.own), channel_id=1, source_target_pairs={{0,3},{1,2},{2,1},{3,0},{4,7},{5,6},{6,5},{7,4},{8,11},{9,10},{10,... | collective-permute-start | bytes 393224 | tf_op jit(solution)/shard_map/ppermute | solution.py:333
  6.9 9.2 %collective-permute-start.1 = (bf16[256,256]{1,0:T(8,128)(2,1)S(1)}, bf16[256,256]{1,0:T(8,128)(2,1)S(1)}, u32[]{:S(2)}, u32[]{:S(2)}) collective-permute-start(bf16[256,256]{1,0:T(8,128)(2,1)S(1)} %get-tuple-element.24.own), channel_id=1, source_target_pairs={{0,1},{1,0},{2,3},{3,2},{4,5},{5,4},{6,7},{7,6},{8,9},{9,8},{10,11... | collective-permute-start | bytes 393224 | tf_op jit(solution)/shard_map/ppermute | solution.py:333
  6.9 10.2 %collective-permute-start.9 = (bf16[256,256]{1,0:T(8,128)(2,1)S(1)}, bf16[256,256]{1,0:T(8,128)(2,1)S(1)}, u32[]{:S(2)}, u32[]{:S(2)}) collective-permute-start(bf16[256,256]{1,0:T(8,128)(2,1)S(1)} %get-tuple-element.33.refs_0_), channel_id=1, source_target_pairs={{0,3},{1,2},{2,1},{3,0},{4,7},{5,6},{6,5},{7,4},{8,11},{9,10},{10,... | collective-permute-start | bytes 393224 | tf_op jit(solution)/shard_map/ppermute | solution.py:333
  7.8 20.3 %collective-permute-start.8 = (bf16[256,256]{1,0:T(8,128)(2,1)S(1)}, bf16[256,256]{1,0:T(8,128)(2,1)S(1)}, u32[]{:S(2)}, u32[]{:S(2)}) collective-permute-start(bf16[256,256]{1,0:T(8,128)(2,1)S(1)} %get-tuple-element.33.refs_0_), channel_id=1, source_target_pairs={{0,1},{1,0},{2,3},{3,2},{4,5},{5,4},{6,7},{7,6},{8,9},{9,8},{10,11... | collective-permute-start | bytes 393224 | tf_op jit(solution)/shard_map/ppermute | solution.py:333
  12.4 9.8 %collective-permute-start.2 = (bf16[256,256]{1,0:T(8,128)(2,1)S(1)}, bf16[256,256]{1,0:T(8,128)(2,1)S(1)}, u32[]{:S(2)}, u32[]{:S(2)}) collective-permute-start(bf16[256,256]{1,0:T(8,128)(2,1)S(1)} %collective-permute-done.across), channel_id=1, source_target_pairs={{0,1},{1,0},{2,3},{3,2},{4,5},{5,4},{6,7},{7,6},{8,9},{9,8},{10,11... | collective-permute-start | bytes 393224 | tf_op jit(solution)/shard_map/ppermute | solution.py:333
  17.2 10.9 %collective-permute-start.10 = (bf16[256,256]{1,0:T(8,128)(2,1)S(1)}, bf16[256,256]{1,0:T(8,128)(2,1)S(1)}, u32[]{:S(2)}, u32[]{:S(2)}) collective-permute-start(bf16[256,256]{1,0:T(8,128)(2,1)S(1)} %collective-permute-done.9.refs_3_), channel_id=1, source_target_pairs={{0,1},{1,0},{2,3},{3,2},{4,5},{5,4},{6,7},{7,6},{8,9},{9,8},{10,11... | collective-permute-start | bytes 393224 | tf_op jit(solution)/shard_map/ppermute | solution.py:333
  22.4 1.6 %collective-permute-start.3 = (bf16[512,256]{1,0:T(8,128)(2,1)S(1)}, bf16[512,256]{1,0:T(8,128)(2,1)S(1)}, u32[]{:S(2)}, u32[]{:S(2)}) collective-permute-start(bf16[512,256]{1,0:T(8,128)(2,1)S(1)} %shard_map.95), channel_id=1, source_target_pairs={{0,4},{4,0},{8,12},{12,8},{16,20},{20,16},{24,28},{28,24},{1,5},{5... | collective-permute-start | bytes 786440 | tf_op jit(solution)/shard_map/ppermute | solution.py:333
  22.7 1.7 %collective-permute-start.4 = (bf16[512,256]{1,0:T(8,128)(2,1)S(1)}, bf16[512,256]{1,0:T(8,128)(2,1)S(1)}, u32[]{:S(2)}, u32[]{:S(2)}) collective-permute-start(bf16[512,256]{1,0:T(8,128)(2,1)S(1)} %shard_map.96), channel_id=1, source_target_pairs={{0,4},{4,0},{8,12},{12,8},{16,20},{20,16},{24,28},{28,24},{1,5},{5... | collective-permute-start | bytes 786440 | tf_op jit(solution)/shard_map/ppermute | solution.py:333
  24.6 9.7 %collective-permute-start.5 = (bf16[256,256]{1,0:T(8,128)(2,1)S(1)}, bf16[256,256]{1,0:T(8,128)(2,1)S(1)}, u32[]{:S(2)}, u32[]{:S(2)}) collective-permute-start(bf16[256,256]{1,0:T(8,128)(2,1)S(1)} %get-tuple-element.28), channel_id=1, source_target_pairs={{0,8},{4,20},{8,0},{12,28},{16,24},{20,4},{24,16},{28,12},{1,9},{5... | collective-permute-start | bytes 393224 | tf_op jit(solution)/shard_map/ppermute | solution.py:340
  26.2 8.4 %collective-permute-start.6 = (bf16[256,256]{1,0:T(8,128)(2,1)S(1)}, bf16[256,256]{1,0:T(8,128)(2,1)S(1)}, u32[]{:S(2)}, u32[]{:S(2)}) collective-permute-start(bf16[256,256]{1,0:T(8,128)(2,1)S(1)} %get-tuple-element.29), channel_id=1, source_target_pairs={{0,16},{4,12},{8,24},{12,4},{16,0},{20,28},{24,8},{28,20},{1,17},{... | collective-permute-start | bytes 393224 | tf_op jit(solution)/shard_map/ppermute | solution.py:340
  27.7 6.9 %collective-permute-start.7 = (bf16[256,256]{1,0:T(8,128)(2,1)S(1)}, bf16[256,256]{1,0:T(8,128)(2,1)S(1)}, u32[]{:S(2)}, u32[]{:S(2)}) collective-permute-start(bf16[256,256]{1,0:T(8,128)(2,1)S(1)} %get-tuple-element.30), channel_id=1, source_target_pairs={{0,24},{4,28},{8,16},{12,20},{16,8},{20,12},{24,0},{28,4},{1,25},{... | collective-permute-start | bytes 393224 | tf_op jit(solution)/shard_map/ppermute | solution.py:340
  29.0 11.7 %copy-start = (f32[256]{0:T(256)S(1)}, f32[256]{0:T(256)}, u32[]{:S(2)}) copy-start(f32[256]{0:T(256)} %param.12) | copy-start | bytes 3076
  29.0 1.6 %collective-permute-start.11 = (bf16[512,256]{1,0:T(8,128)(2,1)S(1)}, bf16[512,256]{1,0:T(8,128)(2,1)S(1)}, u32[]{:S(2)}, u32[]{:S(2)}) collective-permute-start(bf16[512,256]{1,0:T(8,128)(2,1)S(1)} %shard_map.99), channel_id=1, source_target_pairs={{0,4},{4,0},{8,12},{12,8},{16,20},{20,16},{24,28},{28,24},{1,5},{5... | collective-permute-start | bytes 786440 | tf_op jit(solution)/shard_map/ppermute | solution.py:333
  29.1 1.9 %collective-permute-start.12 = (bf16[512,256]{1,0:T(8,128)(2,1)S(1)}, bf16[512,256]{1,0:T(8,128)(2,1)S(1)}, u32[]{:S(2)}, u32[]{:S(2)}) collective-permute-start(bf16[512,256]{1,0:T(8,128)(2,1)S(1)} %shard_map.100), channel_id=1, source_target_pairs={{0,4},{4,0},{8,12},{12,8},{16,20},{20,16},{24,28},{28,24},{1,5},{5... | collective-permute-start | bytes 786440 | tf_op jit(solution)/shard_map/ppermute | solution.py:333
  31.1 6.0 %collective-permute-start.13 = (bf16[256,256]{1,0:T(8,128)(2,1)S(1)}, bf16[256,256]{1,0:T(8,128)(2,1)S(1)}, u32[]{:S(2)}, u32[]{:S(2)}) collective-permute-start(bf16[256,256]{1,0:T(8,128)(2,1)S(1)} %get-tuple-element.38), channel_id=1, source_target_pairs={{0,8},{4,20},{8,0},{12,28},{16,24},{20,4},{24,16},{28,12},{1,9},{5... | collective-permute-start | bytes 393224 | tf_op jit(solution)/shard_map/ppermute | solution.py:340
  32.8 5.3 %collective-permute-start.14 = (bf16[256,256]{1,0:T(8,128)(2,1)S(1)}, bf16[256,256]{1,0:T(8,128)(2,1)S(1)}, u32[]{:S(2)}, u32[]{:S(2)}) collective-permute-start(bf16[256,256]{1,0:T(8,128)(2,1)S(1)} %get-tuple-element.39), channel_id=1, source_target_pairs={{0,16},{4,12},{8,24},{12,4},{16,0},{20,28},{24,8},{28,20},{1,17},{... | collective-permute-start | bytes 393224 | tf_op jit(solution)/shard_map/ppermute | solution.py:340
  34.3 6.4 %collective-permute-start.15 = (bf16[256,256]{1,0:T(8,128)(2,1)S(1)}, bf16[256,256]{1,0:T(8,128)(2,1)S(1)}, u32[]{:S(2)}, u32[]{:S(2)}) collective-permute-start(bf16[256,256]{1,0:T(8,128)(2,1)S(1)} %get-tuple-element.40), channel_id=1, source_target_pairs={{0,24},{4,28},{8,16},{12,20},{16,8},{20,12},{24,0},{28,4},{1,25},{... | collective-permute-start | bytes 393224 | tf_op jit(solution)/shard_map/ppermute | solution.py:340

commit v11 on v9

--- a/solution.py
+++ b/solution.py
@@ -327,12 +327,12 @@
 
     projected, *scaled = project(features, weight, source_norm, CHUNKS)
     matrix = merge_tiles(own_tiles, owners, span, index_args, tile_weights)
-    across = [swap(own, "col", 3) for own in scaled]
+    across = [swap(own, "col", 2) for own in scaled]
     beside = [swap(own, "col", 1) for own in scaled]
     across[0], matrix = lax.optimization_barrier((across[0], matrix))
     passed = [swap(value, "col", 1) for value in across]
     pieces, sent = [], None
-    for blocks, wait in zip(zip(scaled, beside, passed, across), WEIGHTS):
+    for blocks, wait in zip(zip(scaled, beside, across, passed), WEIGHTS):
         if sent is not None:
             pieces[-1] += exchange(sent)
             blocks, _ = lax.optimization_barrier((blocks, sent))

time: 39.3 us -> 40.6 us (1.033)
  waiting for transfers between devices: 11.6 us -> 15.3 us
  starting transfers between devices: 18.4 us -> 15.9 us
    ppermute x8, waiting for transfers between devices: 5.51 us -> 9.23 us  [swap(): return lax.ppermute(value, axis, pairs)]
    ppermute x8, starting transfers between devices: 11.2 us -> 8.84 us  [swap(): return lax.ppermute(value, axis, pairs)]
  transfers between devices with their start and end apart: 14 -> 14, of which waited for: 7 -> 8; matrix products, arithmetic and copies ran while one was open for 0% -> 0% of each run, Pallas kernels for 15% -> 14%
where the time goes in v11:
time: 40.6 us; the launch traced here: 40.5 us
  starting transfers between devices  15.9 us (39%)
  waiting for transfers between devices  15.3 us (38%)
  Pallas kernels  8.49 us (21%)
  between operations  0.74 us (2%)
    ppermute x8, waiting for transfers between devices, swap(): return lax.ppermute(value, axis, pairs)  9.23 us
    ppermute x8, starting transfers between devices, swap(): return lax.ppermute(value, axis, pairs)  8.84 us
    ppermute x6, starting transfers between devices, exchange(): lax.ppermute(value, 'row', [(i, i ^ step[i % 2]) for i in range(owners)])  7.11 us
    ppermute x6, waiting for transfers between devices, exchange(): lax.ppermute(value, 'row', [(i, i ^ step[i % 2]) for i in range(owners)])  6.04 us
    pallas_call x4, Pallas kernels, product(): pl.pallas_call(functools.partial(product_kernel, half * (total // 2)), ou...  2.85 us
    pallas_call x1, Pallas kernels, merge_tiles(): pl.pallas_call(functools.partial(merge_kernel, own_tiles, labels.shape[1]...  2.76 us
    pallas_call x1, Pallas kernels, project(): pl.pallas_call(project_kernel, out_shape=[jax.ShapeDtypeStruct((rows, hid...  1.82 us
    pallas_call x1, Pallas kernels, finish(): pl.pallas_call(functools.partial(finish_kernel, len(pieces)), out_shape=j...  0.88 us
  transfers between devices with their start and end apart: 14, of which 8 were waited for; matrix products, arithmetic and copies ran while one was open for 0% of the time, Pallas kernels for 14%

profile of v11, /device:TPU:0, one launch (start us, length us, event | category | flops | bytes accessed | tf_op | source)
XLA Modules:
  0.0 40.5 jit_solution(7339232722025259935)
XLA Ops:
  0.0 1.8 %shard_map.91 = (f32[256,512]{1,0:T(8,128)S(1)}, bf16[256,256]{1,0:T(8,128)(2,1)S(1)}, bf16[256,256]{1,0:T(8,128)(2,1)S(1)}) custom-call(bf16[256,1024]{1,0:T(8,128)(2,1)} %features_hbm.1, bf16[1024,512]{1,0:T(8,128)(2,1)} %weight_hbm.1, f32[2,128]{1,0:T(2,128)} %bitcast.5), custom_call_target="tpu_custom_call" | custom-call | flops 268435456 | bytes 1572864 | tf_op jit(solution)/shard_map/pallas_call | solution.py:66
  1.8 4.1 %collective-permute-start = (bf16[256,256]{1,0:T(8,128)(2,1)S(1)}, bf16[256,256]{1,0:T(8,128)(2,1)S(1)}, u32[]{:S(2)}, u32[]{:S(2)}) collective-permute-start(bf16[256,256]{1,0:T(8,128)(2,1)S(1)} %get-tuple-element.23.refs_0_), channel_id=1, source_target_pairs={{0,2},{1,3},{2,0},{3,1},{4,6},{5,7},{6,4},{7,5},{8,10},{9,11},{10,... | collective-permute-start | bytes 393224 | tf_op jit(solution)/shard_map/ppermute | solution.py:287
  5.9 1.6 %collective-permute-start.1 = (bf16[256,256]{1,0:T(8,128)(2,1)S(1)}, bf16[256,256]{1,0:T(8,128)(2,1)S(1)}, u32[]{:S(2)}, u32[]{:S(2)}) collective-permute-start(bf16[256,256]{1,0:T(8,128)(2,1)S(1)} %get-tuple-element.23.refs_0_), channel_id=1, source_target_pairs={{0,1},{1,0},{2,3},{3,2},{4,5},{5,4},{6,7},{7,6},{8,9},{9,8},{10,11... | collective-permute-start | bytes 393224 | tf_op jit(solution)/shard_map/ppermute | solution.py:287
  7.5 0.3 collective-permute-start.8
  8.5 2.8 %shard_map.92.matrix = bf16[2048,1024]{1,0:T(8,128)(2,1)S(1)} custom-call(s32[1]{0:T(128)} %bitcast.2.row, s32[1]{0:T(128)} %bitcast.3.column, s32[1]{0:T(128)S(6)} %copy.10.count, s32[1,64]{1,0:T(1,128)} %sources_hbm.1, s32[1,64]{1,0:T(1,128)} %targets_hbm.1, s32[1,16]{1,0:T(1,128)} %labels_hbm.1, bf16[1,64,128,128]{3,2,1,0:T(8,128)(2,1)} %tiles_hbm.1), custom_call_target="tpu_custom_call" | custom-call | flops 8388608 | bytes 12582912 | tf_op jit(solution)/shard_map/pallas_call | solution.py:151
  11.3 2.6 %collective-permute-done.refs_2_ = bf16[256,256]{1,0:T(8,128)(2,1)S(1)} collective-permute-done((bf16[256,256]{1,0:T(8,128)(2,1)S(1)}, bf16[256,256]{1,0:T(8,128)(2,1)S(1)}, u32[]{:S(2)}, u32[]{:S(2)}) %collective-permute-start) | collective-permute-done | bytes 131104 | tf_op jit(solution)/shard_map/ppermute | solution.py:287
  13.9 0.1 collective-permute-start.2
  14.0 2.0 %collective-permute-start.7 = (bf16[256,256]{1,0:T(8,128)(2,1)S(1)}, bf16[256,256]{1,0:T(8,128)(2,1)S(1)}, u32[]{:S(2)}, u32[]{:S(2)}) collective-permute-start(bf16[256,256]{1,0:T(8,128)(2,1)S(1)} %get-tuple-element.31.refs_0_), channel_id=1, source_target_pairs={{0,1},{1,0},{2,3},{3,2},{4,5},{5,4},{6,7},{7,6},{8,9},{9,8},{10,11... | collective-permute-start | bytes 393224 | tf_op jit(solution)/shard_map/ppermute | solution.py:287
  15.9 2.0 %collective-permute-done.8.refs_2_ = bf16[256,256]{1,0:T(8,128)(2,1)S(1)} collective-permute-done((bf16[256,256]{1,0:T(8,128)(2,1)S(1)}, bf16[256,256]{1,0:T(8,128)(2,1)S(1)}, u32[]{:S(2)}, u32[]{:S(2)}) %collective-permute-start.8) | collective-permute-done | bytes 131104 | tf_op jit(solution)/shard_map/ppermute | solution.py:287
  18.0 0.7 %collective-permute-start.9 = (bf16[256,256]{1,0:T(8,128)(2,1)S(1)}, bf16[256,256]{1,0:T(8,128)(2,1)S(1)}, u32[]{:S(2)}, u32[]{:S(2)}) collective-permute-start(bf16[256,256]{1,0:T(8,128)(2,1)S(1)} %collective-permute-done.8.refs_2_), channel_id=1, source_target_pairs={{0,1},{1,0},{2,3},{3,2},{4,5},{5,4},{6,7},{7,6},{8,9},{9,8},{10,11... | collective-permute-start | bytes 393224 | tf_op jit(solution)/shard_map/ppermute | solution.py:287
  18.6 2.2 %collective-permute-done.2.refs_3_ = bf16[256,256]{1,0:T(8,128)(2,1)S(1)} collective-permute-done((bf16[256,256]{1,0:T(8,128)(2,1)S(1)}, bf16[256,256]{1,0:T(8,128)(2,1)S(1)}, u32[]{:S(2)}, u32[]{:S(2)}) %collective-permute-start.2) | collective-permute-done | bytes 131104 | tf_op jit(solution)/shard_map/ppermute | solution.py:287
  20.8 0.7 %shard_map.94 = bf16[1024,256]{1,0:T(8,128)(2,1)S(1)} custom-call(bf16[2048,1024]{1,0:T(8,128)(2,1)S(1)} %shard_map.92.matrix, bf16[256,256]{1,0:T(8,128)(2,1)S(1)} %get-tuple-element.23.refs_0_, bf16[256,256]{1,0:T(8,128)(2,1)S(1)} %collective-permute-done.1.refs_1_, bf16[256,256]{1,0:T(8,128)(2,1)S(1)} %collective-permute-done.refs_2_, ...), custom_call_target="tpu_custom_call" | custom-call | flops 10737418240 | bytes 1 | tf_op jit(solution)/shard_map/pallas_call | solution.py:188
  21.5 0.1 collective-permute-start.3
  21.6 0.7 %shard_map.93.stay = f32[1024,256]{1,0:T(8,128)S(1)} custom-call(bf16[2048,1024]{1,0:T(8,128)(2,1)S(1)} %shard_map.92.matrix, bf16[256,256]{1,0:T(8,128)(2,1)S(1)} %get-tuple-element.23.refs_0_, bf16[256,256]{1,0:T(8,128)(2,1)S(1)} %collective-permute-done.1.refs_1_, bf16[256,256]{1,0:T(8,128)(2,1)S(1)} %collective-permute-done.refs_2_, ...), custom_call_target="tpu_custom_call" | custom-call | flops 10737418240 | bytes 1 | tf_op jit(solution)/shard_map/pallas_call | solution.py:188
  22.3 1.2 %collective-permute-done.3.came = bf16[1024,256]{1,0:T(8,128)(2,1)S(1)} collective-permute-done((bf16[1024,256]{1,0:T(8,128)(2,1)S(1)}, bf16[1024,256]{1,0:T(8,128)(2,1)S(1)}, u32[]{:S(2)}, u32[]{:S(2)}) %collective-permute-start.3) | collective-permute-done | bytes 524320 | tf_op jit(solution)/shard_map/ppermute | solution.py:287
  23.5 0.1 shard_map.95
  23.6 1.7 %collective-permute-start.4 = (bf16[256,256]{1,0:T(8,128)(2,1)S(1)}, bf16[256,256]{1,0:T(8,128)(2,1)S(1)}, u32[]{:S(2)}, u32[]{:S(2)}) collective-permute-start(bf16[256,256]{1,0:T(8,128)(2,1)S(1)} %get-tuple-element.27), channel_id=1, source_target_pairs={{0,8},{4,20},{8,0},{12,28},{16,24},{20,4},{24,16},{28,12},{1,9},{5... | collective-permute-start | bytes 393224 | tf_op jit(solution)/shard_map/ppermute | solution.py:294
  25.3 1.5 %collective-permute-start.5 = (bf16[256,256]{1,0:T(8,128)(2,1)S(1)}, bf16[256,256]{1,0:T(8,128)(2,1)S(1)}, u32[]{:S(2)}, u32[]{:S(2)}) collective-permute-start(bf16[256,256]{1,0:T(8,128)(2,1)S(1)} %get-tuple-element.28), channel_id=1, source_target_pairs={{0,16},{4,12},{8,24},{12,4},{16,0},{20,28},{24,8},{28,20},{1,17},{... | collective-permute-start | bytes 393224 | tf_op jit(solution)/shard_map/ppermute | solution.py:294
  26.8 0.3 collective-permute-start.6
  27.2 0.7 %shard_map.97 = bf16[1024,256]{1,0:T(8,128)(2,1)S(1)} custom-call(bf16[2048,1024]{1,0:T(8,128)(2,1)S(1)} %shard_map.92.matrix, bf16[256,256]{1,0:T(8,128)(2,1)S(1)} %get-tuple-element.31.refs_0_, bf16[256,256]{1,0:T(8,128)(2,1)S(1)} %collective-permute-done.7.refs_1_, bf16[256,256]{1,0:T(8,128)(2,1)S(1)} %collective-permute-done.8.refs_2_, ...), custom_call_target="tpu_custom_call" | custom-call | bytes 1 | tf_op jit(solution)/shard_map/pallas_call | solution.py:188
  27.9 0.0 copy-start
  27.9 0.1 collective-permute-start.10
  28.0 0.7 %shard_map.96.stay = f32[1024,256]{1,0:T(8,128)S(1)} custom-call(bf16[2048,1024]{1,0:T(8,128)(2,1)S(1)} %shard_map.92.matrix, bf16[256,256]{1,0:T(8,128)(2,1)S(1)} %get-tuple-element.31.refs_0_, bf16[256,256]{1,0:T(8,128)(2,1)S(1)} %collective-permute-done.7.refs_1_, bf16[256,256]{1,0:T(8,128)(2,1)S(1)} %collective-permute-done.8.refs_2_, ...), custom_call_target="tpu_custom_call" | custom-call | flops 10737418240 | bytes 1 | tf_op jit(solution)/shard_map/pallas_call | solution.py:188
  28.7 1.2 %collective-permute-done.10.came = bf16[1024,256]{1,0:T(8,128)(2,1)S(1)} collective-permute-done((bf16[1024,256]{1,0:T(8,128)(2,1)S(1)}, bf16[1024,256]{1,0:T(8,128)(2,1)S(1)}, u32[]{:S(2)}, u32[]{:S(2)}) %collective-permute-start.10) | collective-permute-done | bytes 524320 | tf_op jit(solution)/shard_map/ppermute | solution.py:287
  29.9 0.1 shard_map.98
  30.0 1.7 %collective-permute-start.11 = (bf16[256,256]{1,0:T(8,128)(2,1)S(1)}, bf16[256,256]{1,0:T(8,128)(2,1)S(1)}, u32[]{:S(2)}, u32[]{:S(2)}) collective-permute-start(bf16[256,256]{1,0:T(8,128)(2,1)S(1)} %get-tuple-element.36), channel_id=1, source_target_pairs={{0,8},{4,20},{8,0},{12,28},{16,24},{20,4},{24,16},{28,12},{1,9},{5... | collective-permute-start | bytes 393224 | tf_op jit(solution)/shard_map/ppermute | solution.py:294
  31.7 1.5 %collective-permute-start.12 = (bf16[256,256]{1,0:T(8,128)(2,1)S(1)}, bf16[256,256]{1,0:T(8,128)(2,1)S(1)}, u32[]{:S(2)}, u32[]{:S(2)}) collective-permute-start(bf16[256,256]{1,0:T(8,128)(2,1)S(1)} %get-tuple-element.37), channel_id=1, source_target_pairs={{0,16},{4,12},{8,24},{12,4},{16,0},{20,28},{24,8},{28,20},{1,17},{... | collective-permute-start | bytes 393224 | tf_op jit(solution)/shard_map/ppermute | solution.py:294
  33.2 0.3 collective-permute-start.13
  33.5 2.4 %collective-permute-done.11.refs_5_ = bf16[256,256]{1,0:T(8,128)(2,1)S(1)} collective-permute-done((bf16[256,256]{1,0:T(8,128)(2,1)S(1)}, bf16[256,256]{1,0:T(8,128)(2,1)S(1)}, u32[]{:S(2)}, u32[]{:S(2)}) %collective-permute-start.11) | collective-permute-done | bytes 131104 | tf_op jit(solution)/shard_map/ppermute | solution.py:294
  35.9 2.6 %collective-permute-done.12.refs_6_ = bf16[256,256]{1,0:T(8,128)(2,1)S(1)} collective-permute-done((bf16[256,256]{1,0:T(8,128)(2,1)S(1)}, bf16[256,256]{1,0:T(8,128)(2,1)S(1)}, u32[]{:S(2)}, u32[]{:S(2)}) %collective-permute-start.12) | collective-permute-done | bytes 131104 | tf_op jit(solution)/shard_map/ppermute | solution.py:294
  38.5 1.0 %collective-permute-done.13.refs_7_ = bf16[256,256]{1,0:T(8,128)(2,1)S(1)} collective-permute-done((bf16[256,256]{1,0:T(8,128)(2,1)S(1)}, bf16[256,256]{1,0:T(8,128)(2,1)S(1)}, u32[]{:S(2)}, u32[]{:S(2)}) %collective-permute-start.13) | collective-permute-done | bytes 131104 | tf_op jit(solution)/shard_map/ppermute | solution.py:294
  39.6 0.9 %shard_map.99 = bf16[256,512]{1,0:T(8,128)(2,1)} custom-call(f32[256,512]{1,0:T(8,128)S(1)} %get-tuple-element.22.projected, f32[2,128]{1,0:T(2,128)S(1)} %bitcast.4, f32[256,256]{1,0:T(8,128)S(1)} %get-tuple-element.26.refs_0_, bf16[256,256]{1,0:T(8,128)(2,1)S(1)} %collective-permute-done.4.refs_1_, bf16[256,256]{1,0:T(8,128)(2,1)S(1)} %collective-permute-done.5.refs_2_, ...), custom_call_target="tpu_custom_call" | custom-call | flops 786432 | bytes 2097152 | tf_op jit(solution)/shard_map/pallas_call | solution.py:241
  (7 shorter events, 0.0 us)
Async XLA Ops:
  1.8 12.1 %collective-permute-start = (bf16[256,256]{1,0:T(8,128)(2,1)S(1)}, bf16[256,256]{1,0:T(8,128)(2,1)S(1)}, u32[]{:S(2)}, u32[]{:S(2)}) collective-permute-start(bf16[256,256]{1,0:T(8,128)(2,1)S(1)} %get-tuple-element.23.refs_0_), channel_id=1, source_target_pairs={{0,2},{1,3},{2,0},{3,1},{4,6},{5,7},{6,4},{7,5},{8,10},{9,11},{10,... | collective-permute-start | bytes 393224 | tf_op jit(solution)/shard_map/ppermute | solution.py:287
  5.9 12.7 %collective-permute-start.1 = (bf16[256,256]{1,0:T(8,128)(2,1)S(1)}, bf16[256,256]{1,0:T(8,128)(2,1)S(1)}, u32[]{:S(2)}, u32[]{:S(2)}) collective-permute-start(bf16[256,256]{1,0:T(8,128)(2,1)S(1)} %get-tuple-element.23.refs_0_), channel_id=1, source_target_pairs={{0,1},{1,0},{2,3},{3,2},{4,5},{5,4},{6,7},{7,6},{8,9},{9,8},{10,11... | collective-permute-start | bytes 393224 | tf_op jit(solution)/shard_map/ppermute | solution.py:287
  7.5 10.5 %collective-permute-start.8 = (bf16[256,256]{1,0:T(8,128)(2,1)S(1)}, bf16[256,256]{1,0:T(8,128)(2,1)S(1)}, u32[]{:S(2)}, u32[]{:S(2)}) collective-permute-start(bf16[256,256]{1,0:T(8,128)(2,1)S(1)} %get-tuple-element.31.refs_0_), channel_id=1, source_target_pairs={{0,2},{1,3},{2,0},{3,1},{4,6},{5,7},{6,4},{7,5},{8,10},{9,11},{10,... | collective-permute-start | bytes 393224 | tf_op jit(solution)/shard_map/ppermute | solution.py:287
  13.9 6.9 %collective-permute-start.2 = (bf16[256,256]{1,0:T(8,128)(2,1)S(1)}, bf16[256,256]{1,0:T(8,128)(2,1)S(1)}, u32[]{:S(2)}, u32[]{:S(2)}) collective-permute-start(bf16[256,256]{1,0:T(8,128)(2,1)S(1)} %collective-permute-done.refs_2_), channel_id=1, source_target_pairs={{0,1},{1,0},{2,3},{3,2},{4,5},{5,4},{6,7},{7,6},{8,9},{9,8},{10,11... | collective-permute-start | bytes 393224 | tf_op jit(solution)/shard_map/ppermute | solution.py:287
  14.0 13.2 %collective-permute-start.7 = (bf16[256,256]{1,0:T(8,128)(2,1)S(1)}, bf16[256,256]{1,0:T(8,128)(2,1)S(1)}, u32[]{:S(2)}, u32[]{:S(2)}) collective-permute-start(bf16[256,256]{1,0:T(8,128)(2,1)S(1)} %get-tuple-element.31.refs_0_), channel_id=1, source_target_pairs={{0,1},{1,0},{2,3},{3,2},{4,5},{5,4},{6,7},{7,6},{8,9},{9,8},{10,11... | collective-permute-start | bytes 393224 | tf_op jit(solution)/shard_map/ppermute | solution.py:287
  18.0 9.2 %collective-permute-start.9 = (bf16[256,256]{1,0:T(8,128)(2,1)S(1)}, bf16[256,256]{1,0:T(8,128)(2,1)S(1)}, u32[]{:S(2)}, u32[]{:S(2)}) collective-permute-start(bf16[256,256]{1,0:T(8,128)(2,1)S(1)} %collective-permute-done.8.refs_2_), channel_id=1, source_target_pairs={{0,1},{1,0},{2,3},{3,2},{4,5},{5,4},{6,7},{7,6},{8,9},{9,8},{10,11... | collective-permute-start | bytes 393224 | tf_op jit(solution)/shard_map/ppermute | solution.py:287
  21.5 2.0 %collective-permute-start.3 = (bf16[1024,256]{1,0:T(8,128)(2,1)S(1)}, bf16[1024,256]{1,0:T(8,128)(2,1)S(1)}, u32[]{:S(2)}, u32[]{:S(2)}) collective-permute-start(bf16[1024,256]{1,0:T(8,128)(2,1)S(1)} %shard_map.94), channel_id=1, source_target_pairs={{0,4},{4,0},{8,12},{12,8},{16,20},{20,16},{24,28},{28,24},{1,5},{5... | collective-permute-start | bytes 1572872 | tf_op jit(solution)/shard_map/ppermute | solution.py:287
  23.6 9.6 %collective-permute-start.4 = (bf16[256,256]{1,0:T(8,128)(2,1)S(1)}, bf16[256,256]{1,0:T(8,128)(2,1)S(1)}, u32[]{:S(2)}, u32[]{:S(2)}) collective-permute-start(bf16[256,256]{1,0:T(8,128)(2,1)S(1)} %get-tuple-element.27), channel_id=1, source_target_pairs={{0,8},{4,20},{8,0},{12,28},{16,24},{20,4},{24,16},{28,12},{1,9},{5... | collective-permute-start | bytes 393224 | tf_op jit(solution)/shard_map/ppermute | solution.py:294
  25.3 8.2 %collective-permute-start.5 = (bf16[256,256]{1,0:T(8,128)(2,1)S(1)}, bf16[256,256]{1,0:T(8,128)(2,1)S(1)}, u32[]{:S(2)}, u32[]{:S(2)}) collective-permute-start(bf16[256,256]{1,0:T(8,128)(2,1)S(1)} %get-tuple-element.28), channel_id=1, source_target_pairs={{0,16},{4,12},{8,24},{12,4},{16,0},{20,28},{24,8},{28,20},{1,17},{... | collective-permute-start | bytes 393224 | tf_op jit(solution)/shard_map/ppermute | solution.py:294
  26.8 6.7 %collective-permute-start.6 = (bf16[256,256]{1,0:T(8,128)(2,1)S(1)}, bf16[256,256]{1,0:T(8,128)(2,1)S(1)}, u32[]{:S(2)}, u32[]{:S(2)}) collective-permute-start(bf16[256,256]{1,0:T(8,128)(2,1)S(1)} %get-tuple-element.29), channel_id=1, source_target_pairs={{0,24},{4,28},{8,16},{12,20},{16,8},{20,12},{24,0},{28,4},{1,25},{... | collective-permute-start | bytes 393224 | tf_op jit(solution)/shard_map/ppermute | solution.py:294
  27.9 11.7 %copy-start = (f32[256]{0:T(256)S(1)}, f32[256]{0:T(256)}, u32[]{:S(2)}) copy-start(f32[256]{0:T(256)} %param.12) | copy-start | bytes 3076
  27.9 2.0 %collective-permute-start.10 = (bf16[1024,256]{1,0:T(8,128)(2,1)S(1)}, bf16[1024,256]{1,0:T(8,128)(2,1)S(1)}, u32[]{:S(2)}, u32[]{:S(2)}) collective-permute-start(bf16[1024,256]{1,0:T(8,128)(2,1)S(1)} %shard_map.97), channel_id=1, source_target_pairs={{0,4},{4,0},{8,12},{12,8},{16,20},{20,16},{24,28},{28,24},{1,5},{5... | collective-permute-start | bytes 1572872 | tf_op jit(solution)/shard_map/ppermute | solution.py:287
  30.0 6.0 %collective-permute-start.11 = (bf16[256,256]{1,0:T(8,128)(2,1)S(1)}, bf16[256,256]{1,0:T(8,128)(2,1)S(1)}, u32[]{:S(2)}, u32[]{:S(2)}) collective-permute-start(bf16[256,256]{1,0:T(8,128)(2,1)S(1)} %get-tuple-element.36), channel_id=1, source_target_pairs={{0,8},{4,20},{8,0},{12,28},{16,24},{20,4},{24,16},{28,12},{1,9},{5... | collective-permute-start | bytes 393224 | tf_op jit(solution)/shard_map/ppermute | solution.py:294
  31.7 6.9 %collective-permute-start.12 = (bf16[256,256]{1,0:T(8,128)(2,1)S(1)}, bf16[256,256]{1,0:T(8,128)(2,1)S(1)}, u32[]{:S(2)}, u32[]{:S(2)}) collective-permute-start(bf16[256,256]{1,0:T(8,128)(2,1)S(1)} %get-tuple-element.37), channel_id=1, source_target_pairs={{0,16},{4,12},{8,24},{12,4},{16,0},{20,28},{24,8},{28,20},{1,17},{... | collective-permute-start | bytes 393224 | tf_op jit(solution)/shard_map/ppermute | solution.py:294
  33.2 6.4 %collective-permute-start.13 = (bf16[256,256]{1,0:T(8,128)(2,1)S(1)}, bf16[256,256]{1,0:T(8,128)(2,1)S(1)}, u32[]{:S(2)}, u32[]{:S(2)}) collective-permute-start(bf16[256,256]{1,0:T(8,128)(2,1)S(1)} %get-tuple-element.38), channel_id=1, source_target_pairs={{0,24},{4,28},{8,16},{12,20},{16,8},{20,12},{24,0},{28,4},{1,25},{... | collective-permute-start | bytes 393224 | tf_op jit(solution)/shard_map/ppermute | solution.py:294

commit v12 on v10

--- a/solution.py
+++ b/solution.py
@@ -187,7 +187,7 @@
         in_specs=[VMEM] * 4,
         out_specs=VMEM,
         compiler_params=params(16),
-        cost_estimate=cost(20 * total * depth * width, 1),
+        cost_estimate=cost(total * depth * width, 1),
     )(matrix, own, beside, across)
 
 
@@ -240,28 +240,26 @@
     )(matrix, *blocks)
 
 
-def join_kernel(count, stay, *refs):
-    came, (kept, *sent) = refs[:count], refs[count:]
-    rows, part = kept.shape[0], came[0].shape[0]
-    for place, out in enumerate([kept] + sent):
-        start = place * rows
-        other = came[start // part][start % part : start % part + rows, :]
-        value = stay[start : start + rows, :] + other.astype(jnp.float32)
-        out[...] = value.astype(out.dtype)
+def join_kernel(stay, came, kept, *sent):
+    rows = kept.shape[0]
+    value = stay[...].astype(jnp.float32) + came[...].astype(jnp.float32)
+    kept[...] = value[:rows]
+    for place, out in enumerate(sent):
+        out[...] = value[(place + 1) * rows : (place + 2) * rows].astype(out.dtype)
 
 
 def join(stay, came, rows):
     total, width = stay.shape
     parts = total // rows
     return pl.pallas_call(
-        functools.partial(join_kernel, len(came)),
+        join_kernel,
         out_shape=[jax.ShapeDtypeStruct((rows, width), jnp.float32)]
         + [jax.ShapeDtypeStruct((rows, width), jnp.bfloat16)] * (parts - 1),
-        in_specs=[VMEM] * (1 + len(came)),
+        in_specs=[VMEM] * 2,
         out_specs=[VMEM] * parts,
         compiler_params=params(12),
         cost_estimate=cost(1, 1),
-    )(stay, *came)
+    )(stay, came)
 
 
 def finish_kernel(chunks, projected, norm, *refs):
@@ -379,23 +377,17 @@
     onward, matrix = lax.optimization_barrier((across[0], built))
     passed = swap(onward, "col", 1)
     early = early_product(matrix, scaled[0], beside[0], across[0])
-    away = [
-        late_product(matrix, early, passed, k * half // 2, half // 2, jnp.bfloat16, WEIGHTS[0])
-        for k in range(2)
-    ]
+    away = late_product(matrix, early, passed, 0, half, jnp.bfloat16, WEIGHTS[0])
     stay = late_product(matrix, early, passed, half, half, jnp.float32, WEIGHTS[1])
-    kept, *sent = join(stay, [swap(value, "row", 1) for value in away], own_rows)
+    kept, *sent = join(stay, swap(away, "row", 1), own_rows)
     pieces = [[kept] + exchange(sent)]
 
     onward, _ = lax.optimization_barrier((across[1], early))
     blocks = scaled[1], beside[1], swap(onward, "col", 1), across[1]
     blocks, _ = lax.optimization_barrier((blocks, sent))
-    away = [
-        product(matrix, blocks, k * half // 2, half // 2, jnp.bfloat16, WEIGHTS[2])
-        for k in range(2)
-    ]
+    away = product(matrix, blocks, 0, half, jnp.bfloat16, WEIGHTS[2])
     stay = product(matrix, blocks, half, half, jnp.float32, WEIGHTS[3])
-    kept, *sent = join(stay, [swap(value, "row", 1) for value in away], own_rows)
+    kept, *sent = join(stay, swap(away, "row", 1), own_rows)
     pieces.append([kept] + exchange(sent))
     return finish(projected, target_norm, pieces)
 

time: 41.8 us -> 38.9 us (0.931)
  waiting for transfers between devices: 12.6 us -> 11.2 us
  starting transfers between devices: 19.2 us -> 18.1 us
    ppermute x10 -> x8, waiting for transfers between devices: 6.59 us -> 5.14 us  [swap(): return lax.ppermute(value, axis, pairs)]
    ppermute x10 -> x8, starting transfers between devices: 12.1 us -> 11 us  [swap(): return lax.ppermute(value, axis, pairs)]
    pallas_call x3 -> x2, Pallas kernels: 1.6 us -> 1.43 us  [product(): pl.pallas_call(functools.partial(product_kernel, first), out_shape=jax.Sh...]
  transfers between devices with their start and end apart: 16 -> 14, of which waited for: 9 -> 8; matrix products, arithmetic and copies ran while one was open for 0% -> 0% of each run, Pallas kernels for 15% -> 15%
where the time goes in v12:
time: 38.9 us; the launch traced here: 38.8 us
  starting transfers between devices  18.1 us (47%)
  waiting for transfers between devices  11.2 us (29%)
  Pallas kernels  8.67 us (22%)
  between operations  0.75 us (2%)
    ppermute x8, starting transfers between devices, swap(): return lax.ppermute(value, axis, pairs)  11 us
    ppermute x6, starting transfers between devices, exchange(): lax.ppermute(value, 'row', [(i, i ^ step[i % 2]) for i in range(owners)])  7.11 us
    ppermute x6, waiting for transfers between devices, exchange(): lax.ppermute(value, 'row', [(i, i ^ step[i % 2]) for i in range(owners)])  6.06 us
    ppermute x8, waiting for transfers between devices, swap(): return lax.ppermute(value, axis, pairs)  5.14 us
    pallas_call x1, Pallas kernels, merge_tiles(): pl.pallas_call(functools.partial(merge_kernel, own_tiles, labels.shape[1]...  2.75 us
    pallas_call x1, Pallas kernels, project(): pl.pallas_call(project_kernel, out_shape=[jax.ShapeDtypeStruct((rows, hid...  1.82 us
    pallas_call x2, Pallas kernels, product(): pl.pallas_call(functools.partial(product_kernel, first), out_shape=jax.Sh...  1.43 us
    pallas_call x1, Pallas kernels, early_product(): pl.pallas_call(early_kernel, out_shape=jax.ShapeDtypeStruct((total, width...  0.99 us
  transfers between devices with their start and end apart: 14, of which 8 were waited for; matrix products, arithmetic and copies ran while one was open for 0% of the time, Pallas kernels for 15%

profile of v12, /device:TPU:0, one launch (start us, length us, event | category | flops | bytes accessed | tf_op | source)
XLA Modules:
  0.0 38.8 jit_solution(4025543064817027498)
XLA Ops:
  0.0 1.8 %shard_map.91 = (f32[256,512]{1,0:T(8,128)S(1)}, bf16[256,256]{1,0:T(8,128)(2,1)S(1)}, bf16[256,256]{1,0:T(8,128)(2,1)S(1)}) custom-call(bf16[256,1024]{1,0:T(8,128)(2,1)} %features_hbm.1, bf16[1024,512]{1,0:T(8,128)(2,1)} %weight_hbm.1, f32[2,128]{1,0:T(2,128)} %bitcast.5), custom_call_target="tpu_custom_call" | custom-call | flops 268435456 | bytes 1572864 | tf_op jit(solution)/shard_map/pallas_call | solution.py:65
  1.8 5.1 %collective-permute-start = (bf16[256,256]{1,0:T(8,128)(2,1)S(1)}, bf16[256,256]{1,0:T(8,128)(2,1)S(1)}, u32[]{:S(2)}, u32[]{:S(2)}) collective-permute-start(bf16[256,256]{1,0:T(8,128)(2,1)S(1)} %get-tuple-element.24.own), channel_id=1, source_target_pairs={{0,3},{1,2},{2,1},{3,0},{4,7},{5,6},{6,5},{7,4},{8,11},{9,10},{10,... | collective-permute-start | bytes 393224 | tf_op jit(solution)/shard_map/ppermute | solution.py:331
  6.9 0.9 %collective-permute-start.8 = (bf16[256,256]{1,0:T(8,128)(2,1)S(1)}, bf16[256,256]{1,0:T(8,128)(2,1)S(1)}, u32[]{:S(2)}, u32[]{:S(2)}) collective-permute-start(bf16[256,256]{1,0:T(8,128)(2,1)S(1)} %get-tuple-element.33.refs_0_), channel_id=1, source_target_pairs={{0,3},{1,2},{2,1},{3,0},{4,7},{5,6},{6,5},{7,4},{8,11},{9,10},{10,... | collective-permute-start | bytes 393224 | tf_op jit(solution)/shard_map/ppermute | solution.py:331
  8.5 2.8 %shard_map.92.matrix = bf16[2048,1024]{1,0:T(8,128)(2,1)S(1)} custom-call(s32[1]{0:T(128)} %bitcast.2.row, s32[1]{0:T(128)} %bitcast.3.column, s32[1]{0:T(128)S(6)} %copy.10.count, s32[1,64]{1,0:T(1,128)} %sources_hbm.1, s32[1,64]{1,0:T(1,128)} %targets_hbm.1, s32[1,16]{1,0:T(1,128)} %labels_hbm.1, bf16[1,64,128,128]{3,2,1,0:T(8,128)(2,1)} %tiles_hbm.1), custom_call_target="tpu_custom_call" | custom-call | flops 8388608 | bytes 12582912 | tf_op jit(solution)/shard_map/pallas_call | solution.py:150
  11.3 0.1 collective-permute-done.across
  11.3 3.4 %collective-permute-start.2 = (bf16[256,256]{1,0:T(8,128)(2,1)S(1)}, bf16[256,256]{1,0:T(8,128)(2,1)S(1)}, u32[]{:S(2)}, u32[]{:S(2)}) collective-permute-start(bf16[256,256]{1,0:T(8,128)(2,1)S(1)} %collective-permute-done.across), channel_id=1, source_target_pairs={{0,1},{1,0},{2,3},{3,2},{4,5},{5,4},{6,7},{7,6},{8,9},{9,8},{10,11... | collective-permute-start | bytes 393224 | tf_op jit(solution)/shard_map/ppermute | solution.py:331
  14.8 0.0 collective-permute-start.7
  14.8 1.4 %collective-permute-done.1.beside = bf16[256,256]{1,0:T(8,128)(2,1)S(1)} collective-permute-done((bf16[256,256]{1,0:T(8,128)(2,1)S(1)}, bf16[256,256]{1,0:T(8,128)(2,1)S(1)}, u32[]{:S(2)}, u32[]{:S(2)}) %collective-permute-start.1) | collective-permute-done | bytes 131104 | tf_op jit(solution)/shard_map/ppermute | solution.py:331
  16.2 1.0 %shard_map.93.early = f32[2048,256]{1,0:T(8,128)S(1)} custom-call(bf16[2048,1024]{1,0:T(8,128)(2,1)S(1)} %shard_map.92.matrix, bf16[256,256]{1,0:T(8,128)(2,1)S(1)} %get-tuple-element.24.own, bf16[256,256]{1,0:T(8,128)(2,1)S(1)} %collective-permute-done.1.beside, bf16[256,256]{1,0:T(8,128)(2,1)S(1)} %collective-permute-done.across), custom_call_target="tpu_custom_call" | custom-call | flops 536870912 | bytes 1 | tf_op jit(solution)/shard_map/pallas_call | solution.py:184
  17.2 1.4 %collective-permute-start.9 = (bf16[256,256]{1,0:T(8,128)(2,1)S(1)}, bf16[256,256]{1,0:T(8,128)(2,1)S(1)}, u32[]{:S(2)}, u32[]{:S(2)}) collective-permute-start(bf16[256,256]{1,0:T(8,128)(2,1)S(1)} %collective-permute-done.8.refs_3_), channel_id=1, source_target_pairs={{0,1},{1,0},{2,3},{3,2},{4,5},{5,4},{6,7},{7,6},{8,9},{9,8},{10,11... | collective-permute-start | bytes 393224 | tf_op jit(solution)/shard_map/ppermute | solution.py:331
  18.6 0.9 %collective-permute-done.2.passed = bf16[256,256]{1,0:T(8,128)(2,1)S(1)} collective-permute-done((bf16[256,256]{1,0:T(8,128)(2,1)S(1)}, bf16[256,256]{1,0:T(8,128)(2,1)S(1)}, u32[]{:S(2)}, u32[]{:S(2)}) %collective-permute-start.2) | collective-permute-done | bytes 131104 | tf_op jit(solution)/shard_map/ppermute | solution.py:331
  19.5 0.3 shard_map.95
  19.8 0.1 collective-permute-start.3
  19.9 0.3 shard_map.94.stay
  20.2 1.6 %collective-permute-done.3.came = bf16[1024,256]{1,0:T(8,128)(2,1)S(1)} collective-permute-done((bf16[1024,256]{1,0:T(8,128)(2,1)S(1)}, bf16[1024,256]{1,0:T(8,128)(2,1)S(1)}, u32[]{:S(2)}, u32[]{:S(2)}) %collective-permute-start.3) | collective-permute-done | bytes 524320 | tf_op jit(solution)/shard_map/ppermute | solution.py:331
  21.8 0.1 shard_map.96
  21.9 1.7 %collective-permute-start.4 = (bf16[256,256]{1,0:T(8,128)(2,1)S(1)}, bf16[256,256]{1,0:T(8,128)(2,1)S(1)}, u32[]{:S(2)}, u32[]{:S(2)}) collective-permute-start(bf16[256,256]{1,0:T(8,128)(2,1)S(1)} %get-tuple-element.28), channel_id=1, source_target_pairs={{0,8},{4,20},{8,0},{12,28},{16,24},{20,4},{24,16},{28,12},{1,9},{5... | collective-permute-start | bytes 393224 | tf_op jit(solution)/shard_map/ppermute | solution.py:338
  23.6 1.5 %collective-permute-start.5 = (bf16[256,256]{1,0:T(8,128)(2,1)S(1)}, bf16[256,256]{1,0:T(8,128)(2,1)S(1)}, u32[]{:S(2)}, u32[]{:S(2)}) collective-permute-start(bf16[256,256]{1,0:T(8,128)(2,1)S(1)} %get-tuple-element.29), channel_id=1, source_target_pairs={{0,16},{4,12},{8,24},{12,4},{16,0},{20,28},{24,8},{28,20},{1,17},{... | collective-permute-start | bytes 393224 | tf_op jit(solution)/shard_map/ppermute | solution.py:338
  25.2 0.3 collective-permute-start.6
  25.4 0.7 %shard_map.98 = bf16[1024,256]{1,0:T(8,128)(2,1)S(1)} custom-call(bf16[2048,1024]{1,0:T(8,128)(2,1)S(1)} %shard_map.92.matrix, bf16[256,256]{1,0:T(8,128)(2,1)S(1)} %get-tuple-element.33.refs_0_, bf16[256,256]{1,0:T(8,128)(2,1)S(1)} %collective-permute-done.7.refs_1_, bf16[256,256]{1,0:T(8,128)(2,1)S(1)} %collective-permute-done.9.refs_2_, ...), custom_call_target="tpu_custom_call" | custom-call | bytes 1 | tf_op jit(solution)/shard_map/pallas_call | solution.py:232
  26.2 0.0 copy-start
  26.2 0.1 collective-permute-start.10
  26.3 0.7 %shard_map.97.stay = f32[1024,256]{1,0:T(8,128)S(1)} custom-call(bf16[2048,1024]{1,0:T(8,128)(2,1)S(1)} %shard_map.92.matrix, bf16[256,256]{1,0:T(8,128)(2,1)S(1)} %get-tuple-element.33.refs_0_, bf16[256,256]{1,0:T(8,128)(2,1)S(1)} %collective-permute-done.7.refs_1_, bf16[256,256]{1,0:T(8,128)(2,1)S(1)} %collective-permute-done.9.refs_2_, ...), custom_call_target="tpu_custom_call" | custom-call | flops 10737418240 | bytes 1 | tf_op jit(solution)/shard_map/pallas_call | solution.py:232
  27.0 1.2 %collective-permute-done.10.came = bf16[1024,256]{1,0:T(8,128)(2,1)S(1)} collective-permute-done((bf16[1024,256]{1,0:T(8,128)(2,1)S(1)}, bf16[1024,256]{1,0:T(8,128)(2,1)S(1)}, u32[]{:S(2)}, u32[]{:S(2)}) %collective-permute-start.10) | collective-permute-done | bytes 524320 | tf_op jit(solution)/shard_map/ppermute | solution.py:331
  28.2 0.1 shard_map.99
  28.2 1.7 %collective-permute-start.11 = (bf16[256,256]{1,0:T(8,128)(2,1)S(1)}, bf16[256,256]{1,0:T(8,128)(2,1)S(1)}, u32[]{:S(2)}, u32[]{:S(2)}) collective-permute-start(bf16[256,256]{1,0:T(8,128)(2,1)S(1)} %get-tuple-element.38), channel_id=1, source_target_pairs={{0,8},{4,20},{8,0},{12,28},{16,24},{20,4},{24,16},{28,12},{1,9},{5... | collective-permute-start | bytes 393224 | tf_op jit(solution)/shard_map/ppermute | solution.py:338
  30.0 1.5 %collective-permute-start.12 = (bf16[256,256]{1,0:T(8,128)(2,1)S(1)}, bf16[256,256]{1,0:T(8,128)(2,1)S(1)}, u32[]{:S(2)}, u32[]{:S(2)}) collective-permute-start(bf16[256,256]{1,0:T(8,128)(2,1)S(1)} %get-tuple-element.39), channel_id=1, source_target_pairs={{0,16},{4,12},{8,24},{12,4},{16,0},{20,28},{24,8},{28,20},{1,17},{... | collective-permute-start | bytes 393224 | tf_op jit(solution)/shard_map/ppermute | solution.py:338
  31.5 0.3 collective-permute-start.13
  31.8 2.4 %collective-permute-done.11.refs_5_ = bf16[256,256]{1,0:T(8,128)(2,1)S(1)} collective-permute-done((bf16[256,256]{1,0:T(8,128)(2,1)S(1)}, bf16[256,256]{1,0:T(8,128)(2,1)S(1)}, u32[]{:S(2)}, u32[]{:S(2)}) %collective-permute-start.11) | collective-permute-done | bytes 131104 | tf_op jit(solution)/shard_map/ppermute | solution.py:338
  34.2 2.7 %collective-permute-done.12.refs_6_ = bf16[256,256]{1,0:T(8,128)(2,1)S(1)} collective-permute-done((bf16[256,256]{1,0:T(8,128)(2,1)S(1)}, bf16[256,256]{1,0:T(8,128)(2,1)S(1)}, u32[]{:S(2)}, u32[]{:S(2)}) %collective-permute-start.12) | collective-permute-done | bytes 131104 | tf_op jit(solution)/shard_map/ppermute | solution.py:338
  36.8 1.0 %collective-permute-done.13.refs_7_ = bf16[256,256]{1,0:T(8,128)(2,1)S(1)} collective-permute-done((bf16[256,256]{1,0:T(8,128)(2,1)S(1)}, bf16[256,256]{1,0:T(8,128)(2,1)S(1)}, u32[]{:S(2)}, u32[]{:S(2)}) %collective-permute-start.13) | collective-permute-done | bytes 131104 | tf_op jit(solution)/shard_map/ppermute | solution.py:338
  37.9 0.9 %shard_map.100 = bf16[256,512]{1,0:T(8,128)(2,1)} custom-call(f32[256,512]{1,0:T(8,128)S(1)} %get-tuple-element.23.projected, f32[2,128]{1,0:T(2,128)S(1)} %bitcast.4, f32[256,256]{1,0:T(8,128)S(1)} %get-tuple-element.27.refs_0_, bf16[256,256]{1,0:T(8,128)(2,1)S(1)} %collective-permute-done.4.refs_1_, bf16[256,256]{1,0:T(8,128)(2,1)S(1)} %collective-permute-done.5.refs_2_, ...), custom_call_target="tpu_custom_call" | custom-call | flops 786432 | bytes 2097152 | tf_op jit(solution)/shard_map/pallas_call | solution.py:285
  (8 shorter events, 0.0 us)
Async XLA Ops:
  1.8 9.5 %collective-permute-start = (bf16[256,256]{1,0:T(8,128)(2,1)S(1)}, bf16[256,256]{1,0:T(8,128)(2,1)S(1)}, u32[]{:S(2)}, u32[]{:S(2)}) collective-permute-start(bf16[256,256]{1,0:T(8,128)(2,1)S(1)} %get-tuple-element.24.own), channel_id=1, source_target_pairs={{0,3},{1,2},{2,1},{3,0},{4,7},{5,6},{6,5},{7,4},{8,11},{9,10},{10,... | collective-permute-start | bytes 393224 | tf_op jit(solution)/shard_map/ppermute | solution.py:331
  6.9 9.2 %collective-permute-start.1 = (bf16[256,256]{1,0:T(8,128)(2,1)S(1)}, bf16[256,256]{1,0:T(8,128)(2,1)S(1)}, u32[]{:S(2)}, u32[]{:S(2)}) collective-permute-start(bf16[256,256]{1,0:T(8,128)(2,1)S(1)} %get-tuple-element.24.own), channel_id=1, source_target_pairs={{0,1},{1,0},{2,3},{3,2},{4,5},{5,4},{6,7},{7,6},{8,9},{9,8},{10,11... | collective-permute-start | bytes 393224 | tf_op jit(solution)/shard_map/ppermute | solution.py:331
  6.9 10.2 %collective-permute-start.8 = (bf16[256,256]{1,0:T(8,128)(2,1)S(1)}, bf16[256,256]{1,0:T(8,128)(2,1)S(1)}, u32[]{:S(2)}, u32[]{:S(2)}) collective-permute-start(bf16[256,256]{1,0:T(8,128)(2,1)S(1)} %get-tuple-element.33.refs_0_), channel_id=1, source_target_pairs={{0,3},{1,2},{2,1},{3,0},{4,7},{5,6},{6,5},{7,4},{8,11},{9,10},{10,... | collective-permute-start | bytes 393224 | tf_op jit(solution)/shard_map/ppermute | solution.py:331
  11.3 8.2 %collective-permute-start.2 = (bf16[256,256]{1,0:T(8,128)(2,1)S(1)}, bf16[256,256]{1,0:T(8,128)(2,1)S(1)}, u32[]{:S(2)}, u32[]{:S(2)}) collective-permute-start(bf16[256,256]{1,0:T(8,128)(2,1)S(1)} %collective-permute-done.across), channel_id=1, source_target_pairs={{0,1},{1,0},{2,3},{3,2},{4,5},{5,4},{6,7},{7,6},{8,9},{9,8},{10,11... | collective-permute-start | bytes 393224 | tf_op jit(solution)/shard_map/ppermute | solution.py:331
  14.8 10.7 %collective-permute-start.7 = (bf16[256,256]{1,0:T(8,128)(2,1)S(1)}, bf16[256,256]{1,0:T(8,128)(2,1)S(1)}, u32[]{:S(2)}, u32[]{:S(2)}) collective-permute-start(bf16[256,256]{1,0:T(8,128)(2,1)S(1)} %get-tuple-element.33.refs_0_), channel_id=1, source_target_pairs={{0,1},{1,0},{2,3},{3,2},{4,5},{5,4},{6,7},{7,6},{8,9},{9,8},{10,11... | collective-permute-start | bytes 393224 | tf_op jit(solution)/shard_map/ppermute | solution.py:331
  17.2 8.3 %collective-permute-start.9 = (bf16[256,256]{1,0:T(8,128)(2,1)S(1)}, bf16[256,256]{1,0:T(8,128)(2,1)S(1)}, u32[]{:S(2)}, u32[]{:S(2)}) collective-permute-start(bf16[256,256]{1,0:T(8,128)(2,1)S(1)} %collective-permute-done.8.refs_3_), channel_id=1, source_target_pairs={{0,1},{1,0},{2,3},{3,2},{4,5},{5,4},{6,7},{7,6},{8,9},{9,8},{10,11... | collective-permute-start | bytes 393224 | tf_op jit(solution)/shard_map/ppermute | solution.py:331
  19.8 2.0 %collective-permute-start.3 = (bf16[1024,256]{1,0:T(8,128)(2,1)S(1)}, bf16[1024,256]{1,0:T(8,128)(2,1)S(1)}, u32[]{:S(2)}, u32[]{:S(2)}) collective-permute-start(bf16[1024,256]{1,0:T(8,128)(2,1)S(1)} %shard_map.95), channel_id=1, source_target_pairs={{0,4},{4,0},{8,12},{12,8},{16,20},{20,16},{24,28},{28,24},{1,5},{5... | collective-permute-start | bytes 1572872 | tf_op jit(solution)/shard_map/ppermute | solution.py:331
  21.9 9.6 %collective-permute-start.4 = (bf16[256,256]{1,0:T(8,128)(2,1)S(1)}, bf16[256,256]{1,0:T(8,128)(2,1)S(1)}, u32[]{:S(2)}, u32[]{:S(2)}) collective-permute-start(bf16[256,256]{1,0:T(8,128)(2,1)S(1)} %get-tuple-element.28), channel_id=1, source_target_pairs={{0,8},{4,20},{8,0},{12,28},{16,24},{20,4},{24,16},{28,12},{1,9},{5... | collective-permute-start | bytes 393224 | tf_op jit(solution)/shard_map/ppermute | solution.py:338
  23.6 8.2 %collective-permute-start.5 = (bf16[256,256]{1,0:T(8,128)(2,1)S(1)}, bf16[256,256]{1,0:T(8,128)(2,1)S(1)}, u32[]{:S(2)}, u32[]{:S(2)}) collective-permute-start(bf16[256,256]{1,0:T(8,128)(2,1)S(1)} %get-tuple-element.29), channel_id=1, source_target_pairs={{0,16},{4,12},{8,24},{12,4},{16,0},{20,28},{24,8},{28,20},{1,17},{... | collective-permute-start | bytes 393224 | tf_op jit(solution)/shard_map/ppermute | solution.py:338
  25.2 6.6 %collective-permute-start.6 = (bf16[256,256]{1,0:T(8,128)(2,1)S(1)}, bf16[256,256]{1,0:T(8,128)(2,1)S(1)}, u32[]{:S(2)}, u32[]{:S(2)}) collective-permute-start(bf16[256,256]{1,0:T(8,128)(2,1)S(1)} %get-tuple-element.30), channel_id=1, source_target_pairs={{0,24},{4,28},{8,16},{12,20},{16,8},{20,12},{24,0},{28,4},{1,25},{... | collective-permute-start | bytes 393224 | tf_op jit(solution)/shard_map/ppermute | solution.py:338
  26.2 11.7 %copy-start = (f32[256]{0:T(256)S(1)}, f32[256]{0:T(256)}, u32[]{:S(2)}) copy-start(f32[256]{0:T(256)} %param.12) | copy-start | bytes 3076
  26.2 2.0 %collective-permute-start.10 = (bf16[1024,256]{1,0:T(8,128)(2,1)S(1)}, bf16[1024,256]{1,0:T(8,128)(2,1)S(1)}, u32[]{:S(2)}, u32[]{:S(2)}) collective-permute-start(bf16[1024,256]{1,0:T(8,128)(2,1)S(1)} %shard_map.98), channel_id=1, source_target_pairs={{0,4},{4,0},{8,12},{12,8},{16,20},{20,16},{24,28},{28,24},{1,5},{5... | collective-permute-start | bytes 1572872 | tf_op jit(solution)/shard_map/ppermute | solution.py:331
  28.2 5.9 %collective-permute-start.11 = (bf16[256,256]{1,0:T(8,128)(2,1)S(1)}, bf16[256,256]{1,0:T(8,128)(2,1)S(1)}, u32[]{:S(2)}, u32[]{:S(2)}) collective-permute-start(bf16[256,256]{1,0:T(8,128)(2,1)S(1)} %get-tuple-element.38), channel_id=1, source_target_pairs={{0,8},{4,20},{8,0},{12,28},{16,24},{20,4},{24,16},{28,12},{1,9},{5... | collective-permute-start | bytes 393224 | tf_op jit(solution)/shard_map/ppermute | solution.py:338
  30.0 6.9 %collective-permute-start.12 = (bf16[256,256]{1,0:T(8,128)(2,1)S(1)}, bf16[256,256]{1,0:T(8,128)(2,1)S(1)}, u32[]{:S(2)}, u32[]{:S(2)}) collective-permute-start(bf16[256,256]{1,0:T(8,128)(2,1)S(1)} %get-tuple-element.39), channel_id=1, source_target_pairs={{0,16},{4,12},{8,24},{12,4},{16,0},{20,28},{24,8},{28,20},{1,17},{... | collective-permute-start | bytes 393224 | tf_op jit(solution)/shard_map/ppermute | solution.py:338
  31.5 6.3 %collective-permute-start.13 = (bf16[256,256]{1,0:T(8,128)(2,1)S(1)}, bf16[256,256]{1,0:T(8,128)(2,1)S(1)}, u32[]{:S(2)}, u32[]{:S(2)}) collective-permute-start(bf16[256,256]{1,0:T(8,128)(2,1)S(1)} %get-tuple-element.40), channel_id=1, source_target_pairs={{0,24},{4,28},{8,16},{12,20},{16,8},{20,12},{24,0},{28,4},{1,25},{... | collective-permute-start | bytes 393224 | tf_op jit(solution)/shard_map/ppermute | solution.py:338

commit v13 on v12

--- a/solution.py
+++ b/solution.py
@@ -331,13 +331,9 @@
     return lax.ppermute(value, axis, pairs)
 
 
-def exchange(sent):
-    owners = lax.axis_size("row")
-    steps = [(2, 4), (4, 2), (6, 6)]
-    return [
-        lax.ppermute(value, "row", [(i, i ^ step[i % 2]) for i in range(owners)])
-        for value, step in zip(sent, steps)
-    ]
+def exchange(value, k):
+    step = [(2, 4), (4, 2), (6, 6)][k]
+    return lax.ppermute(value, "row", [(i, i ^ step[i % 2]) for i in range(lax.axis_size("row"))])
 
 
 def per_device(
@@ -380,15 +376,17 @@
     away = late_product(matrix, early, passed, 0, half, jnp.bfloat16, WEIGHTS[0])
     stay = late_product(matrix, early, passed, half, half, jnp.float32, WEIGHTS[1])
     kept, *sent = join(stay, swap(away, "row", 1), own_rows)
-    pieces = [[kept] + exchange(sent)]
+    pieces = [[kept, exchange(sent[0], 0)]]
 
     onward, _ = lax.optimization_barrier((across[1], early))
     blocks = scaled[1], beside[1], swap(onward, "col", 1), across[1]
     blocks, _ = lax.optimization_barrier((blocks, sent))
     away = product(matrix, blocks, 0, half, jnp.bfloat16, WEIGHTS[2])
+    sent, away = lax.optimization_barrier((sent, away))
+    pieces[0] += [exchange(sent[k], k) for k in (1, 2)]
     stay = product(matrix, blocks, half, half, jnp.float32, WEIGHTS[3])
     kept, *sent = join(stay, swap(away, "row", 1), own_rows)
-    pieces.append([kept] + exchange(sent))
+    pieces.append([kept] + [exchange(value, k) for k, value in enumerate(sent)])
     return finish(projected, target_norm, pieces)
 
 

time: 38.9 us -> 41.2 us (1.059)
  starting transfers between devices: 18.1 us -> 19.3 us
  waiting for transfers between devices: 11.2 us -> 12.2 us
    ppermute x6, waiting for transfers between devices: 6.06 us -> 7.31 us  [exchange(): lax.ppermute(value, 'row', [(i, i ^ step[i % 2]) for i in range(lax.axis_...]
    ppermute x6, starting transfers between devices: 7.11 us -> 8.31 us  [exchange(): lax.ppermute(value, 'row', [(i, i ^ step[i % 2]) for i in range(lax.axis_...]
  transfers between devices with their start and end apart: 14 -> 14, of which waited for: 8 -> 9; matrix products, arithmetic and copies ran while one was open for 0% -> 0% of each run, Pallas kernels for 15% -> 15%
where the time goes in v13:
time: 41.2 us; the launch traced here: 41 us
  starting transfers between devices  19.3 us (47%)
  waiting for transfers between devices  12.2 us (30%)
  Pallas kernels  8.68 us (21%)
  between operations  0.75 us (2%)
    ppermute x8, starting transfers between devices, swap(): return lax.ppermute(value, axis, pairs)  11 us
    ppermute x6, starting transfers between devices, exchange(): lax.ppermute(value, 'row', [(i, i ^ step[i % 2]) for i in range(lax.axis_...  8.31 us
    ppermute x6, waiting for transfers between devices, exchange(): lax.ppermute(value, 'row', [(i, i ^ step[i % 2]) for i in range(lax.axis_...  7.31 us
    ppermute x8, waiting for transfers between devices, swap(): return lax.ppermute(value, axis, pairs)  4.92 us
    pallas_call x1, Pallas kernels, merge_tiles(): pl.pallas_call(functools.partial(merge_kernel, own_tiles, labels.shape[1]...  2.76 us
    pallas_call x1, Pallas kernels, project(): pl.pallas_call(project_kernel, out_shape=[jax.ShapeDtypeStruct((rows, hid...  1.82 us
    pallas_call x2, Pallas kernels, product(): pl.pallas_call(functools.partial(product_kernel, first), out_shape=jax.Sh...  1.42 us
    pallas_call x1, Pallas kernels, early_product(): pl.pallas_call(early_kernel, out_shape=jax.ShapeDtypeStruct((total, width...  0.99 us
  transfers between devices with their start and end apart: 14, of which 9 were waited for; matrix products, arithmetic and copies ran while one was open for 0% of the time, Pallas kernels for 15%

profile of v13, /device:TPU:0, one launch (start us, length us, event | category | flops | bytes accessed | tf_op | source)
XLA Modules:
  0.0 41.0 jit_solution(6475878745958959792)
XLA Ops:
  0.0 1.8 %shard_map.91 = (f32[256,512]{1,0:T(8,128)S(1)}, bf16[256,256]{1,0:T(8,128)(2,1)S(1)}, bf16[256,256]{1,0:T(8,128)(2,1)S(1)}) custom-call(bf16[256,1024]{1,0:T(8,128)(2,1)} %features_hbm.1, bf16[1024,512]{1,0:T(8,128)(2,1)} %weight_hbm.1, f32[2,128]{1,0:T(2,128)} %bitcast.5), custom_call_target="tpu_custom_call" | custom-call | flops 268435456 | bytes 1572864 | tf_op jit(solution)/shard_map/pallas_call | solution.py:65
  1.8 5.1 %collective-permute-start = (bf16[256,256]{1,0:T(8,128)(2,1)S(1)}, bf16[256,256]{1,0:T(8,128)(2,1)S(1)}, u32[]{:S(2)}, u32[]{:S(2)}) collective-permute-start(bf16[256,256]{1,0:T(8,128)(2,1)S(1)} %get-tuple-element.27.own), channel_id=1, source_target_pairs={{0,3},{1,2},{2,1},{3,0},{4,7},{5,6},{6,5},{7,4},{8,11},{9,10},{10,... | collective-permute-start | bytes 393224 | tf_op jit(solution)/shard_map/ppermute | solution.py:331
  6.9 0.9 %collective-permute-start.6 = (bf16[256,256]{1,0:T(8,128)(2,1)S(1)}, bf16[256,256]{1,0:T(8,128)(2,1)S(1)}, u32[]{:S(2)}, u32[]{:S(2)}) collective-permute-start(bf16[256,256]{1,0:T(8,128)(2,1)S(1)} %get-tuple-element.36.refs_0_), channel_id=1, source_target_pairs={{0,3},{1,2},{2,1},{3,0},{4,7},{5,6},{6,5},{7,4},{8,11},{9,10},{10,... | collective-permute-start | bytes 393224 | tf_op jit(solution)/shard_map/ppermute | solution.py:331
  8.5 2.8 %shard_map.92.matrix = bf16[2048,1024]{1,0:T(8,128)(2,1)S(1)} custom-call(s32[1]{0:T(128)} %bitcast.2.row, s32[1]{0:T(128)} %bitcast.3.column, s32[1]{0:T(128)S(6)} %copy.10.count, s32[1,64]{1,0:T(1,128)} %sources_hbm.1, s32[1,64]{1,0:T(1,128)} %targets_hbm.1, s32[1,16]{1,0:T(1,128)} %labels_hbm.1, bf16[1,64,128,128]{3,2,1,0:T(8,128)(2,1)} %tiles_hbm.1), custom_call_target="tpu_custom_call" | custom-call | flops 8388608 | bytes 12582912 | tf_op jit(solution)/shard_map/pallas_call | solution.py:150
  11.3 0.1 collective-permute-done.across
  11.3 3.4 %collective-permute-start.2 = (bf16[256,256]{1,0:T(8,128)(2,1)S(1)}, bf16[256,256]{1,0:T(8,128)(2,1)S(1)}, u32[]{:S(2)}, u32[]{:S(2)}) collective-permute-start(bf16[256,256]{1,0:T(8,128)(2,1)S(1)} %collective-permute-done.across), channel_id=1, source_target_pairs={{0,1},{1,0},{2,3},{3,2},{4,5},{5,4},{6,7},{7,6},{8,9},{9,8},{10,11... | collective-permute-start | bytes 393224 | tf_op jit(solution)/shard_map/ppermute | solution.py:331
  14.8 0.0 collective-permute-start.5
  14.8 1.4 %collective-permute-done.1.beside = bf16[256,256]{1,0:T(8,128)(2,1)S(1)} collective-permute-done((bf16[256,256]{1,0:T(8,128)(2,1)S(1)}, bf16[256,256]{1,0:T(8,128)(2,1)S(1)}, u32[]{:S(2)}, u32[]{:S(2)}) %collective-permute-start.1) | collective-permute-done | bytes 131104 | tf_op jit(solution)/shard_map/ppermute | solution.py:331
  16.2 1.0 %shard_map.93.early = f32[2048,256]{1,0:T(8,128)S(1)} custom-call(bf16[2048,1024]{1,0:T(8,128)(2,1)S(1)} %shard_map.92.matrix, bf16[256,256]{1,0:T(8,128)(2,1)S(1)} %get-tuple-element.27.own, bf16[256,256]{1,0:T(8,128)(2,1)S(1)} %collective-permute-done.1.beside, bf16[256,256]{1,0:T(8,128)(2,1)S(1)} %collective-permute-done.across), custom_call_target="tpu_custom_call" | custom-call | flops 536870912 | bytes 1 | tf_op jit(solution)/shard_map/pallas_call | solution.py:184
  17.2 1.4 %collective-permute-start.7 = (bf16[256,256]{1,0:T(8,128)(2,1)S(1)}, bf16[256,256]{1,0:T(8,128)(2,1)S(1)}, u32[]{:S(2)}, u32[]{:S(2)}) collective-permute-start(bf16[256,256]{1,0:T(8,128)(2,1)S(1)} %collective-permute-done.6.refs_3_), channel_id=1, source_target_pairs={{0,1},{1,0},{2,3},{3,2},{4,5},{5,4},{6,7},{7,6},{8,9},{9,8},{10,11... | collective-permute-start | bytes 393224 | tf_op jit(solution)/shard_map/ppermute | solution.py:331
  18.6 0.9 %collective-permute-done.2.passed = bf16[256,256]{1,0:T(8,128)(2,1)S(1)} collective-permute-done((bf16[256,256]{1,0:T(8,128)(2,1)S(1)}, bf16[256,256]{1,0:T(8,128)(2,1)S(1)}, u32[]{:S(2)}, u32[]{:S(2)}) %collective-permute-start.2) | collective-permute-done | bytes 131104 | tf_op jit(solution)/shard_map/ppermute | solution.py:331
  19.5 0.3 shard_map.95
  19.8 0.1 collective-permute-start.3
  19.9 0.3 shard_map.94.stay
  20.2 1.6 %collective-permute-done.3.came = bf16[1024,256]{1,0:T(8,128)(2,1)S(1)} collective-permute-done((bf16[1024,256]{1,0:T(8,128)(2,1)S(1)}, bf16[1024,256]{1,0:T(8,128)(2,1)S(1)}, u32[]{:S(2)}, u32[]{:S(2)}) %collective-permute-start.3) | collective-permute-done | bytes 524320 | tf_op jit(solution)/shard_map/ppermute | solution.py:331
  21.8 0.1 shard_map.96
  21.9 1.7 %collective-permute-start.4 = (bf16[256,256]{1,0:T(8,128)(2,1)S(1)}, bf16[256,256]{1,0:T(8,128)(2,1)S(1)}, u32[]{:S(2)}, u32[]{:S(2)}) collective-permute-start(bf16[256,256]{1,0:T(8,128)(2,1)S(1)} %get-tuple-element.31), channel_id=1, source_target_pairs={{0,8},{4,20},{8,0},{12,28},{16,24},{20,4},{24,16},{28,12},{1,9},{5... | collective-permute-start | bytes 393224 | tf_op jit(solution)/shard_map/ppermute | solution.py:336
  23.6 1.0 %collective-permute-done.7.refs_2_ = bf16[256,256]{1,0:T(8,128)(2,1)S(1)} collective-permute-done((bf16[256,256]{1,0:T(8,128)(2,1)S(1)}, bf16[256,256]{1,0:T(8,128)(2,1)S(1)}, u32[]{:S(2)}, u32[]{:S(2)}) %collective-permute-start.7) | collective-permute-done | bytes 131104 | tf_op jit(solution)/shard_map/ppermute | solution.py:331
  24.6 0.7 %shard_map.97 = bf16[1024,256]{1,0:T(8,128)(2,1)S(1)} custom-call(bf16[2048,1024]{1,0:T(8,128)(2,1)S(1)} %shard_map.92.matrix, bf16[256,256]{1,0:T(8,128)(2,1)S(1)} %get-tuple-element.36.refs_0_, bf16[256,256]{1,0:T(8,128)(2,1)S(1)} %collective-permute-done.5.refs_1_, bf16[256,256]{1,0:T(8,128)(2,1)S(1)} %collective-permute-done.7.refs_2_, ...), custom_call_target="tpu_custom_call" | custom-call | bytes 1 | tf_op jit(solution)/shard_map/pallas_call | solution.py:232
  25.3 0.1 collective-permute-start.10
  25.4 0.7 %shard_map.98.stay = f32[1024,256]{1,0:T(8,128)S(1)} custom-call(bf16[2048,1024]{1,0:T(8,128)(2,1)S(1)} %shard_map.92.matrix, bf16[256,256]{1,0:T(8,128)(2,1)S(1)} %get-tuple-element.36.refs_0_, bf16[256,256]{1,0:T(8,128)(2,1)S(1)} %collective-permute-done.5.refs_1_, bf16[256,256]{1,0:T(8,128)(2,1)S(1)} %collective-permute-done.7.refs_2_, ...), custom_call_target="tpu_custom_call" | custom-call | flops 10737418240 | bytes 1 | tf_op jit(solution)/shard_map/pallas_call | solution.py:232
  26.1 1.6 %collective-permute-start.8 = (bf16[256,256]{1,0:T(8,128)(2,1)S(1)}, bf16[256,256]{1,0:T(8,128)(2,1)S(1)}, u32[]{:S(2)}, u32[]{:S(2)}) collective-permute-start(bf16[256,256]{1,0:T(8,128)(2,1)S(1)} %get-tuple-element.40), channel_id=1, source_target_pairs={{0,16},{4,12},{8,24},{12,4},{16,0},{20,28},{24,8},{28,20},{1,17},{... | collective-permute-start | bytes 393224 | tf_op jit(solution)/shard_map/ppermute | solution.py:336
  27.7 1.4 %collective-permute-start.9 = (bf16[256,256]{1,0:T(8,128)(2,1)S(1)}, bf16[256,256]{1,0:T(8,128)(2,1)S(1)}, u32[]{:S(2)}, u32[]{:S(2)}) collective-permute-start(bf16[256,256]{1,0:T(8,128)(2,1)S(1)} %get-tuple-element.41), channel_id=1, source_target_pairs={{0,24},{4,28},{8,16},{12,20},{16,8},{20,12},{24,0},{28,4},{1,25},{... | collective-permute-start | bytes 393224 | tf_op jit(solution)/shard_map/ppermute | solution.py:336
  29.1 0.1 shard_map.99
  29.2 0.6 %collective-permute-start.11 = (bf16[256,256]{1,0:T(8,128)(2,1)S(1)}, bf16[256,256]{1,0:T(8,128)(2,1)S(1)}, u32[]{:S(2)}, u32[]{:S(2)}) collective-permute-start(bf16[256,256]{1,0:T(8,128)(2,1)S(1)} %get-tuple-element.44), channel_id=1, source_target_pairs={{0,8},{4,20},{8,0},{12,28},{16,24},{20,4},{24,16},{28,12},{1,9},{5... | collective-permute-start | bytes 393224 | tf_op jit(solution)/shard_map/ppermute | solution.py:336
  29.8 1.5 %collective-permute-start.12 = (bf16[256,256]{1,0:T(8,128)(2,1)S(1)}, bf16[256,256]{1,0:T(8,128)(2,1)S(1)}, u32[]{:S(2)}, u32[]{:S(2)}) collective-permute-start(bf16[256,256]{1,0:T(8,128)(2,1)S(1)} %get-tuple-element.45), channel_id=1, source_target_pairs={{0,16},{4,12},{8,24},{12,4},{16,0},{20,28},{24,8},{28,20},{1,17},{... | collective-permute-start | bytes 393224 | tf_op jit(solution)/shard_map/ppermute | solution.py:336
  31.4 1.4 %collective-permute-start.13 = (bf16[256,256]{1,0:T(8,128)(2,1)S(1)}, bf16[256,256]{1,0:T(8,128)(2,1)S(1)}, u32[]{:S(2)}, u32[]{:S(2)}) collective-permute-start(bf16[256,256]{1,0:T(8,128)(2,1)S(1)} %get-tuple-element.46), channel_id=1, source_target_pairs={{0,24},{4,28},{8,16},{12,20},{16,8},{20,12},{24,0},{28,4},{1,25},{... | collective-permute-start | bytes 393224 | tf_op jit(solution)/shard_map/ppermute | solution.py:336
  32.8 2.3 %collective-permute-done.9.refs_3_ = bf16[256,256]{1,0:T(8,128)(2,1)S(1)} collective-permute-done((bf16[256,256]{1,0:T(8,128)(2,1)S(1)}, bf16[256,256]{1,0:T(8,128)(2,1)S(1)}, u32[]{:S(2)}, u32[]{:S(2)}) %collective-permute-start.9) | collective-permute-done | bytes 131104 | tf_op jit(solution)/shard_map/ppermute | solution.py:336
  35.1 1.6 %collective-permute-done.11.refs_5_ = bf16[256,256]{1,0:T(8,128)(2,1)S(1)} collective-permute-done((bf16[256,256]{1,0:T(8,128)(2,1)S(1)}, bf16[256,256]{1,0:T(8,128)(2,1)S(1)}, u32[]{:S(2)}, u32[]{:S(2)}) %collective-permute-start.11) | collective-permute-done | bytes 131104 | tf_op jit(solution)/shard_map/ppermute | solution.py:336
  36.6 1.2 %collective-permute-done.12.refs_6_ = bf16[256,256]{1,0:T(8,128)(2,1)S(1)} collective-permute-done((bf16[256,256]{1,0:T(8,128)(2,1)S(1)}, bf16[256,256]{1,0:T(8,128)(2,1)S(1)}, u32[]{:S(2)}, u32[]{:S(2)}) %collective-permute-start.12) | collective-permute-done | bytes 131104 | tf_op jit(solution)/shard_map/ppermute | solution.py:336
  37.8 2.3 %collective-permute-done.13.refs_7_ = bf16[256,256]{1,0:T(8,128)(2,1)S(1)} collective-permute-done((bf16[256,256]{1,0:T(8,128)(2,1)S(1)}, bf16[256,256]{1,0:T(8,128)(2,1)S(1)}, u32[]{:S(2)}, u32[]{:S(2)}) %collective-permute-start.13) | collective-permute-done | bytes 131104 | tf_op jit(solution)/shard_map/ppermute | solution.py:336
  40.1 0.9 %shard_map.100 = bf16[256,512]{1,0:T(8,128)(2,1)} custom-call(f32[256,512]{1,0:T(8,128)S(1)} %get-tuple-element.26.projected, f32[2,128]{1,0:T(2,128)S(1)} %bitcast.4, f32[256,256]{1,0:T(8,128)S(1)} %get-tuple-element.30.refs_0_, bf16[256,256]{1,0:T(8,128)(2,1)S(1)} %collective-permute-done.4.refs_1_, bf16[256,256]{1,0:T(8,128)(2,1)S(1)} %collective-permute-done.8.refs_2_, ...), custom_call_target="tpu_custom_call" | custom-call | flops 786432 | bytes 2097152 | tf_op jit(solution)/shard_map/pallas_call | solution.py:285
  (8 shorter events, 0.0 us)
Async XLA Ops:
  1.8 9.5 %collective-permute-start = (bf16[256,256]{1,0:T(8,128)(2,1)S(1)}, bf16[256,256]{1,0:T(8,128)(2,1)S(1)}, u32[]{:S(2)}, u32[]{:S(2)}) collective-permute-start(bf16[256,256]{1,0:T(8,128)(2,1)S(1)} %get-tuple-element.27.own), channel_id=1, source_target_pairs={{0,3},{1,2},{2,1},{3,0},{4,7},{5,6},{6,5},{7,4},{8,11},{9,10},{10,... | collective-permute-start | bytes 393224 | tf_op jit(solution)/shard_map/ppermute | solution.py:331
  6.9 9.2 %collective-permute-start.1 = (bf16[256,256]{1,0:T(8,128)(2,1)S(1)}, bf16[256,256]{1,0:T(8,128)(2,1)S(1)}, u32[]{:S(2)}, u32[]{:S(2)}) collective-permute-start(bf16[256,256]{1,0:T(8,128)(2,1)S(1)} %get-tuple-element.27.own), channel_id=1, source_target_pairs={{0,1},{1,0},{2,3},{3,2},{4,5},{5,4},{6,7},{7,6},{8,9},{9,8},{10,11... | collective-permute-start | bytes 393224 | tf_op jit(solution)/shard_map/ppermute | solution.py:331
  6.9 10.2 %collective-permute-start.6 = (bf16[256,256]{1,0:T(8,128)(2,1)S(1)}, bf16[256,256]{1,0:T(8,128)(2,1)S(1)}, u32[]{:S(2)}, u32[]{:S(2)}) collective-permute-start(bf16[256,256]{1,0:T(8,128)(2,1)S(1)} %get-tuple-element.36.refs_0_), channel_id=1, source_target_pairs={{0,3},{1,2},{2,1},{3,0},{4,7},{5,6},{6,5},{7,4},{8,11},{9,10},{10,... | collective-permute-start | bytes 393224 | tf_op jit(solution)/shard_map/ppermute | solution.py:331
  11.3 8.2 %collective-permute-start.2 = (bf16[256,256]{1,0:T(8,128)(2,1)S(1)}, bf16[256,256]{1,0:T(8,128)(2,1)S(1)}, u32[]{:S(2)}, u32[]{:S(2)}) collective-permute-start(bf16[256,256]{1,0:T(8,128)(2,1)S(1)} %collective-permute-done.across), channel_id=1, source_target_pairs={{0,1},{1,0},{2,3},{3,2},{4,5},{5,4},{6,7},{7,6},{8,9},{9,8},{10,11... | collective-permute-start | bytes 393224 | tf_op jit(solution)/shard_map/ppermute | solution.py:331
  14.8 8.9 %collective-permute-start.5 = (bf16[256,256]{1,0:T(8,128)(2,1)S(1)}, bf16[256,256]{1,0:T(8,128)(2,1)S(1)}, u32[]{:S(2)}, u32[]{:S(2)}) collective-permute-start(bf16[256,256]{1,0:T(8,128)(2,1)S(1)} %get-tuple-element.36.refs_0_), channel_id=1, source_target_pairs={{0,1},{1,0},{2,3},{3,2},{4,5},{5,4},{6,7},{7,6},{8,9},{9,8},{10,11... | collective-permute-start | bytes 393224 | tf_op jit(solution)/shard_map/ppermute | solution.py:331
  17.2 7.4 %collective-permute-start.7 = (bf16[256,256]{1,0:T(8,128)(2,1)S(1)}, bf16[256,256]{1,0:T(8,128)(2,1)S(1)}, u32[]{:S(2)}, u32[]{:S(2)}) collective-permute-start(bf16[256,256]{1,0:T(8,128)(2,1)S(1)} %collective-permute-done.6.refs_3_), channel_id=1, source_target_pairs={{0,1},{1,0},{2,3},{3,2},{4,5},{5,4},{6,7},{7,6},{8,9},{9,8},{10,11... | collective-permute-start | bytes 393224 | tf_op jit(solution)/shard_map/ppermute | solution.py:331
  19.8 2.0 %collective-permute-start.3 = (bf16[1024,256]{1,0:T(8,128)(2,1)S(1)}, bf16[1024,256]{1,0:T(8,128)(2,1)S(1)}, u32[]{:S(2)}, u32[]{:S(2)}) collective-permute-start(bf16[1024,256]{1,0:T(8,128)(2,1)S(1)} %shard_map.95), channel_id=1, source_target_pairs={{0,4},{4,0},{8,12},{12,8},{16,20},{20,16},{24,28},{28,24},{1,5},{5... | collective-permute-start | bytes 1572872 | tf_op jit(solution)/shard_map/ppermute | solution.py:331
  21.9 9.5 %collective-permute-start.4 = (bf16[256,256]{1,0:T(8,128)(2,1)S(1)}, bf16[256,256]{1,0:T(8,128)(2,1)S(1)}, u32[]{:S(2)}, u32[]{:S(2)}) collective-permute-start(bf16[256,256]{1,0:T(8,128)(2,1)S(1)} %get-tuple-element.31), channel_id=1, source_target_pairs={{0,8},{4,20},{8,0},{12,28},{16,24},{20,4},{24,16},{28,12},{1,9},{5... | collective-permute-start | bytes 393224 | tf_op jit(solution)/shard_map/ppermute | solution.py:336
  25.3 14.8 %copy-start = (f32[256]{0:T(256)S(1)}, f32[256]{0:T(256)}, u32[]{:S(2)}) copy-start(f32[256]{0:T(256)} %param.12) | copy-start | bytes 3076
  25.3 3.8 %collective-permute-start.10 = (bf16[1024,256]{1,0:T(8,128)(2,1)S(1)}, bf16[1024,256]{1,0:T(8,128)(2,1)S(1)}, u32[]{:S(2)}, u32[]{:S(2)}) collective-permute-start(bf16[1024,256]{1,0:T(8,128)(2,1)S(1)} %shard_map.97), channel_id=1, source_target_pairs={{0,4},{4,0},{8,12},{12,8},{16,20},{20,16},{24,28},{28,24},{1,5},{5... | collective-permute-start | bytes 1572872 | tf_op jit(solution)/shard_map/ppermute | solution.py:331
  26.1 6.7 %collective-permute-start.8 = (bf16[256,256]{1,0:T(8,128)(2,1)S(1)}, bf16[256,256]{1,0:T(8,128)(2,1)S(1)}, u32[]{:S(2)}, u32[]{:S(2)}) collective-permute-start(bf16[256,256]{1,0:T(8,128)(2,1)S(1)} %get-tuple-element.40), channel_id=1, source_target_pairs={{0,16},{4,12},{8,24},{12,4},{16,0},{20,28},{24,8},{28,20},{1,17},{... | collective-permute-start | bytes 393224 | tf_op jit(solution)/shard_map/ppermute | solution.py:336
  27.7 7.4 %collective-permute-start.9 = (bf16[256,256]{1,0:T(8,128)(2,1)S(1)}, bf16[256,256]{1,0:T(8,128)(2,1)S(1)}, u32[]{:S(2)}, u32[]{:S(2)}) collective-permute-start(bf16[256,256]{1,0:T(8,128)(2,1)S(1)} %get-tuple-element.41), channel_id=1, source_target_pairs={{0,24},{4,28},{8,16},{12,20},{16,8},{20,12},{24,0},{28,4},{1,25},{... | collective-permute-start | bytes 393224 | tf_op jit(solution)/shard_map/ppermute | solution.py:336
  29.2 7.4 %collective-permute-start.11 = (bf16[256,256]{1,0:T(8,128)(2,1)S(1)}, bf16[256,256]{1,0:T(8,128)(2,1)S(1)}, u32[]{:S(2)}, u32[]{:S(2)}) collective-permute-start(bf16[256,256]{1,0:T(8,128)(2,1)S(1)} %get-tuple-element.44), channel_id=1, source_target_pairs={{0,8},{4,20},{8,0},{12,28},{16,24},{20,4},{24,16},{28,12},{1,9},{5... | collective-permute-start | bytes 393224 | tf_op jit(solution)/shard_map/ppermute | solution.py:336
  29.8 8.0 %collective-permute-start.12 = (bf16[256,256]{1,0:T(8,128)(2,1)S(1)}, bf16[256,256]{1,0:T(8,128)(2,1)S(1)}, u32[]{:S(2)}, u32[]{:S(2)}) collective-permute-start(bf16[256,256]{1,0:T(8,128)(2,1)S(1)} %get-tuple-element.45), channel_id=1, source_target_pairs={{0,16},{4,12},{8,24},{12,4},{16,0},{20,28},{24,8},{28,20},{1,17},{... | collective-permute-start | bytes 393224 | tf_op jit(solution)/shard_map/ppermute | solution.py:336
  31.4 8.7 %collective-permute-start.13 = (bf16[256,256]{1,0:T(8,128)(2,1)S(1)}, bf16[256,256]{1,0:T(8,128)(2,1)S(1)}, u32[]{:S(2)}, u32[]{:S(2)}) collective-permute-start(bf16[256,256]{1,0:T(8,128)(2,1)S(1)} %get-tuple-element.46), channel_id=1, source_target_pairs={{0,24},{4,28},{8,16},{12,20},{16,8},{20,12},{24,0},{28,4},{1,25},{... | collective-permute-start | bytes 393224 | tf_op jit(solution)/shard_map/ppermute | solution.py:336

commit v14 on v12

--- a/solution.py
+++ b/solution.py
@@ -116,7 +116,8 @@
         core, apart = owner % 2, lax.bitwise_xor(row[0], owner)
         x, y = lax.bitwise_and(apart, 2), lax.bitwise_and(lax.shift_right_logical(apart, 1), 2)
         first, second = (x, y) if core == 0 else (y, x)
-        position = jnp.where(my_core == core, 4, 0) + second + lax.shift_right_logical(first, 1)
+        position = jnp.where(my_core == core, 4, 0) + second
+        position += lax.shift_right_logical(jnp.where(second == 0, 2 - first, first), 1)
         base = (position * own_tiles + label) * span
         bases[slot] = jnp.where(label < own_tiles, base, spare)
 
@@ -240,23 +241,22 @@
     )(matrix, *blocks)
 
 
-def join_kernel(stay, came, kept, *sent):
-    rows = kept.shape[0]
-    value = stay[...].astype(jnp.float32) + came[...].astype(jnp.float32)
-    kept[...] = value[:rows]
-    for place, out in enumerate(sent):
-        out[...] = value[(place + 1) * rows : (place + 2) * rows].astype(out.dtype)
-
-
-def join(stay, came, rows):
-    total, width = stay.shape
-    parts = total // rows
-    return pl.pallas_call(
-        join_kernel,
-        out_shape=[jax.ShapeDtypeStruct((rows, width), jnp.float32)]
-        + [jax.ShapeDtypeStruct((rows, width), jnp.bfloat16)] * (parts - 1),
+def join_kernel(first, stay, came, *outs):
+    start = 0
+    for out in outs:
+        rows = out.shape[0]
+        value = stay[first + start : first + start + rows, :]
+        out[...] = (value + came[start : start + rows, :].astype(jnp.float32)).astype(out.dtype)
+        start += rows
+
+
+def join(stay, came, first, rows, dtypes):
+    width = stay.shape[1]
+    return pl.pallas_call(
+        functools.partial(join_kernel, first),
+        out_shape=[jax.ShapeDtypeStruct((rows, width), dtype) for dtype in dtypes],
         in_specs=[VMEM] * 2,
-        out_specs=[VMEM] * parts,
+        out_specs=[VMEM] * len(dtypes),
         compiler_params=params(12),
         cost_estimate=cost(1, 1),
     )(stay, came)
@@ -377,18 +377,26 @@
     onward, matrix = lax.optimization_barrier((across[0], built))
     passed = swap(onward, "col", 1)
     early = early_product(matrix, scaled[0], beside[0], across[0])
-    away = late_product(matrix, early, passed, 0, half, jnp.bfloat16, WEIGHTS[0])
+    away = [
+        late_product(matrix, early, passed, start, count, jnp.bfloat16, WEIGHTS[0])
+        for start, count in ((0, own_rows), (own_rows, half - own_rows))
+    ]
     stay = late_product(matrix, early, passed, half, half, jnp.float32, WEIGHTS[1])
-    kept, *sent = join(stay, swap(away, "row", 1), own_rows)
-    pieces = [[kept] + exchange(sent)]
+    came = [swap(value, "row", 1) for value in away]
+    (lead,) = join(stay, came[0], 0, own_rows, [jnp.bfloat16])
+    kept, *sent = join(stay, came[1], own_rows, own_rows, [jnp.float32] + [jnp.bfloat16] * 2)
+    pieces = [[kept] + exchange([lead] + sent)]
 
     onward, _ = lax.optimization_barrier((across[1], early))
     blocks = scaled[1], beside[1], swap(onward, "col", 1), across[1]
     blocks, _ = lax.optimization_barrier((blocks, sent))
     away = product(matrix, blocks, 0, half, jnp.bfloat16, WEIGHTS[2])
     stay = product(matrix, blocks, half, half, jnp.float32, WEIGHTS[3])
-    kept, *sent = join(stay, swap(away, "row", 1), own_rows)
-    pieces.append([kept] + exchange(sent))
+    came = swap(away, "row", 1)
+    lead, kept, *sent = join(
+        stay, came, 0, own_rows, [jnp.bfloat16, jnp.float32] + [jnp.bfloat16] * 2
+    )
+    pieces.append([kept] + exchange([lead] + sent))
     return finish(projected, target_norm, pieces)
 
 

time: 38.9 us -> 38.7 us (level)
  waiting for transfers between devices: 11.2 us -> 9.78 us
  starting transfers between devices: 18.1 us -> 19.2 us
    ppermute x8 -> x9, waiting for transfers between devices: 5.14 us -> 3.74 us  [swap(): return lax.ppermute(value, axis, pairs)]
    ppermute x8 -> x9, starting transfers between devices: 11 us -> 11.6 us  [swap(): return lax.ppermute(value, axis, pairs)]
    ppermute x6, starting transfers between devices: 7.11 us -> 7.56 us  [exchange(): lax.ppermute(value, 'row', [(i, i ^ step[i % 2]) for i in range(owners)])]
  transfers between devices with their start and end apart: 14 -> 15, of which waited for: 8 -> 7; matrix products, arithmetic and copies ran while one was open for 0% -> 0% of each run, Pallas kernels for 15% -> 16%
where the time goes in v14:
time: 38.7 us; the launch traced here: 38.5 us
  starting transfers between devices  19.2 us (50%)
  waiting for transfers between devices  9.78 us (25%)
  Pallas kernels  8.82 us (23%)
  between operations  0.76 us (2%)
    ppermute x9, starting transfers between devices, swap(): return lax.ppermute(value, axis, pairs)  11.6 us
    ppermute x6, starting transfers between devices, exchange(): lax.ppermute(value, 'row', [(i, i ^ step[i % 2]) for i in range(owners)])  7.56 us
    ppermute x6, waiting for transfers between devices, exchange(): lax.ppermute(value, 'row', [(i, i ^ step[i % 2]) for i in range(owners)])  6.04 us
    ppermute x9, waiting for transfers between devices, swap(): return lax.ppermute(value, axis, pairs)  3.74 us
    pallas_call x1, Pallas kernels, merge_tiles(): pl.pallas_call(functools.partial(merge_kernel, own_tiles, labels.shape[1]...  2.77 us
    pallas_call x1, Pallas kernels, project(): pl.pallas_call(project_kernel, out_shape=[jax.ShapeDtypeStruct((rows, hid...  1.82 us
    pallas_call x2, Pallas kernels, product(): pl.pallas_call(functools.partial(product_kernel, first), out_shape=jax.Sh...  1.42 us
    pallas_call x1, Pallas kernels, early_product(): pl.pallas_call(early_kernel, out_shape=jax.ShapeDtypeStruct((total, width...  0.99 us
  transfers between devices with their start and end apart: 15, of which 7 were waited for; matrix products, arithmetic and copies ran while one was open for 0% of the time, Pallas kernels for 16%

profile of v14, /device:TPU:0, one launch (start us, length us, event | category | flops | bytes accessed | tf_op | source)
XLA Modules:
  0.0 38.5 jit_solution(8025310731031072207)
XLA Ops:
  0.0 1.8 %shard_map.91 = (f32[256,512]{1,0:T(8,128)S(1)}, bf16[256,256]{1,0:T(8,128)(2,1)S(1)}, bf16[256,256]{1,0:T(8,128)(2,1)S(1)}) custom-call(bf16[256,1024]{1,0:T(8,128)(2,1)} %features_hbm.1, bf16[1024,512]{1,0:T(8,128)(2,1)} %weight_hbm.1, f32[2,128]{1,0:T(2,128)} %bitcast.5), custom_call_target="tpu_custom_call" | custom-call | flops 268435456 | bytes 1572864 | tf_op jit(solution)/shard_map/pallas_call | solution.py:65
  1.8 5.1 %collective-permute-start = (bf16[256,256]{1,0:T(8,128)(2,1)S(1)}, bf16[256,256]{1,0:T(8,128)(2,1)S(1)}, u32[]{:S(2)}, u32[]{:S(2)}) collective-permute-start(bf16[256,256]{1,0:T(8,128)(2,1)S(1)} %get-tuple-element.23.own), channel_id=1, source_target_pairs={{0,3},{1,2},{2,1},{3,0},{4,7},{5,6},{6,5},{7,4},{8,11},{9,10},{10,... | collective-permute-start | bytes 393224 | tf_op jit(solution)/shard_map/ppermute | solution.py:331
  6.9 0.9 %collective-permute-start.9 = (bf16[256,256]{1,0:T(8,128)(2,1)S(1)}, bf16[256,256]{1,0:T(8,128)(2,1)S(1)}, u32[]{:S(2)}, u32[]{:S(2)}) collective-permute-start(bf16[256,256]{1,0:T(8,128)(2,1)S(1)} %get-tuple-element.31.refs_0_), channel_id=1, source_target_pairs={{0,3},{1,2},{2,1},{3,0},{4,7},{5,6},{6,5},{7,4},{8,11},{9,10},{10,... | collective-permute-start | bytes 393224 | tf_op jit(solution)/shard_map/ppermute | solution.py:331
  8.5 2.8 %shard_map.92.matrix = bf16[2048,1024]{1,0:T(8,128)(2,1)S(1)} custom-call(s32[1]{0:T(128)} %bitcast.2.row, s32[1]{0:T(128)} %bitcast.3.column, s32[1]{0:T(128)S(6)} %copy.10.count, s32[1,64]{1,0:T(1,128)} %sources_hbm.1, s32[1,64]{1,0:T(1,128)} %targets_hbm.1, s32[1,16]{1,0:T(1,128)} %labels_hbm.1, bf16[1,64,128,128]{3,2,1,0:T(8,128)(2,1)} %tiles_hbm.1), custom_call_target="tpu_custom_call" | custom-call | flops 8388608 | bytes 12582912 | tf_op jit(solution)/shard_map/pallas_call | solution.py:151
  11.3 0.0 collective-permute-done.across
  11.3 3.4 %collective-permute-start.2 = (bf16[256,256]{1,0:T(8,128)(2,1)S(1)}, bf16[256,256]{1,0:T(8,128)(2,1)S(1)}, u32[]{:S(2)}, u32[]{:S(2)}) collective-permute-start(bf16[256,256]{1,0:T(8,128)(2,1)S(1)} %collective-permute-done.across), channel_id=1, source_target_pairs={{0,1},{1,0},{2,3},{3,2},{4,5},{5,4},{6,7},{7,6},{8,9},{9,8},{10,11... | collective-permute-start | bytes 393224 | tf_op jit(solution)/shard_map/ppermute | solution.py:331
  14.8 1.4 %collective-permute-done.1.beside = bf16[256,256]{1,0:T(8,128)(2,1)S(1)} collective-permute-done((bf16[256,256]{1,0:T(8,128)(2,1)S(1)}, bf16[256,256]{1,0:T(8,128)(2,1)S(1)}, u32[]{:S(2)}, u32[]{:S(2)}) %collective-permute-start.1) | collective-permute-done | bytes 131104 | tf_op jit(solution)/shard_map/ppermute | solution.py:331
  16.2 1.0 %shard_map.93.early = f32[2048,256]{1,0:T(8,128)S(1)} custom-call(bf16[2048,1024]{1,0:T(8,128)(2,1)S(1)} %shard_map.92.matrix, bf16[256,256]{1,0:T(8,128)(2,1)S(1)} %get-tuple-element.23.own, bf16[256,256]{1,0:T(8,128)(2,1)S(1)} %collective-permute-done.1.beside, bf16[256,256]{1,0:T(8,128)(2,1)S(1)} %collective-permute-done.across), custom_call_target="tpu_custom_call" | custom-call | flops 536870912 | bytes 1 | tf_op jit(solution)/shard_map/pallas_call | solution.py:185
  17.2 1.4 %collective-permute-start.10 = (bf16[256,256]{1,0:T(8,128)(2,1)S(1)}, bf16[256,256]{1,0:T(8,128)(2,1)S(1)}, u32[]{:S(2)}, u32[]{:S(2)}) collective-permute-start(bf16[256,256]{1,0:T(8,128)(2,1)S(1)} %collective-permute-done.9.refs_3_), channel_id=1, source_target_pairs={{0,1},{1,0},{2,3},{3,2},{4,5},{5,4},{6,7},{7,6},{8,9},{9,8},{10,11... | collective-permute-start | bytes 393224 | tf_op jit(solution)/shard_map/ppermute | solution.py:331
  18.6 0.9 %collective-permute-done.2.passed = bf16[256,256]{1,0:T(8,128)(2,1)S(1)} collective-permute-done((bf16[256,256]{1,0:T(8,128)(2,1)S(1)}, bf16[256,256]{1,0:T(8,128)(2,1)S(1)}, u32[]{:S(2)}, u32[]{:S(2)}) %collective-permute-start.2) | collective-permute-done | bytes 131104 | tf_op jit(solution)/shard_map/ppermute | solution.py:331
  19.5 0.2 shard_map.97
  19.7 0.1 collective-permute-start.4
  19.8 0.3 shard_map.95
  20.1 0.6 %collective-permute-start.3 = (bf16[768,256]{1,0:T(8,128)(2,1)S(1)}, bf16[768,256]{1,0:T(8,128)(2,1)S(1)}, u32[]{:S(2)}, u32[]{:S(2)}) collective-permute-start(bf16[768,256]{1,0:T(8,128)(2,1)S(1)} %shard_map.95), channel_id=1, source_target_pairs={{0,4},{4,0},{8,12},{12,8},{16,20},{20,16},{24,28},{28,24},{1,5},{5... | collective-permute-start | bytes 1179656 | tf_op jit(solution)/shard_map/ppermute | solution.py:331
  20.6 0.3 shard_map.94.stay
  20.9 0.2 collective-permute-done.4.came
  21.1 1.7 %collective-permute-start.5 = (bf16[256,256]{1,0:T(8,128)(2,1)S(1)}, bf16[256,256]{1,0:T(8,128)(2,1)S(1)}, u32[]{:S(2)}, u32[]{:S(2)}) collective-permute-start(bf16[256,256]{1,0:T(8,128)(2,1)S(1)} %shard_map.98), channel_id=1, source_target_pairs={{0,8},{4,20},{8,0},{12,28},{16,24},{20,4},{24,16},{28,12},{1,9},{5... | collective-permute-start | bytes 393224 | tf_op jit(solution)/shard_map/ppermute | solution.py:338
  22.9 0.1 shard_map.96
  23.0 1.6 %collective-permute-start.6 = (bf16[256,256]{1,0:T(8,128)(2,1)S(1)}, bf16[256,256]{1,0:T(8,128)(2,1)S(1)}, u32[]{:S(2)}, u32[]{:S(2)}) collective-permute-start(bf16[256,256]{1,0:T(8,128)(2,1)S(1)} %get-tuple-element.27), channel_id=1, source_target_pairs={{0,16},{4,12},{8,24},{12,4},{16,0},{20,28},{24,8},{28,20},{1,17},{... | collective-permute-start | bytes 393224 | tf_op jit(solution)/shard_map/ppermute | solution.py:338
  24.5 0.7 %collective-permute-start.7 = (bf16[256,256]{1,0:T(8,128)(2,1)S(1)}, bf16[256,256]{1,0:T(8,128)(2,1)S(1)}, u32[]{:S(2)}, u32[]{:S(2)}) collective-permute-start(bf16[256,256]{1,0:T(8,128)(2,1)S(1)} %get-tuple-element.28), channel_id=1, source_target_pairs={{0,24},{4,28},{8,16},{12,20},{16,8},{20,12},{24,0},{28,4},{1,25},{... | collective-permute-start | bytes 393224 | tf_op jit(solution)/shard_map/ppermute | solution.py:338
  25.2 0.7 %shard_map.100 = bf16[1024,256]{1,0:T(8,128)(2,1)S(1)} custom-call(bf16[2048,1024]{1,0:T(8,128)(2,1)S(1)} %shard_map.92.matrix, bf16[256,256]{1,0:T(8,128)(2,1)S(1)} %get-tuple-element.31.refs_0_, bf16[256,256]{1,0:T(8,128)(2,1)S(1)} %collective-permute-done.8.refs_1_, bf16[256,256]{1,0:T(8,128)(2,1)S(1)} %collective-permute-done.10.refs_2_, ...), custom_call_target="tpu_custom_call" | custom-call | bytes 1 | tf_op jit(solution)/shard_map/pallas_call | solution.py:233
  26.0 0.1 collective-permute-start.11
  26.0 0.7 %shard_map.99.stay = f32[1024,256]{1,0:T(8,128)S(1)} custom-call(bf16[2048,1024]{1,0:T(8,128)(2,1)S(1)} %shard_map.92.matrix, bf16[256,256]{1,0:T(8,128)(2,1)S(1)} %get-tuple-element.31.refs_0_, bf16[256,256]{1,0:T(8,128)(2,1)S(1)} %collective-permute-done.8.refs_1_, bf16[256,256]{1,0:T(8,128)(2,1)S(1)} %collective-permute-done.10.refs_2_, ...), custom_call_target="tpu_custom_call" | custom-call | flops 10737418240 | bytes 1 | tf_op jit(solution)/shard_map/pallas_call | solution.py:233
  26.8 1.2 %collective-permute-done.11.came = bf16[1024,256]{1,0:T(8,128)(2,1)S(1)} collective-permute-done((bf16[1024,256]{1,0:T(8,128)(2,1)S(1)}, bf16[1024,256]{1,0:T(8,128)(2,1)S(1)}, u32[]{:S(2)}, u32[]{:S(2)}) %collective-permute-start.11) | collective-permute-done | bytes 524320 | tf_op jit(solution)/shard_map/ppermute | solution.py:331
  27.9 0.1 shard_map.101
  28.0 1.4 %collective-permute-start.12 = (bf16[256,256]{1,0:T(8,128)(2,1)S(1)}, bf16[256,256]{1,0:T(8,128)(2,1)S(1)}, u32[]{:S(2)}, u32[]{:S(2)}) collective-permute-start(bf16[256,256]{1,0:T(8,128)(2,1)S(1)} %get-tuple-element.36), channel_id=1, source_target_pairs={{0,8},{4,20},{8,0},{12,28},{16,24},{20,4},{24,16},{28,12},{1,9},{5... | collective-permute-start | bytes 393224 | tf_op jit(solution)/shard_map/ppermute | solution.py:338
  29.4 1.5 %collective-permute-start.13 = (bf16[256,256]{1,0:T(8,128)(2,1)S(1)}, bf16[256,256]{1,0:T(8,128)(2,1)S(1)}, u32[]{:S(2)}, u32[]{:S(2)}) collective-permute-start(bf16[256,256]{1,0:T(8,128)(2,1)S(1)} %get-tuple-element.37), channel_id=1, source_target_pairs={{0,16},{4,12},{8,24},{12,4},{16,0},{20,28},{24,8},{28,20},{1,17},{... | collective-permute-start | bytes 393224 | tf_op jit(solution)/shard_map/ppermute | solution.py:338
  30.9 0.7 %collective-permute-start.14 = (bf16[256,256]{1,0:T(8,128)(2,1)S(1)}, bf16[256,256]{1,0:T(8,128)(2,1)S(1)}, u32[]{:S(2)}, u32[]{:S(2)}) collective-permute-start(bf16[256,256]{1,0:T(8,128)(2,1)S(1)} %get-tuple-element.38), channel_id=1, source_target_pairs={{0,24},{4,28},{8,16},{12,20},{16,8},{20,12},{24,0},{28,4},{1,25},{... | collective-permute-start | bytes 393224 | tf_op jit(solution)/shard_map/ppermute | solution.py:338
  31.6 2.5 %collective-permute-done.12.refs_5_ = bf16[256,256]{1,0:T(8,128)(2,1)S(1)} collective-permute-done((bf16[256,256]{1,0:T(8,128)(2,1)S(1)}, bf16[256,256]{1,0:T(8,128)(2,1)S(1)}, u32[]{:S(2)}, u32[]{:S(2)}) %collective-permute-start.12) | collective-permute-done | bytes 131104 | tf_op jit(solution)/shard_map/ppermute | solution.py:338
  34.1 0.3 collective-permute-done.13.refs_6_
  34.4 3.2 %collective-permute-done.14.refs_7_ = bf16[256,256]{1,0:T(8,128)(2,1)S(1)} collective-permute-done((bf16[256,256]{1,0:T(8,128)(2,1)S(1)}, bf16[256,256]{1,0:T(8,128)(2,1)S(1)}, u32[]{:S(2)}, u32[]{:S(2)}) %collective-permute-start.14) | collective-permute-done | bytes 131104 | tf_op jit(solution)/shard_map/ppermute | solution.py:338
  37.6 0.9 %shard_map.102 = bf16[256,512]{1,0:T(8,128)(2,1)} custom-call(f32[256,512]{1,0:T(8,128)S(1)} %get-tuple-element.22.projected, f32[2,128]{1,0:T(2,128)S(1)} %bitcast.4, f32[256,256]{1,0:T(8,128)S(1)} %get-tuple-element.26.refs_0_, bf16[256,256]{1,0:T(8,128)(2,1)S(1)} %collective-permute-done.5.refs_1_, bf16[256,256]{1,0:T(8,128)(2,1)S(1)} %collective-permute-done.6.refs_2_, ...), custom_call_target="tpu_custom_call" | custom-call | flops 786432 | bytes 2097152 | tf_op jit(solution)/shard_map/pallas_call | solution.py:285
  (12 shorter events, 0.1 us)
Async XLA Ops:
  1.8 9.5 %collective-permute-start = (bf16[256,256]{1,0:T(8,128)(2,1)S(1)}, bf16[256,256]{1,0:T(8,128)(2,1)S(1)}, u32[]{:S(2)}, u32[]{:S(2)}) collective-permute-start(bf16[256,256]{1,0:T(8,128)(2,1)S(1)} %get-tuple-element.23.own), channel_id=1, source_target_pairs={{0,3},{1,2},{2,1},{3,0},{4,7},{5,6},{6,5},{7,4},{8,11},{9,10},{10,... | collective-permute-start | bytes 393224 | tf_op jit(solution)/shard_map/ppermute | solution.py:331
  6.9 9.2 %collective-permute-start.1 = (bf16[256,256]{1,0:T(8,128)(2,1)S(1)}, bf16[256,256]{1,0:T(8,128)(2,1)S(1)}, u32[]{:S(2)}, u32[]{:S(2)}) collective-permute-start(bf16[256,256]{1,0:T(8,128)(2,1)S(1)} %get-tuple-element.23.own), channel_id=1, source_target_pairs={{0,1},{1,0},{2,3},{3,2},{4,5},{5,4},{6,7},{7,6},{8,9},{9,8},{10,11... | collective-permute-start | bytes 393224 | tf_op jit(solution)/shard_map/ppermute | solution.py:331
  6.9 10.2 %collective-permute-start.9 = (bf16[256,256]{1,0:T(8,128)(2,1)S(1)}, bf16[256,256]{1,0:T(8,128)(2,1)S(1)}, u32[]{:S(2)}, u32[]{:S(2)}) collective-permute-start(bf16[256,256]{1,0:T(8,128)(2,1)S(1)} %get-tuple-element.31.refs_0_), channel_id=1, source_target_pairs={{0,3},{1,2},{2,1},{3,0},{4,7},{5,6},{6,5},{7,4},{8,11},{9,10},{10,... | collective-permute-start | bytes 393224 | tf_op jit(solution)/shard_map/ppermute | solution.py:331
  11.3 8.2 %collective-permute-start.2 = (bf16[256,256]{1,0:T(8,128)(2,1)S(1)}, bf16[256,256]{1,0:T(8,128)(2,1)S(1)}, u32[]{:S(2)}, u32[]{:S(2)}) collective-permute-start(bf16[256,256]{1,0:T(8,128)(2,1)S(1)} %collective-permute-done.across), channel_id=1, source_target_pairs={{0,1},{1,0},{2,3},{3,2},{4,5},{5,4},{6,7},{7,6},{8,9},{9,8},{10,11... | collective-permute-start | bytes 393224 | tf_op jit(solution)/shard_map/ppermute | solution.py:331
  14.8 10.5 %collective-permute-start.8 = (bf16[256,256]{1,0:T(8,128)(2,1)S(1)}, bf16[256,256]{1,0:T(8,128)(2,1)S(1)}, u32[]{:S(2)}, u32[]{:S(2)}) collective-permute-start(bf16[256,256]{1,0:T(8,128)(2,1)S(1)} %get-tuple-element.31.refs_0_), channel_id=1, source_target_pairs={{0,1},{1,0},{2,3},{3,2},{4,5},{5,4},{6,7},{7,6},{8,9},{9,8},{10,11... | collective-permute-start | bytes 393224 | tf_op jit(solution)/shard_map/ppermute | solution.py:331
  17.2 8.0 %collective-permute-start.10 = (bf16[256,256]{1,0:T(8,128)(2,1)S(1)}, bf16[256,256]{1,0:T(8,128)(2,1)S(1)}, u32[]{:S(2)}, u32[]{:S(2)}) collective-permute-start(bf16[256,256]{1,0:T(8,128)(2,1)S(1)} %collective-permute-done.9.refs_3_), channel_id=1, source_target_pairs={{0,1},{1,0},{2,3},{3,2},{4,5},{5,4},{6,7},{7,6},{8,9},{9,8},{10,11... | collective-permute-start | bytes 393224 | tf_op jit(solution)/shard_map/ppermute | solution.py:331
  19.7 1.4 %collective-permute-start.4 = (bf16[256,256]{1,0:T(8,128)(2,1)S(1)}, bf16[256,256]{1,0:T(8,128)(2,1)S(1)}, u32[]{:S(2)}, u32[]{:S(2)}) collective-permute-start(bf16[256,256]{1,0:T(8,128)(2,1)S(1)} %shard_map.97), channel_id=1, source_target_pairs={{0,4},{4,0},{8,12},{12,8},{16,20},{20,16},{24,28},{28,24},{1,5},{5... | collective-permute-start | bytes 393224 | tf_op jit(solution)/shard_map/ppermute | solution.py:331
  20.1 2.8 %collective-permute-start.3 = (bf16[768,256]{1,0:T(8,128)(2,1)S(1)}, bf16[768,256]{1,0:T(8,128)(2,1)S(1)}, u32[]{:S(2)}, u32[]{:S(2)}) collective-permute-start(bf16[768,256]{1,0:T(8,128)(2,1)S(1)} %shard_map.95), channel_id=1, source_target_pairs={{0,4},{4,0},{8,12},{12,8},{16,20},{20,16},{24,28},{28,24},{1,5},{5... | collective-permute-start | bytes 1179656 | tf_op jit(solution)/shard_map/ppermute | solution.py:331
  21.1 9.8 %collective-permute-start.5 = (bf16[256,256]{1,0:T(8,128)(2,1)S(1)}, bf16[256,256]{1,0:T(8,128)(2,1)S(1)}, u32[]{:S(2)}, u32[]{:S(2)}) collective-permute-start(bf16[256,256]{1,0:T(8,128)(2,1)S(1)} %shard_map.98), channel_id=1, source_target_pairs={{0,8},{4,20},{8,0},{12,28},{16,24},{20,4},{24,16},{28,12},{1,9},{5... | collective-permute-start | bytes 393224 | tf_op jit(solution)/shard_map/ppermute | solution.py:338
  23.0 8.6 %collective-permute-start.6 = (bf16[256,256]{1,0:T(8,128)(2,1)S(1)}, bf16[256,256]{1,0:T(8,128)(2,1)S(1)}, u32[]{:S(2)}, u32[]{:S(2)}) collective-permute-start(bf16[256,256]{1,0:T(8,128)(2,1)S(1)} %get-tuple-element.27), channel_id=1, source_target_pairs={{0,16},{4,12},{8,24},{12,4},{16,0},{20,28},{24,8},{28,20},{1,17},{... | collective-permute-start | bytes 393224 | tf_op jit(solution)/shard_map/ppermute | solution.py:338
  24.5 7.1 %collective-permute-start.7 = (bf16[256,256]{1,0:T(8,128)(2,1)S(1)}, bf16[256,256]{1,0:T(8,128)(2,1)S(1)}, u32[]{:S(2)}, u32[]{:S(2)}) collective-permute-start(bf16[256,256]{1,0:T(8,128)(2,1)S(1)} %get-tuple-element.28), channel_id=1, source_target_pairs={{0,24},{4,28},{8,16},{12,20},{16,8},{20,12},{24,0},{28,4},{1,25},{... | collective-permute-start | bytes 393224 | tf_op jit(solution)/shard_map/ppermute | solution.py:338
  26.0 11.7 %copy-start = (f32[256]{0:T(256)S(1)}, f32[256]{0:T(256)}, u32[]{:S(2)}) copy-start(f32[256]{0:T(256)} %param.12) | copy-start | bytes 3076
  26.0 2.0 %collective-permute-start.11 = (bf16[1024,256]{1,0:T(8,128)(2,1)S(1)}, bf16[1024,256]{1,0:T(8,128)(2,1)S(1)}, u32[]{:S(2)}, u32[]{:S(2)}) collective-permute-start(bf16[1024,256]{1,0:T(8,128)(2,1)S(1)} %shard_map.100), channel_id=1, source_target_pairs={{0,4},{4,0},{8,12},{12,8},{16,20},{20,16},{24,28},{28,24},{1,5},{5... | collective-permute-start | bytes 1572872 | tf_op jit(solution)/shard_map/ppermute | solution.py:331
  28.0 6.1 %collective-permute-start.12 = (bf16[256,256]{1,0:T(8,128)(2,1)S(1)}, bf16[256,256]{1,0:T(8,128)(2,1)S(1)}, u32[]{:S(2)}, u32[]{:S(2)}) collective-permute-start(bf16[256,256]{1,0:T(8,128)(2,1)S(1)} %get-tuple-element.36), channel_id=1, source_target_pairs={{0,8},{4,20},{8,0},{12,28},{16,24},{20,4},{24,16},{28,12},{1,9},{5... | collective-permute-start | bytes 393224 | tf_op jit(solution)/shard_map/ppermute | solution.py:338
  29.4 5.1 %collective-permute-start.13 = (bf16[256,256]{1,0:T(8,128)(2,1)S(1)}, bf16[256,256]{1,0:T(8,128)(2,1)S(1)}, u32[]{:S(2)}, u32[]{:S(2)}) collective-permute-start(bf16[256,256]{1,0:T(8,128)(2,1)S(1)} %get-tuple-element.37), channel_id=1, source_target_pairs={{0,16},{4,12},{8,24},{12,4},{16,0},{20,28},{24,8},{28,20},{1,17},{... | collective-permute-start | bytes 393224 | tf_op jit(solution)/shard_map/ppermute | solution.py:338
  30.9 6.7 %collective-permute-start.14 = (bf16[256,256]{1,0:T(8,128)(2,1)S(1)}, bf16[256,256]{1,0:T(8,128)(2,1)S(1)}, u32[]{:S(2)}, u32[]{:S(2)}) collective-permute-start(bf16[256,256]{1,0:T(8,128)(2,1)S(1)} %get-tuple-element.38), channel_id=1, source_target_pairs={{0,24},{4,28},{8,16},{12,20},{16,8},{20,12},{24,0},{28,4},{1,25},{... | collective-permute-start | bytes 393224 | tf_op jit(solution)/shard_map/ppermute | solution.py:338

commit v15 on v14

--- a/solution.py
+++ b/solution.py
@@ -34,28 +34,30 @@
 
 def project_kernel(features_hbm, weight_hbm, norm_hbm, projected, *refs):
     *scaled, features, weight, norm, sems = refs
+    width, lanes = scaled[0].shape[1], norm.shape[1]
+    spans = [slice(k * width, (k + 1) * width) for k in range(len(scaled))]
     copies = [
-        pltpu.make_async_copy(source, target, sems.at[k])
-        for k, (source, target) in enumerate(
-            [(weight_hbm, weight), (features_hbm, features), (norm_hbm, norm)]
-        )
-    ]
-    for copy in copies:
-        copy.start()
-    for copy in copies:
-        copy.wait()
-    lanes = norm.shape[1]
-    value = jnp.dot(features[...], weight[...], preferred_element_type=jnp.float32)
-    projected[...] = value
-    width = scaled[0].shape[1]
-    for part in range(norm.shape[0]):
-        factor = rows_to_lanes(norm[part : part + 1, :], lanes)
-        for column in range(0, value.shape[1], lanes):
+        pltpu.make_async_copy(features_hbm, features, sems.at[0]),
+        pltpu.make_async_copy(norm_hbm, norm, sems.at[1]),
+    ]
+    copies += [
+        pltpu.make_async_copy(weight_hbm.at[:, span], weight.at[:, span], sems.at[2 + k])
+        for k, span in enumerate(spans)
+    ]
+    for k in (0, 2, 1, *range(3, len(copies))):
+        copies[k].start()
+    copies[0].wait()
+    copies[1].wait()
+    for k, (span, target) in enumerate(zip(spans, scaled)):
+        copies[2 + k].wait()
+        value = jnp.dot(features[...], weight[:, span], preferred_element_type=jnp.float32)
+        projected[:, span] = value
+        for part in range(norm.shape[0]):
+            factor = rows_to_lanes(norm[part : part + 1, :], lanes)
             here = slice(part * lanes, (part + 1) * lanes)
-            piece = factor * value[here, column : column + lanes]
-            target = scaled[column // width]
-            start = column % width
-            target[here, start : start + lanes] = piece.astype(target.dtype)
+            for column in range(0, width, lanes):
+                piece = factor * value[here, column : column + lanes]
+                target[here, column : column + lanes] = piece.astype(target.dtype)
 
 
 def project(features, weight, source_norm, chunks):
@@ -72,7 +74,7 @@
             pltpu.VMEM(features.shape, features.dtype),
             pltpu.VMEM(weight.shape, weight.dtype),
             pltpu.VMEM(norm.shape, norm.dtype),
-            pltpu.SemaphoreType.DMA((3,)),
+            pltpu.SemaphoreType.DMA((2 + chunks,)),
         ],
         compiler_params=params(12),
         cost_estimate=cost(2 * rows * depth * hidden, 2 * depth * (rows + hidden)),
@@ -262,34 +264,60 @@
     )(stay, came)
 
 
-def finish_kernel(chunks, projected, norm, *refs):
-    out = refs[-1]
-    per_chunk = (len(refs) - 1) // chunks
+def activate(projected, norm, pieces, start, out):
     lanes = norm.shape[1]
-    width = refs[0].shape[1]
     for part in range(norm.shape[0]):
         factor = rows_to_lanes(norm[part : part + 1, :], lanes)
         here = slice(part * lanes, (part + 1) * lanes)
         for column in range(0, out.shape[1], lanes):
-            pieces = refs[column // width * per_chunk : (column // width + 1) * per_chunk]
-            start = column % width
-            value = projected[here, column : column + lanes]
+            span = slice(column, column + lanes)
+            value = projected[here, start + column : start + column + lanes]
             for piece in pieces:
-                value += piece[here, start : start + lanes].astype(jnp.float32)
-            out[here, column : column + lanes] = jnp.maximum(factor * value, 0.0).astype(out.dtype)
+                value += piece[here, span].astype(jnp.float32)
+            out[here, span] = jnp.maximum(factor * value, 0.0).astype(out.dtype)
+
+
+def first_kernel(projected, norm, *refs):
+    *pieces, out = refs
+    activate(projected, norm, pieces, 0, out)
+
+
+def last_kernel(ready, projected, norm, *refs):
+    *pieces, out, rest, sems = refs
+    width = ready.shape[1]
+    early = pltpu.make_async_copy(ready, out.at[:, :width], sems.at[0])
+    early.start()
+    activate(projected, norm, pieces, width, rest)
+    late = pltpu.make_async_copy(rest, out.at[:, width:], sems.at[1])
+    late.start()
+    early.wait()
+    late.wait()
 
 
 def finish(projected, target_norm, pieces):
     rows, hidden = projected.shape
-    flat = [piece for chunk in pieces for piece in chunk]
-    return pl.pallas_call(
-        functools.partial(finish_kernel, len(pieces)),
+    norm = target_norm.reshape(-1, 128)
+    width = pieces[0][0].shape[1]
+    ready = pl.pallas_call(
+        first_kernel,
+        out_shape=jax.ShapeDtypeStruct((rows, width), jnp.bfloat16),
+        in_specs=[VMEM] * (2 + len(pieces[0])),
+        out_specs=VMEM,
+        compiler_params=params(12),
+        cost_estimate=cost(6 * rows * width, 16 * rows * width),
+    )(projected, norm, *pieces[0])
+    return pl.pallas_call(
+        last_kernel,
         out_shape=jax.ShapeDtypeStruct((rows, hidden), jnp.bfloat16),
-        in_specs=[VMEM] * (2 + len(flat)),
-        out_specs=VMEM,
+        in_specs=[VMEM] * (3 + len(pieces[1])),
+        out_specs=HBM,
+        scratch_shapes=[
+            pltpu.VMEM((rows, hidden - width), jnp.bfloat16),
+            pltpu.SemaphoreType.DMA((2,)),
+        ],
         compiler_params=params(12),
-        cost_estimate=cost(6 * rows * hidden, 16 * rows * hidden),
-    )(projected, target_norm.reshape(-1, 128), *flat)
+        cost_estimate=cost(6 * rows * width, 16 * rows * width),
+    )(ready, projected, norm, *pieces[1])
 
 
 def visit_kernel(own_tiles, per_owner, sources, targets, count, labels, tiles, blocks, out, total):

time: 38.7 us -> 38.8 us (level)
    pallas_call x1 -> x2, Pallas kernels: 0.89 us -> 0.88 us  [the longest x1 0.78 us: finish(): pl.pallas_call(last_kernel, out_shape=jax.ShapeDtypeStruct((rows, hidden)...]
where the time goes in v15:
time: 38.8 us; the launch traced here: 38.7 us
  starting transfers between devices  19.2 us (49%)
  waiting for transfers between devices  9.67 us (25%)
  Pallas kernels  9.06 us (23%)
  between operations  0.77 us (2%)
    ppermute x9, starting transfers between devices, swap(): return lax.ppermute(value, axis, pairs)  11.6 us
    ppermute x6, starting transfers between devices, exchange(): lax.ppermute(value, 'row', [(i, i ^ step[i % 2]) for i in range(owners)])  7.56 us
    ppermute x6, waiting for transfers between devices, exchange(): lax.ppermute(value, 'row', [(i, i ^ step[i % 2]) for i in range(owners)])  5.93 us
    ppermute x9, waiting for transfers between devices, swap(): return lax.ppermute(value, axis, pairs)  3.74 us
    pallas_call x1, Pallas kernels, merge_tiles(): pl.pallas_call(functools.partial(merge_kernel, own_tiles, labels.shape[1]...  2.77 us
    pallas_call x1, Pallas kernels, project(): pl.pallas_call(project_kernel, out_shape=[jax.ShapeDtypeStruct((rows, hid...  2.07 us
    pallas_call x2, Pallas kernels, product(): pl.pallas_call(functools.partial(product_kernel, first), out_shape=jax.Sh...  1.42 us
    pallas_call x1, Pallas kernels, early_product(): pl.pallas_call(early_kernel, out_shape=jax.ShapeDtypeStruct((total, width...  0.99 us
  transfers between devices with their start and end apart: 15, of which 7 were waited for; matrix products, arithmetic and copies ran while one was open for 0% of the time, Pallas kernels for 16%

profile of v15, /device:TPU:0, one launch (start us, length us, event | category | flops | bytes accessed | tf_op | source)
XLA Modules:
  0.0 38.7 jit_solution(5045620581457680134)
XLA Ops:
  0.0 2.1 %shard_map.91 = (f32[256,512]{1,0:T(8,128)S(1)}, bf16[256,256]{1,0:T(8,128)(2,1)S(1)}, bf16[256,256]{1,0:T(8,128)(2,1)S(1)}) custom-call(bf16[256,1024]{1,0:T(8,128)(2,1)} %features_hbm.1, bf16[1024,512]{1,0:T(8,128)(2,1)} %weight_hbm.1, f32[2,128]{1,0:T(2,128)} %bitcast.6), custom_call_target="tpu_custom_call" | custom-call | flops 268435456 | bytes 1572864 | tf_op jit(solution)/shard_map/pallas_call | solution.py:67
  2.1 5.1 %collective-permute-start = (bf16[256,256]{1,0:T(8,128)(2,1)S(1)}, bf16[256,256]{1,0:T(8,128)(2,1)S(1)}, u32[]{:S(2)}, u32[]{:S(2)}) collective-permute-start(bf16[256,256]{1,0:T(8,128)(2,1)S(1)} %get-tuple-element.23.own), channel_id=1, source_target_pairs={{0,3},{1,2},{2,1},{3,0},{4,7},{5,6},{6,5},{7,4},{8,11},{9,10},{10,... | collective-permute-start | bytes 393224 | tf_op jit(solution)/shard_map/ppermute | solution.py:359
  7.2 0.9 %collective-permute-start.9 = (bf16[256,256]{1,0:T(8,128)(2,1)S(1)}, bf16[256,256]{1,0:T(8,128)(2,1)S(1)}, u32[]{:S(2)}, u32[]{:S(2)}) collective-permute-start(bf16[256,256]{1,0:T(8,128)(2,1)S(1)} %get-tuple-element.31.refs_0_), channel_id=1, source_target_pairs={{0,3},{1,2},{2,1},{3,0},{4,7},{5,6},{6,5},{7,4},{8,11},{9,10},{10,... | collective-permute-start | bytes 393224 | tf_op jit(solution)/shard_map/ppermute | solution.py:359
  8.7 2.8 %shard_map.92.matrix = bf16[2048,1024]{1,0:T(8,128)(2,1)S(1)} custom-call(s32[1]{0:T(128)} %bitcast.2.row, s32[1]{0:T(128)} %bitcast.3.column, s32[1]{0:T(128)S(6)} %copy.10.count, s32[1,64]{1,0:T(1,128)} %sources_hbm.1, s32[1,64]{1,0:T(1,128)} %targets_hbm.1, s32[1,16]{1,0:T(1,128)} %labels_hbm.1, bf16[1,64,128,128]{3,2,1,0:T(8,128)(2,1)} %tiles_hbm.1), custom_call_target="tpu_custom_call" | custom-call | flops 8388608 | bytes 12582912 | tf_op jit(solution)/shard_map/pallas_call | solution.py:153
  11.6 3.4 %collective-permute-start.2 = (bf16[256,256]{1,0:T(8,128)(2,1)S(1)}, bf16[256,256]{1,0:T(8,128)(2,1)S(1)}, u32[]{:S(2)}, u32[]{:S(2)}) collective-permute-start(bf16[256,256]{1,0:T(8,128)(2,1)S(1)} %collective-permute-done.across), channel_id=1, source_target_pairs={{0,1},{1,0},{2,3},{3,2},{4,5},{5,4},{6,7},{7,6},{8,9},{9,8},{10,11... | collective-permute-start | bytes 393224 | tf_op jit(solution)/shard_map/ppermute | solution.py:359
  15.1 1.4 %collective-permute-done.1.beside = bf16[256,256]{1,0:T(8,128)(2,1)S(1)} collective-permute-done((bf16[256,256]{1,0:T(8,128)(2,1)S(1)}, bf16[256,256]{1,0:T(8,128)(2,1)S(1)}, u32[]{:S(2)}, u32[]{:S(2)}) %collective-permute-start.1) | collective-permute-done | bytes 131104 | tf_op jit(solution)/shard_map/ppermute | solution.py:359
  16.4 1.0 %shard_map.93.early = f32[2048,256]{1,0:T(8,128)S(1)} custom-call(bf16[2048,1024]{1,0:T(8,128)(2,1)S(1)} %shard_map.92.matrix, bf16[256,256]{1,0:T(8,128)(2,1)S(1)} %get-tuple-element.23.own, bf16[256,256]{1,0:T(8,128)(2,1)S(1)} %collective-permute-done.1.beside, bf16[256,256]{1,0:T(8,128)(2,1)S(1)} %collective-permute-done.across), custom_call_target="tpu_custom_call" | custom-call | flops 536870912 | bytes 1 | tf_op jit(solution)/shard_map/pallas_call | solution.py:187
  17.4 1.4 %collective-permute-start.10 = (bf16[256,256]{1,0:T(8,128)(2,1)S(1)}, bf16[256,256]{1,0:T(8,128)(2,1)S(1)}, u32[]{:S(2)}, u32[]{:S(2)}) collective-permute-start(bf16[256,256]{1,0:T(8,128)(2,1)S(1)} %collective-permute-done.9.refs_3_), channel_id=1, source_target_pairs={{0,1},{1,0},{2,3},{3,2},{4,5},{5,4},{6,7},{7,6},{8,9},{9,8},{10,11... | collective-permute-start | bytes 393224 | tf_op jit(solution)/shard_map/ppermute | solution.py:359
  18.8 0.9 %collective-permute-done.2.passed = bf16[256,256]{1,0:T(8,128)(2,1)S(1)} collective-permute-done((bf16[256,256]{1,0:T(8,128)(2,1)S(1)}, bf16[256,256]{1,0:T(8,128)(2,1)S(1)}, u32[]{:S(2)}, u32[]{:S(2)}) %collective-permute-start.2) | collective-permute-done | bytes 131104 | tf_op jit(solution)/shard_map/ppermute | solution.py:359
  19.8 0.2 shard_map.97
  20.0 0.1 collective-permute-start.4
  20.0 0.3 shard_map.95
  20.3 0.6 %collective-permute-start.3 = (bf16[768,256]{1,0:T(8,128)(2,1)S(1)}, bf16[768,256]{1,0:T(8,128)(2,1)S(1)}, u32[]{:S(2)}, u32[]{:S(2)}) collective-permute-start(bf16[768,256]{1,0:T(8,128)(2,1)S(1)} %shard_map.95), channel_id=1, source_target_pairs={{0,4},{4,0},{8,12},{12,8},{16,20},{20,16},{24,28},{28,24},{1,5},{5... | collective-permute-start | bytes 1179656 | tf_op jit(solution)/shard_map/ppermute | solution.py:359
  20.9 0.3 shard_map.94.stay
  21.2 0.2 collective-permute-done.4.came
  21.4 1.7 %collective-permute-start.5 = (bf16[256,256]{1,0:T(8,128)(2,1)S(1)}, bf16[256,256]{1,0:T(8,128)(2,1)S(1)}, u32[]{:S(2)}, u32[]{:S(2)}) collective-permute-start(bf16[256,256]{1,0:T(8,128)(2,1)S(1)} %shard_map.98), channel_id=1, source_target_pairs={{0,8},{4,20},{8,0},{12,28},{16,24},{20,4},{24,16},{28,12},{1,9},{5... | collective-permute-start | bytes 393224 | tf_op jit(solution)/shard_map/ppermute | solution.py:366
  23.1 0.1 shard_map.96
  23.2 1.6 %collective-permute-start.6 = (bf16[256,256]{1,0:T(8,128)(2,1)S(1)}, bf16[256,256]{1,0:T(8,128)(2,1)S(1)}, u32[]{:S(2)}, u32[]{:S(2)}) collective-permute-start(bf16[256,256]{1,0:T(8,128)(2,1)S(1)} %get-tuple-element.27), channel_id=1, source_target_pairs={{0,16},{4,12},{8,24},{12,4},{16,0},{20,28},{24,8},{28,20},{1,17},{... | collective-permute-start | bytes 393224 | tf_op jit(solution)/shard_map/ppermute | solution.py:366
  24.8 0.7 %collective-permute-start.7 = (bf16[256,256]{1,0:T(8,128)(2,1)S(1)}, bf16[256,256]{1,0:T(8,128)(2,1)S(1)}, u32[]{:S(2)}, u32[]{:S(2)}) collective-permute-start(bf16[256,256]{1,0:T(8,128)(2,1)S(1)} %get-tuple-element.28), channel_id=1, source_target_pairs={{0,24},{4,28},{8,16},{12,20},{16,8},{20,12},{24,0},{28,4},{1,25},{... | collective-permute-start | bytes 393224 | tf_op jit(solution)/shard_map/ppermute | solution.py:366
  25.5 0.7 %shard_map.101 = bf16[1024,256]{1,0:T(8,128)(2,1)S(1)} custom-call(bf16[2048,1024]{1,0:T(8,128)(2,1)S(1)} %shard_map.92.matrix, bf16[256,256]{1,0:T(8,128)(2,1)S(1)} %get-tuple-element.31.refs_0_, bf16[256,256]{1,0:T(8,128)(2,1)S(1)} %collective-permute-done.8.refs_1_, bf16[256,256]{1,0:T(8,128)(2,1)S(1)} %collective-permute-done.10.refs_2_, ...), custom_call_target="tpu_custom_call" | custom-call | bytes 1 | tf_op jit(solution)/shard_map/pallas_call | solution.py:235
  26.2 0.1 collective-permute-start.11
  26.3 0.7 %shard_map.100.stay = f32[1024,256]{1,0:T(8,128)S(1)} custom-call(bf16[2048,1024]{1,0:T(8,128)(2,1)S(1)} %shard_map.92.matrix, bf16[256,256]{1,0:T(8,128)(2,1)S(1)} %get-tuple-element.31.refs_0_, bf16[256,256]{1,0:T(8,128)(2,1)S(1)} %collective-permute-done.8.refs_1_, bf16[256,256]{1,0:T(8,128)(2,1)S(1)} %collective-permute-done.10.refs_2_, ...), custom_call_target="tpu_custom_call" | custom-call | flops 10737418240 | bytes 1 | tf_op jit(solution)/shard_map/pallas_call | solution.py:235
  27.0 1.2 %collective-permute-done.11.came = bf16[1024,256]{1,0:T(8,128)(2,1)S(1)} collective-permute-done((bf16[1024,256]{1,0:T(8,128)(2,1)S(1)}, bf16[1024,256]{1,0:T(8,128)(2,1)S(1)}, u32[]{:S(2)}, u32[]{:S(2)}) %collective-permute-start.11) | collective-permute-done | bytes 524320 | tf_op jit(solution)/shard_map/ppermute | solution.py:359
  28.2 0.1 shard_map.102
  28.3 1.4 %collective-permute-start.12 = (bf16[256,256]{1,0:T(8,128)(2,1)S(1)}, bf16[256,256]{1,0:T(8,128)(2,1)S(1)}, u32[]{:S(2)}, u32[]{:S(2)}) collective-permute-start(bf16[256,256]{1,0:T(8,128)(2,1)S(1)} %get-tuple-element.36), channel_id=1, source_target_pairs={{0,8},{4,20},{8,0},{12,28},{16,24},{20,4},{24,16},{28,12},{1,9},{5... | collective-permute-start | bytes 393224 | tf_op jit(solution)/shard_map/ppermute | solution.py:366
  29.6 1.5 %collective-permute-start.13 = (bf16[256,256]{1,0:T(8,128)(2,1)S(1)}, bf16[256,256]{1,0:T(8,128)(2,1)S(1)}, u32[]{:S(2)}, u32[]{:S(2)}) collective-permute-start(bf16[256,256]{1,0:T(8,128)(2,1)S(1)} %get-tuple-element.37), channel_id=1, source_target_pairs={{0,16},{4,12},{8,24},{12,4},{16,0},{20,28},{24,8},{28,20},{1,17},{... | collective-permute-start | bytes 393224 | tf_op jit(solution)/shard_map/ppermute | solution.py:366
  31.2 0.7 %collective-permute-start.14 = (bf16[256,256]{1,0:T(8,128)(2,1)S(1)}, bf16[256,256]{1,0:T(8,128)(2,1)S(1)}, u32[]{:S(2)}, u32[]{:S(2)}) collective-permute-start(bf16[256,256]{1,0:T(8,128)(2,1)S(1)} %get-tuple-element.38), channel_id=1, source_target_pairs={{0,24},{4,28},{8,16},{12,20},{16,8},{20,12},{24,0},{28,4},{1,25},{... | collective-permute-start | bytes 393224 | tf_op jit(solution)/shard_map/ppermute | solution.py:366
  31.9 0.1 shard_map.99.ready
  32.0 2.4 %collective-permute-done.12.refs_1_ = bf16[256,256]{1,0:T(8,128)(2,1)S(1)} collective-permute-done((bf16[256,256]{1,0:T(8,128)(2,1)S(1)}, bf16[256,256]{1,0:T(8,128)(2,1)S(1)}, u32[]{:S(2)}, u32[]{:S(2)}) %collective-permute-start.12) | collective-permute-done | bytes 131104 | tf_op jit(solution)/shard_map/ppermute | solution.py:366
  34.4 0.3 collective-permute-done.13.refs_2_
  34.7 3.2 %collective-permute-done.14.refs_3_ = bf16[256,256]{1,0:T(8,128)(2,1)S(1)} collective-permute-done((bf16[256,256]{1,0:T(8,128)(2,1)S(1)}, bf16[256,256]{1,0:T(8,128)(2,1)S(1)}, u32[]{:S(2)}, u32[]{:S(2)}) %collective-permute-start.14) | collective-permute-done | bytes 131104 | tf_op jit(solution)/shard_map/ppermute | solution.py:366
  37.9 0.8 %shard_map.103 = bf16[256,512]{1,0:T(8,128)(2,1)} custom-call(bf16[256,256]{1,0:T(8,128)(2,1)S(1)} %shard_map.99.ready, f32[256,512]{1,0:T(8,128)S(1)} %get-tuple-element.22.projected, f32[2,128]{1,0:T(2,128)S(1)} %bitcast.5, f32[256,256]{1,0:T(8,128)S(1)} %get-tuple-element.35.refs_0_, bf16[256,256]{1,0:T(8,128)(2,1)S(1)} %collective-permute-done.12.refs_1_, ...), custom_call_target="tpu_custom_call" | custom-call | flops 393216 | bytes 1048576 | tf_op jit(solution)/shard_map/pallas_call | solution.py:309
  (13 shorter events, 0.1 us)
Async XLA Ops:
  2.1 9.5 %collective-permute-start = (bf16[256,256]{1,0:T(8,128)(2,1)S(1)}, bf16[256,256]{1,0:T(8,128)(2,1)S(1)}, u32[]{:S(2)}, u32[]{:S(2)}) collective-permute-start(bf16[256,256]{1,0:T(8,128)(2,1)S(1)} %get-tuple-element.23.own), channel_id=1, source_target_pairs={{0,3},{1,2},{2,1},{3,0},{4,7},{5,6},{6,5},{7,4},{8,11},{9,10},{10,... | collective-permute-start | bytes 393224 | tf_op jit(solution)/shard_map/ppermute | solution.py:359
  7.2 9.2 %collective-permute-start.1 = (bf16[256,256]{1,0:T(8,128)(2,1)S(1)}, bf16[256,256]{1,0:T(8,128)(2,1)S(1)}, u32[]{:S(2)}, u32[]{:S(2)}) collective-permute-start(bf16[256,256]{1,0:T(8,128)(2,1)S(1)} %get-tuple-element.23.own), channel_id=1, source_target_pairs={{0,1},{1,0},{2,3},{3,2},{4,5},{5,4},{6,7},{7,6},{8,9},{9,8},{10,11... | collective-permute-start | bytes 393224 | tf_op jit(solution)/shard_map/ppermute | solution.py:359
  7.2 10.2 %collective-permute-start.9 = (bf16[256,256]{1,0:T(8,128)(2,1)S(1)}, bf16[256,256]{1,0:T(8,128)(2,1)S(1)}, u32[]{:S(2)}, u32[]{:S(2)}) collective-permute-start(bf16[256,256]{1,0:T(8,128)(2,1)S(1)} %get-tuple-element.31.refs_0_), channel_id=1, source_target_pairs={{0,3},{1,2},{2,1},{3,0},{4,7},{5,6},{6,5},{7,4},{8,11},{9,10},{10,... | collective-permute-start | bytes 393224 | tf_op jit(solution)/shard_map/ppermute | solution.py:359
  11.6 8.2 %collective-permute-start.2 = (bf16[256,256]{1,0:T(8,128)(2,1)S(1)}, bf16[256,256]{1,0:T(8,128)(2,1)S(1)}, u32[]{:S(2)}, u32[]{:S(2)}) collective-permute-start(bf16[256,256]{1,0:T(8,128)(2,1)S(1)} %collective-permute-done.across), channel_id=1, source_target_pairs={{0,1},{1,0},{2,3},{3,2},{4,5},{5,4},{6,7},{7,6},{8,9},{9,8},{10,11... | collective-permute-start | bytes 393224 | tf_op jit(solution)/shard_map/ppermute | solution.py:359
  15.0 10.5 %collective-permute-start.8 = (bf16[256,256]{1,0:T(8,128)(2,1)S(1)}, bf16[256,256]{1,0:T(8,128)(2,1)S(1)}, u32[]{:S(2)}, u32[]{:S(2)}) collective-permute-start(bf16[256,256]{1,0:T(8,128)(2,1)S(1)} %get-tuple-element.31.refs_0_), channel_id=1, source_target_pairs={{0,1},{1,0},{2,3},{3,2},{4,5},{5,4},{6,7},{7,6},{8,9},{9,8},{10,11... | collective-permute-start | bytes 393224 | tf_op jit(solution)/shard_map/ppermute | solution.py:359
  17.4 8.1 %collective-permute-start.10 = (bf16[256,256]{1,0:T(8,128)(2,1)S(1)}, bf16[256,256]{1,0:T(8,128)(2,1)S(1)}, u32[]{:S(2)}, u32[]{:S(2)}) collective-permute-start(bf16[256,256]{1,0:T(8,128)(2,1)S(1)} %collective-permute-done.9.refs_3_), channel_id=1, source_target_pairs={{0,1},{1,0},{2,3},{3,2},{4,5},{5,4},{6,7},{7,6},{8,9},{9,8},{10,11... | collective-permute-start | bytes 393224 | tf_op jit(solution)/shard_map/ppermute | solution.py:359
  20.0 1.4 %collective-permute-start.4 = (bf16[256,256]{1,0:T(8,128)(2,1)S(1)}, bf16[256,256]{1,0:T(8,128)(2,1)S(1)}, u32[]{:S(2)}, u32[]{:S(2)}) collective-permute-start(bf16[256,256]{1,0:T(8,128)(2,1)S(1)} %shard_map.97), channel_id=1, source_target_pairs={{0,4},{4,0},{8,12},{12,8},{16,20},{20,16},{24,28},{28,24},{1,5},{5... | collective-permute-start | bytes 393224 | tf_op jit(solution)/shard_map/ppermute | solution.py:359
  20.3 2.8 %collective-permute-start.3 = (bf16[768,256]{1,0:T(8,128)(2,1)S(1)}, bf16[768,256]{1,0:T(8,128)(2,1)S(1)}, u32[]{:S(2)}, u32[]{:S(2)}) collective-permute-start(bf16[768,256]{1,0:T(8,128)(2,1)S(1)} %shard_map.95), channel_id=1, source_target_pairs={{0,4},{4,0},{8,12},{12,8},{16,20},{20,16},{24,28},{28,24},{1,5},{5... | collective-permute-start | bytes 1179656 | tf_op jit(solution)/shard_map/ppermute | solution.py:359
  21.4 9.8 %collective-permute-start.5 = (bf16[256,256]{1,0:T(8,128)(2,1)S(1)}, bf16[256,256]{1,0:T(8,128)(2,1)S(1)}, u32[]{:S(2)}, u32[]{:S(2)}) collective-permute-start(bf16[256,256]{1,0:T(8,128)(2,1)S(1)} %shard_map.98), channel_id=1, source_target_pairs={{0,8},{4,20},{8,0},{12,28},{16,24},{20,4},{24,16},{28,12},{1,9},{5... | collective-permute-start | bytes 393224 | tf_op jit(solution)/shard_map/ppermute | solution.py:366
  23.2 8.6 %collective-permute-start.6 = (bf16[256,256]{1,0:T(8,128)(2,1)S(1)}, bf16[256,256]{1,0:T(8,128)(2,1)S(1)}, u32[]{:S(2)}, u32[]{:S(2)}) collective-permute-start(bf16[256,256]{1,0:T(8,128)(2,1)S(1)} %get-tuple-element.27), channel_id=1, source_target_pairs={{0,16},{4,12},{8,24},{12,4},{16,0},{20,28},{24,8},{28,20},{1,17},{... | collective-permute-start | bytes 393224 | tf_op jit(solution)/shard_map/ppermute | solution.py:366
  24.8 7.1 %collective-permute-start.7 = (bf16[256,256]{1,0:T(8,128)(2,1)S(1)}, bf16[256,256]{1,0:T(8,128)(2,1)S(1)}, u32[]{:S(2)}, u32[]{:S(2)}) collective-permute-start(bf16[256,256]{1,0:T(8,128)(2,1)S(1)} %get-tuple-element.28), channel_id=1, source_target_pairs={{0,24},{4,28},{8,16},{12,20},{16,8},{20,12},{24,0},{28,4},{1,25},{... | collective-permute-start | bytes 393224 | tf_op jit(solution)/shard_map/ppermute | solution.py:366
  26.2 5.7 %copy-start = (f32[256]{0:T(256)S(1)}, f32[256]{0:T(256)}, u32[]{:S(2)}) copy-start(f32[256]{0:T(256)} %param.12) | copy-start | bytes 3076
  26.2 2.0 %collective-permute-start.11 = (bf16[1024,256]{1,0:T(8,128)(2,1)S(1)}, bf16[1024,256]{1,0:T(8,128)(2,1)S(1)}, u32[]{:S(2)}, u32[]{:S(2)}) collective-permute-start(bf16[1024,256]{1,0:T(8,128)(2,1)S(1)} %shard_map.101), channel_id=1, source_target_pairs={{0,4},{4,0},{8,12},{12,8},{16,20},{20,16},{24,28},{28,24},{1,5},{5... | collective-permute-start | bytes 1572872 | tf_op jit(solution)/shard_map/ppermute | solution.py:359
  28.3 6.1 %collective-permute-start.12 = (bf16[256,256]{1,0:T(8,128)(2,1)S(1)}, bf16[256,256]{1,0:T(8,128)(2,1)S(1)}, u32[]{:S(2)}, u32[]{:S(2)}) collective-permute-start(bf16[256,256]{1,0:T(8,128)(2,1)S(1)} %get-tuple-element.36), channel_id=1, source_target_pairs={{0,8},{4,20},{8,0},{12,28},{16,24},{20,4},{24,16},{28,12},{1,9},{5... | collective-permute-start | bytes 393224 | tf_op jit(solution)/shard_map/ppermute | solution.py:366
  29.6 5.1 %collective-permute-start.13 = (bf16[256,256]{1,0:T(8,128)(2,1)S(1)}, bf16[256,256]{1,0:T(8,128)(2,1)S(1)}, u32[]{:S(2)}, u32[]{:S(2)}) collective-permute-start(bf16[256,256]{1,0:T(8,128)(2,1)S(1)} %get-tuple-element.37), channel_id=1, source_target_pairs={{0,16},{4,12},{8,24},{12,4},{16,0},{20,28},{24,8},{28,20},{1,17},{... | collective-permute-start | bytes 393224 | tf_op jit(solution)/shard_map/ppermute | solution.py:366
  31.2 6.7 %collective-permute-start.14 = (bf16[256,256]{1,0:T(8,128)(2,1)S(1)}, bf16[256,256]{1,0:T(8,128)(2,1)S(1)}, u32[]{:S(2)}, u32[]{:S(2)}) collective-permute-start(bf16[256,256]{1,0:T(8,128)(2,1)S(1)} %get-tuple-element.38), channel_id=1, source_target_pairs={{0,24},{4,28},{8,16},{12,20},{16,8},{20,12},{24,0},{28,4},{1,25},{... | collective-permute-start | bytes 393224 | tf_op jit(solution)/shard_map/ppermute | solution.py:366

commit v16 on v15

--- a/solution.py
+++ b/solution.py
@@ -35,29 +35,36 @@
 def project_kernel(features_hbm, weight_hbm, norm_hbm, projected, *refs):
     *scaled, features, weight, norm, sems = refs
     width, lanes = scaled[0].shape[1], norm.shape[1]
-    spans = [slice(k * width, (k + 1) * width) for k in range(len(scaled))]
+    half = weight.shape[0] // 2
+    top, bottom = slice(0, half), slice(half, 2 * half)
     copies = [
-        pltpu.make_async_copy(features_hbm, features, sems.at[0]),
-        pltpu.make_async_copy(norm_hbm, norm, sems.at[1]),
+        pltpu.make_async_copy(source, target, sems.at[k])
+        for k, (source, target) in enumerate(
+            [
+                (weight_hbm.at[top], weight.at[top]),
+                (features_hbm, features),
+                (norm_hbm, norm),
+                (weight_hbm.at[bottom], weight.at[bottom]),
+            ]
+        )
     ]
-    copies += [
-        pltpu.make_async_copy(weight_hbm.at[:, span], weight.at[:, span], sems.at[2 + k])
-        for k, span in enumerate(spans)
-    ]
-    for k in (0, 2, 1, *range(3, len(copies))):
-        copies[k].start()
-    copies[0].wait()
-    copies[1].wait()
-    for k, (span, target) in enumerate(zip(spans, scaled)):
-        copies[2 + k].wait()
-        value = jnp.dot(features[...], weight[:, span], preferred_element_type=jnp.float32)
-        projected[:, span] = value
-        for part in range(norm.shape[0]):
-            factor = rows_to_lanes(norm[part : part + 1, :], lanes)
-            here = slice(part * lanes, (part + 1) * lanes)
-            for column in range(0, width, lanes):
-                piece = factor * value[here, column : column + lanes]
-                target[here, column : column + lanes] = piece.astype(target.dtype)
+    for copy in copies:
+        copy.start()
+    for copy in copies[:3]:
+        copy.wait()
+    value = jnp.dot(features[:, top], weight[top, :], preferred_element_type=jnp.float32)
+    copies[3].wait()
+    value += jnp.dot(features[:, bottom], weight[bottom, :], preferred_element_type=jnp.float32)
+    projected[...] = value
+    for part in range(norm.shape[0]):
+        factor = rows_to_lanes(norm[part : part + 1, :], lanes)
+        for column in range(0, value.shape[1], lanes):
+            piece = value[part * lanes : (part + 1) * lanes, column : column + lanes]
+            target = scaled[column // width]
+            start = column % width
+            target[part * lanes : (part + 1) * lanes, start : start + lanes] = (
+                factor * piece
+            ).astype(target.dtype)
 
 
 def project(features, weight, source_norm, chunks):
@@ -74,7 +81,7 @@
             pltpu.VMEM(features.shape, features.dtype),
             pltpu.VMEM(weight.shape, weight.dtype),
             pltpu.VMEM(norm.shape, norm.dtype),
-            pltpu.SemaphoreType.DMA((2 + chunks,)),
+            pltpu.SemaphoreType.DMA((4,)),
         ],
         compiler_params=params(12),
         cost_estimate=cost(2 * rows * depth * hidden, 2 * depth * (rows + hidden)),

time: 38.8 us -> 38.6 us (level)
  transfers between devices with their start and end apart: 15 -> 15, of which waited for: 7 -> 8; matrix products, arithmetic and copies ran while one was open for 0% -> 0% of each run, Pallas kernels for 16% -> 16%
where the time goes in v16:
time: 38.6 us; the launch traced here: 38.4 us
  starting transfers between devices  19.2 us (50%)
  waiting for transfers between devices  9.66 us (25%)
  Pallas kernels  8.83 us (23%)
  between operations  0.77 us (2%)
    ppermute x9, starting transfers between devices, swap(): return lax.ppermute(value, axis, pairs)  11.6 us
    ppermute x6, starting transfers between devices, exchange(): lax.ppermute(value, 'row', [(i, i ^ step[i % 2]) for i in range(owners)])  7.55 us
    ppermute x6, waiting for transfers between devices, exchange(): lax.ppermute(value, 'row', [(i, i ^ step[i % 2]) for i in range(owners)])  5.92 us
    ppermute x9, waiting for transfers between devices, swap(): return lax.ppermute(value, axis, pairs)  3.74 us
    pallas_call x1, Pallas kernels, merge_tiles(): pl.pallas_call(functools.partial(merge_kernel, own_tiles, labels.shape[1]...  2.77 us
    pallas_call x1, Pallas kernels, project(): pl.pallas_call(project_kernel, out_shape=[jax.ShapeDtypeStruct((rows, hid...  1.85 us
    pallas_call x2, Pallas kernels, product(): pl.pallas_call(functools.partial(product_kernel, first), out_shape=jax.Sh...  1.42 us
    pallas_call x1, Pallas kernels, early_product(): pl.pallas_call(early_kernel, out_shape=jax.ShapeDtypeStruct((total, width...  0.98 us
  transfers between devices with their start and end apart: 15, of which 8 were waited for; matrix products, arithmetic and copies ran while one was open for 0% of the time, Pallas kernels for 16%

profile of v16, /device:TPU:0, one launch (start us, length us, event | category | flops | bytes accessed | tf_op | source)
XLA Modules:
  0.0 38.4 jit_solution(9185304088463532854)
XLA Ops:
  0.0 1.8 %shard_map.91 = (f32[256,512]{1,0:T(8,128)S(1)}, bf16[256,256]{1,0:T(8,128)(2,1)S(1)}, bf16[256,256]{1,0:T(8,128)(2,1)S(1)}) custom-call(bf16[256,1024]{1,0:T(8,128)(2,1)} %features_hbm.1, bf16[1024,512]{1,0:T(8,128)(2,1)} %weight_hbm.1, f32[2,128]{1,0:T(2,128)} %bitcast.6), custom_call_target="tpu_custom_call" | custom-call | flops 268435456 | bytes 1572864 | tf_op jit(solution)/shard_map/pallas_call | solution.py:74
  1.9 5.1 %collective-permute-start = (bf16[256,256]{1,0:T(8,128)(2,1)S(1)}, bf16[256,256]{1,0:T(8,128)(2,1)S(1)}, u32[]{:S(2)}, u32[]{:S(2)}) collective-permute-start(bf16[256,256]{1,0:T(8,128)(2,1)S(1)} %get-tuple-element.23.own), channel_id=1, source_target_pairs={{0,3},{1,2},{2,1},{3,0},{4,7},{5,6},{6,5},{7,4},{8,11},{9,10},{10,... | collective-permute-start | bytes 393224 | tf_op jit(solution)/shard_map/ppermute | solution.py:366
  7.0 0.9 %collective-permute-start.9 = (bf16[256,256]{1,0:T(8,128)(2,1)S(1)}, bf16[256,256]{1,0:T(8,128)(2,1)S(1)}, u32[]{:S(2)}, u32[]{:S(2)}) collective-permute-start(bf16[256,256]{1,0:T(8,128)(2,1)S(1)} %get-tuple-element.31.refs_0_), channel_id=1, source_target_pairs={{0,3},{1,2},{2,1},{3,0},{4,7},{5,6},{6,5},{7,4},{8,11},{9,10},{10,... | collective-permute-start | bytes 393224 | tf_op jit(solution)/shard_map/ppermute | solution.py:366
  8.5 2.8 %shard_map.92.matrix = bf16[2048,1024]{1,0:T(8,128)(2,1)S(1)} custom-call(s32[1]{0:T(128)} %bitcast.2.row, s32[1]{0:T(128)} %bitcast.3.column, s32[1]{0:T(128)S(6)} %copy.10.count, s32[1,64]{1,0:T(1,128)} %sources_hbm.1, s32[1,64]{1,0:T(1,128)} %targets_hbm.1, s32[1,16]{1,0:T(1,128)} %labels_hbm.1, bf16[1,64,128,128]{3,2,1,0:T(8,128)(2,1)} %tiles_hbm.1), custom_call_target="tpu_custom_call" | custom-call | flops 8388608 | bytes 12582912 | tf_op jit(solution)/shard_map/pallas_call | solution.py:160
  11.3 3.4 %collective-permute-start.2 = (bf16[256,256]{1,0:T(8,128)(2,1)S(1)}, bf16[256,256]{1,0:T(8,128)(2,1)S(1)}, u32[]{:S(2)}, u32[]{:S(2)}) collective-permute-start(bf16[256,256]{1,0:T(8,128)(2,1)S(1)} %collective-permute-done.across), channel_id=1, source_target_pairs={{0,1},{1,0},{2,3},{3,2},{4,5},{5,4},{6,7},{7,6},{8,9},{9,8},{10,11... | collective-permute-start | bytes 393224 | tf_op jit(solution)/shard_map/ppermute | solution.py:366
  14.8 1.4 %collective-permute-done.1.beside = bf16[256,256]{1,0:T(8,128)(2,1)S(1)} collective-permute-done((bf16[256,256]{1,0:T(8,128)(2,1)S(1)}, bf16[256,256]{1,0:T(8,128)(2,1)S(1)}, u32[]{:S(2)}, u32[]{:S(2)}) %collective-permute-start.1) | collective-permute-done | bytes 131104 | tf_op jit(solution)/shard_map/ppermute | solution.py:366
  16.2 1.0 %shard_map.93.early = f32[2048,256]{1,0:T(8,128)S(1)} custom-call(bf16[2048,1024]{1,0:T(8,128)(2,1)S(1)} %shard_map.92.matrix, bf16[256,256]{1,0:T(8,128)(2,1)S(1)} %get-tuple-element.23.own, bf16[256,256]{1,0:T(8,128)(2,1)S(1)} %collective-permute-done.1.beside, bf16[256,256]{1,0:T(8,128)(2,1)S(1)} %collective-permute-done.across), custom_call_target="tpu_custom_call" | custom-call | flops 536870912 | bytes 1 | tf_op jit(solution)/shard_map/pallas_call | solution.py:194
  17.2 1.4 %collective-permute-start.10 = (bf16[256,256]{1,0:T(8,128)(2,1)S(1)}, bf16[256,256]{1,0:T(8,128)(2,1)S(1)}, u32[]{:S(2)}, u32[]{:S(2)}) collective-permute-start(bf16[256,256]{1,0:T(8,128)(2,1)S(1)} %collective-permute-done.9.refs_3_), channel_id=1, source_target_pairs={{0,1},{1,0},{2,3},{3,2},{4,5},{5,4},{6,7},{7,6},{8,9},{9,8},{10,11... | collective-permute-start | bytes 393224 | tf_op jit(solution)/shard_map/ppermute | solution.py:366
  18.6 0.9 %collective-permute-done.2.passed = bf16[256,256]{1,0:T(8,128)(2,1)S(1)} collective-permute-done((bf16[256,256]{1,0:T(8,128)(2,1)S(1)}, bf16[256,256]{1,0:T(8,128)(2,1)S(1)}, u32[]{:S(2)}, u32[]{:S(2)}) %collective-permute-start.2) | collective-permute-done | bytes 131104 | tf_op jit(solution)/shard_map/ppermute | solution.py:366
  19.5 0.2 shard_map.97
  19.7 0.1 collective-permute-start.4
  19.8 0.3 shard_map.95
  20.1 0.6 %collective-permute-start.3 = (bf16[768,256]{1,0:T(8,128)(2,1)S(1)}, bf16[768,256]{1,0:T(8,128)(2,1)S(1)}, u32[]{:S(2)}, u32[]{:S(2)}) collective-permute-start(bf16[768,256]{1,0:T(8,128)(2,1)S(1)} %shard_map.95), channel_id=1, source_target_pairs={{0,4},{4,0},{8,12},{12,8},{16,20},{20,16},{24,28},{28,24},{1,5},{5... | collective-permute-start | bytes 1179656 | tf_op jit(solution)/shard_map/ppermute | solution.py:366
  20.7 0.3 shard_map.94.stay
  21.0 0.2 collective-permute-done.4.came
  21.2 1.7 %collective-permute-start.5 = (bf16[256,256]{1,0:T(8,128)(2,1)S(1)}, bf16[256,256]{1,0:T(8,128)(2,1)S(1)}, u32[]{:S(2)}, u32[]{:S(2)}) collective-permute-start(bf16[256,256]{1,0:T(8,128)(2,1)S(1)} %shard_map.98), channel_id=1, source_target_pairs={{0,8},{4,20},{8,0},{12,28},{16,24},{20,4},{24,16},{28,12},{1,9},{5... | collective-permute-start | bytes 393224 | tf_op jit(solution)/shard_map/ppermute | solution.py:373
  22.9 0.1 shard_map.96
  23.0 1.6 %collective-permute-start.6 = (bf16[256,256]{1,0:T(8,128)(2,1)S(1)}, bf16[256,256]{1,0:T(8,128)(2,1)S(1)}, u32[]{:S(2)}, u32[]{:S(2)}) collective-permute-start(bf16[256,256]{1,0:T(8,128)(2,1)S(1)} %get-tuple-element.27), channel_id=1, source_target_pairs={{0,16},{4,12},{8,24},{12,4},{16,0},{20,28},{24,8},{28,20},{1,17},{... | collective-permute-start | bytes 393224 | tf_op jit(solution)/shard_map/ppermute | solution.py:373
  24.6 0.7 %collective-permute-start.7 = (bf16[256,256]{1,0:T(8,128)(2,1)S(1)}, bf16[256,256]{1,0:T(8,128)(2,1)S(1)}, u32[]{:S(2)}, u32[]{:S(2)}) collective-permute-start(bf16[256,256]{1,0:T(8,128)(2,1)S(1)} %get-tuple-element.28), channel_id=1, source_target_pairs={{0,24},{4,28},{8,16},{12,20},{16,8},{20,12},{24,0},{28,4},{1,25},{... | collective-permute-start | bytes 393224 | tf_op jit(solution)/shard_map/ppermute | solution.py:373
  25.3 0.7 %shard_map.101 = bf16[1024,256]{1,0:T(8,128)(2,1)S(1)} custom-call(bf16[2048,1024]{1,0:T(8,128)(2,1)S(1)} %shard_map.92.matrix, bf16[256,256]{1,0:T(8,128)(2,1)S(1)} %get-tuple-element.31.refs_0_, bf16[256,256]{1,0:T(8,128)(2,1)S(1)} %collective-permute-done.8.refs_1_, bf16[256,256]{1,0:T(8,128)(2,1)S(1)} %collective-permute-done.10.refs_2_, ...), custom_call_target="tpu_custom_call" | custom-call | bytes 1 | tf_op jit(solution)/shard_map/pallas_call | solution.py:242
  26.0 0.1 collective-permute-start.11
  26.1 0.7 %shard_map.100.stay = f32[1024,256]{1,0:T(8,128)S(1)} custom-call(bf16[2048,1024]{1,0:T(8,128)(2,1)S(1)} %shard_map.92.matrix, bf16[256,256]{1,0:T(8,128)(2,1)S(1)} %get-tuple-element.31.refs_0_, bf16[256,256]{1,0:T(8,128)(2,1)S(1)} %collective-permute-done.8.refs_1_, bf16[256,256]{1,0:T(8,128)(2,1)S(1)} %collective-permute-done.10.refs_2_, ...), custom_call_target="tpu_custom_call" | custom-call | flops 10737418240 | bytes 1 | tf_op jit(solution)/shard_map/pallas_call | solution.py:242
  26.8 1.2 %collective-permute-done.11.came = bf16[1024,256]{1,0:T(8,128)(2,1)S(1)} collective-permute-done((bf16[1024,256]{1,0:T(8,128)(2,1)S(1)}, bf16[1024,256]{1,0:T(8,128)(2,1)S(1)}, u32[]{:S(2)}, u32[]{:S(2)}) %collective-permute-start.11) | collective-permute-done | bytes 524320 | tf_op jit(solution)/shard_map/ppermute | solution.py:366
  28.0 0.1 shard_map.102
  28.1 1.3 %collective-permute-start.12 = (bf16[256,256]{1,0:T(8,128)(2,1)S(1)}, bf16[256,256]{1,0:T(8,128)(2,1)S(1)}, u32[]{:S(2)}, u32[]{:S(2)}) collective-permute-start(bf16[256,256]{1,0:T(8,128)(2,1)S(1)} %get-tuple-element.36), channel_id=1, source_target_pairs={{0,8},{4,20},{8,0},{12,28},{16,24},{20,4},{24,16},{28,12},{1,9},{5... | collective-permute-start | bytes 393224 | tf_op jit(solution)/shard_map/ppermute | solution.py:373
  29.4 1.5 %collective-permute-start.13 = (bf16[256,256]{1,0:T(8,128)(2,1)S(1)}, bf16[256,256]{1,0:T(8,128)(2,1)S(1)}, u32[]{:S(2)}, u32[]{:S(2)}) collective-permute-start(bf16[256,256]{1,0:T(8,128)(2,1)S(1)} %get-tuple-element.37), channel_id=1, source_target_pairs={{0,16},{4,12},{8,24},{12,4},{16,0},{20,28},{24,8},{28,20},{1,17},{... | collective-permute-start | bytes 393224 | tf_op jit(solution)/shard_map/ppermute | solution.py:373
  30.9 0.7 %collective-permute-start.14 = (bf16[256,256]{1,0:T(8,128)(2,1)S(1)}, bf16[256,256]{1,0:T(8,128)(2,1)S(1)}, u32[]{:S(2)}, u32[]{:S(2)}) collective-permute-start(bf16[256,256]{1,0:T(8,128)(2,1)S(1)} %get-tuple-element.38), channel_id=1, source_target_pairs={{0,24},{4,28},{8,16},{12,20},{16,8},{20,12},{24,0},{28,4},{1,25},{... | collective-permute-start | bytes 393224 | tf_op jit(solution)/shard_map/ppermute | solution.py:373
  31.6 0.1 shard_map.99.ready
  31.7 2.4 %collective-permute-done.12.refs_1_ = bf16[256,256]{1,0:T(8,128)(2,1)S(1)} collective-permute-done((bf16[256,256]{1,0:T(8,128)(2,1)S(1)}, bf16[256,256]{1,0:T(8,128)(2,1)S(1)}, u32[]{:S(2)}, u32[]{:S(2)}) %collective-permute-start.12) | collective-permute-done | bytes 131104 | tf_op jit(solution)/shard_map/ppermute | solution.py:373
  34.2 0.3 collective-permute-done.13.refs_2_
  34.5 3.2 %collective-permute-done.14.refs_3_ = bf16[256,256]{1,0:T(8,128)(2,1)S(1)} collective-permute-done((bf16[256,256]{1,0:T(8,128)(2,1)S(1)}, bf16[256,256]{1,0:T(8,128)(2,1)S(1)}, u32[]{:S(2)}, u32[]{:S(2)}) %collective-permute-start.14) | collective-permute-done | bytes 131104 | tf_op jit(solution)/shard_map/ppermute | solution.py:373
  37.7 0.8 %shard_map.103 = bf16[256,512]{1,0:T(8,128)(2,1)} custom-call(bf16[256,256]{1,0:T(8,128)(2,1)S(1)} %shard_map.99.ready, f32[256,512]{1,0:T(8,128)S(1)} %get-tuple-element.22.projected, f32[2,128]{1,0:T(2,128)S(1)} %bitcast.5, f32[256,256]{1,0:T(8,128)S(1)} %get-tuple-element.35.refs_0_, bf16[256,256]{1,0:T(8,128)(2,1)S(1)} %collective-permute-done.12.refs_1_, ...), custom_call_target="tpu_custom_call" | custom-call | flops 393216 | bytes 1048576 | tf_op jit(solution)/shard_map/pallas_call | solution.py:316
  (13 shorter events, 0.1 us)
Async XLA Ops:
  1.9 9.5 %collective-permute-start = (bf16[256,256]{1,0:T(8,128)(2,1)S(1)}, bf16[256,256]{1,0:T(8,128)(2,1)S(1)}, u32[]{:S(2)}, u32[]{:S(2)}) collective-permute-start(bf16[256,256]{1,0:T(8,128)(2,1)S(1)} %get-tuple-element.23.own), channel_id=1, source_target_pairs={{0,3},{1,2},{2,1},{3,0},{4,7},{5,6},{6,5},{7,4},{8,11},{9,10},{10,... | collective-permute-start | bytes 393224 | tf_op jit(solution)/shard_map/ppermute | solution.py:366
  7.0 9.2 %collective-permute-start.1 = (bf16[256,256]{1,0:T(8,128)(2,1)S(1)}, bf16[256,256]{1,0:T(8,128)(2,1)S(1)}, u32[]{:S(2)}, u32[]{:S(2)}) collective-permute-start(bf16[256,256]{1,0:T(8,128)(2,1)S(1)} %get-tuple-element.23.own), channel_id=1, source_target_pairs={{0,1},{1,0},{2,3},{3,2},{4,5},{5,4},{6,7},{7,6},{8,9},{9,8},{10,11... | collective-permute-start | bytes 393224 | tf_op jit(solution)/shard_map/ppermute | solution.py:366
  7.0 10.2 %collective-permute-start.9 = (bf16[256,256]{1,0:T(8,128)(2,1)S(1)}, bf16[256,256]{1,0:T(8,128)(2,1)S(1)}, u32[]{:S(2)}, u32[]{:S(2)}) collective-permute-start(bf16[256,256]{1,0:T(8,128)(2,1)S(1)} %get-tuple-element.31.refs_0_), channel_id=1, source_target_pairs={{0,3},{1,2},{2,1},{3,0},{4,7},{5,6},{6,5},{7,4},{8,11},{9,10},{10,... | collective-permute-start | bytes 393224 | tf_op jit(solution)/shard_map/ppermute | solution.py:366
  11.3 8.2 %collective-permute-start.2 = (bf16[256,256]{1,0:T(8,128)(2,1)S(1)}, bf16[256,256]{1,0:T(8,128)(2,1)S(1)}, u32[]{:S(2)}, u32[]{:S(2)}) collective-permute-start(bf16[256,256]{1,0:T(8,128)(2,1)S(1)} %collective-permute-done.across), channel_id=1, source_target_pairs={{0,1},{1,0},{2,3},{3,2},{4,5},{5,4},{6,7},{7,6},{8,9},{9,8},{10,11... | collective-permute-start | bytes 393224 | tf_op jit(solution)/shard_map/ppermute | solution.py:366
  14.8 10.5 %collective-permute-start.8 = (bf16[256,256]{1,0:T(8,128)(2,1)S(1)}, bf16[256,256]{1,0:T(8,128)(2,1)S(1)}, u32[]{:S(2)}, u32[]{:S(2)}) collective-permute-start(bf16[256,256]{1,0:T(8,128)(2,1)S(1)} %get-tuple-element.31.refs_0_), channel_id=1, source_target_pairs={{0,1},{1,0},{2,3},{3,2},{4,5},{5,4},{6,7},{7,6},{8,9},{9,8},{10,11... | collective-permute-start | bytes 393224 | tf_op jit(solution)/shard_map/ppermute | solution.py:366
  17.2 8.1 %collective-permute-start.10 = (bf16[256,256]{1,0:T(8,128)(2,1)S(1)}, bf16[256,256]{1,0:T(8,128)(2,1)S(1)}, u32[]{:S(2)}, u32[]{:S(2)}) collective-permute-start(bf16[256,256]{1,0:T(8,128)(2,1)S(1)} %collective-permute-done.9.refs_3_), channel_id=1, source_target_pairs={{0,1},{1,0},{2,3},{3,2},{4,5},{5,4},{6,7},{7,6},{8,9},{9,8},{10,11... | collective-permute-start | bytes 393224 | tf_op jit(solution)/shard_map/ppermute | solution.py:366
  19.7 1.4 %collective-permute-start.4 = (bf16[256,256]{1,0:T(8,128)(2,1)S(1)}, bf16[256,256]{1,0:T(8,128)(2,1)S(1)}, u32[]{:S(2)}, u32[]{:S(2)}) collective-permute-start(bf16[256,256]{1,0:T(8,128)(2,1)S(1)} %shard_map.97), channel_id=1, source_target_pairs={{0,4},{4,0},{8,12},{12,8},{16,20},{20,16},{24,28},{28,24},{1,5},{5... | collective-permute-start | bytes 393224 | tf_op jit(solution)/shard_map/ppermute | solution.py:366
  20.1 2.8 %collective-permute-start.3 = (bf16[768,256]{1,0:T(8,128)(2,1)S(1)}, bf16[768,256]{1,0:T(8,128)(2,1)S(1)}, u32[]{:S(2)}, u32[]{:S(2)}) collective-permute-start(bf16[768,256]{1,0:T(8,128)(2,1)S(1)} %shard_map.95), channel_id=1, source_target_pairs={{0,4},{4,0},{8,12},{12,8},{16,20},{20,16},{24,28},{28,24},{1,5},{5... | collective-permute-start | bytes 1179656 | tf_op jit(solution)/shard_map/ppermute | solution.py:366
  21.2 9.8 %collective-permute-start.5 = (bf16[256,256]{1,0:T(8,128)(2,1)S(1)}, bf16[256,256]{1,0:T(8,128)(2,1)S(1)}, u32[]{:S(2)}, u32[]{:S(2)}) collective-permute-start(bf16[256,256]{1,0:T(8,128)(2,1)S(1)} %shard_map.98), channel_id=1, source_target_pairs={{0,8},{4,20},{8,0},{12,28},{16,24},{20,4},{24,16},{28,12},{1,9},{5... | collective-permute-start | bytes 393224 | tf_op jit(solution)/shard_map/ppermute | solution.py:373
  23.0 8.6 %collective-permute-start.6 = (bf16[256,256]{1,0:T(8,128)(2,1)S(1)}, bf16[256,256]{1,0:T(8,128)(2,1)S(1)}, u32[]{:S(2)}, u32[]{:S(2)}) collective-permute-start(bf16[256,256]{1,0:T(8,128)(2,1)S(1)} %get-tuple-element.27), channel_id=1, source_target_pairs={{0,16},{4,12},{8,24},{12,4},{16,0},{20,28},{24,8},{28,20},{1,17},{... | collective-permute-start | bytes 393224 | tf_op jit(solution)/shard_map/ppermute | solution.py:373
  24.6 7.1 %collective-permute-start.7 = (bf16[256,256]{1,0:T(8,128)(2,1)S(1)}, bf16[256,256]{1,0:T(8,128)(2,1)S(1)}, u32[]{:S(2)}, u32[]{:S(2)}) collective-permute-start(bf16[256,256]{1,0:T(8,128)(2,1)S(1)} %get-tuple-element.28), channel_id=1, source_target_pairs={{0,24},{4,28},{8,16},{12,20},{16,8},{20,12},{24,0},{28,4},{1,25},{... | collective-permute-start | bytes 393224 | tf_op jit(solution)/shard_map/ppermute | solution.py:373
  26.0 5.6 %copy-start = (f32[256]{0:T(256)S(1)}, f32[256]{0:T(256)}, u32[]{:S(2)}) copy-start(f32[256]{0:T(256)} %param.12) | copy-start | bytes 3076
  26.0 2.0 %collective-permute-start.11 = (bf16[1024,256]{1,0:T(8,128)(2,1)S(1)}, bf16[1024,256]{1,0:T(8,128)(2,1)S(1)}, u32[]{:S(2)}, u32[]{:S(2)}) collective-permute-start(bf16[1024,256]{1,0:T(8,128)(2,1)S(1)} %shard_map.101), channel_id=1, source_target_pairs={{0,4},{4,0},{8,12},{12,8},{16,20},{20,16},{24,28},{28,24},{1,5},{5... | collective-permute-start | bytes 1572872 | tf_op jit(solution)/shard_map/ppermute | solution.py:366
  28.1 6.1 %collective-permute-start.12 = (bf16[256,256]{1,0:T(8,128)(2,1)S(1)}, bf16[256,256]{1,0:T(8,128)(2,1)S(1)}, u32[]{:S(2)}, u32[]{:S(2)}) collective-permute-start(bf16[256,256]{1,0:T(8,128)(2,1)S(1)} %get-tuple-element.36), channel_id=1, source_target_pairs={{0,8},{4,20},{8,0},{12,28},{16,24},{20,4},{24,16},{28,12},{1,9},{5... | collective-permute-start | bytes 393224 | tf_op jit(solution)/shard_map/ppermute | solution.py:373
  29.4 5.1 %collective-permute-start.13 = (bf16[256,256]{1,0:T(8,128)(2,1)S(1)}, bf16[256,256]{1,0:T(8,128)(2,1)S(1)}, u32[]{:S(2)}, u32[]{:S(2)}) collective-permute-start(bf16[256,256]{1,0:T(8,128)(2,1)S(1)} %get-tuple-element.37), channel_id=1, source_target_pairs={{0,16},{4,12},{8,24},{12,4},{16,0},{20,28},{24,8},{28,20},{1,17},{... | collective-permute-start | bytes 393224 | tf_op jit(solution)/shard_map/ppermute | solution.py:373
  30.9 6.7 %collective-permute-start.14 = (bf16[256,256]{1,0:T(8,128)(2,1)S(1)}, bf16[256,256]{1,0:T(8,128)(2,1)S(1)}, u32[]{:S(2)}, u32[]{:S(2)}) collective-permute-start(bf16[256,256]{1,0:T(8,128)(2,1)S(1)} %get-tuple-element.38), channel_id=1, source_target_pairs={{0,24},{4,28},{8,16},{12,20},{16,8},{20,12},{24,0},{28,4},{1,25},{... | collective-permute-start | bytes 393224 | tf_op jit(solution)/shard_map/ppermute | solution.py:373

commit v17 on v16

--- a/solution.py
+++ b/solution.py
@@ -425,12 +425,14 @@
     onward, _ = lax.optimization_barrier((across[1], early))
     blocks = scaled[1], beside[1], swap(onward, "col", 1), across[1]
     blocks, _ = lax.optimization_barrier((blocks, sent))
-    away = product(matrix, blocks, 0, half, jnp.bfloat16, WEIGHTS[2])
+    away = [
+        product(matrix, blocks, start, count, jnp.bfloat16, WEIGHTS[2])
+        for start, count in ((0, own_rows), (own_rows, half - own_rows))
+    ]
     stay = product(matrix, blocks, half, half, jnp.float32, WEIGHTS[3])
-    came = swap(away, "row", 1)
-    lead, kept, *sent = join(
-        stay, came, 0, own_rows, [jnp.bfloat16, jnp.float32] + [jnp.bfloat16] * 2
-    )
+    came = [swap(value, "row", 1) for value in away]
+    (lead,) = join(stay, came[0], 0, own_rows, [jnp.bfloat16])
+    kept, *sent = join(stay, came[1], own_rows, own_rows, [jnp.float32] + [jnp.bfloat16] * 2)
     pieces.append([kept] + exchange([lead] + sent))
     return finish(projected, target_norm, pieces)
 

time: 38.6 us -> 38.7 us (level)
  waiting for transfers between devices: 9.66 us -> 9.03 us
  starting transfers between devices: 19.2 us -> 19.7 us
    ppermute x9 -> x10, waiting for transfers between devices: 3.74 us -> 2.69 us  [swap(): return lax.ppermute(value, axis, pairs)]
    ppermute x9 -> x10, starting transfers between devices: 11.6 us -> 12.1 us  [swap(): return lax.ppermute(value, axis, pairs)]
    ppermute x6, waiting for transfers between devices: 5.92 us -> 6.35 us  [exchange(): lax.ppermute(value, 'row', [(i, i ^ step[i % 2]) for i in range(owners)])]
    pallas_call x2 -> x3, Pallas kernels: 1.42 us -> 1.6 us  [product(): pl.pallas_call(functools.partial(product_kernel, first), out_shape=jax.Sh...]
  transfers between devices with their start and end apart: 15 -> 16, of which waited for: 8 -> 9; matrix products, arithmetic and copies ran while one was open for 0% -> 0% of each run, Pallas kernels for 16% -> 16%
where the time goes in v17:
time: 38.7 us; the launch traced here: 38.6 us
  starting transfers between devices  19.7 us (51%)
  waiting for transfers between devices  9.03 us (23%)
  Pallas kernels  9 us (23%)
  between operations  0.78 us (2%)
    ppermute x10, starting transfers between devices, swap(): return lax.ppermute(value, axis, pairs)  12.1 us
    ppermute x6, starting transfers between devices, exchange(): lax.ppermute(value, 'row', [(i, i ^ step[i % 2]) for i in range(owners)])  7.62 us
    ppermute x6, waiting for transfers between devices, exchange(): lax.ppermute(value, 'row', [(i, i ^ step[i % 2]) for i in range(owners)])  6.35 us
    pallas_call x1, Pallas kernels, merge_tiles(): pl.pallas_call(functools.partial(merge_kernel, own_tiles, labels.shape[1]...  2.76 us
    ppermute x10, waiting for transfers between devices, swap(): return lax.ppermute(value, axis, pairs)  2.69 us
    pallas_call x1, Pallas kernels, project(): pl.pallas_call(project_kernel, out_shape=[jax.ShapeDtypeStruct((rows, hid...  1.85 us
    pallas_call x3, Pallas kernels, product(): pl.pallas_call(functools.partial(product_kernel, first), out_shape=jax.Sh...  1.6 us
    pallas_call x1, Pallas kernels, early_product(): pl.pallas_call(early_kernel, out_shape=jax.ShapeDtypeStruct((total, width...  0.98 us
  transfers between devices with their start and end apart: 16, of which 9 were waited for; matrix products, arithmetic and copies ran while one was open for 0% of the time, Pallas kernels for 16%

profile of v17, /device:TPU:0, one launch (start us, length us, event | category | flops | bytes accessed | tf_op | source)
XLA Modules:
  0.0 38.6 jit_solution(9948406265523469360)
XLA Ops:
  0.0 1.8 %shard_map.91 = (f32[256,512]{1,0:T(8,128)S(1)}, bf16[256,256]{1,0:T(8,128)(2,1)S(1)}, bf16[256,256]{1,0:T(8,128)(2,1)S(1)}) custom-call(bf16[256,1024]{1,0:T(8,128)(2,1)} %features_hbm.1, bf16[1024,512]{1,0:T(8,128)(2,1)} %weight_hbm.1, f32[2,128]{1,0:T(2,128)} %bitcast.6), custom_call_target="tpu_custom_call" | custom-call | flops 268435456 | bytes 1572864 | tf_op jit(solution)/shard_map/pallas_call | solution.py:74
  1.9 5.1 %collective-permute-start = (bf16[256,256]{1,0:T(8,128)(2,1)S(1)}, bf16[256,256]{1,0:T(8,128)(2,1)S(1)}, u32[]{:S(2)}, u32[]{:S(2)}) collective-permute-start(bf16[256,256]{1,0:T(8,128)(2,1)S(1)} %get-tuple-element.22.own), channel_id=1, source_target_pairs={{0,3},{1,2},{2,1},{3,0},{4,7},{5,6},{6,5},{7,4},{8,11},{9,10},{10,... | collective-permute-start | bytes 393224 | tf_op jit(solution)/shard_map/ppermute | solution.py:366
  7.0 0.9 %collective-permute-start.9 = (bf16[256,256]{1,0:T(8,128)(2,1)S(1)}, bf16[256,256]{1,0:T(8,128)(2,1)S(1)}, u32[]{:S(2)}, u32[]{:S(2)}) collective-permute-start(bf16[256,256]{1,0:T(8,128)(2,1)S(1)} %get-tuple-element.30.refs_0_), channel_id=1, source_target_pairs={{0,3},{1,2},{2,1},{3,0},{4,7},{5,6},{6,5},{7,4},{8,11},{9,10},{10,... | collective-permute-start | bytes 393224 | tf_op jit(solution)/shard_map/ppermute | solution.py:366
  8.5 2.8 %shard_map.92.matrix = bf16[2048,1024]{1,0:T(8,128)(2,1)S(1)} custom-call(s32[1]{0:T(128)} %bitcast.2.row, s32[1]{0:T(128)} %bitcast.3.column, s32[1]{0:T(128)S(6)} %copy.10.count, s32[1,64]{1,0:T(1,128)} %sources_hbm.1, s32[1,64]{1,0:T(1,128)} %targets_hbm.1, s32[1,16]{1,0:T(1,128)} %labels_hbm.1, bf16[1,64,128,128]{3,2,1,0:T(8,128)(2,1)} %tiles_hbm.1), custom_call_target="tpu_custom_call" | custom-call | flops 8388608 | bytes 12582912 | tf_op jit(solution)/shard_map/pallas_call | solution.py:160
  11.3 3.4 %collective-permute-start.2 = (bf16[256,256]{1,0:T(8,128)(2,1)S(1)}, bf16[256,256]{1,0:T(8,128)(2,1)S(1)}, u32[]{:S(2)}, u32[]{:S(2)}) collective-permute-start(bf16[256,256]{1,0:T(8,128)(2,1)S(1)} %collective-permute-done.across), channel_id=1, source_target_pairs={{0,1},{1,0},{2,3},{3,2},{4,5},{5,4},{6,7},{7,6},{8,9},{9,8},{10,11... | collective-permute-start | bytes 393224 | tf_op jit(solution)/shard_map/ppermute | solution.py:366
  14.8 1.4 %collective-permute-done.1.beside = bf16[256,256]{1,0:T(8,128)(2,1)S(1)} collective-permute-done((bf16[256,256]{1,0:T(8,128)(2,1)S(1)}, bf16[256,256]{1,0:T(8,128)(2,1)S(1)}, u32[]{:S(2)}, u32[]{:S(2)}) %collective-permute-start.1) | collective-permute-done | bytes 131104 | tf_op jit(solution)/shard_map/ppermute | solution.py:366
  16.2 1.0 %shard_map.93.early = f32[2048,256]{1,0:T(8,128)S(1)} custom-call(bf16[2048,1024]{1,0:T(8,128)(2,1)S(1)} %shard_map.92.matrix, bf16[256,256]{1,0:T(8,128)(2,1)S(1)} %get-tuple-element.22.own, bf16[256,256]{1,0:T(8,128)(2,1)S(1)} %collective-permute-done.1.beside, bf16[256,256]{1,0:T(8,128)(2,1)S(1)} %collective-permute-done.across), custom_call_target="tpu_custom_call" | custom-call | flops 536870912 | bytes 1 | tf_op jit(solution)/shard_map/pallas_call | solution.py:194
  17.2 1.4 %collective-permute-start.10 = (bf16[256,256]{1,0:T(8,128)(2,1)S(1)}, bf16[256,256]{1,0:T(8,128)(2,1)S(1)}, u32[]{:S(2)}, u32[]{:S(2)}) collective-permute-start(bf16[256,256]{1,0:T(8,128)(2,1)S(1)} %collective-permute-done.9.refs_3_), channel_id=1, source_target_pairs={{0,1},{1,0},{2,3},{3,2},{4,5},{5,4},{6,7},{7,6},{8,9},{9,8},{10,11... | collective-permute-start | bytes 393224 | tf_op jit(solution)/shard_map/ppermute | solution.py:366
  18.6 0.9 %collective-permute-done.2.passed = bf16[256,256]{1,0:T(8,128)(2,1)S(1)} collective-permute-done((bf16[256,256]{1,0:T(8,128)(2,1)S(1)}, bf16[256,256]{1,0:T(8,128)(2,1)S(1)}, u32[]{:S(2)}, u32[]{:S(2)}) %collective-permute-start.2) | collective-permute-done | bytes 131104 | tf_op jit(solution)/shard_map/ppermute | solution.py:366
  19.5 0.2 shard_map.97
  19.7 0.1 collective-permute-start.4
  19.8 0.3 shard_map.95
  20.1 0.6 %collective-permute-start.3 = (bf16[768,256]{1,0:T(8,128)(2,1)S(1)}, bf16[768,256]{1,0:T(8,128)(2,1)S(1)}, u32[]{:S(2)}, u32[]{:S(2)}) collective-permute-start(bf16[768,256]{1,0:T(8,128)(2,1)S(1)} %shard_map.95), channel_id=1, source_target_pairs={{0,4},{4,0},{8,12},{12,8},{16,20},{20,16},{24,28},{28,24},{1,5},{5... | collective-permute-start | bytes 1179656 | tf_op jit(solution)/shard_map/ppermute | solution.py:366
  20.7 0.3 shard_map.94.stay
  21.0 0.2 collective-permute-done.4.came
  21.2 1.7 %collective-permute-start.5 = (bf16[256,256]{1,0:T(8,128)(2,1)S(1)}, bf16[256,256]{1,0:T(8,128)(2,1)S(1)}, u32[]{:S(2)}, u32[]{:S(2)}) collective-permute-start(bf16[256,256]{1,0:T(8,128)(2,1)S(1)} %shard_map.98), channel_id=1, source_target_pairs={{0,8},{4,20},{8,0},{12,28},{16,24},{20,4},{24,16},{28,12},{1,9},{5... | collective-permute-start | bytes 393224 | tf_op jit(solution)/shard_map/ppermute | solution.py:373
  23.0 1.6 %collective-permute-start.6 = (bf16[256,256]{1,0:T(8,128)(2,1)S(1)}, bf16[256,256]{1,0:T(8,128)(2,1)S(1)}, u32[]{:S(2)}, u32[]{:S(2)}) collective-permute-start(bf16[256,256]{1,0:T(8,128)(2,1)S(1)} %get-tuple-element.26), channel_id=1, source_target_pairs={{0,16},{4,12},{8,24},{12,4},{16,0},{20,28},{24,8},{28,20},{1,17},{... | collective-permute-start | bytes 393224 | tf_op jit(solution)/shard_map/ppermute | solution.py:373
  24.6 0.7 %collective-permute-start.7 = (bf16[256,256]{1,0:T(8,128)(2,1)S(1)}, bf16[256,256]{1,0:T(8,128)(2,1)S(1)}, u32[]{:S(2)}, u32[]{:S(2)}) collective-permute-start(bf16[256,256]{1,0:T(8,128)(2,1)S(1)} %get-tuple-element.27), channel_id=1, source_target_pairs={{0,24},{4,28},{8,16},{12,20},{16,8},{20,12},{24,0},{28,4},{1,25},{... | collective-permute-start | bytes 393224 | tf_op jit(solution)/shard_map/ppermute | solution.py:373
  25.3 0.3 shard_map.103
  25.6 0.6 %shard_map.101 = bf16[768,256]{1,0:T(8,128)(2,1)S(1)} custom-call(bf16[2048,1024]{1,0:T(8,128)(2,1)S(1)} %shard_map.92.matrix, bf16[256,256]{1,0:T(8,128)(2,1)S(1)} %get-tuple-element.30.refs_0_, bf16[256,256]{1,0:T(8,128)(2,1)S(1)} %collective-permute-done.8.refs_1_, bf16[256,256]{1,0:T(8,128)(2,1)S(1)} %collective-permute-done.10.refs_2_, ...), custom_call_target="tpu_custom_call" | custom-call | bytes 1 | tf_op jit(solution)/shard_map/pallas_call | solution.py:242
  26.2 0.5 %collective-permute-start.11 = (bf16[768,256]{1,0:T(8,128)(2,1)S(1)}, bf16[768,256]{1,0:T(8,128)(2,1)S(1)}, u32[]{:S(2)}, u32[]{:S(2)}) collective-permute-start(bf16[768,256]{1,0:T(8,128)(2,1)S(1)} %shard_map.101), channel_id=1, source_target_pairs={{0,4},{4,0},{8,12},{12,8},{16,20},{20,16},{24,28},{28,24},{1,5},{5... | collective-permute-start | bytes 1179656 | tf_op jit(solution)/shard_map/ppermute | solution.py:366
  26.7 0.7 %shard_map.100.stay = f32[1024,256]{1,0:T(8,128)S(1)} custom-call(bf16[2048,1024]{1,0:T(8,128)(2,1)S(1)} %shard_map.92.matrix, bf16[256,256]{1,0:T(8,128)(2,1)S(1)} %get-tuple-element.30.refs_0_, bf16[256,256]{1,0:T(8,128)(2,1)S(1)} %collective-permute-done.8.refs_1_, bf16[256,256]{1,0:T(8,128)(2,1)S(1)} %collective-permute-done.10.refs_2_, ...), custom_call_target="tpu_custom_call" | custom-call | flops 10737418240 | bytes 1 | tf_op jit(solution)/shard_map/pallas_call | solution.py:242
  27.5 0.1 collective-permute-done.12.came
  27.6 1.3 %collective-permute-start.13 = (bf16[256,256]{1,0:T(8,128)(2,1)S(1)}, bf16[256,256]{1,0:T(8,128)(2,1)S(1)}, u32[]{:S(2)}, u32[]{:S(2)}) collective-permute-start(bf16[256,256]{1,0:T(8,128)(2,1)S(1)} %shard_map.104), channel_id=1, source_target_pairs={{0,8},{4,20},{8,0},{12,28},{16,24},{20,4},{24,16},{28,12},{1,9},{5... | collective-permute-start | bytes 393224 | tf_op jit(solution)/shard_map/ppermute | solution.py:373
  29.0 1.6 %collective-permute-start.14 = (bf16[256,256]{1,0:T(8,128)(2,1)S(1)}, bf16[256,256]{1,0:T(8,128)(2,1)S(1)}, u32[]{:S(2)}, u32[]{:S(2)}) collective-permute-start(bf16[256,256]{1,0:T(8,128)(2,1)S(1)} %get-tuple-element.35), channel_id=1, source_target_pairs={{0,16},{4,12},{8,24},{12,4},{16,0},{20,28},{24,8},{28,20},{1,17},{... | collective-permute-start | bytes 393224 | tf_op jit(solution)/shard_map/ppermute | solution.py:373
  30.6 0.7 %collective-permute-start.15 = (bf16[256,256]{1,0:T(8,128)(2,1)S(1)}, bf16[256,256]{1,0:T(8,128)(2,1)S(1)}, u32[]{:S(2)}, u32[]{:S(2)}) collective-permute-start(bf16[256,256]{1,0:T(8,128)(2,1)S(1)} %get-tuple-element.36), channel_id=1, source_target_pairs={{0,24},{4,28},{8,16},{12,20},{16,8},{20,12},{24,0},{28,4},{1,25},{... | collective-permute-start | bytes 393224 | tf_op jit(solution)/shard_map/ppermute | solution.py:373
  31.3 0.3 collective-permute-done.7.refs_3_
  31.7 0.1 shard_map.99.ready
  31.8 1.8 %collective-permute-done.13.refs_1_ = bf16[256,256]{1,0:T(8,128)(2,1)S(1)} collective-permute-done((bf16[256,256]{1,0:T(8,128)(2,1)S(1)}, bf16[256,256]{1,0:T(8,128)(2,1)S(1)}, u32[]{:S(2)}, u32[]{:S(2)}) %collective-permute-start.13) | collective-permute-done | bytes 131104 | tf_op jit(solution)/shard_map/ppermute | solution.py:373
  33.6 0.8 %collective-permute-done.14.refs_2_ = bf16[256,256]{1,0:T(8,128)(2,1)S(1)} collective-permute-done((bf16[256,256]{1,0:T(8,128)(2,1)S(1)}, bf16[256,256]{1,0:T(8,128)(2,1)S(1)}, u32[]{:S(2)}, u32[]{:S(2)}) %collective-permute-start.14) | collective-permute-done | bytes 131104 | tf_op jit(solution)/shard_map/ppermute | solution.py:373
  34.4 3.4 %collective-permute-done.15.refs_3_ = bf16[256,256]{1,0:T(8,128)(2,1)S(1)} collective-permute-done((bf16[256,256]{1,0:T(8,128)(2,1)S(1)}, bf16[256,256]{1,0:T(8,128)(2,1)S(1)}, u32[]{:S(2)}, u32[]{:S(2)}) %collective-permute-start.15) | collective-permute-done | bytes 131104 | tf_op jit(solution)/shard_map/ppermute | solution.py:373
  37.8 0.8 %shard_map.105 = bf16[256,512]{1,0:T(8,128)(2,1)} custom-call(bf16[256,256]{1,0:T(8,128)(2,1)S(1)} %shard_map.99.ready, f32[256,512]{1,0:T(8,128)S(1)} %get-tuple-element.21.projected, f32[2,128]{1,0:T(2,128)S(1)} %bitcast.5, f32[256,256]{1,0:T(8,128)S(1)} %get-tuple-element.34.refs_0_, bf16[256,256]{1,0:T(8,128)(2,1)S(1)} %collective-permute-done.13.refs_1_, ...), custom_call_target="tpu_custom_call" | custom-call | flops 393216 | bytes 1048576 | tf_op jit(solution)/shard_map/pallas_call | solution.py:316
  (17 shorter events, 0.4 us)
Async XLA Ops:
  1.9 9.5 %collective-permute-start = (bf16[256,256]{1,0:T(8,128)(2,1)S(1)}, bf16[256,256]{1,0:T(8,128)(2,1)S(1)}, u32[]{:S(2)}, u32[]{:S(2)}) collective-permute-start(bf16[256,256]{1,0:T(8,128)(2,1)S(1)} %get-tuple-element.22.own), channel_id=1, source_target_pairs={{0,3},{1,2},{2,1},{3,0},{4,7},{5,6},{6,5},{7,4},{8,11},{9,10},{10,... | collective-permute-start | bytes 393224 | tf_op jit(solution)/shard_map/ppermute | solution.py:366
  7.0 9.2 %collective-permute-start.1 = (bf16[256,256]{1,0:T(8,128)(2,1)S(1)}, bf16[256,256]{1,0:T(8,128)(2,1)S(1)}, u32[]{:S(2)}, u32[]{:S(2)}) collective-permute-start(bf16[256,256]{1,0:T(8,128)(2,1)S(1)} %get-tuple-element.22.own), channel_id=1, source_target_pairs={{0,1},{1,0},{2,3},{3,2},{4,5},{5,4},{6,7},{7,6},{8,9},{9,8},{10,11... | collective-permute-start | bytes 393224 | tf_op jit(solution)/shard_map/ppermute | solution.py:366
  7.0 10.2 %collective-permute-start.9 = (bf16[256,256]{1,0:T(8,128)(2,1)S(1)}, bf16[256,256]{1,0:T(8,128)(2,1)S(1)}, u32[]{:S(2)}, u32[]{:S(2)}) collective-permute-start(bf16[256,256]{1,0:T(8,128)(2,1)S(1)} %get-tuple-element.30.refs_0_), channel_id=1, source_target_pairs={{0,3},{1,2},{2,1},{3,0},{4,7},{5,6},{6,5},{7,4},{8,11},{9,10},{10,... | collective-permute-start | bytes 393224 | tf_op jit(solution)/shard_map/ppermute | solution.py:366
  11.3 8.2 %collective-permute-start.2 = (bf16[256,256]{1,0:T(8,128)(2,1)S(1)}, bf16[256,256]{1,0:T(8,128)(2,1)S(1)}, u32[]{:S(2)}, u32[]{:S(2)}) collective-permute-start(bf16[256,256]{1,0:T(8,128)(2,1)S(1)} %collective-permute-done.across), channel_id=1, source_target_pairs={{0,1},{1,0},{2,3},{3,2},{4,5},{5,4},{6,7},{7,6},{8,9},{9,8},{10,11... | collective-permute-start | bytes 393224 | tf_op jit(solution)/shard_map/ppermute | solution.py:366
  14.8 10.5 %collective-permute-start.8 = (bf16[256,256]{1,0:T(8,128)(2,1)S(1)}, bf16[256,256]{1,0:T(8,128)(2,1)S(1)}, u32[]{:S(2)}, u32[]{:S(2)}) collective-permute-start(bf16[256,256]{1,0:T(8,128)(2,1)S(1)} %get-tuple-element.30.refs_0_), channel_id=1, source_target_pairs={{0,1},{1,0},{2,3},{3,2},{4,5},{5,4},{6,7},{7,6},{8,9},{9,8},{10,11... | collective-permute-start | bytes 393224 | tf_op jit(solution)/shard_map/ppermute | solution.py:366
  17.2 8.1 %collective-permute-start.10 = (bf16[256,256]{1,0:T(8,128)(2,1)S(1)}, bf16[256,256]{1,0:T(8,128)(2,1)S(1)}, u32[]{:S(2)}, u32[]{:S(2)}) collective-permute-start(bf16[256,256]{1,0:T(8,128)(2,1)S(1)} %collective-permute-done.9.refs_3_), channel_id=1, source_target_pairs={{0,1},{1,0},{2,3},{3,2},{4,5},{5,4},{6,7},{7,6},{8,9},{9,8},{10,11... | collective-permute-start | bytes 393224 | tf_op jit(solution)/shard_map/ppermute | solution.py:366
  19.7 1.4 %collective-permute-start.4 = (bf16[256,256]{1,0:T(8,128)(2,1)S(1)}, bf16[256,256]{1,0:T(8,128)(2,1)S(1)}, u32[]{:S(2)}, u32[]{:S(2)}) collective-permute-start(bf16[256,256]{1,0:T(8,128)(2,1)S(1)} %shard_map.97), channel_id=1, source_target_pairs={{0,4},{4,0},{8,12},{12,8},{16,20},{20,16},{24,28},{28,24},{1,5},{5... | collective-permute-start | bytes 393224 | tf_op jit(solution)/shard_map/ppermute | solution.py:366
  20.1 2.8 %collective-permute-start.3 = (bf16[768,256]{1,0:T(8,128)(2,1)S(1)}, bf16[768,256]{1,0:T(8,128)(2,1)S(1)}, u32[]{:S(2)}, u32[]{:S(2)}) collective-permute-start(bf16[768,256]{1,0:T(8,128)(2,1)S(1)} %shard_map.95), channel_id=1, source_target_pairs={{0,4},{4,0},{8,12},{12,8},{16,20},{20,16},{24,28},{28,24},{1,5},{5... | collective-permute-start | bytes 1179656 | tf_op jit(solution)/shard_map/ppermute | solution.py:366
  21.2 9.4 %collective-permute-start.5 = (bf16[256,256]{1,0:T(8,128)(2,1)S(1)}, bf16[256,256]{1,0:T(8,128)(2,1)S(1)}, u32[]{:S(2)}, u32[]{:S(2)}) collective-permute-start(bf16[256,256]{1,0:T(8,128)(2,1)S(1)} %shard_map.98), channel_id=1, source_target_pairs={{0,8},{4,20},{8,0},{12,28},{16,24},{20,4},{24,16},{28,12},{1,9},{5... | collective-permute-start | bytes 393224 | tf_op jit(solution)/shard_map/ppermute | solution.py:373
  23.0 8.3 %collective-permute-start.6 = (bf16[256,256]{1,0:T(8,128)(2,1)S(1)}, bf16[256,256]{1,0:T(8,128)(2,1)S(1)}, u32[]{:S(2)}, u32[]{:S(2)}) collective-permute-start(bf16[256,256]{1,0:T(8,128)(2,1)S(1)} %get-tuple-element.26), channel_id=1, source_target_pairs={{0,16},{4,12},{8,24},{12,4},{16,0},{20,28},{24,8},{28,20},{1,17},{... | collective-permute-start | bytes 393224 | tf_op jit(solution)/shard_map/ppermute | solution.py:373
  24.6 7.1 %collective-permute-start.7 = (bf16[256,256]{1,0:T(8,128)(2,1)S(1)}, bf16[256,256]{1,0:T(8,128)(2,1)S(1)}, u32[]{:S(2)}, u32[]{:S(2)}) collective-permute-start(bf16[256,256]{1,0:T(8,128)(2,1)S(1)} %get-tuple-element.27), channel_id=1, source_target_pairs={{0,24},{4,28},{8,16},{12,20},{16,8},{20,12},{24,0},{28,4},{1,25},{... | collective-permute-start | bytes 393224 | tf_op jit(solution)/shard_map/ppermute | solution.py:373
  26.2 1.4 %collective-permute-start.12 = (bf16[256,256]{1,0:T(8,128)(2,1)S(1)}, bf16[256,256]{1,0:T(8,128)(2,1)S(1)}, u32[]{:S(2)}, u32[]{:S(2)}) collective-permute-start(bf16[256,256]{1,0:T(8,128)(2,1)S(1)} %shard_map.103), channel_id=1, source_target_pairs={{0,4},{4,0},{8,12},{12,8},{16,20},{20,16},{24,28},{28,24},{1,5},{5... | collective-permute-start | bytes 393224 | tf_op jit(solution)/shard_map/ppermute | solution.py:366
  26.2 2.7 %collective-permute-start.11 = (bf16[768,256]{1,0:T(8,128)(2,1)S(1)}, bf16[768,256]{1,0:T(8,128)(2,1)S(1)}, u32[]{:S(2)}, u32[]{:S(2)}) collective-permute-start(bf16[768,256]{1,0:T(8,128)(2,1)S(1)} %shard_map.101), channel_id=1, source_target_pairs={{0,4},{4,0},{8,12},{12,8},{16,20},{20,16},{24,28},{28,24},{1,5},{5... | collective-permute-start | bytes 1179656 | tf_op jit(solution)/shard_map/ppermute | solution.py:366
  27.5 4.2 %copy-start = (f32[256]{0:T(256)S(1)}, f32[256]{0:T(256)}, u32[]{:S(2)}) copy-start(f32[256]{0:T(256)} %param.12) | copy-start | bytes 3076
  27.6 5.9 %collective-permute-start.13 = (bf16[256,256]{1,0:T(8,128)(2,1)S(1)}, bf16[256,256]{1,0:T(8,128)(2,1)S(1)}, u32[]{:S(2)}, u32[]{:S(2)}) collective-permute-start(bf16[256,256]{1,0:T(8,128)(2,1)S(1)} %shard_map.104), channel_id=1, source_target_pairs={{0,8},{4,20},{8,0},{12,28},{16,24},{20,4},{24,16},{28,12},{1,9},{5... | collective-permute-start | bytes 393224 | tf_op jit(solution)/shard_map/ppermute | solution.py:373
  29.0 5.3 %collective-permute-start.14 = (bf16[256,256]{1,0:T(8,128)(2,1)S(1)}, bf16[256,256]{1,0:T(8,128)(2,1)S(1)}, u32[]{:S(2)}, u32[]{:S(2)}) collective-permute-start(bf16[256,256]{1,0:T(8,128)(2,1)S(1)} %get-tuple-element.35), channel_id=1, source_target_pairs={{0,16},{4,12},{8,24},{12,4},{16,0},{20,28},{24,8},{28,20},{1,17},{... | collective-permute-start | bytes 393224 | tf_op jit(solution)/shard_map/ppermute | solution.py:373
  30.6 7.2 %collective-permute-start.15 = (bf16[256,256]{1,0:T(8,128)(2,1)S(1)}, bf16[256,256]{1,0:T(8,128)(2,1)S(1)}, u32[]{:S(2)}, u32[]{:S(2)}) collective-permute-start(bf16[256,256]{1,0:T(8,128)(2,1)S(1)} %get-tuple-element.36), channel_id=1, source_target_pairs={{0,24},{4,28},{8,16},{12,20},{16,8},{20,12},{24,0},{28,4},{1,25},{... | collective-permute-start | bytes 393224 | tf_op jit(solution)/shard_map/ppermute | solution.py:373

commit v18 on v16

--- a/solution.py
+++ b/solution.py
@@ -32,59 +32,52 @@
     return jnp.broadcast_to(row, (lanes, row.shape[1])).T
 
 
-def project_kernel(features_hbm, weight_hbm, norm_hbm, projected, *refs):
-    *scaled, features, weight, norm, sems = refs
-    width, lanes = scaled[0].shape[1], norm.shape[1]
-    half = weight.shape[0] // 2
-    top, bottom = slice(0, half), slice(half, 2 * half)
+def project_kernel(start, features_hbm, weight_hbm, norm_hbm, projected, scaled, *refs):
+    features, weight, norm, sems = refs
+    width, lanes = scaled.shape[1], norm.shape[1]
     copies = [
         pltpu.make_async_copy(source, target, sems.at[k])
         for k, (source, target) in enumerate(
             [
-                (weight_hbm.at[top], weight.at[top]),
+                (weight_hbm.at[:, start : start + width], weight),
                 (features_hbm, features),
                 (norm_hbm, norm),
-                (weight_hbm.at[bottom], weight.at[bottom]),
             ]
         )
     ]
     for copy in copies:
         copy.start()
-    for copy in copies[:3]:
+    for copy in copies:
         copy.wait()
-    value = jnp.dot(features[:, top], weight[top, :], preferred_element_type=jnp.float32)
-    copies[3].wait()
-    value += jnp.dot(features[:, bottom], weight[bottom, :], preferred_element_type=jnp.float32)
+    value = jnp.dot(features[...], weight[...], preferred_element_type=jnp.float32)
     projected[...] = value
     for part in range(norm.shape[0]):
         factor = rows_to_lanes(norm[part : part + 1, :], lanes)
-        for column in range(0, value.shape[1], lanes):
-            piece = value[part * lanes : (part + 1) * lanes, column : column + lanes]
-            target = scaled[column // width]
-            start = column % width
-            target[part * lanes : (part + 1) * lanes, start : start + lanes] = (
-                factor * piece
-            ).astype(target.dtype)
-
-
-def project(features, weight, source_norm, chunks):
+        here = slice(part * lanes, (part + 1) * lanes)
+        for column in range(0, width, lanes):
+            piece = factor * value[here, column : column + lanes]
+            scaled[here, column : column + lanes] = piece.astype(scaled.dtype)
+
+
+def project(features, weight, source_norm, start, width):
     rows, depth = features.shape
-    hidden = weight.shape[1]
     norm = source_norm.reshape(-1, 128)
     return pl.pallas_call(
-        project_kernel,
-        out_shape=[jax.ShapeDtypeStruct((rows, hidden), jnp.float32)]
-        + [jax.ShapeDtypeStruct((rows, hidden // chunks), jnp.bfloat16)] * chunks,
+        functools.partial(project_kernel, start),
+        out_shape=[
+            jax.ShapeDtypeStruct((rows, width), jnp.float32),
+            jax.ShapeDtypeStruct((rows, width), jnp.bfloat16),
+        ],
         in_specs=[HBM] * 3,
-        out_specs=[VMEM] * (1 + chunks),
+        out_specs=[VMEM] * 2,
         scratch_shapes=[
             pltpu.VMEM(features.shape, features.dtype),
-            pltpu.VMEM(weight.shape, weight.dtype),
+            pltpu.VMEM((depth, width), weight.dtype),
             pltpu.VMEM(norm.shape, norm.dtype),
-            pltpu.SemaphoreType.DMA((4,)),
+            pltpu.SemaphoreType.DMA((3,)),
         ],
         compiler_params=params(12),
-        cost_estimate=cost(2 * rows * depth * hidden, 2 * depth * (rows + hidden)),
+        cost_estimate=cost(2 * rows * depth * width, 2 * depth * (rows + width)),
     )(*in_hbm(features, weight, norm))
 
 
@@ -271,14 +264,14 @@
     )(stay, came)
 
 
-def activate(projected, norm, pieces, start, out):
+def activate(projected, norm, pieces, out):
     lanes = norm.shape[1]
     for part in range(norm.shape[0]):
         factor = rows_to_lanes(norm[part : part + 1, :], lanes)
         here = slice(part * lanes, (part + 1) * lanes)
         for column in range(0, out.shape[1], lanes):
             span = slice(column, column + lanes)
-            value = projected[here, start + column : start + column + lanes]
+            value = projected[here, span]
             for piece in pieces:
                 value += piece[here, span].astype(jnp.float32)
             out[here, span] = jnp.maximum(factor * value, 0.0).astype(out.dtype)
@@ -286,7 +279,7 @@
 
 def first_kernel(projected, norm, *refs):
     *pieces, out = refs
-    activate(projected, norm, pieces, 0, out)
+    activate(projected, norm, pieces, out)
 
 
 def last_kernel(ready, projected, norm, *refs):
@@ -294,7 +287,7 @@
     width = ready.shape[1]
     early = pltpu.make_async_copy(ready, out.at[:, :width], sems.at[0])
     early.start()
-    activate(projected, norm, pieces, width, rest)
+    activate(projected, norm, pieces, rest)
     late = pltpu.make_async_copy(rest, out.at[:, width:], sems.at[1])
     late.start()
     early.wait()
@@ -302,9 +295,9 @@
 
 
 def finish(projected, target_norm, pieces):
-    rows, hidden = projected.shape
     norm = target_norm.reshape(-1, 128)
-    width = pieces[0][0].shape[1]
+    rows, width = projected[0].shape
+    rest = projected[1].shape[1]
     ready = pl.pallas_call(
         first_kernel,
         out_shape=jax.ShapeDtypeStruct((rows, width), jnp.bfloat16),
@@ -312,19 +305,19 @@
         out_specs=VMEM,
         compiler_params=params(12),
         cost_estimate=cost(6 * rows * width, 16 * rows * width),
-    )(projected, norm, *pieces[0])
+    )(projected[0], norm, *pieces[0])
     return pl.pallas_call(
         last_kernel,
-        out_shape=jax.ShapeDtypeStruct((rows, hidden), jnp.bfloat16),
+        out_shape=jax.ShapeDtypeStruct((rows, width + rest), jnp.bfloat16),
         in_specs=[VMEM] * (3 + len(pieces[1])),
         out_specs=HBM,
         scratch_shapes=[
-            pltpu.VMEM((rows, hidden - width), jnp.bfloat16),
+            pltpu.VMEM((rows, rest), jnp.bfloat16),
             pltpu.SemaphoreType.DMA((2,)),
         ],
         compiler_params=params(12),
-        cost_estimate=cost(6 * rows * width, 16 * rows * width),
-    )(ready, projected, norm, *pieces[1])
+        cost_estimate=cost(6 * rows * rest, 16 * rows * rest),
+    )(ready, projected[1], norm, *pieces[1])
 
 
 def visit_kernel(own_tiles, per_owner, sources, targets, count, labels, tiles, blocks, out, total):
@@ -404,7 +397,10 @@
         gathered = jnp.sum(arrived.astype(jnp.float32), axis=0) + projected
         return jnp.maximum(target_norm[:, None] * gathered, 0.0).astype(jnp.bfloat16)
 
-    projected, *scaled = project(features, weight, source_norm, CHUNKS)
+    width = weight.shape[1] // CHUNKS
+    projected, scaled = zip(
+        *(project(features, weight, source_norm, k * width, width) for k in range(CHUNKS))
+    )
     built = merge_tiles(own_tiles, owners, span, index_args, tile_weights)
     half = built.shape[0] // 2
     across = [swap(own, "col", 3) for own in scaled]

time: 38.6 us -> 38.4 us (level)
  Pallas kernels: 8.83 us -> 10 us
  starting transfers between devices: 19.2 us -> 18.2 us
  waiting for transfers between devices: 9.66 us -> 9.18 us
    pallas_call x2 -> x3, Pallas kernels: 2.63 us -> 3.85 us  [the longest x2 3.07 us: project(): pl.pallas_call(functools.partial(project_kernel, start), out_shape=[jax.S...]
    ppermute x9, starting transfers between devices: 11.6 us -> 11 us  [swap(): return lax.ppermute(value, axis, pairs)]
    ppermute x9, waiting for transfers between devices: 3.74 us -> 3.26 us  [swap(): return lax.ppermute(value, axis, pairs)]
  transfers between devices with their start and end apart: 15 -> 15, of which waited for: 8 -> 7; matrix products, arithmetic and copies ran while one was open for 0% -> 0% of each run, Pallas kernels for 16% -> 20%
where the time goes in v18:
time: 38.4 us; the launch traced here: 38.2 us
  starting transfers between devices  18.2 us (47%)
  Pallas kernels  10 us (26%)
  waiting for transfers between devices  9.18 us (24%)
  between operations  0.78 us (2%)
    ppermute x9, starting transfers between devices, swap(): return lax.ppermute(value, axis, pairs)  11 us
    ppermute x6, starting transfers between devices, exchange(): lax.ppermute(value, 'row', [(i, i ^ step[i % 2]) for i in range(owners)])  7.17 us
    ppermute x6, waiting for transfers between devices, exchange(): lax.ppermute(value, 'row', [(i, i ^ step[i % 2]) for i in range(owners)])  5.92 us
    ppermute x9, waiting for transfers between devices, swap(): return lax.ppermute(value, axis, pairs)  3.26 us
    pallas_call x2, Pallas kernels, project(): pl.pallas_call(functools.partial(project_kernel, start), out_shape=[jax.S...  3.07 us
    pallas_call x1, Pallas kernels, merge_tiles(): pl.pallas_call(functools.partial(merge_kernel, own_tiles, labels.shape[1]...  2.76 us
    pallas_call x2, Pallas kernels, product(): pl.pallas_call(functools.partial(product_kernel, first), out_shape=jax.Sh...  1.42 us
    pallas_call x1, Pallas kernels, early_product(): pl.pallas_call(early_kernel, out_shape=jax.ShapeDtypeStruct((total, width...  0.99 us
  transfers between devices with their start and end apart: 15, of which 7 were waited for; matrix products, arithmetic and copies ran while one was open for 0% of the time, Pallas kernels for 20%

profile of v18, /device:TPU:0, one launch (start us, length us, event | category | flops | bytes accessed | tf_op | source)
XLA Modules:
  0.0 38.2 jit_solution(10271357433340615422)
XLA Ops:
  0.0 1.5 %shard_map.91 = (f32[256,256]{1,0:T(8,128)S(1)}, bf16[256,256]{1,0:T(8,128)(2,1)S(1)}) custom-call(bf16[256,1024]{1,0:T(8,128)(2,1)} %features_hbm.3, bf16[1024,512]{1,0:T(8,128)(2,1)} %weight_hbm.3, f32[2,128]{1,0:T(2,128)} %bitcast.6), custom_call_target="tpu_custom_call" | custom-call | flops 134217728 | bytes 1048576 | tf_op jit(solution)/shard_map/pallas_call | solution.py:65
  1.5 5.1 %collective-permute-start = (bf16[256,256]{1,0:T(8,128)(2,1)S(1)}, bf16[256,256]{1,0:T(8,128)(2,1)S(1)}, u32[]{:S(2)}, u32[]{:S(2)}) collective-permute-start(bf16[256,256]{1,0:T(8,128)(2,1)S(1)} %get-tuple-element.24.own), channel_id=1, source_target_pairs={{0,3},{1,2},{2,1},{3,0},{4,7},{5,6},{6,5},{7,4},{8,11},{9,10},{10,... | collective-permute-start | bytes 393224 | tf_op jit(solution)/shard_map/ppermute | solution.py:359
  6.7 1.5 %shard_map.100 = (f32[256,256]{1,0:T(8,128)S(1)}, bf16[256,256]{1,0:T(8,128)(2,1)S(1)}) custom-call(bf16[256,1024]{1,0:T(8,128)(2,1)} %features_hbm.3, bf16[1024,512]{1,0:T(8,128)(2,1)} %weight_hbm.3, f32[2,128]{1,0:T(2,128)} %bitcast.7), custom_call_target="tpu_custom_call" | custom-call | flops 134217728 | bytes 1048576 | tf_op jit(solution)/shard_map/pallas_call | solution.py:65
  8.2 1.0 %collective-permute-start.9 = (bf16[256,256]{1,0:T(8,128)(2,1)S(1)}, bf16[256,256]{1,0:T(8,128)(2,1)S(1)}, u32[]{:S(2)}, u32[]{:S(2)}) collective-permute-start(bf16[256,256]{1,0:T(8,128)(2,1)S(1)} %get-tuple-element.33.refs_0_), channel_id=1, source_target_pairs={{0,3},{1,2},{2,1},{3,0},{4,7},{5,6},{6,5},{7,4},{8,11},{9,10},{10,... | collective-permute-start | bytes 393224 | tf_op jit(solution)/shard_map/ppermute | solution.py:359
  9.8 2.8 %shard_map.92.matrix = bf16[2048,1024]{1,0:T(8,128)(2,1)S(1)} custom-call(s32[1]{0:T(128)} %bitcast.2.row, s32[1]{0:T(128)} %bitcast.3.column, s32[1]{0:T(128)S(6)} %copy.10.count, s32[1,64]{1,0:T(1,128)} %sources_hbm.1, s32[1,64]{1,0:T(1,128)} %targets_hbm.1, s32[1,16]{1,0:T(1,128)} %labels_hbm.1, bf16[1,64,128,128]{3,2,1,0:T(8,128)(2,1)} %tiles_hbm.1), custom_call_target="tpu_custom_call" | custom-call | flops 8388608 | bytes 12582912 | tf_op jit(solution)/shard_map/pallas_call | solution.py:153
  12.6 1.2 %collective-permute-start.2 = (bf16[256,256]{1,0:T(8,128)(2,1)S(1)}, bf16[256,256]{1,0:T(8,128)(2,1)S(1)}, u32[]{:S(2)}, u32[]{:S(2)}) collective-permute-start(bf16[256,256]{1,0:T(8,128)(2,1)S(1)} %collective-permute-done.across), channel_id=1, source_target_pairs={{0,1},{1,0},{2,3},{3,2},{4,5},{5,4},{6,7},{7,6},{8,9},{9,8},{10,11... | collective-permute-start | bytes 393224 | tf_op jit(solution)/shard_map/ppermute | solution.py:359
  13.8 0.9 %collective-permute-start.8 = (bf16[256,256]{1,0:T(8,128)(2,1)S(1)}, bf16[256,256]{1,0:T(8,128)(2,1)S(1)}, u32[]{:S(2)}, u32[]{:S(2)}) collective-permute-start(bf16[256,256]{1,0:T(8,128)(2,1)S(1)} %get-tuple-element.33.refs_0_), channel_id=1, source_target_pairs={{0,1},{1,0},{2,3},{3,2},{4,5},{5,4},{6,7},{7,6},{8,9},{9,8},{10,11... | collective-permute-start | bytes 393224 | tf_op jit(solution)/shard_map/ppermute | solution.py:359
  14.7 1.0 %shard_map.93.early = f32[2048,256]{1,0:T(8,128)S(1)} custom-call(bf16[2048,1024]{1,0:T(8,128)(2,1)S(1)} %shard_map.92.matrix, bf16[256,256]{1,0:T(8,128)(2,1)S(1)} %get-tuple-element.24.own, bf16[256,256]{1,0:T(8,128)(2,1)S(1)} %collective-permute-done.1.beside, bf16[256,256]{1,0:T(8,128)(2,1)S(1)} %collective-permute-done.across), custom_call_target="tpu_custom_call" | custom-call | flops 536870912 | bytes 1 | tf_op jit(solution)/shard_map/pallas_call | solution.py:187
  15.7 0.5 %collective-permute-done.9.refs_3_ = bf16[256,256]{1,0:T(8,128)(2,1)S(1)} collective-permute-done((bf16[256,256]{1,0:T(8,128)(2,1)S(1)}, bf16[256,256]{1,0:T(8,128)(2,1)S(1)}, u32[]{:S(2)}, u32[]{:S(2)}) %collective-permute-start.9) | collective-permute-done | bytes 131104 | tf_op jit(solution)/shard_map/ppermute | solution.py:359
  16.2 2.1 %collective-permute-start.10 = (bf16[256,256]{1,0:T(8,128)(2,1)S(1)}, bf16[256,256]{1,0:T(8,128)(2,1)S(1)}, u32[]{:S(2)}, u32[]{:S(2)}) collective-permute-start(bf16[256,256]{1,0:T(8,128)(2,1)S(1)} %collective-permute-done.9.refs_3_), channel_id=1, source_target_pairs={{0,1},{1,0},{2,3},{3,2},{4,5},{5,4},{6,7},{7,6},{8,9},{9,8},{10,11... | collective-permute-start | bytes 393224 | tf_op jit(solution)/shard_map/ppermute | solution.py:359
  18.3 0.7 %collective-permute-done.2.passed = bf16[256,256]{1,0:T(8,128)(2,1)S(1)} collective-permute-done((bf16[256,256]{1,0:T(8,128)(2,1)S(1)}, bf16[256,256]{1,0:T(8,128)(2,1)S(1)}, u32[]{:S(2)}, u32[]{:S(2)}) %collective-permute-start.2) | collective-permute-done | bytes 131104 | tf_op jit(solution)/shard_map/ppermute | solution.py:359
  19.0 0.3 shard_map.95
  19.4 0.2 shard_map.97
  19.6 0.6 %collective-permute-start.4 = (bf16[256,256]{1,0:T(8,128)(2,1)S(1)}, bf16[256,256]{1,0:T(8,128)(2,1)S(1)}, u32[]{:S(2)}, u32[]{:S(2)}) collective-permute-start(bf16[256,256]{1,0:T(8,128)(2,1)S(1)} %shard_map.97), channel_id=1, source_target_pairs={{0,4},{4,0},{8,12},{12,8},{16,20},{20,16},{24,28},{28,24},{1,5},{5... | collective-permute-start | bytes 393224 | tf_op jit(solution)/shard_map/ppermute | solution.py:359
  20.1 0.3 shard_map.94.stay
  20.4 0.8 %collective-permute-done.4.came = bf16[256,256]{1,0:T(8,128)(2,1)S(1)} collective-permute-done((bf16[256,256]{1,0:T(8,128)(2,1)S(1)}, bf16[256,256]{1,0:T(8,128)(2,1)S(1)}, u32[]{:S(2)}, u32[]{:S(2)}) %collective-permute-start.4) | collective-permute-done | bytes 131104 | tf_op jit(solution)/shard_map/ppermute | solution.py:359
  21.3 1.6 %collective-permute-start.5 = (bf16[256,256]{1,0:T(8,128)(2,1)S(1)}, bf16[256,256]{1,0:T(8,128)(2,1)S(1)}, u32[]{:S(2)}, u32[]{:S(2)}) collective-permute-start(bf16[256,256]{1,0:T(8,128)(2,1)S(1)} %shard_map.98), channel_id=1, source_target_pairs={{0,8},{4,20},{8,0},{12,28},{16,24},{20,4},{24,16},{28,12},{1,9},{5... | collective-permute-start | bytes 393224 | tf_op jit(solution)/shard_map/ppermute | solution.py:366
  22.9 1.6 %collective-permute-start.6 = (bf16[256,256]{1,0:T(8,128)(2,1)S(1)}, bf16[256,256]{1,0:T(8,128)(2,1)S(1)}, u32[]{:S(2)}, u32[]{:S(2)}) collective-permute-start(bf16[256,256]{1,0:T(8,128)(2,1)S(1)} %get-tuple-element.28), channel_id=1, source_target_pairs={{0,16},{4,12},{8,24},{12,4},{16,0},{20,28},{24,8},{28,20},{1,17},{... | collective-permute-start | bytes 393224 | tf_op jit(solution)/shard_map/ppermute | solution.py:366
  24.5 0.5 %collective-permute-start.7 = (bf16[256,256]{1,0:T(8,128)(2,1)S(1)}, bf16[256,256]{1,0:T(8,128)(2,1)S(1)}, u32[]{:S(2)}, u32[]{:S(2)}) collective-permute-start(bf16[256,256]{1,0:T(8,128)(2,1)S(1)} %get-tuple-element.29), channel_id=1, source_target_pairs={{0,24},{4,28},{8,16},{12,20},{16,8},{20,12},{24,0},{28,4},{1,25},{... | collective-permute-start | bytes 393224 | tf_op jit(solution)/shard_map/ppermute | solution.py:366
  25.0 0.7 %shard_map.102 = bf16[1024,256]{1,0:T(8,128)(2,1)S(1)} custom-call(bf16[2048,1024]{1,0:T(8,128)(2,1)S(1)} %shard_map.92.matrix, bf16[256,256]{1,0:T(8,128)(2,1)S(1)} %get-tuple-element.33.refs_0_, bf16[256,256]{1,0:T(8,128)(2,1)S(1)} %collective-permute-done.8.refs_1_, bf16[256,256]{1,0:T(8,128)(2,1)S(1)} %collective-permute-done.10.refs_2_, ...), custom_call_target="tpu_custom_call" | custom-call | bytes 1 | tf_op jit(solution)/shard_map/pallas_call | solution.py:235
  25.7 0.1 collective-permute-start.11
  25.8 0.7 %shard_map.101.stay = f32[1024,256]{1,0:T(8,128)S(1)} custom-call(bf16[2048,1024]{1,0:T(8,128)(2,1)S(1)} %shard_map.92.matrix, bf16[256,256]{1,0:T(8,128)(2,1)S(1)} %get-tuple-element.33.refs_0_, bf16[256,256]{1,0:T(8,128)(2,1)S(1)} %collective-permute-done.8.refs_1_, bf16[256,256]{1,0:T(8,128)(2,1)S(1)} %collective-permute-done.10.refs_2_, ...), custom_call_target="tpu_custom_call" | custom-call | flops 10737418240 | bytes 1 | tf_op jit(solution)/shard_map/pallas_call | solution.py:235
  26.5 1.2 %collective-permute-done.11.came = bf16[1024,256]{1,0:T(8,128)(2,1)S(1)} collective-permute-done((bf16[1024,256]{1,0:T(8,128)(2,1)S(1)}, bf16[1024,256]{1,0:T(8,128)(2,1)S(1)}, u32[]{:S(2)}, u32[]{:S(2)}) %collective-permute-start.11) | collective-permute-done | bytes 524320 | tf_op jit(solution)/shard_map/ppermute | solution.py:359
  27.7 0.1 shard_map.103
  27.8 1.6 %collective-permute-start.12 = (bf16[256,256]{1,0:T(8,128)(2,1)S(1)}, bf16[256,256]{1,0:T(8,128)(2,1)S(1)}, u32[]{:S(2)}, u32[]{:S(2)}) collective-permute-start(bf16[256,256]{1,0:T(8,128)(2,1)S(1)} %get-tuple-element.38), channel_id=1, source_target_pairs={{0,8},{4,20},{8,0},{12,28},{16,24},{20,4},{24,16},{28,12},{1,9},{5... | collective-permute-start | bytes 393224 | tf_op jit(solution)/shard_map/ppermute | solution.py:366
  29.4 1.5 %collective-permute-start.13 = (bf16[256,256]{1,0:T(8,128)(2,1)S(1)}, bf16[256,256]{1,0:T(8,128)(2,1)S(1)}, u32[]{:S(2)}, u32[]{:S(2)}) collective-permute-start(bf16[256,256]{1,0:T(8,128)(2,1)S(1)} %get-tuple-element.39), channel_id=1, source_target_pairs={{0,16},{4,12},{8,24},{12,4},{16,0},{20,28},{24,8},{28,20},{1,17},{... | collective-permute-start | bytes 393224 | tf_op jit(solution)/shard_map/ppermute | solution.py:366
  30.9 0.5 %collective-permute-start.14 = (bf16[256,256]{1,0:T(8,128)(2,1)S(1)}, bf16[256,256]{1,0:T(8,128)(2,1)S(1)}, u32[]{:S(2)}, u32[]{:S(2)}) collective-permute-start(bf16[256,256]{1,0:T(8,128)(2,1)S(1)} %get-tuple-element.40), channel_id=1, source_target_pairs={{0,24},{4,28},{8,16},{12,20},{16,8},{20,12},{24,0},{28,4},{1,25},{... | collective-permute-start | bytes 393224 | tf_op jit(solution)/shard_map/ppermute | solution.py:366
  31.4 0.1 shard_map.99.ready
  31.5 2.4 %collective-permute-done.12.refs_1_ = bf16[256,256]{1,0:T(8,128)(2,1)S(1)} collective-permute-done((bf16[256,256]{1,0:T(8,128)(2,1)S(1)}, bf16[256,256]{1,0:T(8,128)(2,1)S(1)}, u32[]{:S(2)}, u32[]{:S(2)}) %collective-permute-start.12) | collective-permute-done | bytes 131104 | tf_op jit(solution)/shard_map/ppermute | solution.py:366
  33.9 0.8 %collective-permute-done.13.refs_2_ = bf16[256,256]{1,0:T(8,128)(2,1)S(1)} collective-permute-done((bf16[256,256]{1,0:T(8,128)(2,1)S(1)}, bf16[256,256]{1,0:T(8,128)(2,1)S(1)}, u32[]{:S(2)}, u32[]{:S(2)}) %collective-permute-start.13) | collective-permute-done | bytes 131104 | tf_op jit(solution)/shard_map/ppermute | solution.py:366
  34.7 2.7 %collective-permute-done.14.refs_3_ = bf16[256,256]{1,0:T(8,128)(2,1)S(1)} collective-permute-done((bf16[256,256]{1,0:T(8,128)(2,1)S(1)}, bf16[256,256]{1,0:T(8,128)(2,1)S(1)}, u32[]{:S(2)}, u32[]{:S(2)}) %collective-permute-start.14) | collective-permute-done | bytes 131104 | tf_op jit(solution)/shard_map/ppermute | solution.py:366
  37.4 0.8 %shard_map.104 = bf16[256,512]{1,0:T(8,128)(2,1)} custom-call(bf16[256,256]{1,0:T(8,128)(2,1)S(1)} %shard_map.99.ready, f32[256,256]{1,0:T(8,128)S(1)} %get-tuple-element.30.projected, f32[2,128]{1,0:T(2,128)S(1)} %bitcast.5, f32[256,256]{1,0:T(8,128)S(1)} %get-tuple-element.37.refs_0_, bf16[256,256]{1,0:T(8,128)(2,1)S(1)} %collective-permute-done.12.refs_1_, ...), custom_call_target="tpu_custom_call" | custom-call | flops 393216 | bytes 1048576 | tf_op jit(solution)/shard_map/pallas_call | solution.py:309
  (14 shorter events, 0.2 us)
Async XLA Ops:
  1.5 11.0 %collective-permute-start = (bf16[256,256]{1,0:T(8,128)(2,1)S(1)}, bf16[256,256]{1,0:T(8,128)(2,1)S(1)}, u32[]{:S(2)}, u32[]{:S(2)}) collective-permute-start(bf16[256,256]{1,0:T(8,128)(2,1)S(1)} %get-tuple-element.24.own), channel_id=1, source_target_pairs={{0,3},{1,2},{2,1},{3,0},{4,7},{5,6},{6,5},{7,4},{8,11},{9,10},{10,... | collective-permute-start | bytes 393224 | tf_op jit(solution)/shard_map/ppermute | solution.py:359
  6.7 8.0 %collective-permute-start.1 = (bf16[256,256]{1,0:T(8,128)(2,1)S(1)}, bf16[256,256]{1,0:T(8,128)(2,1)S(1)}, u32[]{:S(2)}, u32[]{:S(2)}) collective-permute-start(bf16[256,256]{1,0:T(8,128)(2,1)S(1)} %get-tuple-element.24.own), channel_id=1, source_target_pairs={{0,1},{1,0},{2,3},{3,2},{4,5},{5,4},{6,7},{7,6},{8,9},{9,8},{10,11... | collective-permute-start | bytes 393224 | tf_op jit(solution)/shard_map/ppermute | solution.py:359
  8.2 8.0 %collective-permute-start.9 = (bf16[256,256]{1,0:T(8,128)(2,1)S(1)}, bf16[256,256]{1,0:T(8,128)(2,1)S(1)}, u32[]{:S(2)}, u32[]{:S(2)}) collective-permute-start(bf16[256,256]{1,0:T(8,128)(2,1)S(1)} %get-tuple-element.33.refs_0_), channel_id=1, source_target_pairs={{0,3},{1,2},{2,1},{3,0},{4,7},{5,6},{6,5},{7,4},{8,11},{9,10},{10,... | collective-permute-start | bytes 393224 | tf_op jit(solution)/shard_map/ppermute | solution.py:359
  12.6 6.4 %collective-permute-start.2 = (bf16[256,256]{1,0:T(8,128)(2,1)S(1)}, bf16[256,256]{1,0:T(8,128)(2,1)S(1)}, u32[]{:S(2)}, u32[]{:S(2)}) collective-permute-start(bf16[256,256]{1,0:T(8,128)(2,1)S(1)} %collective-permute-done.across), channel_id=1, source_target_pairs={{0,1},{1,0},{2,3},{3,2},{4,5},{5,4},{6,7},{7,6},{8,9},{9,8},{10,11... | collective-permute-start | bytes 393224 | tf_op jit(solution)/shard_map/ppermute | solution.py:359
  13.8 11.2 %collective-permute-start.8 = (bf16[256,256]{1,0:T(8,128)(2,1)S(1)}, bf16[256,256]{1,0:T(8,128)(2,1)S(1)}, u32[]{:S(2)}, u32[]{:S(2)}) collective-permute-start(bf16[256,256]{1,0:T(8,128)(2,1)S(1)} %get-tuple-element.33.refs_0_), channel_id=1, source_target_pairs={{0,1},{1,0},{2,3},{3,2},{4,5},{5,4},{6,7},{7,6},{8,9},{9,8},{10,11... | collective-permute-start | bytes 393224 | tf_op jit(solution)/shard_map/ppermute | solution.py:359
  16.2 8.8 %collective-permute-start.10 = (bf16[256,256]{1,0:T(8,128)(2,1)S(1)}, bf16[256,256]{1,0:T(8,128)(2,1)S(1)}, u32[]{:S(2)}, u32[]{:S(2)}) collective-permute-start(bf16[256,256]{1,0:T(8,128)(2,1)S(1)} %collective-permute-done.9.refs_3_), channel_id=1, source_target_pairs={{0,1},{1,0},{2,3},{3,2},{4,5},{5,4},{6,7},{7,6},{8,9},{9,8},{10,11... | collective-permute-start | bytes 393224 | tf_op jit(solution)/shard_map/ppermute | solution.py:359
  19.3 3.6 %collective-permute-start.3 = (bf16[768,256]{1,0:T(8,128)(2,1)S(1)}, bf16[768,256]{1,0:T(8,128)(2,1)S(1)}, u32[]{:S(2)}, u32[]{:S(2)}) collective-permute-start(bf16[768,256]{1,0:T(8,128)(2,1)S(1)} %shard_map.95), channel_id=1, source_target_pairs={{0,4},{4,0},{8,12},{12,8},{16,20},{20,16},{24,28},{28,24},{1,5},{5... | collective-permute-start | bytes 1179656 | tf_op jit(solution)/shard_map/ppermute | solution.py:359
  19.6 1.7 %collective-permute-start.4 = (bf16[256,256]{1,0:T(8,128)(2,1)S(1)}, bf16[256,256]{1,0:T(8,128)(2,1)S(1)}, u32[]{:S(2)}, u32[]{:S(2)}) collective-permute-start(bf16[256,256]{1,0:T(8,128)(2,1)S(1)} %shard_map.97), channel_id=1, source_target_pairs={{0,4},{4,0},{8,12},{12,8},{16,20},{20,16},{24,28},{28,24},{1,5},{5... | collective-permute-start | bytes 393224 | tf_op jit(solution)/shard_map/ppermute | solution.py:359
  21.3 9.6 %collective-permute-start.5 = (bf16[256,256]{1,0:T(8,128)(2,1)S(1)}, bf16[256,256]{1,0:T(8,128)(2,1)S(1)}, u32[]{:S(2)}, u32[]{:S(2)}) collective-permute-start(bf16[256,256]{1,0:T(8,128)(2,1)S(1)} %shard_map.98), channel_id=1, source_target_pairs={{0,8},{4,20},{8,0},{12,28},{16,24},{20,4},{24,16},{28,12},{1,9},{5... | collective-permute-start | bytes 393224 | tf_op jit(solution)/shard_map/ppermute | solution.py:366
  22.9 8.4 %collective-permute-start.6 = (bf16[256,256]{1,0:T(8,128)(2,1)S(1)}, bf16[256,256]{1,0:T(8,128)(2,1)S(1)}, u32[]{:S(2)}, u32[]{:S(2)}) collective-permute-start(bf16[256,256]{1,0:T(8,128)(2,1)S(1)} %get-tuple-element.28), channel_id=1, source_target_pairs={{0,16},{4,12},{8,24},{12,4},{16,0},{20,28},{24,8},{28,20},{1,17},{... | collective-permute-start | bytes 393224 | tf_op jit(solution)/shard_map/ppermute | solution.py:366
  24.5 6.8 %collective-permute-start.7 = (bf16[256,256]{1,0:T(8,128)(2,1)S(1)}, bf16[256,256]{1,0:T(8,128)(2,1)S(1)}, u32[]{:S(2)}, u32[]{:S(2)}) collective-permute-start(bf16[256,256]{1,0:T(8,128)(2,1)S(1)} %get-tuple-element.29), channel_id=1, source_target_pairs={{0,24},{4,28},{8,16},{12,20},{16,8},{20,12},{24,0},{28,4},{1,25},{... | collective-permute-start | bytes 393224 | tf_op jit(solution)/shard_map/ppermute | solution.py:366
  25.7 5.6 %copy-start = (f32[256]{0:T(256)S(1)}, f32[256]{0:T(256)}, u32[]{:S(2)}) copy-start(f32[256]{0:T(256)} %param.12) | copy-start | bytes 3076
  25.7 2.0 %collective-permute-start.11 = (bf16[1024,256]{1,0:T(8,128)(2,1)S(1)}, bf16[1024,256]{1,0:T(8,128)(2,1)S(1)}, u32[]{:S(2)}, u32[]{:S(2)}) collective-permute-start(bf16[1024,256]{1,0:T(8,128)(2,1)S(1)} %shard_map.102), channel_id=1, source_target_pairs={{0,4},{4,0},{8,12},{12,8},{16,20},{20,16},{24,28},{28,24},{1,5},{5... | collective-permute-start | bytes 1572872 | tf_op jit(solution)/shard_map/ppermute | solution.py:359
  27.8 6.1 %collective-permute-start.12 = (bf16[256,256]{1,0:T(8,128)(2,1)S(1)}, bf16[256,256]{1,0:T(8,128)(2,1)S(1)}, u32[]{:S(2)}, u32[]{:S(2)}) collective-permute-start(bf16[256,256]{1,0:T(8,128)(2,1)S(1)} %get-tuple-element.38), channel_id=1, source_target_pairs={{0,8},{4,20},{8,0},{12,28},{16,24},{20,4},{24,16},{28,12},{1,9},{5... | collective-permute-start | bytes 393224 | tf_op jit(solution)/shard_map/ppermute | solution.py:366
  29.4 5.3 %collective-permute-start.13 = (bf16[256,256]{1,0:T(8,128)(2,1)S(1)}, bf16[256,256]{1,0:T(8,128)(2,1)S(1)}, u32[]{:S(2)}, u32[]{:S(2)}) collective-permute-start(bf16[256,256]{1,0:T(8,128)(2,1)S(1)} %get-tuple-element.39), channel_id=1, source_target_pairs={{0,16},{4,12},{8,24},{12,4},{16,0},{20,28},{24,8},{28,20},{1,17},{... | collective-permute-start | bytes 393224 | tf_op jit(solution)/shard_map/ppermute | solution.py:366
  30.9 6.5 %collective-permute-start.14 = (bf16[256,256]{1,0:T(8,128)(2,1)S(1)}, bf16[256,256]{1,0:T(8,128)(2,1)S(1)}, u32[]{:S(2)}, u32[]{:S(2)}) collective-permute-start(bf16[256,256]{1,0:T(8,128)(2,1)S(1)} %get-tuple-element.40), channel_id=1, source_target_pairs={{0,24},{4,28},{8,16},{12,20},{16,8},{20,12},{24,0},{28,4},{1,25},{... | collective-permute-start | bytes 393224 | tf_op jit(solution)/shard_map/ppermute | solution.py:366

commit v19 on v18

--- a/solution.py
+++ b/solution.py
@@ -408,10 +408,13 @@
     onward, matrix = lax.optimization_barrier((across[0], built))
     passed = swap(onward, "col", 1)
     early = early_product(matrix, scaled[0], beside[0], across[0])
-    away = [
-        late_product(matrix, early, passed, start, count, jnp.bfloat16, WEIGHTS[0])
-        for start, count in ((0, own_rows), (own_rows, half - own_rows))
-    ]
+    away = [late_product(matrix, early, passed, 0, own_rows, jnp.bfloat16, WEIGHTS[0])]
+    after, _ = lax.optimization_barrier((passed, away[0]))
+    away.append(
+        late_product(
+            matrix, early, after, own_rows, half - own_rows, jnp.bfloat16, WEIGHTS[0]
+        )
+    )
     stay = late_product(matrix, early, passed, half, half, jnp.float32, WEIGHTS[1])
     came = [swap(value, "row", 1) for value in away]
     (lead,) = join(stay, came[0], 0, own_rows, [jnp.bfloat16])

time: 38.4 us -> 37.9 us (0.987)
  waiting for transfers between devices: 9.18 us -> 8.54 us
    ppermute x9, waiting for transfers between devices: 3.26 us -> 2.62 us  [swap(): return lax.ppermute(value, axis, pairs)]
where the time goes in v19:
time: 37.9 us; the launch traced here: 37.8 us
  starting transfers between devices  18.4 us (49%)
  Pallas kernels  10 us (26%)
  waiting for transfers between devices  8.54 us (23%)
  between operations  0.78 us (2%)
    ppermute x9, starting transfers between devices, swap(): return lax.ppermute(value, axis, pairs)  11 us
    ppermute x6, starting transfers between devices, exchange(): lax.ppermute(value, 'row', [(i, i ^ step[i % 2]) for i in range(owners)])  7.39 us
    ppermute x6, waiting for transfers between devices, exchange(): lax.ppermute(value, 'row', [(i, i ^ step[i % 2]) for i in range(owners)])  5.92 us
    pallas_call x2, Pallas kernels, project(): pl.pallas_call(functools.partial(project_kernel, start), out_shape=[jax.S...  3.07 us
    pallas_call x1, Pallas kernels, merge_tiles(): pl.pallas_call(functools.partial(merge_kernel, own_tiles, labels.shape[1]...  2.76 us
    ppermute x9, waiting for transfers between devices, swap(): return lax.ppermute(value, axis, pairs)  2.62 us
    pallas_call x2, Pallas kernels, product(): pl.pallas_call(functools.partial(product_kernel, first), out_shape=jax.Sh...  1.42 us
    pallas_call x1, Pallas kernels, early_product(): pl.pallas_call(early_kernel, out_shape=jax.ShapeDtypeStruct((total, width...  0.99 us
  transfers between devices with their start and end apart: 15, of which 7 were waited for; matrix products, arithmetic and copies ran while one was open for 0% of the time, Pallas kernels for 20%

profile of v19, /device:TPU:0, one launch (start us, length us, event | category | flops | bytes accessed | tf_op | source)
XLA Modules:
  0.0 37.8 jit_solution(2499729469329315323)
XLA Ops:
  0.0 1.5 %shard_map.91 = (f32[256,256]{1,0:T(8,128)S(1)}, bf16[256,256]{1,0:T(8,128)(2,1)S(1)}) custom-call(bf16[256,1024]{1,0:T(8,128)(2,1)} %features_hbm.3, bf16[1024,512]{1,0:T(8,128)(2,1)} %weight_hbm.3, f32[2,128]{1,0:T(2,128)} %bitcast.6), custom_call_target="tpu_custom_call" | custom-call | flops 134217728 | bytes 1048576 | tf_op jit(solution)/shard_map/pallas_call | solution.py:65
  1.5 5.1 %collective-permute-start = (bf16[256,256]{1,0:T(8,128)(2,1)S(1)}, bf16[256,256]{1,0:T(8,128)(2,1)S(1)}, u32[]{:S(2)}, u32[]{:S(2)}) collective-permute-start(bf16[256,256]{1,0:T(8,128)(2,1)S(1)} %get-tuple-element.25.own), channel_id=1, source_target_pairs={{0,3},{1,2},{2,1},{3,0},{4,7},{5,6},{6,5},{7,4},{8,11},{9,10},{10,... | collective-permute-start | bytes 393224 | tf_op jit(solution)/shard_map/ppermute | solution.py:359
  6.7 1.5 %shard_map.100 = (f32[256,256]{1,0:T(8,128)S(1)}, bf16[256,256]{1,0:T(8,128)(2,1)S(1)}) custom-call(bf16[256,1024]{1,0:T(8,128)(2,1)} %features_hbm.3, bf16[1024,512]{1,0:T(8,128)(2,1)} %weight_hbm.3, f32[2,128]{1,0:T(2,128)} %bitcast.7), custom_call_target="tpu_custom_call" | custom-call | flops 134217728 | bytes 1048576 | tf_op jit(solution)/shard_map/pallas_call | solution.py:65
  8.2 1.0 %collective-permute-start.9 = (bf16[256,256]{1,0:T(8,128)(2,1)S(1)}, bf16[256,256]{1,0:T(8,128)(2,1)S(1)}, u32[]{:S(2)}, u32[]{:S(2)}) collective-permute-start(bf16[256,256]{1,0:T(8,128)(2,1)S(1)} %get-tuple-element.35.refs_0_), channel_id=1, source_target_pairs={{0,3},{1,2},{2,1},{3,0},{4,7},{5,6},{6,5},{7,4},{8,11},{9,10},{10,... | collective-permute-start | bytes 393224 | tf_op jit(solution)/shard_map/ppermute | solution.py:359
  9.8 2.8 %shard_map.92.matrix = bf16[2048,1024]{1,0:T(8,128)(2,1)S(1)} custom-call(s32[1]{0:T(128)} %bitcast.2.row, s32[1]{0:T(128)} %bitcast.3.column, s32[1]{0:T(128)S(6)} %copy.10.count, s32[1,64]{1,0:T(1,128)} %sources_hbm.1, s32[1,64]{1,0:T(1,128)} %targets_hbm.1, s32[1,16]{1,0:T(1,128)} %labels_hbm.1, bf16[1,64,128,128]{3,2,1,0:T(8,128)(2,1)} %tiles_hbm.1), custom_call_target="tpu_custom_call" | custom-call | flops 8388608 | bytes 12582912 | tf_op jit(solution)/shard_map/pallas_call | solution.py:153
  12.6 1.2 %collective-permute-start.2 = (bf16[256,256]{1,0:T(8,128)(2,1)S(1)}, bf16[256,256]{1,0:T(8,128)(2,1)S(1)}, u32[]{:S(2)}, u32[]{:S(2)}) collective-permute-start(bf16[256,256]{1,0:T(8,128)(2,1)S(1)} %collective-permute-done.across), channel_id=1, source_target_pairs={{0,1},{1,0},{2,3},{3,2},{4,5},{5,4},{6,7},{7,6},{8,9},{9,8},{10,11... | collective-permute-start | bytes 393224 | tf_op jit(solution)/shard_map/ppermute | solution.py:359
  13.8 0.9 %collective-permute-start.8 = (bf16[256,256]{1,0:T(8,128)(2,1)S(1)}, bf16[256,256]{1,0:T(8,128)(2,1)S(1)}, u32[]{:S(2)}, u32[]{:S(2)}) collective-permute-start(bf16[256,256]{1,0:T(8,128)(2,1)S(1)} %get-tuple-element.35.refs_0_), channel_id=1, source_target_pairs={{0,1},{1,0},{2,3},{3,2},{4,5},{5,4},{6,7},{7,6},{8,9},{9,8},{10,11... | collective-permute-start | bytes 393224 | tf_op jit(solution)/shard_map/ppermute | solution.py:359
  14.7 1.0 %shard_map.93.early = f32[2048,256]{1,0:T(8,128)S(1)} custom-call(bf16[2048,1024]{1,0:T(8,128)(2,1)S(1)} %shard_map.92.matrix, bf16[256,256]{1,0:T(8,128)(2,1)S(1)} %get-tuple-element.25.own, bf16[256,256]{1,0:T(8,128)(2,1)S(1)} %collective-permute-done.1.beside, bf16[256,256]{1,0:T(8,128)(2,1)S(1)} %collective-permute-done.across), custom_call_target="tpu_custom_call" | custom-call | flops 536870912 | bytes 1 | tf_op jit(solution)/shard_map/pallas_call | solution.py:187
  15.7 0.5 %collective-permute-done.9.refs_3_ = bf16[256,256]{1,0:T(8,128)(2,1)S(1)} collective-permute-done((bf16[256,256]{1,0:T(8,128)(2,1)S(1)}, bf16[256,256]{1,0:T(8,128)(2,1)S(1)}, u32[]{:S(2)}, u32[]{:S(2)}) %collective-permute-start.9) | collective-permute-done | bytes 131104 | tf_op jit(solution)/shard_map/ppermute | solution.py:359
  16.2 2.1 %collective-permute-start.10 = (bf16[256,256]{1,0:T(8,128)(2,1)S(1)}, bf16[256,256]{1,0:T(8,128)(2,1)S(1)}, u32[]{:S(2)}, u32[]{:S(2)}) collective-permute-start(bf16[256,256]{1,0:T(8,128)(2,1)S(1)} %collective-permute-done.9.refs_3_), channel_id=1, source_target_pairs={{0,1},{1,0},{2,3},{3,2},{4,5},{5,4},{6,7},{7,6},{8,9},{9,8},{10,11... | collective-permute-start | bytes 393224 | tf_op jit(solution)/shard_map/ppermute | solution.py:359
  18.3 0.7 %collective-permute-done.2.passed = bf16[256,256]{1,0:T(8,128)(2,1)S(1)} collective-permute-done((bf16[256,256]{1,0:T(8,128)(2,1)S(1)}, bf16[256,256]{1,0:T(8,128)(2,1)S(1)}, u32[]{:S(2)}, u32[]{:S(2)}) %collective-permute-start.2) | collective-permute-done | bytes 131104 | tf_op jit(solution)/shard_map/ppermute | solution.py:359
  19.0 0.2 shard_map.95
  19.2 0.1 collective-permute-start.4
  19.3 0.3 shard_map.96
  19.6 0.6 %collective-permute-start.3 = (bf16[768,256]{1,0:T(8,128)(2,1)S(1)}, bf16[768,256]{1,0:T(8,128)(2,1)S(1)}, u32[]{:S(2)}, u32[]{:S(2)}) collective-permute-start(bf16[768,256]{1,0:T(8,128)(2,1)S(1)} %shard_map.96), channel_id=1, source_target_pairs={{0,4},{4,0},{8,12},{12,8},{16,20},{20,16},{24,28},{28,24},{1,5},{5... | collective-permute-start | bytes 1179656 | tf_op jit(solution)/shard_map/ppermute | solution.py:359
  20.1 0.3 shard_map.94.stay
  20.4 0.2 collective-permute-done.4.came
  20.7 1.6 %collective-permute-start.5 = (bf16[256,256]{1,0:T(8,128)(2,1)S(1)}, bf16[256,256]{1,0:T(8,128)(2,1)S(1)}, u32[]{:S(2)}, u32[]{:S(2)}) collective-permute-start(bf16[256,256]{1,0:T(8,128)(2,1)S(1)} %shard_map.98), channel_id=1, source_target_pairs={{0,8},{4,20},{8,0},{12,28},{16,24},{20,4},{24,16},{28,12},{1,9},{5... | collective-permute-start | bytes 393224 | tf_op jit(solution)/shard_map/ppermute | solution.py:366
  22.3 1.6 %collective-permute-start.6 = (bf16[256,256]{1,0:T(8,128)(2,1)S(1)}, bf16[256,256]{1,0:T(8,128)(2,1)S(1)}, u32[]{:S(2)}, u32[]{:S(2)}) collective-permute-start(bf16[256,256]{1,0:T(8,128)(2,1)S(1)} %get-tuple-element.30), channel_id=1, source_target_pairs={{0,16},{4,12},{8,24},{12,4},{16,0},{20,28},{24,8},{28,20},{1,17},{... | collective-permute-start | bytes 393224 | tf_op jit(solution)/shard_map/ppermute | solution.py:366
  23.9 0.7 %collective-permute-start.7 = (bf16[256,256]{1,0:T(8,128)(2,1)S(1)}, bf16[256,256]{1,0:T(8,128)(2,1)S(1)}, u32[]{:S(2)}, u32[]{:S(2)}) collective-permute-start(bf16[256,256]{1,0:T(8,128)(2,1)S(1)} %get-tuple-element.31), channel_id=1, source_target_pairs={{0,24},{4,28},{8,16},{12,20},{16,8},{20,12},{24,0},{28,4},{1,25},{... | collective-permute-start | bytes 393224 | tf_op jit(solution)/shard_map/ppermute | solution.py:366
  24.6 0.7 %shard_map.102 = bf16[1024,256]{1,0:T(8,128)(2,1)S(1)} custom-call(bf16[2048,1024]{1,0:T(8,128)(2,1)S(1)} %shard_map.92.matrix, bf16[256,256]{1,0:T(8,128)(2,1)S(1)} %get-tuple-element.35.refs_0_, bf16[256,256]{1,0:T(8,128)(2,1)S(1)} %collective-permute-done.8.refs_1_, bf16[256,256]{1,0:T(8,128)(2,1)S(1)} %collective-permute-done.10.refs_2_, ...), custom_call_target="tpu_custom_call" | custom-call | bytes 1 | tf_op jit(solution)/shard_map/pallas_call | solution.py:235
  25.4 0.7 %shard_map.101.stay = f32[1024,256]{1,0:T(8,128)S(1)} custom-call(bf16[2048,1024]{1,0:T(8,128)(2,1)S(1)} %shard_map.92.matrix, bf16[256,256]{1,0:T(8,128)(2,1)S(1)} %get-tuple-element.35.refs_0_, bf16[256,256]{1,0:T(8,128)(2,1)S(1)} %collective-permute-done.8.refs_1_, bf16[256,256]{1,0:T(8,128)(2,1)S(1)} %collective-permute-done.10.refs_2_, ...), custom_call_target="tpu_custom_call" | custom-call | flops 10737418240 | bytes 1 | tf_op jit(solution)/shard_map/pallas_call | solution.py:235
  26.1 1.2 %collective-permute-done.11.came = bf16[1024,256]{1,0:T(8,128)(2,1)S(1)} collective-permute-done((bf16[1024,256]{1,0:T(8,128)(2,1)S(1)}, bf16[1024,256]{1,0:T(8,128)(2,1)S(1)}, u32[]{:S(2)}, u32[]{:S(2)}) %collective-permute-start.11) | collective-permute-done | bytes 524320 | tf_op jit(solution)/shard_map/ppermute | solution.py:359
  27.3 0.1 shard_map.103
  27.4 1.3 %collective-permute-start.12 = (bf16[256,256]{1,0:T(8,128)(2,1)S(1)}, bf16[256,256]{1,0:T(8,128)(2,1)S(1)}, u32[]{:S(2)}, u32[]{:S(2)}) collective-permute-start(bf16[256,256]{1,0:T(8,128)(2,1)S(1)} %get-tuple-element.40), channel_id=1, source_target_pairs={{0,8},{4,20},{8,0},{12,28},{16,24},{20,4},{24,16},{28,12},{1,9},{5... | collective-permute-start | bytes 393224 | tf_op jit(solution)/shard_map/ppermute | solution.py:366
  28.7 1.5 %collective-permute-start.13 = (bf16[256,256]{1,0:T(8,128)(2,1)S(1)}, bf16[256,256]{1,0:T(8,128)(2,1)S(1)}, u32[]{:S(2)}, u32[]{:S(2)}) collective-permute-start(bf16[256,256]{1,0:T(8,128)(2,1)S(1)} %get-tuple-element.41), channel_id=1, source_target_pairs={{0,16},{4,12},{8,24},{12,4},{16,0},{20,28},{24,8},{28,20},{1,17},{... | collective-permute-start | bytes 393224 | tf_op jit(solution)/shard_map/ppermute | solution.py:366
  30.3 0.7 %collective-permute-start.14 = (bf16[256,256]{1,0:T(8,128)(2,1)S(1)}, bf16[256,256]{1,0:T(8,128)(2,1)S(1)}, u32[]{:S(2)}, u32[]{:S(2)}) collective-permute-start(bf16[256,256]{1,0:T(8,128)(2,1)S(1)} %get-tuple-element.42), channel_id=1, source_target_pairs={{0,24},{4,28},{8,16},{12,20},{16,8},{20,12},{24,0},{28,4},{1,25},{... | collective-permute-start | bytes 393224 | tf_op jit(solution)/shard_map/ppermute | solution.py:366
  30.9 0.1 shard_map.99.ready
  31.1 2.4 %collective-permute-done.12.refs_1_ = bf16[256,256]{1,0:T(8,128)(2,1)S(1)} collective-permute-done((bf16[256,256]{1,0:T(8,128)(2,1)S(1)}, bf16[256,256]{1,0:T(8,128)(2,1)S(1)}, u32[]{:S(2)}, u32[]{:S(2)}) %collective-permute-start.12) | collective-permute-done | bytes 131104 | tf_op jit(solution)/shard_map/ppermute | solution.py:366
  33.5 0.3 collective-permute-done.13.refs_2_
  33.8 3.2 %collective-permute-done.14.refs_3_ = bf16[256,256]{1,0:T(8,128)(2,1)S(1)} collective-permute-done((bf16[256,256]{1,0:T(8,128)(2,1)S(1)}, bf16[256,256]{1,0:T(8,128)(2,1)S(1)}, u32[]{:S(2)}, u32[]{:S(2)}) %collective-permute-start.14) | collective-permute-done | bytes 131104 | tf_op jit(solution)/shard_map/ppermute | solution.py:366
  37.0 0.8 %shard_map.104 = bf16[256,512]{1,0:T(8,128)(2,1)} custom-call(bf16[256,256]{1,0:T(8,128)(2,1)S(1)} %shard_map.99.ready, f32[256,256]{1,0:T(8,128)S(1)} %get-tuple-element.32.projected, f32[2,128]{1,0:T(2,128)S(1)} %bitcast.5, f32[256,256]{1,0:T(8,128)S(1)} %get-tuple-element.39.refs_0_, bf16[256,256]{1,0:T(8,128)(2,1)S(1)} %collective-permute-done.12.refs_1_, ...), custom_call_target="tpu_custom_call" | custom-call | flops 393216 | bytes 1048576 | tf_op jit(solution)/shard_map/pallas_call | solution.py:309
  (14 shorter events, 0.2 us)
Async XLA Ops:
  1.5 11.0 %collective-permute-start = (bf16[256,256]{1,0:T(8,128)(2,1)S(1)}, bf16[256,256]{1,0:T(8,128)(2,1)S(1)}, u32[]{:S(2)}, u32[]{:S(2)}) collective-permute-start(bf16[256,256]{1,0:T(8,128)(2,1)S(1)} %get-tuple-element.25.own), channel_id=1, source_target_pairs={{0,3},{1,2},{2,1},{3,0},{4,7},{5,6},{6,5},{7,4},{8,11},{9,10},{10,... | collective-permute-start | bytes 393224 | tf_op jit(solution)/shard_map/ppermute | solution.py:359
  6.7 8.0 %collective-permute-start.1 = (bf16[256,256]{1,0:T(8,128)(2,1)S(1)}, bf16[256,256]{1,0:T(8,128)(2,1)S(1)}, u32[]{:S(2)}, u32[]{:S(2)}) collective-permute-start(bf16[256,256]{1,0:T(8,128)(2,1)S(1)} %get-tuple-element.25.own), channel_id=1, source_target_pairs={{0,1},{1,0},{2,3},{3,2},{4,5},{5,4},{6,7},{7,6},{8,9},{9,8},{10,11... | collective-permute-start | bytes 393224 | tf_op jit(solution)/shard_map/ppermute | solution.py:359
  8.2 8.0 %collective-permute-start.9 = (bf16[256,256]{1,0:T(8,128)(2,1)S(1)}, bf16[256,256]{1,0:T(8,128)(2,1)S(1)}, u32[]{:S(2)}, u32[]{:S(2)}) collective-permute-start(bf16[256,256]{1,0:T(8,128)(2,1)S(1)} %get-tuple-element.35.refs_0_), channel_id=1, source_target_pairs={{0,3},{1,2},{2,1},{3,0},{4,7},{5,6},{6,5},{7,4},{8,11},{9,10},{10,... | collective-permute-start | bytes 393224 | tf_op jit(solution)/shard_map/ppermute | solution.py:359
  12.6 6.4 %collective-permute-start.2 = (bf16[256,256]{1,0:T(8,128)(2,1)S(1)}, bf16[256,256]{1,0:T(8,128)(2,1)S(1)}, u32[]{:S(2)}, u32[]{:S(2)}) collective-permute-start(bf16[256,256]{1,0:T(8,128)(2,1)S(1)} %collective-permute-done.across), channel_id=1, source_target_pairs={{0,1},{1,0},{2,3},{3,2},{4,5},{5,4},{6,7},{7,6},{8,9},{9,8},{10,11... | collective-permute-start | bytes 393224 | tf_op jit(solution)/shard_map/ppermute | solution.py:359
  13.8 10.8 %collective-permute-start.8 = (bf16[256,256]{1,0:T(8,128)(2,1)S(1)}, bf16[256,256]{1,0:T(8,128)(2,1)S(1)}, u32[]{:S(2)}, u32[]{:S(2)}) collective-permute-start(bf16[256,256]{1,0:T(8,128)(2,1)S(1)} %get-tuple-element.35.refs_0_), channel_id=1, source_target_pairs={{0,1},{1,0},{2,3},{3,2},{4,5},{5,4},{6,7},{7,6},{8,9},{9,8},{10,11... | collective-permute-start | bytes 393224 | tf_op jit(solution)/shard_map/ppermute | solution.py:359
  16.2 8.4 %collective-permute-start.10 = (bf16[256,256]{1,0:T(8,128)(2,1)S(1)}, bf16[256,256]{1,0:T(8,128)(2,1)S(1)}, u32[]{:S(2)}, u32[]{:S(2)}) collective-permute-start(bf16[256,256]{1,0:T(8,128)(2,1)S(1)} %collective-permute-done.9.refs_3_), channel_id=1, source_target_pairs={{0,1},{1,0},{2,3},{3,2},{4,5},{5,4},{6,7},{7,6},{8,9},{9,8},{10,11... | collective-permute-start | bytes 393224 | tf_op jit(solution)/shard_map/ppermute | solution.py:359
  19.2 1.4 %collective-permute-start.4 = (bf16[256,256]{1,0:T(8,128)(2,1)S(1)}, bf16[256,256]{1,0:T(8,128)(2,1)S(1)}, u32[]{:S(2)}, u32[]{:S(2)}) collective-permute-start(bf16[256,256]{1,0:T(8,128)(2,1)S(1)} %shard_map.95), channel_id=1, source_target_pairs={{0,4},{4,0},{8,12},{12,8},{16,20},{20,16},{24,28},{28,24},{1,5},{5... | collective-permute-start | bytes 393224 | tf_op jit(solution)/shard_map/ppermute | solution.py:359
  19.6 2.7 %collective-permute-start.3 = (bf16[768,256]{1,0:T(8,128)(2,1)S(1)}, bf16[768,256]{1,0:T(8,128)(2,1)S(1)}, u32[]{:S(2)}, u32[]{:S(2)}) collective-permute-start(bf16[768,256]{1,0:T(8,128)(2,1)S(1)} %shard_map.96), channel_id=1, source_target_pairs={{0,4},{4,0},{8,12},{12,8},{16,20},{20,16},{24,28},{28,24},{1,5},{5... | collective-permute-start | bytes 1179656 | tf_op jit(solution)/shard_map/ppermute | solution.py:359
  20.7 9.6 %collective-permute-start.5 = (bf16[256,256]{1,0:T(8,128)(2,1)S(1)}, bf16[256,256]{1,0:T(8,128)(2,1)S(1)}, u32[]{:S(2)}, u32[]{:S(2)}) collective-permute-start(bf16[256,256]{1,0:T(8,128)(2,1)S(1)} %shard_map.98), channel_id=1, source_target_pairs={{0,8},{4,20},{8,0},{12,28},{16,24},{20,4},{24,16},{28,12},{1,9},{5... | collective-permute-start | bytes 393224 | tf_op jit(solution)/shard_map/ppermute | solution.py:366
  22.3 8.6 %collective-permute-start.6 = (bf16[256,256]{1,0:T(8,128)(2,1)S(1)}, bf16[256,256]{1,0:T(8,128)(2,1)S(1)}, u32[]{:S(2)}, u32[]{:S(2)}) collective-permute-start(bf16[256,256]{1,0:T(8,128)(2,1)S(1)} %get-tuple-element.30), channel_id=1, source_target_pairs={{0,16},{4,12},{8,24},{12,4},{16,0},{20,28},{24,8},{28,20},{1,17},{... | collective-permute-start | bytes 393224 | tf_op jit(solution)/shard_map/ppermute | solution.py:366
  23.9 7.0 %collective-permute-start.7 = (bf16[256,256]{1,0:T(8,128)(2,1)S(1)}, bf16[256,256]{1,0:T(8,128)(2,1)S(1)}, u32[]{:S(2)}, u32[]{:S(2)}) collective-permute-start(bf16[256,256]{1,0:T(8,128)(2,1)S(1)} %get-tuple-element.31), channel_id=1, source_target_pairs={{0,24},{4,28},{8,16},{12,20},{16,8},{20,12},{24,0},{28,4},{1,25},{... | collective-permute-start | bytes 393224 | tf_op jit(solution)/shard_map/ppermute | solution.py:366
  25.3 5.6 %copy-start = (f32[256]{0:T(256)S(1)}, f32[256]{0:T(256)}, u32[]{:S(2)}) copy-start(f32[256]{0:T(256)} %param.12) | copy-start | bytes 3076
  25.3 2.0 %collective-permute-start.11 = (bf16[1024,256]{1,0:T(8,128)(2,1)S(1)}, bf16[1024,256]{1,0:T(8,128)(2,1)S(1)}, u32[]{:S(2)}, u32[]{:S(2)}) collective-permute-start(bf16[1024,256]{1,0:T(8,128)(2,1)S(1)} %shard_map.102), channel_id=1, source_target_pairs={{0,4},{4,0},{8,12},{12,8},{16,20},{20,16},{24,28},{28,24},{1,5},{5... | collective-permute-start | bytes 1572872 | tf_op jit(solution)/shard_map/ppermute | solution.py:359
  27.4 6.1 %collective-permute-start.12 = (bf16[256,256]{1,0:T(8,128)(2,1)S(1)}, bf16[256,256]{1,0:T(8,128)(2,1)S(1)}, u32[]{:S(2)}, u32[]{:S(2)}) collective-permute-start(bf16[256,256]{1,0:T(8,128)(2,1)S(1)} %get-tuple-element.40), channel_id=1, source_target_pairs={{0,8},{4,20},{8,0},{12,28},{16,24},{20,4},{24,16},{28,12},{1,9},{5... | collective-permute-start | bytes 393224 | tf_op jit(solution)/shard_map/ppermute | solution.py:366
  28.7 5.0 %collective-permute-start.13 = (bf16[256,256]{1,0:T(8,128)(2,1)S(1)}, bf16[256,256]{1,0:T(8,128)(2,1)S(1)}, u32[]{:S(2)}, u32[]{:S(2)}) collective-permute-start(bf16[256,256]{1,0:T(8,128)(2,1)S(1)} %get-tuple-element.41), channel_id=1, source_target_pairs={{0,16},{4,12},{8,24},{12,4},{16,0},{20,28},{24,8},{28,20},{1,17},{... | collective-permute-start | bytes 393224 | tf_op jit(solution)/shard_map/ppermute | solution.py:366
  30.3 6.7 %collective-permute-start.14 = (bf16[256,256]{1,0:T(8,128)(2,1)S(1)}, bf16[256,256]{1,0:T(8,128)(2,1)S(1)}, u32[]{:S(2)}, u32[]{:S(2)}) collective-permute-start(bf16[256,256]{1,0:T(8,128)(2,1)S(1)} %get-tuple-element.42), channel_id=1, source_target_pairs={{0,24},{4,28},{8,16},{12,20},{16,8},{20,12},{24,0},{28,4},{1,25},{... | collective-permute-start | bytes 393224 | tf_op jit(solution)/shard_map/ppermute | solution.py:366

commit v20 on v19

--- a/solution.py
+++ b/solution.py
@@ -32,8 +32,9 @@
     return jnp.broadcast_to(row, (lanes, row.shape[1])).T
 
 
-def project_kernel(start, features_hbm, weight_hbm, norm_hbm, projected, scaled, *refs):
-    features, weight, norm, sems = refs
+def project_kernel(start, extra, features_hbm, weight_hbm, norm_hbm, *refs):
+    extra_hbm, (projected, scaled), refs = refs[:extra], refs[extra : extra + 2], refs[extra + 2 :]
+    staged, (features, weight, norm, sems) = refs[:extra], refs[extra:]
     width, lanes = scaled.shape[1], norm.shape[1]
     copies = [
         pltpu.make_async_copy(source, target, sems.at[k])
@@ -42,6 +43,7 @@
                 (weight_hbm.at[:, start : start + width], weight),
                 (features_hbm, features),
                 (norm_hbm, norm),
+                *zip(extra_hbm, staged),
             ]
         )
     ]
@@ -59,36 +61,37 @@
             scaled[here, column : column + lanes] = piece.astype(scaled.dtype)
 
 
-def project(features, weight, source_norm, start, width):
+def project(features, weight, source_norm, start, width, *extra):
     rows, depth = features.shape
     norm = source_norm.reshape(-1, 128)
     return pl.pallas_call(
-        functools.partial(project_kernel, start),
+        functools.partial(project_kernel, start, len(extra)),
         out_shape=[
             jax.ShapeDtypeStruct((rows, width), jnp.float32),
             jax.ShapeDtypeStruct((rows, width), jnp.bfloat16),
-        ],
-        in_specs=[HBM] * 3,
-        out_specs=[VMEM] * 2,
+        ]
+        + [jax.ShapeDtypeStruct(value.shape, value.dtype) for value in extra],
+        in_specs=[HBM] * (3 + len(extra)),
+        out_specs=[VMEM] * (2 + len(extra)),
         scratch_shapes=[
             pltpu.VMEM(features.shape, features.dtype),
             pltpu.VMEM((depth, width), weight.dtype),
             pltpu.VMEM(norm.shape, norm.dtype),
-            pltpu.SemaphoreType.DMA((3,)),
+            pltpu.SemaphoreType.DMA((3 + len(extra),)),
         ],
         compiler_params=params(12),
         cost_estimate=cost(2 * rows * depth * width, 2 * depth * (rows + width)),
-    )(*in_hbm(features, weight, norm))
+    )(*in_hbm(features, weight, norm, *extra))
 
 
 def merge_kernel(
-    own_tiles, per_owner, row, column, count, sources_hbm, targets_hbm, labels_hbm, tiles_hbm, out,
+    own_tiles, per_owner, row, column, count, sources_in, targets_in, labels_in, tiles_hbm, out,
     total, tiles, sources, targets, labels, bases, seen, sems, tile_sems,
 ):
     small = [
         pltpu.make_async_copy(source, target, sems.at[k])
         for k, (source, target) in enumerate(
-            [(sources_hbm, sources), (targets_hbm, targets), (labels_hbm, labels)]
+            [(sources_in, sources), (targets_in, targets), (labels_in, labels)]
         )
     ]
     parts = tile_sems.shape[0]
@@ -153,7 +156,7 @@
     return pl.pallas_call(
         functools.partial(merge_kernel, own_tiles, labels.shape[1] // owners),
         out_shape=jax.ShapeDtypeStruct((places * rows, span * rows), jnp.bfloat16),
-        in_specs=[SMEM] * 3 + [HBM] * 4,
+        in_specs=[SMEM] * 3 + [VMEM] * 3 + [HBM],
         out_specs=VMEM,
         scratch_shapes=[
             pltpu.VMEM((places * span + 1, rows, rows), jnp.float32),
@@ -168,7 +171,7 @@
         ],
         compiler_params=params(24),
         cost_estimate=cost(8 * MIB, 12 * MIB),
-    )(row, column, count, *in_hbm(sources, targets, labels, tile_weights))
+    )(row, column, count, sources, targets, labels, *in_hbm(tile_weights))
 
 
 def early_kernel(matrix, own, beside, across, out):
@@ -398,9 +401,13 @@
         return jnp.maximum(target_norm[:, None] * gathered, 0.0).astype(jnp.bfloat16)
 
     width = weight.shape[1] // CHUNKS
-    projected, scaled = zip(
-        *(project(features, weight, source_norm, k * width, width) for k in range(CHUNKS))
-    )
+    first = project(features, weight, source_norm, 0, width)
+    second = project(
+        features, weight, source_norm, width, width, tile_source, tile_target, mirror_tile
+    )
+    projected, scaled = zip(first, second[:2])
+    sources, targets, labels = second[2:]
+    index_args = sources, targets, tile_count, labels
     built = merge_tiles(own_tiles, owners, span, index_args, tile_weights)
     half = built.shape[0] // 2
     across = [swap(own, "col", 3) for own in scaled]

time: 37.9 us -> 38 us (level)
  transfers between devices with their start and end apart: 15 -> 15, of which waited for: 7 -> 8; matrix products, arithmetic and copies ran while one was open for 0% -> 0% of each run, Pallas kernels for 20% -> 21%
where the time goes in v20:
time: 38 us; the launch traced here: 37.8 us
  starting transfers between devices  18.4 us (48%)
  Pallas kernels  10.1 us (27%)
  waiting for transfers between devices  8.54 us (22%)
  between operations  0.78 us (2%)
    ppermute x9, starting transfers between devices, swap(): return lax.ppermute(value, axis, pairs)  11 us
    ppermute x6, starting transfers between devices, exchange(): lax.ppermute(value, 'row', [(i, i ^ step[i % 2]) for i in range(owners)])  7.38 us
    ppermute x6, waiting for transfers between devices, exchange(): lax.ppermute(value, 'row', [(i, i ^ step[i % 2]) for i in range(owners)])  5.93 us
    pallas_call x2, Pallas kernels, project(): pl.pallas_call(functools.partial(project_kernel, start, len(extra)), out_...  3.1 us
    pallas_call x1, Pallas kernels, merge_tiles(): pl.pallas_call(functools.partial(merge_kernel, own_tiles, labels.shape[1]...  2.76 us
    ppermute x9, waiting for transfers between devices, swap(): return lax.ppermute(value, axis, pairs)  2.62 us
    pallas_call x2, Pallas kernels, product(): pl.pallas_call(functools.partial(product_kernel, first), out_shape=jax.Sh...  1.42 us
    pallas_call x1, Pallas kernels, early_product(): pl.pallas_call(early_kernel, out_shape=jax.ShapeDtypeStruct((total, width...  1 us
  transfers between devices with their start and end apart: 15, of which 8 were waited for; matrix products, arithmetic and copies ran while one was open for 0% of the time, Pallas kernels for 21%

profile of v20, /device:TPU:0, one launch (start us, length us, event | category | flops | bytes accessed | tf_op | source)
XLA Modules:
  0.0 37.8 jit_solution(5302341073333701770)
XLA Ops:
  0.0 1.5 %shard_map.91 = (f32[256,256]{1,0:T(8,128)S(1)}, bf16[256,256]{1,0:T(8,128)(2,1)S(1)}) custom-call(bf16[256,1024]{1,0:T(8,128)(2,1)} %features_hbm.3, bf16[1024,512]{1,0:T(8,128)(2,1)} %weight_hbm.3, f32[2,128]{1,0:T(2,128)} %bitcast.6), custom_call_target="tpu_custom_call" | custom-call | flops 134217728 | bytes 1048576 | tf_op jit(solution)/shard_map/pallas_call | solution.py:67
  1.5 5.1 %collective-permute-start = (bf16[256,256]{1,0:T(8,128)(2,1)S(1)}, bf16[256,256]{1,0:T(8,128)(2,1)S(1)}, u32[]{:S(2)}, u32[]{:S(2)}) collective-permute-start(bf16[256,256]{1,0:T(8,128)(2,1)S(1)} %get-tuple-element.28.own), channel_id=1, source_target_pairs={{0,3},{1,2},{2,1},{3,0},{4,7},{5,6},{6,5},{7,4},{8,11},{9,10},{10,... | collective-permute-start | bytes 393224 | tf_op jit(solution)/shard_map/ppermute | solution.py:362
  6.7 1.6 %shard_map.92 = (f32[256,256]{1,0:T(8,128)S(1)}, bf16[256,256]{1,0:T(8,128)(2,1)S(1)}, s32[1,64]{1,0:T(1,128)S(1)}, s32[1,64]{1,0:T(1,128)S(1)}, s32[1,16]{1,0:T(1,128)S(1)}) custom-call(bf16[256,1024]{1,0:T(8,128)(2,1)} %features_hbm.3, bf16[1024,512]{1,0:T(8,128)(2,1)} %weight_hbm.3, f32[2,128]{1,0:T(2,128)} %bitcast.7, s32[1,64]{1,0:T(1,128)} %refs_0_.1, ...), custom_call_target="tpu_custom_call" | custom-call | flops 134217728 | bytes 1048576 | tf_op jit(solution)/shard_map/pallas_call | solution.py:67
  8.2 1.0 %collective-permute-start.9 = (bf16[256,256]{1,0:T(8,128)(2,1)S(1)}, bf16[256,256]{1,0:T(8,128)(2,1)S(1)}, u32[]{:S(2)}, u32[]{:S(2)}) collective-permute-start(bf16[256,256]{1,0:T(8,128)(2,1)S(1)} %get-tuple-element.41.refs_0_), channel_id=1, source_target_pairs={{0,3},{1,2},{2,1},{3,0},{4,7},{5,6},{6,5},{7,4},{8,11},{9,10},{10,... | collective-permute-start | bytes 393224 | tf_op jit(solution)/shard_map/ppermute | solution.py:362
  9.8 2.8 %shard_map.93.matrix = bf16[2048,1024]{1,0:T(8,128)(2,1)S(1)} custom-call(s32[1]{0:T(128)} %bitcast.2.row, s32[1]{0:T(128)} %bitcast.3.column, s32[1]{0:T(128)S(6)} %copy.10.count, s32[1,64]{1,0:T(1,128)S(1)} %get-tuple-element.29.sources_in, s32[1,64]{1,0:T(1,128)S(1)} %get-tuple-element.30.targets_in, s32[1,16]{1,0:T(1,128)S(1)} %get-tuple-element.31.labels_in, ...), custom_call_target="tpu_custom_call" | custom-call | flops 8388608 | bytes 12582912 | tf_op jit(solution)/shard_map/pallas_call | solution.py:156
  12.6 1.2 %collective-permute-start.2 = (bf16[256,256]{1,0:T(8,128)(2,1)S(1)}, bf16[256,256]{1,0:T(8,128)(2,1)S(1)}, u32[]{:S(2)}, u32[]{:S(2)}) collective-permute-start(bf16[256,256]{1,0:T(8,128)(2,1)S(1)} %collective-permute-done.across), channel_id=1, source_target_pairs={{0,1},{1,0},{2,3},{3,2},{4,5},{5,4},{6,7},{7,6},{8,9},{9,8},{10,11... | collective-permute-start | bytes 393224 | tf_op jit(solution)/shard_map/ppermute | solution.py:362
  13.8 0.9 %collective-permute-start.8 = (bf16[256,256]{1,0:T(8,128)(2,1)S(1)}, bf16[256,256]{1,0:T(8,128)(2,1)S(1)}, u32[]{:S(2)}, u32[]{:S(2)}) collective-permute-start(bf16[256,256]{1,0:T(8,128)(2,1)S(1)} %get-tuple-element.41.refs_0_), channel_id=1, source_target_pairs={{0,1},{1,0},{2,3},{3,2},{4,5},{5,4},{6,7},{7,6},{8,9},{9,8},{10,11... | collective-permute-start | bytes 393224 | tf_op jit(solution)/shard_map/ppermute | solution.py:362
  14.7 1.0 %shard_map.94.early = f32[2048,256]{1,0:T(8,128)S(1)} custom-call(bf16[2048,1024]{1,0:T(8,128)(2,1)S(1)} %shard_map.93.matrix, bf16[256,256]{1,0:T(8,128)(2,1)S(1)} %get-tuple-element.28.own, bf16[256,256]{1,0:T(8,128)(2,1)S(1)} %collective-permute-done.1.beside, bf16[256,256]{1,0:T(8,128)(2,1)S(1)} %collective-permute-done.across), custom_call_target="tpu_custom_call" | custom-call | flops 536870912 | bytes 1 | tf_op jit(solution)/shard_map/pallas_call | solution.py:190
  15.7 0.5 %collective-permute-done.9.refs_3_ = bf16[256,256]{1,0:T(8,128)(2,1)S(1)} collective-permute-done((bf16[256,256]{1,0:T(8,128)(2,1)S(1)}, bf16[256,256]{1,0:T(8,128)(2,1)S(1)}, u32[]{:S(2)}, u32[]{:S(2)}) %collective-permute-start.9) | collective-permute-done | bytes 131104 | tf_op jit(solution)/shard_map/ppermute | solution.py:362
  16.2 2.1 %collective-permute-start.10 = (bf16[256,256]{1,0:T(8,128)(2,1)S(1)}, bf16[256,256]{1,0:T(8,128)(2,1)S(1)}, u32[]{:S(2)}, u32[]{:S(2)}) collective-permute-start(bf16[256,256]{1,0:T(8,128)(2,1)S(1)} %collective-permute-done.9.refs_3_), channel_id=1, source_target_pairs={{0,1},{1,0},{2,3},{3,2},{4,5},{5,4},{6,7},{7,6},{8,9},{9,8},{10,11... | collective-permute-start | bytes 393224 | tf_op jit(solution)/shard_map/ppermute | solution.py:362
  18.3 0.8 %collective-permute-done.2.passed = bf16[256,256]{1,0:T(8,128)(2,1)S(1)} collective-permute-done((bf16[256,256]{1,0:T(8,128)(2,1)S(1)}, bf16[256,256]{1,0:T(8,128)(2,1)S(1)}, u32[]{:S(2)}, u32[]{:S(2)}) %collective-permute-start.2) | collective-permute-done | bytes 131104 | tf_op jit(solution)/shard_map/ppermute | solution.py:362
  19.1 0.2 shard_map.96
  19.3 0.3 shard_map.97
  19.6 0.6 %collective-permute-start.3 = (bf16[768,256]{1,0:T(8,128)(2,1)S(1)}, bf16[768,256]{1,0:T(8,128)(2,1)S(1)}, u32[]{:S(2)}, u32[]{:S(2)}) collective-permute-start(bf16[768,256]{1,0:T(8,128)(2,1)S(1)} %shard_map.97), channel_id=1, source_target_pairs={{0,4},{4,0},{8,12},{12,8},{16,20},{20,16},{24,28},{28,24},{1,5},{5... | collective-permute-start | bytes 1179656 | tf_op jit(solution)/shard_map/ppermute | solution.py:362
  20.2 0.3 shard_map.95.stay
  20.5 0.2 collective-permute-done.4.came
  20.7 1.6 %collective-permute-start.5 = (bf16[256,256]{1,0:T(8,128)(2,1)S(1)}, bf16[256,256]{1,0:T(8,128)(2,1)S(1)}, u32[]{:S(2)}, u32[]{:S(2)}) collective-permute-start(bf16[256,256]{1,0:T(8,128)(2,1)S(1)} %shard_map.99), channel_id=1, source_target_pairs={{0,8},{4,20},{8,0},{12,28},{16,24},{20,4},{24,16},{28,12},{1,9},{5... | collective-permute-start | bytes 393224 | tf_op jit(solution)/shard_map/ppermute | solution.py:369
  22.3 1.6 %collective-permute-start.6 = (bf16[256,256]{1,0:T(8,128)(2,1)S(1)}, bf16[256,256]{1,0:T(8,128)(2,1)S(1)}, u32[]{:S(2)}, u32[]{:S(2)}) collective-permute-start(bf16[256,256]{1,0:T(8,128)(2,1)S(1)} %get-tuple-element.36), channel_id=1, source_target_pairs={{0,16},{4,12},{8,24},{12,4},{16,0},{20,28},{24,8},{28,20},{1,17},{... | collective-permute-start | bytes 393224 | tf_op jit(solution)/shard_map/ppermute | solution.py:369
  23.9 0.7 %collective-permute-start.7 = (bf16[256,256]{1,0:T(8,128)(2,1)S(1)}, bf16[256,256]{1,0:T(8,128)(2,1)S(1)}, u32[]{:S(2)}, u32[]{:S(2)}) collective-permute-start(bf16[256,256]{1,0:T(8,128)(2,1)S(1)} %get-tuple-element.37), channel_id=1, source_target_pairs={{0,24},{4,28},{8,16},{12,20},{16,8},{20,12},{24,0},{28,4},{1,25},{... | collective-permute-start | bytes 393224 | tf_op jit(solution)/shard_map/ppermute | solution.py:369
  24.6 0.7 %shard_map.102 = bf16[1024,256]{1,0:T(8,128)(2,1)S(1)} custom-call(bf16[2048,1024]{1,0:T(8,128)(2,1)S(1)} %shard_map.93.matrix, bf16[256,256]{1,0:T(8,128)(2,1)S(1)} %get-tuple-element.41.refs_0_, bf16[256,256]{1,0:T(8,128)(2,1)S(1)} %collective-permute-done.8.refs_1_, bf16[256,256]{1,0:T(8,128)(2,1)S(1)} %collective-permute-done.10.refs_2_, ...), custom_call_target="tpu_custom_call" | custom-call | bytes 1 | tf_op jit(solution)/shard_map/pallas_call | solution.py:238
  25.4 0.7 %shard_map.101.stay = f32[1024,256]{1,0:T(8,128)S(1)} custom-call(bf16[2048,1024]{1,0:T(8,128)(2,1)S(1)} %shard_map.93.matrix, bf16[256,256]{1,0:T(8,128)(2,1)S(1)} %get-tuple-element.41.refs_0_, bf16[256,256]{1,0:T(8,128)(2,1)S(1)} %collective-permute-done.8.refs_1_, bf16[256,256]{1,0:T(8,128)(2,1)S(1)} %collective-permute-done.10.refs_2_, ...), custom_call_target="tpu_custom_call" | custom-call | flops 10737418240 | bytes 1 | tf_op jit(solution)/shard_map/pallas_call | solution.py:238
  26.1 1.2 %collective-permute-done.11.came = bf16[1024,256]{1,0:T(8,128)(2,1)S(1)} collective-permute-done((bf16[1024,256]{1,0:T(8,128)(2,1)S(1)}, bf16[1024,256]{1,0:T(8,128)(2,1)S(1)}, u32[]{:S(2)}, u32[]{:S(2)}) %collective-permute-start.11) | collective-permute-done | bytes 524320 | tf_op jit(solution)/shard_map/ppermute | solution.py:362
  27.3 0.1 shard_map.103
  27.4 1.3 %collective-permute-start.12 = (bf16[256,256]{1,0:T(8,128)(2,1)S(1)}, bf16[256,256]{1,0:T(8,128)(2,1)S(1)}, u32[]{:S(2)}, u32[]{:S(2)}) collective-permute-start(bf16[256,256]{1,0:T(8,128)(2,1)S(1)} %get-tuple-element.46), channel_id=1, source_target_pairs={{0,8},{4,20},{8,0},{12,28},{16,24},{20,4},{24,16},{28,12},{1,9},{5... | collective-permute-start | bytes 393224 | tf_op jit(solution)/shard_map/ppermute | solution.py:369
  28.7 1.5 %collective-permute-start.13 = (bf16[256,256]{1,0:T(8,128)(2,1)S(1)}, bf16[256,256]{1,0:T(8,128)(2,1)S(1)}, u32[]{:S(2)}, u32[]{:S(2)}) collective-permute-start(bf16[256,256]{1,0:T(8,128)(2,1)S(1)} %get-tuple-element.47), channel_id=1, source_target_pairs={{0,16},{4,12},{8,24},{12,4},{16,0},{20,28},{24,8},{28,20},{1,17},{... | collective-permute-start | bytes 393224 | tf_op jit(solution)/shard_map/ppermute | solution.py:369
  30.3 0.7 %collective-permute-start.14 = (bf16[256,256]{1,0:T(8,128)(2,1)S(1)}, bf16[256,256]{1,0:T(8,128)(2,1)S(1)}, u32[]{:S(2)}, u32[]{:S(2)}) collective-permute-start(bf16[256,256]{1,0:T(8,128)(2,1)S(1)} %get-tuple-element.48), channel_id=1, source_target_pairs={{0,24},{4,28},{8,16},{12,20},{16,8},{20,12},{24,0},{28,4},{1,25},{... | collective-permute-start | bytes 393224 | tf_op jit(solution)/shard_map/ppermute | solution.py:369
  31.0 0.1 collective-permute-done.7.refs_3_
  31.1 0.1 shard_map.100.ready
  31.2 2.4 %collective-permute-done.12.refs_1_ = bf16[256,256]{1,0:T(8,128)(2,1)S(1)} collective-permute-done((bf16[256,256]{1,0:T(8,128)(2,1)S(1)}, bf16[256,256]{1,0:T(8,128)(2,1)S(1)}, u32[]{:S(2)}, u32[]{:S(2)}) %collective-permute-start.12) | collective-permute-done | bytes 131104 | tf_op jit(solution)/shard_map/ppermute | solution.py:369
  33.5 0.4 %collective-permute-done.13.refs_2_ = bf16[256,256]{1,0:T(8,128)(2,1)S(1)} collective-permute-done((bf16[256,256]{1,0:T(8,128)(2,1)S(1)}, bf16[256,256]{1,0:T(8,128)(2,1)S(1)}, u32[]{:S(2)}, u32[]{:S(2)}) %collective-permute-start.13) | collective-permute-done | bytes 131104 | tf_op jit(solution)/shard_map/ppermute | solution.py:369
  33.9 3.1 %collective-permute-done.14.refs_3_ = bf16[256,256]{1,0:T(8,128)(2,1)S(1)} collective-permute-done((bf16[256,256]{1,0:T(8,128)(2,1)S(1)}, bf16[256,256]{1,0:T(8,128)(2,1)S(1)}, u32[]{:S(2)}, u32[]{:S(2)}) %collective-permute-start.14) | collective-permute-done | bytes 131104 | tf_op jit(solution)/shard_map/ppermute | solution.py:369
  37.0 0.8 %shard_map.104 = bf16[256,512]{1,0:T(8,128)(2,1)} custom-call(bf16[256,256]{1,0:T(8,128)(2,1)S(1)} %shard_map.100.ready, f32[256,256]{1,0:T(8,128)S(1)} %get-tuple-element.38.projected, f32[2,128]{1,0:T(2,128)S(1)} %bitcast.5, f32[256,256]{1,0:T(8,128)S(1)} %get-tuple-element.45.refs_0_, bf16[256,256]{1,0:T(8,128)(2,1)S(1)} %collective-permute-done.12.refs_1_, ...), custom_call_target="tpu_custom_call" | custom-call | flops 393216 | bytes 1048576 | tf_op jit(solution)/shard_map/pallas_call | solution.py:312
  (14 shorter events, 0.3 us)
Async XLA Ops:
  1.5 11.1 %collective-permute-start = (bf16[256,256]{1,0:T(8,128)(2,1)S(1)}, bf16[256,256]{1,0:T(8,128)(2,1)S(1)}, u32[]{:S(2)}, u32[]{:S(2)}) collective-permute-start(bf16[256,256]{1,0:T(8,128)(2,1)S(1)} %get-tuple-element.28.own), channel_id=1, source_target_pairs={{0,3},{1,2},{2,1},{3,0},{4,7},{5,6},{6,5},{7,4},{8,11},{9,10},{10,... | collective-permute-start | bytes 393224 | tf_op jit(solution)/shard_map/ppermute | solution.py:362
  6.7 8.1 %collective-permute-start.1 = (bf16[256,256]{1,0:T(8,128)(2,1)S(1)}, bf16[256,256]{1,0:T(8,128)(2,1)S(1)}, u32[]{:S(2)}, u32[]{:S(2)}) collective-permute-start(bf16[256,256]{1,0:T(8,128)(2,1)S(1)} %get-tuple-element.28.own), channel_id=1, source_target_pairs={{0,1},{1,0},{2,3},{3,2},{4,5},{5,4},{6,7},{7,6},{8,9},{9,8},{10,11... | collective-permute-start | bytes 393224 | tf_op jit(solution)/shard_map/ppermute | solution.py:362
  8.2 7.9 %collective-permute-start.9 = (bf16[256,256]{1,0:T(8,128)(2,1)S(1)}, bf16[256,256]{1,0:T(8,128)(2,1)S(1)}, u32[]{:S(2)}, u32[]{:S(2)}) collective-permute-start(bf16[256,256]{1,0:T(8,128)(2,1)S(1)} %get-tuple-element.41.refs_0_), channel_id=1, source_target_pairs={{0,3},{1,2},{2,1},{3,0},{4,7},{5,6},{6,5},{7,4},{8,11},{9,10},{10,... | collective-permute-start | bytes 393224 | tf_op jit(solution)/shard_map/ppermute | solution.py:362
  12.6 6.4 %collective-permute-start.2 = (bf16[256,256]{1,0:T(8,128)(2,1)S(1)}, bf16[256,256]{1,0:T(8,128)(2,1)S(1)}, u32[]{:S(2)}, u32[]{:S(2)}) collective-permute-start(bf16[256,256]{1,0:T(8,128)(2,1)S(1)} %collective-permute-done.across), channel_id=1, source_target_pairs={{0,1},{1,0},{2,3},{3,2},{4,5},{5,4},{6,7},{7,6},{8,9},{9,8},{10,11... | collective-permute-start | bytes 393224 | tf_op jit(solution)/shard_map/ppermute | solution.py:362
  13.8 10.8 %collective-permute-start.8 = (bf16[256,256]{1,0:T(8,128)(2,1)S(1)}, bf16[256,256]{1,0:T(8,128)(2,1)S(1)}, u32[]{:S(2)}, u32[]{:S(2)}) collective-permute-start(bf16[256,256]{1,0:T(8,128)(2,1)S(1)} %get-tuple-element.41.refs_0_), channel_id=1, source_target_pairs={{0,1},{1,0},{2,3},{3,2},{4,5},{5,4},{6,7},{7,6},{8,9},{9,8},{10,11... | collective-permute-start | bytes 393224 | tf_op jit(solution)/shard_map/ppermute | solution.py:362
  16.2 8.4 %collective-permute-start.10 = (bf16[256,256]{1,0:T(8,128)(2,1)S(1)}, bf16[256,256]{1,0:T(8,128)(2,1)S(1)}, u32[]{:S(2)}, u32[]{:S(2)}) collective-permute-start(bf16[256,256]{1,0:T(8,128)(2,1)S(1)} %collective-permute-done.9.refs_3_), channel_id=1, source_target_pairs={{0,1},{1,0},{2,3},{3,2},{4,5},{5,4},{6,7},{7,6},{8,9},{9,8},{10,11... | collective-permute-start | bytes 393224 | tf_op jit(solution)/shard_map/ppermute | solution.py:362
  19.3 1.4 %collective-permute-start.4 = (bf16[256,256]{1,0:T(8,128)(2,1)S(1)}, bf16[256,256]{1,0:T(8,128)(2,1)S(1)}, u32[]{:S(2)}, u32[]{:S(2)}) collective-permute-start(bf16[256,256]{1,0:T(8,128)(2,1)S(1)} %shard_map.96), channel_id=1, source_target_pairs={{0,4},{4,0},{8,12},{12,8},{16,20},{20,16},{24,28},{28,24},{1,5},{5... | collective-permute-start | bytes 393224 | tf_op jit(solution)/shard_map/ppermute | solution.py:362
  19.6 2.7 %collective-permute-start.3 = (bf16[768,256]{1,0:T(8,128)(2,1)S(1)}, bf16[768,256]{1,0:T(8,128)(2,1)S(1)}, u32[]{:S(2)}, u32[]{:S(2)}) collective-permute-start(bf16[768,256]{1,0:T(8,128)(2,1)S(1)} %shard_map.97), channel_id=1, source_target_pairs={{0,4},{4,0},{8,12},{12,8},{16,20},{20,16},{24,28},{28,24},{1,5},{5... | collective-permute-start | bytes 1179656 | tf_op jit(solution)/shard_map/ppermute | solution.py:362
  20.7 9.6 %collective-permute-start.5 = (bf16[256,256]{1,0:T(8,128)(2,1)S(1)}, bf16[256,256]{1,0:T(8,128)(2,1)S(1)}, u32[]{:S(2)}, u32[]{:S(2)}) collective-permute-start(bf16[256,256]{1,0:T(8,128)(2,1)S(1)} %shard_map.99), channel_id=1, source_target_pairs={{0,8},{4,20},{8,0},{12,28},{16,24},{20,4},{24,16},{28,12},{1,9},{5... | collective-permute-start | bytes 393224 | tf_op jit(solution)/shard_map/ppermute | solution.py:369
  22.3 8.6 %collective-permute-start.6 = (bf16[256,256]{1,0:T(8,128)(2,1)S(1)}, bf16[256,256]{1,0:T(8,128)(2,1)S(1)}, u32[]{:S(2)}, u32[]{:S(2)}) collective-permute-start(bf16[256,256]{1,0:T(8,128)(2,1)S(1)} %get-tuple-element.36), channel_id=1, source_target_pairs={{0,16},{4,12},{8,24},{12,4},{16,0},{20,28},{24,8},{28,20},{1,17},{... | collective-permute-start | bytes 393224 | tf_op jit(solution)/shard_map/ppermute | solution.py:369
  23.9 7.1 %collective-permute-start.7 = (bf16[256,256]{1,0:T(8,128)(2,1)S(1)}, bf16[256,256]{1,0:T(8,128)(2,1)S(1)}, u32[]{:S(2)}, u32[]{:S(2)}) collective-permute-start(bf16[256,256]{1,0:T(8,128)(2,1)S(1)} %get-tuple-element.37), channel_id=1, source_target_pairs={{0,24},{4,28},{8,16},{12,20},{16,8},{20,12},{24,0},{28,4},{1,25},{... | collective-permute-start | bytes 393224 | tf_op jit(solution)/shard_map/ppermute | solution.py:369
  25.3 5.7 %copy-start = (f32[256]{0:T(256)S(1)}, f32[256]{0:T(256)}, u32[]{:S(2)}) copy-start(f32[256]{0:T(256)} %param.12) | copy-start | bytes 3076
  25.3 2.0 %collective-permute-start.11 = (bf16[1024,256]{1,0:T(8,128)(2,1)S(1)}, bf16[1024,256]{1,0:T(8,128)(2,1)S(1)}, u32[]{:S(2)}, u32[]{:S(2)}) collective-permute-start(bf16[1024,256]{1,0:T(8,128)(2,1)S(1)} %shard_map.102), channel_id=1, source_target_pairs={{0,4},{4,0},{8,12},{12,8},{16,20},{20,16},{24,28},{28,24},{1,5},{5... | collective-permute-start | bytes 1572872 | tf_op jit(solution)/shard_map/ppermute | solution.py:362
  27.4 6.1 %collective-permute-start.12 = (bf16[256,256]{1,0:T(8,128)(2,1)S(1)}, bf16[256,256]{1,0:T(8,128)(2,1)S(1)}, u32[]{:S(2)}, u32[]{:S(2)}) collective-permute-start(bf16[256,256]{1,0:T(8,128)(2,1)S(1)} %get-tuple-element.46), channel_id=1, source_target_pairs={{0,8},{4,20},{8,0},{12,28},{16,24},{20,4},{24,16},{28,12},{1,9},{5... | collective-permute-start | bytes 393224 | tf_op jit(solution)/shard_map/ppermute | solution.py:369
  28.7 5.2 %collective-permute-start.13 = (bf16[256,256]{1,0:T(8,128)(2,1)S(1)}, bf16[256,256]{1,0:T(8,128)(2,1)S(1)}, u32[]{:S(2)}, u32[]{:S(2)}) collective-permute-start(bf16[256,256]{1,0:T(8,128)(2,1)S(1)} %get-tuple-element.47), channel_id=1, source_target_pairs={{0,16},{4,12},{8,24},{12,4},{16,0},{20,28},{24,8},{28,20},{1,17},{... | collective-permute-start | bytes 393224 | tf_op jit(solution)/shard_map/ppermute | solution.py:369
  30.3 6.7 %collective-permute-start.14 = (bf16[256,256]{1,0:T(8,128)(2,1)S(1)}, bf16[256,256]{1,0:T(8,128)(2,1)S(1)}, u32[]{:S(2)}, u32[]{:S(2)}) collective-permute-start(bf16[256,256]{1,0:T(8,128)(2,1)S(1)} %get-tuple-element.48), channel_id=1, source_target_pairs={{0,24},{4,28},{8,16},{12,20},{16,8},{20,12},{24,0},{28,4},{1,25},{... | collective-permute-start | bytes 393224 | tf_op jit(solution)/shard_map/ppermute | solution.py:369

commit v21 on v20

--- a/solution.py
+++ b/solution.py
@@ -136,7 +136,7 @@
 
     for k, copy in enumerate(large):
         copy.wait()
-        pl.loop(k * each, (k + 1) * each, unroll=4)(add)
+        pl.loop(k * each, (k + 1) * each, unroll=min(each, 16))(add)
 
     for place in range(places):
         for source in range(span):

time: 38 us -> 37.9 us (level)
  transfers between devices with their start and end apart: 15 -> 15, of which waited for: 8 -> 7; matrix products, arithmetic and copies ran while one was open for 0% -> 0% of each run, Pallas kernels for 21% -> 20%
where the time goes in v21:
time: 37.9 us; the launch traced here: 37.7 us
  starting transfers between devices  18.4 us (49%)
  Pallas kernels  10 us (26%)
  waiting for transfers between devices  8.54 us (23%)
  between operations  0.78 us (2%)
    ppermute x9, starting transfers between devices, swap(): return lax.ppermute(value, axis, pairs)  11 us
    ppermute x6, starting transfers between devices, exchange(): lax.ppermute(value, 'row', [(i, i ^ step[i % 2]) for i in range(owners)])  7.39 us
    ppermute x6, waiting for transfers between devices, exchange(): lax.ppermute(value, 'row', [(i, i ^ step[i % 2]) for i in range(owners)])  5.93 us
    pallas_call x2, Pallas kernels, project(): pl.pallas_call(functools.partial(project_kernel, start, len(extra)), out_...  3.1 us
    pallas_call x1, Pallas kernels, merge_tiles(): pl.pallas_call(functools.partial(merge_kernel, own_tiles, labels.shape[1]...  2.73 us
    ppermute x9, waiting for transfers between devices, swap(): return lax.ppermute(value, axis, pairs)  2.62 us
    pallas_call x2, Pallas kernels, product(): pl.pallas_call(functools.partial(product_kernel, first), out_shape=jax.Sh...  1.41 us
    pallas_call x1, Pallas kernels, early_product(): pl.pallas_call(early_kernel, out_shape=jax.ShapeDtypeStruct((total, width...  1 us
  transfers between devices with their start and end apart: 15, of which 7 were waited for; matrix products, arithmetic and copies ran while one was open for 0% of the time, Pallas kernels for 20%

profile of v21, /device:TPU:0, one launch (start us, length us, event | category | flops | bytes accessed | tf_op | source)
XLA Modules:
  0.0 37.7 jit_solution(8577134607825441695)
XLA Ops:
  0.0 1.5 %shard_map.91 = (f32[256,256]{1,0:T(8,128)S(1)}, bf16[256,256]{1,0:T(8,128)(2,1)S(1)}) custom-call(bf16[256,1024]{1,0:T(8,128)(2,1)} %features_hbm.3, bf16[1024,512]{1,0:T(8,128)(2,1)} %weight_hbm.3, f32[2,128]{1,0:T(2,128)} %bitcast.6), custom_call_target="tpu_custom_call" | custom-call | flops 134217728 | bytes 1048576 | tf_op jit(solution)/shard_map/pallas_call | solution.py:67
  1.5 5.1 %collective-permute-start = (bf16[256,256]{1,0:T(8,128)(2,1)S(1)}, bf16[256,256]{1,0:T(8,128)(2,1)S(1)}, u32[]{:S(2)}, u32[]{:S(2)}) collective-permute-start(bf16[256,256]{1,0:T(8,128)(2,1)S(1)} %get-tuple-element.28.own), channel_id=1, source_target_pairs={{0,3},{1,2},{2,1},{3,0},{4,7},{5,6},{6,5},{7,4},{8,11},{9,10},{10,... | collective-permute-start | bytes 393224 | tf_op jit(solution)/shard_map/ppermute | solution.py:362
  6.7 1.6 %shard_map.92 = (f32[256,256]{1,0:T(8,128)S(1)}, bf16[256,256]{1,0:T(8,128)(2,1)S(1)}, s32[1,64]{1,0:T(1,128)S(1)}, s32[1,64]{1,0:T(1,128)S(1)}, s32[1,16]{1,0:T(1,128)S(1)}) custom-call(bf16[256,1024]{1,0:T(8,128)(2,1)} %features_hbm.3, bf16[1024,512]{1,0:T(8,128)(2,1)} %weight_hbm.3, f32[2,128]{1,0:T(2,128)} %bitcast.7, s32[1,64]{1,0:T(1,128)} %refs_0_.1, ...), custom_call_target="tpu_custom_call" | custom-call | flops 134217728 | bytes 1048576 | tf_op jit(solution)/shard_map/pallas_call | solution.py:67
  8.2 1.0 %collective-permute-start.9 = (bf16[256,256]{1,0:T(8,128)(2,1)S(1)}, bf16[256,256]{1,0:T(8,128)(2,1)S(1)}, u32[]{:S(2)}, u32[]{:S(2)}) collective-permute-start(bf16[256,256]{1,0:T(8,128)(2,1)S(1)} %get-tuple-element.41.refs_0_), channel_id=1, source_target_pairs={{0,3},{1,2},{2,1},{3,0},{4,7},{5,6},{6,5},{7,4},{8,11},{9,10},{10,... | collective-permute-start | bytes 393224 | tf_op jit(solution)/shard_map/ppermute | solution.py:362
  9.8 2.7 %shard_map.93.matrix = bf16[2048,1024]{1,0:T(8,128)(2,1)S(1)} custom-call(s32[1]{0:T(128)} %bitcast.2.row, s32[1]{0:T(128)} %bitcast.3.column, s32[1]{0:T(128)S(6)} %copy.10.count, s32[1,64]{1,0:T(1,128)S(1)} %get-tuple-element.29.sources_in, s32[1,64]{1,0:T(1,128)S(1)} %get-tuple-element.30.targets_in, s32[1,16]{1,0:T(1,128)S(1)} %get-tuple-element.31.labels_in, ...), custom_call_target="tpu_custom_call" | custom-call | flops 8388608 | bytes 12582912 | tf_op jit(solution)/shard_map/pallas_call | solution.py:156
  12.6 1.2 %collective-permute-start.2 = (bf16[256,256]{1,0:T(8,128)(2,1)S(1)}, bf16[256,256]{1,0:T(8,128)(2,1)S(1)}, u32[]{:S(2)}, u32[]{:S(2)}) collective-permute-start(bf16[256,256]{1,0:T(8,128)(2,1)S(1)} %collective-permute-done.across), channel_id=1, source_target_pairs={{0,1},{1,0},{2,3},{3,2},{4,5},{5,4},{6,7},{7,6},{8,9},{9,8},{10,11... | collective-permute-start | bytes 393224 | tf_op jit(solution)/shard_map/ppermute | solution.py:362
  13.8 0.9 %collective-permute-start.8 = (bf16[256,256]{1,0:T(8,128)(2,1)S(1)}, bf16[256,256]{1,0:T(8,128)(2,1)S(1)}, u32[]{:S(2)}, u32[]{:S(2)}) collective-permute-start(bf16[256,256]{1,0:T(8,128)(2,1)S(1)} %get-tuple-element.41.refs_0_), channel_id=1, source_target_pairs={{0,1},{1,0},{2,3},{3,2},{4,5},{5,4},{6,7},{7,6},{8,9},{9,8},{10,11... | collective-permute-start | bytes 393224 | tf_op jit(solution)/shard_map/ppermute | solution.py:362
  14.7 1.0 %shard_map.94.early = f32[2048,256]{1,0:T(8,128)S(1)} custom-call(bf16[2048,1024]{1,0:T(8,128)(2,1)S(1)} %shard_map.93.matrix, bf16[256,256]{1,0:T(8,128)(2,1)S(1)} %get-tuple-element.28.own, bf16[256,256]{1,0:T(8,128)(2,1)S(1)} %collective-permute-done.1.beside, bf16[256,256]{1,0:T(8,128)(2,1)S(1)} %collective-permute-done.across), custom_call_target="tpu_custom_call" | custom-call | flops 536870912 | bytes 1 | tf_op jit(solution)/shard_map/pallas_call | solution.py:190
  15.7 0.5 %collective-permute-done.9.refs_3_ = bf16[256,256]{1,0:T(8,128)(2,1)S(1)} collective-permute-done((bf16[256,256]{1,0:T(8,128)(2,1)S(1)}, bf16[256,256]{1,0:T(8,128)(2,1)S(1)}, u32[]{:S(2)}, u32[]{:S(2)}) %collective-permute-start.9) | collective-permute-done | bytes 131104 | tf_op jit(solution)/shard_map/ppermute | solution.py:362
  16.2 2.1 %collective-permute-start.10 = (bf16[256,256]{1,0:T(8,128)(2,1)S(1)}, bf16[256,256]{1,0:T(8,128)(2,1)S(1)}, u32[]{:S(2)}, u32[]{:S(2)}) collective-permute-start(bf16[256,256]{1,0:T(8,128)(2,1)S(1)} %collective-permute-done.9.refs_3_), channel_id=1, source_target_pairs={{0,1},{1,0},{2,3},{3,2},{4,5},{5,4},{6,7},{7,6},{8,9},{9,8},{10,11... | collective-permute-start | bytes 393224 | tf_op jit(solution)/shard_map/ppermute | solution.py:362
  18.3 0.7 %collective-permute-done.2.passed = bf16[256,256]{1,0:T(8,128)(2,1)S(1)} collective-permute-done((bf16[256,256]{1,0:T(8,128)(2,1)S(1)}, bf16[256,256]{1,0:T(8,128)(2,1)S(1)}, u32[]{:S(2)}, u32[]{:S(2)}) %collective-permute-start.2) | collective-permute-done | bytes 131104 | tf_op jit(solution)/shard_map/ppermute | solution.py:362
  19.0 0.2 shard_map.96
  19.2 0.1 collective-permute-start.4
  19.3 0.3 shard_map.97
  19.6 0.6 %collective-permute-start.3 = (bf16[768,256]{1,0:T(8,128)(2,1)S(1)}, bf16[768,256]{1,0:T(8,128)(2,1)S(1)}, u32[]{:S(2)}, u32[]{:S(2)}) collective-permute-start(bf16[768,256]{1,0:T(8,128)(2,1)S(1)} %shard_map.97), channel_id=1, source_target_pairs={{0,4},{4,0},{8,12},{12,8},{16,20},{20,16},{24,28},{28,24},{1,5},{5... | collective-permute-start | bytes 1179656 | tf_op jit(solution)/shard_map/ppermute | solution.py:362
  20.1 0.3 shard_map.95.stay
  20.4 0.2 collective-permute-done.4.came
  20.7 1.6 %collective-permute-start.5 = (bf16[256,256]{1,0:T(8,128)(2,1)S(1)}, bf16[256,256]{1,0:T(8,128)(2,1)S(1)}, u32[]{:S(2)}, u32[]{:S(2)}) collective-permute-start(bf16[256,256]{1,0:T(8,128)(2,1)S(1)} %shard_map.99), channel_id=1, source_target_pairs={{0,8},{4,20},{8,0},{12,28},{16,24},{20,4},{24,16},{28,12},{1,9},{5... | collective-permute-start | bytes 393224 | tf_op jit(solution)/shard_map/ppermute | solution.py:369
  22.3 1.6 %collective-permute-start.6 = (bf16[256,256]{1,0:T(8,128)(2,1)S(1)}, bf16[256,256]{1,0:T(8,128)(2,1)S(1)}, u32[]{:S(2)}, u32[]{:S(2)}) collective-permute-start(bf16[256,256]{1,0:T(8,128)(2,1)S(1)} %get-tuple-element.36), channel_id=1, source_target_pairs={{0,16},{4,12},{8,24},{12,4},{16,0},{20,28},{24,8},{28,20},{1,17},{... | collective-permute-start | bytes 393224 | tf_op jit(solution)/shard_map/ppermute | solution.py:369
  23.9 0.7 %collective-permute-start.7 = (bf16[256,256]{1,0:T(8,128)(2,1)S(1)}, bf16[256,256]{1,0:T(8,128)(2,1)S(1)}, u32[]{:S(2)}, u32[]{:S(2)}) collective-permute-start(bf16[256,256]{1,0:T(8,128)(2,1)S(1)} %get-tuple-element.37), channel_id=1, source_target_pairs={{0,24},{4,28},{8,16},{12,20},{16,8},{20,12},{24,0},{28,4},{1,25},{... | collective-permute-start | bytes 393224 | tf_op jit(solution)/shard_map/ppermute | solution.py:369
  24.6 0.7 %shard_map.102 = bf16[1024,256]{1,0:T(8,128)(2,1)S(1)} custom-call(bf16[2048,1024]{1,0:T(8,128)(2,1)S(1)} %shard_map.93.matrix, bf16[256,256]{1,0:T(8,128)(2,1)S(1)} %get-tuple-element.41.refs_0_, bf16[256,256]{1,0:T(8,128)(2,1)S(1)} %collective-permute-done.8.refs_1_, bf16[256,256]{1,0:T(8,128)(2,1)S(1)} %collective-permute-done.10.refs_2_, ...), custom_call_target="tpu_custom_call" | custom-call | bytes 1 | tf_op jit(solution)/shard_map/pallas_call | solution.py:238
  25.4 0.7 %shard_map.101.stay = f32[1024,256]{1,0:T(8,128)S(1)} custom-call(bf16[2048,1024]{1,0:T(8,128)(2,1)S(1)} %shard_map.93.matrix, bf16[256,256]{1,0:T(8,128)(2,1)S(1)} %get-tuple-element.41.refs_0_, bf16[256,256]{1,0:T(8,128)(2,1)S(1)} %collective-permute-done.8.refs_1_, bf16[256,256]{1,0:T(8,128)(2,1)S(1)} %collective-permute-done.10.refs_2_, ...), custom_call_target="tpu_custom_call" | custom-call | flops 10737418240 | bytes 1 | tf_op jit(solution)/shard_map/pallas_call | solution.py:238
  26.1 1.2 %collective-permute-done.11.came = bf16[1024,256]{1,0:T(8,128)(2,1)S(1)} collective-permute-done((bf16[1024,256]{1,0:T(8,128)(2,1)S(1)}, bf16[1024,256]{1,0:T(8,128)(2,1)S(1)}, u32[]{:S(2)}, u32[]{:S(2)}) %collective-permute-start.11) | collective-permute-done | bytes 524320 | tf_op jit(solution)/shard_map/ppermute | solution.py:362
  27.3 0.1 shard_map.103
  27.4 1.3 %collective-permute-start.12 = (bf16[256,256]{1,0:T(8,128)(2,1)S(1)}, bf16[256,256]{1,0:T(8,128)(2,1)S(1)}, u32[]{:S(2)}, u32[]{:S(2)}) collective-permute-start(bf16[256,256]{1,0:T(8,128)(2,1)S(1)} %get-tuple-element.46), channel_id=1, source_target_pairs={{0,8},{4,20},{8,0},{12,28},{16,24},{20,4},{24,16},{28,12},{1,9},{5... | collective-permute-start | bytes 393224 | tf_op jit(solution)/shard_map/ppermute | solution.py:369
  28.7 1.5 %collective-permute-start.13 = (bf16[256,256]{1,0:T(8,128)(2,1)S(1)}, bf16[256,256]{1,0:T(8,128)(2,1)S(1)}, u32[]{:S(2)}, u32[]{:S(2)}) collective-permute-start(bf16[256,256]{1,0:T(8,128)(2,1)S(1)} %get-tuple-element.47), channel_id=1, source_target_pairs={{0,16},{4,12},{8,24},{12,4},{16,0},{20,28},{24,8},{28,20},{1,17},{... | collective-permute-start | bytes 393224 | tf_op jit(solution)/shard_map/ppermute | solution.py:369
  30.3 0.7 %collective-permute-start.14 = (bf16[256,256]{1,0:T(8,128)(2,1)S(1)}, bf16[256,256]{1,0:T(8,128)(2,1)S(1)}, u32[]{:S(2)}, u32[]{:S(2)}) collective-permute-start(bf16[256,256]{1,0:T(8,128)(2,1)S(1)} %get-tuple-element.48), channel_id=1, source_target_pairs={{0,24},{4,28},{8,16},{12,20},{16,8},{20,12},{24,0},{28,4},{1,25},{... | collective-permute-start | bytes 393224 | tf_op jit(solution)/shard_map/ppermute | solution.py:369
  30.9 0.1 shard_map.100.ready
  31.0 2.4 %collective-permute-done.12.refs_1_ = bf16[256,256]{1,0:T(8,128)(2,1)S(1)} collective-permute-done((bf16[256,256]{1,0:T(8,128)(2,1)S(1)}, bf16[256,256]{1,0:T(8,128)(2,1)S(1)}, u32[]{:S(2)}, u32[]{:S(2)}) %collective-permute-start.12) | collective-permute-done | bytes 131104 | tf_op jit(solution)/shard_map/ppermute | solution.py:369
  33.5 0.3 collective-permute-done.13.refs_2_
  33.8 3.2 %collective-permute-done.14.refs_3_ = bf16[256,256]{1,0:T(8,128)(2,1)S(1)} collective-permute-done((bf16[256,256]{1,0:T(8,128)(2,1)S(1)}, bf16[256,256]{1,0:T(8,128)(2,1)S(1)}, u32[]{:S(2)}, u32[]{:S(2)}) %collective-permute-start.14) | collective-permute-done | bytes 131104 | tf_op jit(solution)/shard_map/ppermute | solution.py:369
  37.0 0.8 %shard_map.104 = bf16[256,512]{1,0:T(8,128)(2,1)} custom-call(bf16[256,256]{1,0:T(8,128)(2,1)S(1)} %shard_map.100.ready, f32[256,256]{1,0:T(8,128)S(1)} %get-tuple-element.38.projected, f32[2,128]{1,0:T(2,128)S(1)} %bitcast.5, f32[256,256]{1,0:T(8,128)S(1)} %get-tuple-element.45.refs_0_, bf16[256,256]{1,0:T(8,128)(2,1)S(1)} %collective-permute-done.12.refs_1_, ...), custom_call_target="tpu_custom_call" | custom-call | flops 393216 | bytes 1048576 | tf_op jit(solution)/shard_map/pallas_call | solution.py:312
  (14 shorter events, 0.2 us)
Async XLA Ops:
  1.5 11.0 %collective-permute-start = (bf16[256,256]{1,0:T(8,128)(2,1)S(1)}, bf16[256,256]{1,0:T(8,128)(2,1)S(1)}, u32[]{:S(2)}, u32[]{:S(2)}) collective-permute-start(bf16[256,256]{1,0:T(8,128)(2,1)S(1)} %get-tuple-element.28.own), channel_id=1, source_target_pairs={{0,3},{1,2},{2,1},{3,0},{4,7},{5,6},{6,5},{7,4},{8,11},{9,10},{10,... | collective-permute-start | bytes 393224 | tf_op jit(solution)/shard_map/ppermute | solution.py:362
  6.7 8.0 %collective-permute-start.1 = (bf16[256,256]{1,0:T(8,128)(2,1)S(1)}, bf16[256,256]{1,0:T(8,128)(2,1)S(1)}, u32[]{:S(2)}, u32[]{:S(2)}) collective-permute-start(bf16[256,256]{1,0:T(8,128)(2,1)S(1)} %get-tuple-element.28.own), channel_id=1, source_target_pairs={{0,1},{1,0},{2,3},{3,2},{4,5},{5,4},{6,7},{7,6},{8,9},{9,8},{10,11... | collective-permute-start | bytes 393224 | tf_op jit(solution)/shard_map/ppermute | solution.py:362
  8.2 7.9 %collective-permute-start.9 = (bf16[256,256]{1,0:T(8,128)(2,1)S(1)}, bf16[256,256]{1,0:T(8,128)(2,1)S(1)}, u32[]{:S(2)}, u32[]{:S(2)}) collective-permute-start(bf16[256,256]{1,0:T(8,128)(2,1)S(1)} %get-tuple-element.41.refs_0_), channel_id=1, source_target_pairs={{0,3},{1,2},{2,1},{3,0},{4,7},{5,6},{6,5},{7,4},{8,11},{9,10},{10,... | collective-permute-start | bytes 393224 | tf_op jit(solution)/shard_map/ppermute | solution.py:362
  12.6 6.4 %collective-permute-start.2 = (bf16[256,256]{1,0:T(8,128)(2,1)S(1)}, bf16[256,256]{1,0:T(8,128)(2,1)S(1)}, u32[]{:S(2)}, u32[]{:S(2)}) collective-permute-start(bf16[256,256]{1,0:T(8,128)(2,1)S(1)} %collective-permute-done.across), channel_id=1, source_target_pairs={{0,1},{1,0},{2,3},{3,2},{4,5},{5,4},{6,7},{7,6},{8,9},{9,8},{10,11... | collective-permute-start | bytes 393224 | tf_op jit(solution)/shard_map/ppermute | solution.py:362
  13.8 10.8 %collective-permute-start.8 = (bf16[256,256]{1,0:T(8,128)(2,1)S(1)}, bf16[256,256]{1,0:T(8,128)(2,1)S(1)}, u32[]{:S(2)}, u32[]{:S(2)}) collective-permute-start(bf16[256,256]{1,0:T(8,128)(2,1)S(1)} %get-tuple-element.41.refs_0_), channel_id=1, source_target_pairs={{0,1},{1,0},{2,3},{3,2},{4,5},{5,4},{6,7},{7,6},{8,9},{9,8},{10,11... | collective-permute-start | bytes 393224 | tf_op jit(solution)/shard_map/ppermute | solution.py:362
  16.2 8.4 %collective-permute-start.10 = (bf16[256,256]{1,0:T(8,128)(2,1)S(1)}, bf16[256,256]{1,0:T(8,128)(2,1)S(1)}, u32[]{:S(2)}, u32[]{:S(2)}) collective-permute-start(bf16[256,256]{1,0:T(8,128)(2,1)S(1)} %collective-permute-done.9.refs_3_), channel_id=1, source_target_pairs={{0,1},{1,0},{2,3},{3,2},{4,5},{5,4},{6,7},{7,6},{8,9},{9,8},{10,11... | collective-permute-start | bytes 393224 | tf_op jit(solution)/shard_map/ppermute | solution.py:362
  19.2 1.4 %collective-permute-start.4 = (bf16[256,256]{1,0:T(8,128)(2,1)S(1)}, bf16[256,256]{1,0:T(8,128)(2,1)S(1)}, u32[]{:S(2)}, u32[]{:S(2)}) collective-permute-start(bf16[256,256]{1,0:T(8,128)(2,1)S(1)} %shard_map.96), channel_id=1, source_target_pairs={{0,4},{4,0},{8,12},{12,8},{16,20},{20,16},{24,28},{28,24},{1,5},{5... | collective-permute-start | bytes 393224 | tf_op jit(solution)/shard_map/ppermute | solution.py:362
  19.6 2.7 %collective-permute-start.3 = (bf16[768,256]{1,0:T(8,128)(2,1)S(1)}, bf16[768,256]{1,0:T(8,128)(2,1)S(1)}, u32[]{:S(2)}, u32[]{:S(2)}) collective-permute-start(bf16[768,256]{1,0:T(8,128)(2,1)S(1)} %shard_map.97), channel_id=1, source_target_pairs={{0,4},{4,0},{8,12},{12,8},{16,20},{20,16},{24,28},{28,24},{1,5},{5... | collective-permute-start | bytes 1179656 | tf_op jit(solution)/shard_map/ppermute | solution.py:362
  20.7 9.6 %collective-permute-start.5 = (bf16[256,256]{1,0:T(8,128)(2,1)S(1)}, bf16[256,256]{1,0:T(8,128)(2,1)S(1)}, u32[]{:S(2)}, u32[]{:S(2)}) collective-permute-start(bf16[256,256]{1,0:T(8,128)(2,1)S(1)} %shard_map.99), channel_id=1, source_target_pairs={{0,8},{4,20},{8,0},{12,28},{16,24},{20,4},{24,16},{28,12},{1,9},{5... | collective-permute-start | bytes 393224 | tf_op jit(solution)/shard_map/ppermute | solution.py:369
  22.3 8.6 %collective-permute-start.6 = (bf16[256,256]{1,0:T(8,128)(2,1)S(1)}, bf16[256,256]{1,0:T(8,128)(2,1)S(1)}, u32[]{:S(2)}, u32[]{:S(2)}) collective-permute-start(bf16[256,256]{1,0:T(8,128)(2,1)S(1)} %get-tuple-element.36), channel_id=1, source_target_pairs={{0,16},{4,12},{8,24},{12,4},{16,0},{20,28},{24,8},{28,20},{1,17},{... | collective-permute-start | bytes 393224 | tf_op jit(solution)/shard_map/ppermute | solution.py:369
  23.9 7.1 %collective-permute-start.7 = (bf16[256,256]{1,0:T(8,128)(2,1)S(1)}, bf16[256,256]{1,0:T(8,128)(2,1)S(1)}, u32[]{:S(2)}, u32[]{:S(2)}) collective-permute-start(bf16[256,256]{1,0:T(8,128)(2,1)S(1)} %get-tuple-element.37), channel_id=1, source_target_pairs={{0,24},{4,28},{8,16},{12,20},{16,8},{20,12},{24,0},{28,4},{1,25},{... | collective-permute-start | bytes 393224 | tf_op jit(solution)/shard_map/ppermute | solution.py:369
  25.3 5.6 %copy-start = (f32[256]{0:T(256)S(1)}, f32[256]{0:T(256)}, u32[]{:S(2)}) copy-start(f32[256]{0:T(256)} %param.12) | copy-start | bytes 3076
  25.3 2.0 %collective-permute-start.11 = (bf16[1024,256]{1,0:T(8,128)(2,1)S(1)}, bf16[1024,256]{1,0:T(8,128)(2,1)S(1)}, u32[]{:S(2)}, u32[]{:S(2)}) collective-permute-start(bf16[1024,256]{1,0:T(8,128)(2,1)S(1)} %shard_map.102), channel_id=1, source_target_pairs={{0,4},{4,0},{8,12},{12,8},{16,20},{20,16},{24,28},{28,24},{1,5},{5... | collective-permute-start | bytes 1572872 | tf_op jit(solution)/shard_map/ppermute | solution.py:362
  27.4 6.1 %collective-permute-start.12 = (bf16[256,256]{1,0:T(8,128)(2,1)S(1)}, bf16[256,256]{1,0:T(8,128)(2,1)S(1)}, u32[]{:S(2)}, u32[]{:S(2)}) collective-permute-start(bf16[256,256]{1,0:T(8,128)(2,1)S(1)} %get-tuple-element.46), channel_id=1, source_target_pairs={{0,8},{4,20},{8,0},{12,28},{16,24},{20,4},{24,16},{28,12},{1,9},{5... | collective-permute-start | bytes 393224 | tf_op jit(solution)/shard_map/ppermute | solution.py:369
  28.7 5.1 %collective-permute-start.13 = (bf16[256,256]{1,0:T(8,128)(2,1)S(1)}, bf16[256,256]{1,0:T(8,128)(2,1)S(1)}, u32[]{:S(2)}, u32[]{:S(2)}) collective-permute-start(bf16[256,256]{1,0:T(8,128)(2,1)S(1)} %get-tuple-element.47), channel_id=1, source_target_pairs={{0,16},{4,12},{8,24},{12,4},{16,0},{20,28},{24,8},{28,20},{1,17},{... | collective-permute-start | bytes 393224 | tf_op jit(solution)/shard_map/ppermute | solution.py:369
  30.3 6.7 %collective-permute-start.14 = (bf16[256,256]{1,0:T(8,128)(2,1)S(1)}, bf16[256,256]{1,0:T(8,128)(2,1)S(1)}, u32[]{:S(2)}, u32[]{:S(2)}) collective-permute-start(bf16[256,256]{1,0:T(8,128)(2,1)S(1)} %get-tuple-element.48), channel_id=1, source_target_pairs={{0,24},{4,28},{8,16},{12,20},{16,8},{20,12},{24,0},{28,4},{1,25},{... | collective-permute-start | bytes 393224 | tf_op jit(solution)/shard_map/ppermute | solution.py:369
